TPU v7x, 32 devices: a whole 2x2x4 slice. The times are simulated.
32 devices in a mesh: groups: 2 (over y), gy: 4 (over x, core), gx: 4 (over z).
Axes of the slice: x: 2, y: 2, z: 4, core: 2. Of those that a mesh axis runs over, the one named last changes fastest.
Arguments:
- tokens: bfloat16 [128, 128, 768], P(('groups', 'gy'), 'gx'), parts along dimension 0, may hold values from -6 to 6
- conv_kernel: bfloat16 [7, 7, 768], replicated, may hold values from -0.875 to 0.875
- project_in: bfloat16 [768, 2304], P(('gy', 'gx')), may hold values from -0.21875 to 0.21875
- project_out: bfloat16 [768, 768], P(('gy', 'gx')), may hold values from -0.21875 to 0.21875
- rel_bias: float32 [24, 64, 64], replicated, may hold values from -4 to 4
- expert_in: bfloat16 [32, 1536, 768], P('gy'), may hold values from -0.21875 to 0.21875
- expert_out: bfloat16 [32, 1536, 768], P('gy'), may hold values from -0.15625 to 0.15625
- const_table: float32 [16, 768], replicated, may hold values from -5 to 5
- expert_ids: int32 [128, 128], P(('groups', 'gy'), 'gx'), parts along dimension 0, may hold values from 0 to 33, as said below
- slots: int32 [128, 128], P(('groups', 'gy'), 'gx'), parts along dimension 0, may hold values from 0 to 15, as said below
- const_index: int32 [128, 128], P(('groups', 'gy'), 'gx'), parts along dimension 0, may hold values from 0 to 15
Outputs:
- output: bfloat16 [128, 128, 768], P(('groups', 'gy'), 'gx'), parts along dimension 0
There are 2 independent parts, one for each index of `groups`. A program takes and returns all parts, laid end to end along the dimension named above; an argument that names none is the same for every part. Nothing has to cross between parts.
Inputs may be any that keep to these rules, and one draw needn't show every extreme that they name: `expert_ids`: values below 32 name real experts, 32 the constant expert, 33 the zero expert. Among the tokens of one tile no real expert is named more than 16 times, and in every tile some real expert is named exactly 16 times. Tokens of one tile that name the same real expert have distinct slots; tokens of the constant or zero expert have slot 0.
All inputs are finite; a program needn't handle non-finite values.
Results may differ from a plain program's by a relative error of at most 0.008.
Values may be sent and summed in bfloat16 or wider, within the bound.
No kernel may reach another device: no remote copies, remote signals or barrier semaphores. Data moves between devices by JAX's collectives and lax.ppermute only.
A program may use at most 128 MiB of HBM per device.

v0:
```python
import jax
import jax.numpy as jnp
from jax import lax
from jax.sharding import PartitionSpec as P

HD = 32
EXPERTS = 32
WIN = 8
SHIFT = 4
KERNEL = 7
CAP = 16


def shifted(x, axis, by):
    size = lax.axis_size(axis)
    return lax.ppermute(x, axis, [(i, (i + by) % size) for i in range(size)])


def layer_norm(values):
    values = values.astype(jnp.float32)
    centred = values - jnp.mean(values, axis=-1, keepdims=True)
    spread = jnp.mean(centred * centred, axis=-1, keepdims=True)
    return (centred * lax.rsqrt(spread + 1e-05)).astype(jnp.bfloat16)


def to_windows(grid_field):
    height, width_all, channels = grid_field.shape
    blocks = grid_field.reshape(height // WIN, WIN, width_all // WIN, WIN, channels)
    return blocks.transpose(0, 2, 1, 3, 4).reshape(-1, WIN * WIN, channels)


def from_windows(blocks, height, width_all):
    channels = blocks.shape[-1]
    grid_field = blocks.reshape(height // WIN, width_all // WIN, WIN, WIN, channels)
    return grid_field.transpose(0, 2, 1, 3, 4).reshape(height, width_all, channels)


def attend(region, side_rows, side_cols, project_in, project_out, rel_bias):
    height, width_all, channels = region.shape
    head_count = channels // HD
    row_total = height * width_all
    normed = layer_norm(region).reshape(row_total, channels)
    columns = normed
    mixed = jnp.dot(
        columns,
        lax.all_gather(project_in, ("gy", "gx"), axis=0, tiled=True),
        preferred_element_type=jnp.float32,
    )
    mixed = mixed.astype(jnp.bfloat16)
    windows = to_windows(mixed.reshape(height, width_all, 3 * channels))
    window_count = windows.shape[0]
    query_part = windows[:, :, :channels].reshape(window_count, WIN * WIN, head_count, HD)
    key_part = windows[:, :, channels : 2 * channels].reshape(
        window_count, WIN * WIN, head_count, HD
    )
    value_part = windows[:, :, 2 * channels :].reshape(window_count, WIN * WIN, head_count, HD)
    scores = jnp.einsum("wqhd,wkhd->whqk", query_part, key_part, preferred_element_type=jnp.float32)
    scores = scores * HD ** (-0.5) + rel_bias[None]
    labels = side_rows.astype(jnp.int32)[:, None] * 2 + side_cols.astype(jnp.int32)[None, :]
    label_win = to_windows(labels[:, :, None]).reshape(window_count, WIN * WIN)
    allowed = label_win[:, :, None] == label_win[:, None, :]
    weights = jnp.where(allowed[:, None], jnp.exp(scores), 0.0)
    weights_norm = (weights / jnp.sum(weights, axis=-1, keepdims=True)).astype(jnp.bfloat16)
    context = jnp.einsum(
        "whqk,wkhd->wqhd", weights_norm, value_part, preferred_element_type=jnp.float32
    ).astype(jnp.bfloat16)
    context = from_windows(context.reshape(window_count, WIN * WIN, channels), height, width_all)
    context = context.reshape(row_total, channels)
    columns = context
    update = jnp.dot(
        columns,
        lax.all_gather(project_out, ("gy", "gx"), axis=0, tiled=True),
        preferred_element_type=jnp.float32,
    )
    summed = region.astype(jnp.float32).reshape(row_total, channels) + update
    return summed.astype(jnp.bfloat16).reshape(height, width_all, channels)


def position_code(
    extended, conv_kernel, first_row, first_col, height_all, width_all, region_rows, region_cols
):
    widened = extended.astype(jnp.float32)
    margin = KERNEL // 2
    row_global = first_row + jnp.arange(region_rows)
    col_global = first_col + jnp.arange(region_cols)
    summed = jnp.zeros((region_rows, region_cols, widened.shape[-1]), jnp.float32)
    for row_off in range(KERNEL):
        row_ok = (
            jnp.floor_divide(row_global + row_off - margin, height_all)
            == jnp.floor_divide(row_global, height_all)
        ).astype(jnp.float32)
        for col_off in range(KERNEL):
            col_ok = (
                jnp.floor_divide(col_global + col_off - margin, width_all)
                == jnp.floor_divide(col_global, width_all)
            ).astype(jnp.float32)
            weight = conv_kernel[row_off, col_off].astype(jnp.float32)
            masked = widened[row_off : row_off + region_rows, col_off : col_off + region_cols] * (
                row_ok[:, None, None] * col_ok[None, :, None]
            )
            summed = summed + masked * weight
    centre = widened[margin : margin + region_rows, margin : margin + region_cols]
    return (centre + summed).astype(jnp.bfloat16)


def shards(
    tokens,
    conv_kernel,
    project_in,
    project_out,
    rel_bias,
    expert_in,
    expert_out,
    const_table,
    expert_ids,
    slots,
    const_index,
):
    tile_rows, tile_cols, channels = tokens.shape
    grid_rows = lax.axis_size("gy")
    grid_cols = lax.axis_size("gx")
    height_all = tile_rows * grid_rows
    width_all = tile_cols * grid_cols
    first_row = lax.axis_index("gy") * tile_rows - SHIFT
    first_col = lax.axis_index("gx") * tile_cols - SHIFT
    reach = KERNEL // 2 + SHIFT
    above = shifted(tokens[tile_rows - reach :], "gy", 1)
    stacked = jnp.concatenate([above, tokens], axis=0)
    beside = shifted(stacked[:, tile_cols - reach :], "gx", 1)
    extended = jnp.concatenate([beside, stacked], axis=1)
    encoded = position_code(
        extended, conv_kernel, first_row, first_col, height_all, width_all, tile_rows, tile_cols
    )
    side_rows = (first_row + jnp.arange(tile_rows)) % height_all >= height_all - SHIFT
    side_cols = (first_col + jnp.arange(tile_cols)) % width_all >= width_all - SHIFT
    rolled_out = attend(encoded, side_rows, side_cols, project_in, project_out, rel_bias)
    below = shifted(rolled_out[:SHIFT], "gy", -1)
    joined = jnp.concatenate([rolled_out, below], axis=0)
    right_side = shifted(joined[:, :SHIFT], "gx", -1)
    joined = jnp.concatenate([joined, right_side], axis=1)
    attended = joined[SHIFT : SHIFT + tile_rows, SHIFT : SHIFT + tile_cols]
    normed = layer_norm(attended).reshape(tile_rows * tile_cols, channels)
    expert_of = expert_ids.reshape(-1)
    slot_of = slots.reshape(-1)
    is_real = expert_of < EXPERTS
    row_experts = EXPERTS // grid_rows
    slot_groups = CAP // grid_cols
    tile_count = grid_rows * grid_cols
    buffer_size = CAP * EXPERTS
    target = expert_of // row_experts * grid_cols + slot_of // slot_groups
    position = jnp.where(
        is_real,
        (target * slot_groups + slot_of % slot_groups) * row_experts + expert_of % row_experts,
        buffer_size,
    )
    buffer = jnp.zeros((buffer_size, channels), jnp.bfloat16).at[position].set(normed, mode="drop")
    outgoing = buffer.reshape(tile_count, slot_groups, row_experts, channels)
    incoming = lax.all_to_all(outgoing, ("gy", "gx"), split_axis=0, concat_axis=0, tiled=True)
    flat_rows = incoming.reshape(-1, row_experts, channels)
    hidden = jnp.einsum("nrd,rfd->nrf", flat_rows, expert_in, preferred_element_type=jnp.float32)
    hidden = jax.nn.gelu(hidden, approximate=False).astype(jnp.bfloat16)
    result = jnp.einsum("nrf,rfd->nrd", hidden, expert_out, preferred_element_type=jnp.float32)
    results = lax.all_to_all(
        result.astype(jnp.bfloat16).reshape(incoming.shape),
        ("gy", "gx"),
        split_axis=0,
        concat_axis=0,
        tiled=True,
    )
    picked = results.reshape(buffer_size, channels)[jnp.minimum(position, buffer_size - 1)].astype(
        jnp.float32
    )
    table_rows = const_table.shape[0]
    selector = (const_index.reshape(-1)[:, None] == jnp.arange(table_rows)[None, :]).astype(
        jnp.float32
    )
    constant = jnp.dot(selector, const_table, precision=lax.Precision.HIGHEST)
    mixture = jnp.where(
        is_real[:, None], picked, jnp.where((expert_of == EXPERTS)[:, None], constant, 0.0)
    )
    output = attended.reshape(tile_rows * tile_cols, channels).astype(jnp.float32) + mixture
    return output.astype(jnp.bfloat16).reshape(tile_rows, tile_cols, channels)


def solution(mesh):
    placed = (
        P(("groups", "gy"), "gx", None),
        P(),
        P(("gy", "gx"), None),
        P(("gy", "gx"), None),
        P(),
        P("gy", None, None),
        P("gy", None, None),
        P(),
        P(("groups", "gy"), "gx"),
        P(("groups", "gy"), "gx"),
        P(("groups", "gy"), "gx"),
    )
    return jax.shard_map(
        shards,
        mesh=mesh,
        in_specs=placed,
        out_specs=P(("groups", "gy"), "gx", None),
        check_vma=False,
    )
```

profile of v0, /device:TPU:1, one launch (start us, length us, event | category | flops | bytes accessed | tf_op | source)
XLA Modules:
  0.0 200.6 jit_solution(7501466030233019114)
XLA Ops:
  6.5 0.7 all-gather.3.cloned.1.call-update
  7.3 1.0 slice.322
  8.3 2.7 %collective-permute-start = (bf16[7,32,768]{2,1,0:T(8,128)(2,1)S(1)}, bf16[7,32,768]{2,1,0:T(8,128)(2,1)S(1)}, u32[]{:S(2)}, u32[]{:S(2)}) collective-permute-start(bf16[7,32,768]{2,1,0:T(8,128)(2,1)S(1)} %slice.322), channel_id=1, source_target_pairs={{0,4},{4,8},{8,12},{12,0},{1,5},{5,9},{9,13},{13,1},{2,6},{6,10},{... | collective-permute-start | bytes 1032200 | tf_op jit(solution)/shard_map/ppermute | solution.py:16
  11.1 2.0 convert_reduce_fusion.50
  13.1 2.0 %convert_reduce_fusion.49 = (f32[768]{0:T(1024)}, f32[768]{0:T(1024)}, f32[768]{0:T(1024)}, f32[768]{0:T(1024)}, f32[768]{0:T(1024)}, /*index=5*/f32[768]{0:T(10...) fusion(bf16[7,7,768]{2,1,0:T(8,128)(2,1)} %param.12), kind=kLoop, calls=%fused_computation.339 | loop fusion | flops 14592 | bytes 87552 | tf_op jit(solution)/shard_map/mul | solution.py:101
  15.1 0.6 broadcast_select_fusion.6
  15.7 0.6 broadcast_select_fusion.8
  16.3 0.6 broadcast_select_fusion.10
  16.9 0.5 broadcast_select_fusion
  17.4 0.6 broadcast_select_fusion.2
  18.2 1.6 convert_reduce_fusion.48
  20.1 1.0 copy-done.2
  21.3 1.3 collective-permute-start.1
  22.6 0.6 broadcast_select_fusion.4
  23.2 1.2 copy.29
  24.3 0.7 reshape.2138
  25.0 0.7 reshape.2139
  25.8 11.4 %collective-permute-done.1 = bf16[23,7,768]{2,1,0:T(8,128)(2,1)S(1)} collective-permute-done((bf16[23,7,768]{2,1,0:T(8,128)(2,1)S(1)}, bf16[23,7,768]{2,1,0:T(8,128)(2,1)S(1)}, u32[]{:S(2)}, u32[]{:S(2)}) %collective-permute-start.1) | collective-permute-done | bytes 247328 | tf_op jit(solution)/shard_map/ppermute | solution.py:16
  37.1 1.6 maximum_convert_fusion
  38.7 15.3 %convert_reduce_fusion.1 = (f32[16,32]{1,0:T(8,128)S(1)}, bf16[16,32,768]{2,1,0:T(8,128)(2,1)}) fusion(f32[768]{0:T(1024)} %get-tuple-element.52, f32[16,32]{1,0:T(8,128)S(1)} %get-tuple-element.95, f32[23,39,768]{2,1,0:T(8,128)S(1)} %maximum_convert_fusion, f32[768]{0:T(1024)} %get-tuple-element.53, f32[16,32]{1,0:T(8,128)S(1)} %get-tuple-element.96, ...), kind=kLoop, calls=%fused_computation.219 | loop fusion | flops 58588672 | bytes 78084224 | tf_op jit(solution)/shard_map/reduce_sum | solution.py:21
  54.0 1.5 multiply_reduce_fusion.1
  55.6 1.4 multiply_convert_fusion.1
  56.9 5.9 %all-gather.3.cloned.1.call-done = bf16[768,2304]{1,0:T(8,128)(2,1)} async-done(((bf16[48,2304]{1,0:T(8,128)(2,1)}), bf16[768,2304]{1,0:T(8,128)(2,1)}) %all-gather.3.cloned.1.call-update) | async-done | bytes 3538960 | tf_op jit(solution)/shard_map/all_gather | solution.py:46
  62.9 4.0 %convolution_convert_fusion = bf16[512,2304]{1,0:T(8,128)(2,1)S(1)} fusion(bf16[512,768]{1,0:T(8,128)(2,1)S(1)} %bitcast.138, bf16[768,2304]{1,0:T(8,128)(2,1)} %all-gather.3.cloned.1.call-done), kind=kOutput, calls=%fused_computation.6 | convolution fusion | flops 1813118976 | bytes 6684672 | tf_op jit(solution)/shard_map/dot_general | solution.py:44
  67.3 1.6 copy.27
  68.9 1.5 copy.28
  70.4 0.8 copy.26
  71.5 4.2 %fusion = (f32[8,24,64]{2,1,0:T(8,128)S(1)}, f32[8,24,64,64]{2,3,1,0:T(8,128)S(1)}) fusion(f32[24,64,64]{1,2,0:T(8,128)S(1)} %copy-done.5, pred[8,64,64]{1,2,0:T(8,128)(4,1)S(1)} %broadcast_compare_fusion, bf16[8,64,24,32]{1,3,2,0:T(8,128)(2,1)} %bitcast.136, bf16[8,64,24,32]{1,3,2,0:T(8,128)(2,1)} %bitcast.137), kind=kOutput, calls=%fused_computation.4 | convolution fusion | flops 53465088 | bytes 5193728 | tf_op jit(solution)/shard_map/wqhd,wkhd->whqk/dot_general | solution.py:57
  75.7 2.9 %fusion.153 = bf16[8,64,24,32]{1,3,2,0:T(8,128)(2,1)} fusion(bf16[8,64,24,32]{1,3,2,0:T(8,128)(2,1)S(1)} %bitcast.135, f32[8,24,64,64]{2,3,1,0:T(8,128)S(1)} %get-tuple-element.102, f32[8,24,64]{2,1,0:T(8,128)S(1)} %get-tuple-element.101, f32[24,64,64]{1,2,0:T(8,128)S(1)} %copy-done.5, pred[8,64,64]{1,2,0:T(8,128)(4,1)S(1)} %broadcast_compare_fusion), kind=kOutput, calls=%fused_computation.217 | convolution fusion | flops 54657024 | bytes 5193728 | tf_op jit(solution)/shard_map/whqk,wkhd->wqhd/dot_general | solution.py:64
  78.6 3.4 %copy.31 = bf16[8,64,24,32]{3,2,1,0:T(8,128)(2,1)S(1)} copy(bf16[8,64,24,32]{1,3,2,0:T(8,128)(2,1)} %fusion.153) | data formatting | bytes 1572864 | tf_op jit(solution)/shard_map/convert_element_type | solution.py:66
  82.0 3.0 %reshape_reshape.10 = bf16[2,4,8,8,768]{4,3,2,1,0:T(8,128)(2,1)} reshape(bf16[8,64,24,32]{3,2,1,0:T(8,128)(2,1)S(1)} %copy.31) | data formatting | bytes 1572864 | tf_op jit(solution)/shard_map/reshape;reshape | solution.py:34
  85.0 1.3 copy.32
  86.3 16.3 %all-gather.5.cloned.1.call-done = bf16[768,768]{1,0:T(8,128)(2,1)} async-done(((bf16[48,768]{1,0:T(8,128)(2,1)}), bf16[768,768]{1,0:T(8,128)(2,1)}) %all-gather.5.cloned.1.call-update) | async-done | bytes 1179664 | tf_op jit(solution)/shard_map/all_gather | solution.py:72
  102.5 2.0 %fusion.122 = bf16[512,768]{1,0:T(8,128)(2,1)S(1)} fusion(bf16[512,768]{1,0:T(8,128)(2,1)S(1)} %bitcast.139, bf16[768,768]{1,0:T(8,128)(2,1)} %all-gather.5.cloned.1.call-done, bf16[16,32,768]{2,1,0:T(8,128)(2,1)S(1)} %copy-done.1), kind=kOutput, calls=%fused_computation.182 | convolution fusion | flops 605159424 | bytes 3538944 | tf_op jit(solution)/shard_map/dot_general | solution.py:70
  104.6 0.3 collective-permute-start.2
  105.0 4.8 %collective-permute-done.2 = bf16[4,32,768]{2,1,0:T(8,128)(2,1)S(1)} collective-permute-done((bf16[4,32,768]{2,1,0:T(8,128)(2,1)S(1)}, bf16[4,32,768]{2,1,0:T(8,128)(2,1)S(1)}, u32[]{:S(2)}, u32[]{:S(2)}) %collective-permute-start.2) | collective-permute-done | bytes 196640 | tf_op jit(solution)/shard_map/ppermute | solution.py:16
  109.8 2.1 %collective-permute-start.3 = (bf16[20,4,768]{2,1,0:T(4,128)(2,1)S(1)}, bf16[20,4,768]{2,1,0:T(4,128)(2,1)S(1)}, u32[]{:S(2)}, u32[]{:S(2)}) collective-permute-start(bf16[20,4,768]{2,1,0:T(4,128)(2,1)S(1)} %pad_maximum_fusion.2), channel_id=1, source_target_pairs={{0,3},{1,0},{2,1},{3,2},{4,7},{5,4},{6,5},{7,6},{8,11},{9,8},{10,9... | collective-permute-start | bytes 368648 | tf_op jit(solution)/shard_map/ppermute | solution.py:16
  111.9 2.5 %collective-permute-done.3 = bf16[20,4,768]{2,1,0:T(4,128)(2,1)S(1)} collective-permute-done((bf16[20,4,768]{2,1,0:T(4,128)(2,1)S(1)}, bf16[20,4,768]{2,1,0:T(4,128)(2,1)S(1)}, u32[]{:S(2)}, u32[]{:S(2)}) %collective-permute-start.3) | collective-permute-done | bytes 122912 | tf_op jit(solution)/shard_map/ppermute | solution.py:16
  114.3 0.4 convert_reduce_fusion
  114.7 0.3 multiply_reduce_fusion
  115.3 2.9 %scatter_custom_fusion = bf16[512,768]{1,0:T(8,128)(2,1)S(1)} fusion(s32[512]{0:T(512)S(1)} %bitcast.144, bf16[512,768]{1,0:T(8,128)(2,1)S(1)} %bitcast.140, bf16[]{:T(256)} %constant.515.clone.1), kind=kCustom, calls=%fused_computation.227 | custom fusion | bytes 786434 | tf_op jit(solution)/shard_map/scatter | solution.py:156
  118.2 27.2 %all_to_all.10 = bf16[16,4,8,768]{3,2,1,0:T(8,128)(2,1)S(1)} all-to-all(bf16[16,4,8,768]{3,2,1,0:T(8,128)(2,1)S(1)} %bitcast.132), channel_id=1, replica_groups=mesh['groups'=2,'gy'=4,'gx'=4] {'gy','gx'}, dimensions={0} | all-to-all | bytes 1572864 | tf_op jit(solution)/shard_map/all_to_all | solution.py:158
  145.4 18.0 %fusion.157 = bf16[64,8,768]{2,0,1:T(8,128)(2,1)S(1)} fusion(bf16[8,1536,768]{2,1,0:T(8,128)(2,1)} %param.17, bf16[8,1536,768]{2,1,0:T(8,128)(2,1)} %param.16, bf16[64,8,768]{2,1,0:T(8,128)(2,1)S(1)} %bitcast.141), kind=kOutput, calls=%fused_computation.222 | convolution fusion | flops 2467430400 | bytes 39321600 | tf_op jit(solution)/shard_map/nrf,rfd->nrd/dot_general | solution.py:162
  163.6 1.3 copy.34
  164.9 4.2 %all-to-all-start.1 = ((bf16[16,4,8,768]{3,1,2,0:T(4,128)(2,1)}), bf16[16,4,8,768]{3,1,2,0:T(4,128)(2,1)S(1)}, u32[]{:S(2)}, u32[]{:S(2)}) async-start(bf16[16,4,8,768]{3,1,2,0:T(4,128)(2,1)} %copy.34), calls=%async_computation.1 | async-start | bytes 1572864 | tf_op jit(solution)/shard_map/all_to_all | solution.py:163
  169.4 20.4 %all-to-all-done.1 = bf16[16,4,8,768]{3,1,2,0:T(4,128)(2,1)S(1)} async-done(((bf16[16,4,8,768]{3,1,2,0:T(4,128)(2,1)}), bf16[16,4,8,768]{3,1,2,0:T(4,128)(2,1)S(1)}, u32[]{:S(2)}, u32[]{:S(2)}) %all-to-all-start.1) | async-done | bytes 786464 | tf_op jit(solution)/shard_map/all_to_all | solution.py:163
  189.8 2.0 %gather_fusion = bf16[512,768]{1,0:T(8,128)(2,1)S(1)} fusion(bf16[512,768]{1,0:T(8,128)(2,1)S(1)} %bitcast.128, s32[1024]{0:T(1024)S(1)} %pad_clamp_fusion), kind=kCustom, calls=%fused_computation | custom fusion | bytes 1574912 | tf_op jit(solution)/shard_map/gather | solution.py:170
  191.9 1.9 fusion.121
  (58 shorter events, 2.4 us)
Async XLA Ops:
  6.5 185.3 %copy-start = (f32[16,768]{1,0:T(8,128)S(1)}, f32[16,768]{1,0:T(8,128)}, u32[]{:S(2)}) copy-start(f32[16,768]{1,0:T(8,128)} %param.18) | copy-start | bytes 147460
  6.5 13.5 %copy-start.3 = (bf16[16,32,768]{2,1,0:T(8,128)(2,1)S(1)}, bf16[16,32,768]{2,1,0:T(8,128)(2,1)}, u32[]{:S(2)}) copy-start(bf16[16,32,768]{2,1,0:T(8,128)(2,1)} %param.11) | copy-start | bytes 2359300
  6.5 56.3 %all-gather.3.cloned.1.call-start = ((), (), s32[]{:S(2)}) async-start(), calls=%async_computation.2 | async-start | bytes 3760128 | tf_op jit(solution)/shard_map/all_gather | solution.py:46
  7.3 95.3 %all-gather.5.cloned.1.call-start = ((), (), s32[]{:S(2)}) async-start(), calls=%async_computation.3 | async-start | bytes 1253376 | tf_op jit(solution)/shard_map/all_gather | solution.py:72
  8.3 11.7 %collective-permute-start = (bf16[7,32,768]{2,1,0:T(8,128)(2,1)S(1)}, bf16[7,32,768]{2,1,0:T(8,128)(2,1)S(1)}, u32[]{:S(2)}, u32[]{:S(2)}) collective-permute-start(bf16[7,32,768]{2,1,0:T(8,128)(2,1)S(1)} %slice.322), channel_id=1, source_target_pairs={{0,4},{4,8},{8,12},{12,0},{1,5},{5,9},{9,13},{13,1},{2,6},{6,10},{... | collective-permute-start | bytes 1032200 | tf_op jit(solution)/shard_map/ppermute | solution.py:16
  13.1 10.0 %copy-start.4 = (f32[24,64,64]{2,1,0:T(8,128)S(1)}, f32[24,64,64]{2,1,0:T(8,128)}, u32[]{:S(2)}) copy-start(f32[24,64,64]{2,1,0:T(8,128)} %param.15) | copy-start | bytes 1179652
  20.1 4.3 %copy-start.6 = (s32[16,32]{1,0:T(8,128)S(1)}, s32[16,32]{1,0:T(8,128)}, u32[]{:S(2)}) copy-start(s32[16,32]{1,0:T(8,128)} %param.19) | copy-start | bytes 6148
  20.1 4.9 %copy-start.7 = (s32[16,32]{1,0:T(8,128)S(1)}, s32[16,32]{1,0:T(8,128)}, u32[]{:S(2)}) copy-start(s32[16,32]{1,0:T(8,128)} %param.20) | copy-start | bytes 6148
  20.1 1.1 copy-start.2
  21.3 15.9 %collective-permute-start.1 = (bf16[23,7,768]{2,1,0:T(8,128)(2,1)S(1)}, bf16[23,7,768]{2,1,0:T(8,128)(2,1)S(1)}, u32[]{:S(2)}, u32[]{:S(2)}) collective-permute-start(bf16[23,7,768]{2,1,0:T(8,128)(2,1)S(1)} %slice.431), channel_id=1, source_target_pairs={{0,1},{1,2},{2,3},{3,0},{4,5},{5,6},{6,7},{7,4},{8,9},{9,10},{10,1... | collective-permute-start | bytes 741896 | tf_op jit(solution)/shard_map/ppermute | solution.py:16
  70.4 1.1 copy-start.5
  85.0 17.6 %copy-start.1 = (bf16[16,32,768]{2,1,0:T(8,128)(2,1)S(1)}, bf16[16,32,768]{2,1,0:T(8,128)(2,1)}, u32[]{:S(2)}) copy-start(bf16[16,32,768]{2,1,0:T(8,128)(2,1)} %get-tuple-element.59) | copy-start | bytes 2359300
  102.5 2.4 %copy-start.9 = (s32[512,1]{0,1:T(1,128)S(1)}, s32[512,1]{0,1:T(1,128)}, u32[]{:S(2)}) copy-start(s32[512,1]{0,1:T(1,128)} %reshape.2138) | copy-start | bytes 6148
  102.5 2.4 %copy-start.10 = (s32[512,1]{0,1:T(1,128)S(1)}, s32[512,1]{0,1:T(1,128)}, u32[]{:S(2)}) copy-start(s32[512,1]{0,1:T(1,128)} %reshape.2139) | copy-start | bytes 6148
  104.6 5.1 %collective-permute-start.2 = (bf16[4,32,768]{2,1,0:T(8,128)(2,1)S(1)}, bf16[4,32,768]{2,1,0:T(8,128)(2,1)S(1)}, u32[]{:S(2)}, u32[]{:S(2)}) collective-permute-start(bf16[4,32,768]{2,1,0:T(8,128)(2,1)S(1)} %bitcast.142), channel_id=1, source_target_pairs={{0,12},{4,0},{8,4},{12,8},{1,13},{5,1},{9,5},{13,9},{2,14},{6,2},{... | collective-permute-start | bytes 589832 | tf_op jit(solution)/shard_map/ppermute | solution.py:16
  109.8 4.5 %collective-permute-start.3 = (bf16[20,4,768]{2,1,0:T(4,128)(2,1)S(1)}, bf16[20,4,768]{2,1,0:T(4,128)(2,1)S(1)}, u32[]{:S(2)}, u32[]{:S(2)}) collective-permute-start(bf16[20,4,768]{2,1,0:T(4,128)(2,1)S(1)} %pad_maximum_fusion.2), channel_id=1, source_target_pairs={{0,3},{1,0},{2,1},{3,2},{4,7},{5,4},{6,5},{7,6},{8,11},{9,8},{10,9... | collective-permute-start | bytes 368648 | tf_op jit(solution)/shard_map/ppermute | solution.py:16
  163.6 5.7 %copy-start.8 = (s32[16,32]{1,0:T(8,128)S(1)}, s32[16,32]{1,0:T(8,128)}, u32[]{:S(2)}) copy-start(s32[16,32]{1,0:T(8,128)} %param.21) | copy-start | bytes 6148
  164.9 24.9 %all-to-all-start.1 = ((bf16[16,4,8,768]{3,1,2,0:T(4,128)(2,1)}), bf16[16,4,8,768]{3,1,2,0:T(4,128)(2,1)S(1)}, u32[]{:S(2)}, u32[]{:S(2)}) async-start(bf16[16,4,8,768]{3,1,2,0:T(4,128)(2,1)} %copy.34), calls=%async_computation.1 | async-start | bytes 1572864 | tf_op jit(solution)/shard_map/all_to_all | solution.py:163
Sparse Core Ops, SparseCore 0:
  9.7 53.1 all-gather.2
  65.2 37.3 all-gather.4
where the time goes:
time: 202 us; the launch traced here: 201 us
  waiting for transfers between devices  61.9 us (31%)
  matrix products  33.1 us (16%)
  other arithmetic  30.4 us (15%)
  blocking collectives  27.2 us (13%)
  local copies, waits for them, and re-layouts  23.8 us (12%)
  between operations  13.7 us (7%)
  starting transfers between devices  10.6 us (5%)
    all_to_all x1, blocking collectives, shards(): lax.all_to_all(outgoing, ('gy', 'gx'), split_axis=0, concat_axis=0, tiled...  27.2 us
    all_to_all x1, waiting for transfers between devices, shards(): lax.all_to_all(result.astype(jnp.bfloat16).reshape(incoming.shape), ('gy'...  20.4 us
    ppermute x4, waiting for transfers between devices, shifted(): return lax.ppermute(x, axis, [(i, (i + by) % size) for i in range(size)])  18.6 us
    dot_general x1, matrix products, shards(): jnp.einsum('nrf,rfd->nrd', hidden, expert_out, preferred_element_type=jnp...  18 us
    all_gather x1, waiting for transfers between devices, attend(): lax.all_gather(project_out, ('gy', 'gx'), axis=0, tiled=True)  16.3 us
    reduce_sum x2, other arithmetic, layer_norm(): centred = values - jnp.mean(values, axis=-1, keepdims=True)  15.7 us
    ppermute x4, starting transfers between devices, shifted(): return lax.ppermute(x, axis, [(i, (i + by) % size) for i in range(size)])  6.36 us
    all_gather x1, waiting for transfers between devices, attend(): lax.all_gather(project_in, ('gy', 'gx'), axis=0, tiled=True)  5.91 us
  transfers between devices with their start and end apart: 7, of which 6 were waited for; matrix products, arithmetic and copies ran while one was open for 28% of the time, Pallas kernels for 0%

commit v1 on v0

--- a/solution.py
+++ b/solution.py
@@ -144,31 +144,22 @@
     slot_of = slots.reshape(-1)
     is_real = expert_of < EXPERTS
     row_experts = EXPERTS // grid_rows
-    slot_groups = CAP // grid_cols
-    tile_count = grid_rows * grid_cols
     buffer_size = CAP * EXPERTS
-    target = expert_of // row_experts * grid_cols + slot_of // slot_groups
-    position = jnp.where(
-        is_real,
-        (target * slot_groups + slot_of % slot_groups) * row_experts + expert_of % row_experts,
-        buffer_size,
+    position = jnp.where(is_real, expert_of * CAP + slot_of, buffer_size)
+    place = jnp.arange(buffer_size, dtype=jnp.int32)
+    onehot = (position[None, :] == place[:, None]).astype(jnp.bfloat16)
+    buffer = jnp.dot(onehot, normed, preferred_element_type=jnp.float32).astype(jnp.bfloat16)
+    outgoing = buffer.reshape(grid_rows, row_experts, CAP, channels)
+    incoming = lax.all_to_all(outgoing, "gy", split_axis=0, concat_axis=0, tiled=True)
+    hidden = jnp.einsum("nrsd,rfd->rnsf", incoming, expert_in, preferred_element_type=jnp.float32)
+    hidden = jax.nn.gelu(hidden, approximate=False).astype(jnp.bfloat16)
+    result = jnp.einsum("rnsf,rfd->nrsd", hidden, expert_out, preferred_element_type=jnp.float32)
+    results = lax.all_to_all(
+        result.astype(jnp.bfloat16), "gy", split_axis=0, concat_axis=0, tiled=True
     )
-    buffer = jnp.zeros((buffer_size, channels), jnp.bfloat16).at[position].set(normed, mode="drop")
-    outgoing = buffer.reshape(tile_count, slot_groups, row_experts, channels)
-    incoming = lax.all_to_all(outgoing, ("gy", "gx"), split_axis=0, concat_axis=0, tiled=True)
-    flat_rows = incoming.reshape(-1, row_experts, channels)
-    hidden = jnp.einsum("nrd,rfd->nrf", flat_rows, expert_in, preferred_element_type=jnp.float32)
-    hidden = jax.nn.gelu(hidden, approximate=False).astype(jnp.bfloat16)
-    result = jnp.einsum("nrf,rfd->nrd", hidden, expert_out, preferred_element_type=jnp.float32)
-    results = lax.all_to_all(
-        result.astype(jnp.bfloat16).reshape(incoming.shape),
-        ("gy", "gx"),
-        split_axis=0,
-        concat_axis=0,
-        tiled=True,
-    )
-    picked = results.reshape(buffer_size, channels)[jnp.minimum(position, buffer_size - 1)].astype(
-        jnp.float32
+    back = (position[:, None] == place[None, :]).astype(jnp.bfloat16)
+    picked = jnp.dot(
+        back, results.reshape(buffer_size, channels), preferred_element_type=jnp.float32
     )
     table_rows = const_table.shape[0]
     selector = (const_index.reshape(-1)[:, None] == jnp.arange(table_rows)[None, :]).astype(

time: 202 us -> 177 us (0.88)
  blocking collectives: 27.2 us -> 13.6 us
  waiting for transfers between devices: 61.9 us -> 50.2 us
  local copies, waits for them, and re-layouts: 23.8 us -> 17.6 us
  matrix products: 33.1 us -> 37.4 us
    all_to_all x1, blocking collectives: 27.2 us -> 13.6 us  [shards(): lax.all_to_all(outgoing, 'gy', split_axis=0, concat_axis=0, tiled=True)]
    all_to_all x1, waiting for transfers between devices: 20.4 us -> 9.78 us  [shards(): lax.all_to_all(result.astype(jnp.bfloat16), 'gy', split_axis=0, concat_ax...]
    dot_general x1 -> x4, matrix products: 18 us -> 23.5 us  [the longest x1 11.4 us: shards(): jnp.einsum('rnsf,rfd->nrsd', hidden, expert_out, preferred_element_type=j...]
    scatter x1 -> x0, local copies, waits for them, and re-layouts: 2.87 us -> none  [shards(): jnp.zeros((buffer_size, channels), jnp.bfloat16).at[position]]
    reshape x4 -> x0, local copies, waits for them, and re-layouts: 2.77 us -> none  [the longest x2 1.44 us: shards(): result.astype(jnp.bfloat16).reshape(incoming.shape)]
    gather x1 -> x0, local copies, waits for them, and re-layouts: 2.03 us -> none  [shards(): results.reshape(buffer_size, channels)]
  transfers between devices with their start and end apart: 7 -> 7, of which waited for: 6 -> 6; matrix products, arithmetic and copies ran while one was open for 28% -> 33% of each run, Pallas kernels for 0% -> 0%
where the time goes in v1:
time: 177 us; the launch traced here: 175 us
  waiting for transfers between devices  50.2 us (28%)
  matrix products  37.4 us (21%)
  other arithmetic  31.6 us (18%)
  local copies, waits for them, and re-layouts  17.6 us (10%)
  between operations  13.7 us (8%)
  blocking collectives  13.6 us (8%)
  starting transfers between devices  10.9 us (6%)
    ppermute x4, waiting for transfers between devices, shifted(): return lax.ppermute(x, axis, [(i, (i + by) % size) for i in range(size)])  18.4 us
    all_gather x1, waiting for transfers between devices, attend(): lax.all_gather(project_out, ('gy', 'gx'), axis=0, tiled=True)  16.3 us
    reduce_sum x2, other arithmetic, layer_norm(): centred = values - jnp.mean(values, axis=-1, keepdims=True)  15.7 us
    all_to_all x1, blocking collectives, shards(): lax.all_to_all(outgoing, 'gy', split_axis=0, concat_axis=0, tiled=True)  13.6 us
    dot_general x1, matrix products, shards(): jnp.einsum('rnsf,rfd->nrsd', hidden, expert_out, preferred_element_type=j...  11.4 us
    dot_general x1, matrix products, shards(): jnp.einsum('nrsd,rfd->rnsf', incoming, expert_in, preferred_element_type=...  9.92 us
    all_to_all x1, waiting for transfers between devices, shards(): lax.all_to_all(result.astype(jnp.bfloat16), 'gy', split_axis=0, concat_ax...  9.78 us
    ppermute x4, starting transfers between devices, shifted(): return lax.ppermute(x, axis, [(i, (i + by) % size) for i in range(size)])  6.36 us
  transfers between devices with their start and end apart: 7, of which 6 were waited for; matrix products, arithmetic and copies ran while one was open for 33% of the time, Pallas kernels for 0%

profile of v1, /device:TPU:1, one launch (start us, length us, event | category | flops | bytes accessed | tf_op | source)
XLA Modules:
  0.0 175.0 jit_solution(924828014919475012)
XLA Ops:
  6.5 0.7 all-gather.3.cloned.1.call-update
  7.3 1.0 slice.322
  8.3 2.7 %collective-permute-start = (bf16[7,32,768]{2,1,0:T(8,128)(2,1)S(1)}, bf16[7,32,768]{2,1,0:T(8,128)(2,1)S(1)}, u32[]{:S(2)}, u32[]{:S(2)}) collective-permute-start(bf16[7,32,768]{2,1,0:T(8,128)(2,1)S(1)} %slice.322), channel_id=1, source_target_pairs={{0,4},{4,8},{8,12},{12,0},{1,5},{5,9},{9,13},{13,1},{2,6},{6,10},{... | collective-permute-start | bytes 1032200 | tf_op jit(solution)/shard_map/ppermute | solution.py:16
  11.1 2.0 %convert_reduce_fusion.50 = (f32[768]{0:T(1024)S(1)}, f32[768]{0:T(1024)S(1)}, f32[768]{0:T(1024)S(1)}, f32[768]{0:T(1024)S(1)}, f32[768]{0:T(1024)S(1)}, /*inde...) fusion(bf16[7,7,768]{2,1,0:T(8,128)(2,1)} %param.12), kind=kLoop, calls=%fused_computation.334 | loop fusion | flops 14592 | bytes 87552 | tf_op jit(solution)/shard_map/mul | solution.py:101
  13.1 2.0 %convert_reduce_fusion.49 = (f32[768]{0:T(1024)}, f32[768]{0:T(1024)}, f32[768]{0:T(1024)}, f32[768]{0:T(1024)}, f32[768]{0:T(1024)}, /*index=5*/f32[768]{0:T(10...) fusion(bf16[7,7,768]{2,1,0:T(8,128)(2,1)} %param.12), kind=kLoop, calls=%fused_computation.333 | loop fusion | flops 14592 | bytes 87552 | tf_op jit(solution)/shard_map/mul | solution.py:101
  15.1 0.6 broadcast_select_fusion.7
  15.7 0.6 broadcast_select_fusion.9
  16.3 0.6 broadcast_select_fusion.11
  16.9 0.6 broadcast_select_fusion.1
  17.5 0.5 broadcast_select_fusion.3
  18.2 1.3 broadcast_compare_fusion.1
  19.5 1.6 convert_reduce_fusion.48
  21.4 1.0 copy-done.2
  22.5 1.3 collective-permute-start.1
  23.9 0.6 broadcast_select_fusion.5
  24.5 1.2 copy.29
  25.6 0.6 lt.32
  26.3 11.2 %collective-permute-done.1 = bf16[23,7,768]{2,1,0:T(8,128)(2,1)S(1)} collective-permute-done((bf16[23,7,768]{2,1,0:T(8,128)(2,1)S(1)}, bf16[23,7,768]{2,1,0:T(8,128)(2,1)S(1)}, u32[]{:S(2)}, u32[]{:S(2)}) %collective-permute-start.1) | collective-permute-done | bytes 247328 | tf_op jit(solution)/shard_map/ppermute | solution.py:16
  37.5 1.6 maximum_convert_fusion
  39.1 15.3 %convert_reduce_fusion.1 = (f32[16,32]{1,0:T(8,128)S(1)}, bf16[16,32,768]{2,1,0:T(8,128)(2,1)}) fusion(f32[768]{0:T(1024)} %get-tuple-element.54, f32[16,32]{1,0:T(8,128)S(1)} %get-tuple-element.95, f32[23,39,768]{2,1,0:T(8,128)S(1)} %maximum_convert_fusion, f32[768]{0:T(1024)} %get-tuple-element.55, f32[16,32]{1,0:T(8,128)S(1)} %get-tuple-element.96, ...), kind=kLoop, calls=%fused_computation.219 | loop fusion | flops 58588672 | bytes 78084224 | tf_op jit(solution)/shard_map/reduce_sum | solution.py:21
  54.4 1.5 multiply_reduce_fusion.1
  55.9 1.4 multiply_convert_fusion.1
  57.3 5.0 %all-gather.3.cloned.1.call-done = bf16[768,2304]{1,0:T(8,128)(2,1)} async-done(((bf16[48,2304]{1,0:T(8,128)(2,1)}), bf16[768,2304]{1,0:T(8,128)(2,1)}) %all-gather.3.cloned.1.call-update) | async-done | bytes 3538960 | tf_op jit(solution)/shard_map/all_gather | solution.py:46
  62.3 4.0 %convolution_convert_fusion = bf16[512,2304]{1,0:T(8,128)(2,1)S(1)} fusion(bf16[512,768]{1,0:T(8,128)(2,1)S(1)} %bitcast.71, bf16[768,2304]{1,0:T(8,128)(2,1)} %all-gather.3.cloned.1.call-done), kind=kOutput, calls=%fused_computation.8 | convolution fusion | flops 1813118976 | bytes 6684672 | tf_op jit(solution)/shard_map/dot_general | solution.py:44
  66.8 1.6 copy.27
  68.3 1.5 copy.28
  69.9 0.8 copy.26
  71.0 4.2 %fusion.4 = (f32[8,24,64]{2,1,0:T(8,128)S(1)}, f32[8,24,64,64]{2,3,1,0:T(8,128)S(1)}) fusion(f32[24,64,64]{1,2,0:T(8,128)S(1)} %copy-done.5, pred[8,64,64]{1,2,0:T(8,128)(4,1)S(1)} %broadcast_compare_fusion, bf16[8,64,24,32]{1,3,2,0:T(8,128)(2,1)} %bitcast.68, bf16[8,64,24,32]{1,3,2,0:T(8,128)(2,1)} %bitcast.69), kind=kOutput, calls=%fused_computation.6 | convolution fusion | flops 53465088 | bytes 5193728 | tf_op jit(solution)/shard_map/wqhd,wkhd->whqk/dot_general | solution.py:57
  75.2 2.9 %fusion.148 = bf16[8,64,24,32]{1,3,2,0:T(8,128)(2,1)} fusion(bf16[8,64,24,32]{1,3,2,0:T(8,128)(2,1)S(1)} %bitcast.67, f32[8,24,64,64]{2,3,1,0:T(8,128)S(1)} %get-tuple-element.102, f32[8,24,64]{2,1,0:T(8,128)S(1)} %get-tuple-element.101, f32[24,64,64]{1,2,0:T(8,128)S(1)} %copy-done.5, pred[8,64,64]{1,2,0:T(8,128)(4,1)S(1)} %broadcast_compare_fusion), kind=kOutput, calls=%fused_computation.217 | convolution fusion | flops 54657024 | bytes 5193728 | tf_op jit(solution)/shard_map/whqk,wkhd->wqhd/dot_general | solution.py:64
  78.0 3.4 %copy.31 = bf16[8,64,24,32]{3,2,1,0:T(8,128)(2,1)S(1)} copy(bf16[8,64,24,32]{1,3,2,0:T(8,128)(2,1)} %fusion.148) | data formatting | bytes 1572864 | tf_op jit(solution)/shard_map/convert_element_type | solution.py:66
  81.4 3.0 %reshape_reshape.10 = bf16[2,4,8,8,768]{4,3,2,1,0:T(8,128)(2,1)} reshape(bf16[8,64,24,32]{3,2,1,0:T(8,128)(2,1)S(1)} %copy.31) | data formatting | bytes 1572864 | tf_op jit(solution)/shard_map/reshape;reshape | solution.py:34
  84.4 1.3 copy.32
  85.7 16.3 %all-gather.5.cloned.1.call-done = bf16[768,768]{1,0:T(8,128)(2,1)} async-done(((bf16[48,768]{1,0:T(8,128)(2,1)}), bf16[768,768]{1,0:T(8,128)(2,1)}) %all-gather.5.cloned.1.call-update) | async-done | bytes 1179664 | tf_op jit(solution)/shard_map/all_gather | solution.py:72
  102.0 2.1 %fusion.117 = bf16[512,768]{1,0:T(8,128)(2,1)S(1)} fusion(bf16[512,768]{1,0:T(8,128)(2,1)S(1)} %bitcast.72, bf16[768,768]{1,0:T(8,128)(2,1)} %all-gather.5.cloned.1.call-done, bf16[16,32,768]{2,1,0:T(8,128)(2,1)S(1)} %copy-done.1), kind=kOutput, calls=%fused_computation.182 | convolution fusion | flops 605159424 | bytes 3538944 | tf_op jit(solution)/shard_map/dot_general | solution.py:70
  104.5 4.8 %collective-permute-done.2 = bf16[4,32,768]{2,1,0:T(8,128)(2,1)S(1)} collective-permute-done((bf16[4,32,768]{2,1,0:T(8,128)(2,1)S(1)}, bf16[4,32,768]{2,1,0:T(8,128)(2,1)S(1)}, u32[]{:S(2)}, u32[]{:S(2)}) %collective-permute-start.2) | collective-permute-done | bytes 196640 | tf_op jit(solution)/shard_map/ppermute | solution.py:16
  109.3 2.1 %collective-permute-start.3 = (bf16[20,4,768]{2,1,0:T(4,128)(2,1)S(1)}, bf16[20,4,768]{2,1,0:T(4,128)(2,1)S(1)}, u32[]{:S(2)}, u32[]{:S(2)}) collective-permute-start(bf16[20,4,768]{2,1,0:T(4,128)(2,1)S(1)} %pad_maximum_fusion.2), channel_id=1, source_target_pairs={{0,3},{1,0},{2,1},{3,2},{4,7},{5,4},{6,5},{7,6},{8,11},{9,8},{10,9... | collective-permute-start | bytes 368648 | tf_op jit(solution)/shard_map/ppermute | solution.py:16
  111.4 2.4 %collective-permute-done.3 = bf16[20,4,768]{2,1,0:T(4,128)(2,1)S(1)} collective-permute-done((bf16[20,4,768]{2,1,0:T(4,128)(2,1)S(1)}, bf16[20,4,768]{2,1,0:T(4,128)(2,1)S(1)}, u32[]{:S(2)}, u32[]{:S(2)}) %collective-permute-start.3) | collective-permute-done | bytes 122912 | tf_op jit(solution)/shard_map/ppermute | solution.py:16
  113.8 0.4 convert_reduce_fusion
  114.2 0.3 multiply_reduce_fusion
  114.8 0.6 convolution_convert_fusion.1
  115.4 13.6 %all_to_all.10 = bf16[4,8,16,768]{3,2,1,0:T(8,128)(2,1)S(1)} all-to-all(bf16[4,8,16,768]{3,2,1,0:T(8,128)(2,1)S(1)} %bitcast.74), channel_id=1, replica_groups=mesh['groups'=2,'gy'=4,'gx'=4] {'gy'}, dimensions={0} | all-to-all | bytes 1572864 | tf_op jit(solution)/shard_map/all_to_all | solution.py:153
  129.0 9.9 %fusion.161 = (u8[4,16,1536]{2,1,0:T(8,128)(4,1)S(1)}, u8[4,16,1536]{2,1,0:T(8,128)(4,1)S(1)}, f32[8,4,16,1536]{3,2,1,0:T(8,128)S(1)}) fusion(bf16[8,1536,768]{2,1,0:T(8,128)(2,1)} %param.16, bf16[4,8,16,768]{3,2,1,0:T(8,128)(2,1)S(1)} %all_to_all.10), kind=kOutput, calls=%fused_computation.230 | convolution fusion | flops 1217986560 | bytes 23003136 | tf_op jit(solution)/shard_map/nrsd,rfd->rnsf/dot_general | solution.py:154
  139.0 11.4 %fusion.154 = bf16[4,8,16,768]{3,2,0,1:T(8,128)(2,1)S(1)} fusion(bf16[8,1536,768]{2,1,0:T(8,128)(2,1)} %param.17, f32[8,4,16,1536]{3,2,1,0:T(8,128)S(1)} %get-tuple-element.103, u8[4,16,1536]{2,1,0:T(8,128)(4,1)S(1)} %get-tuple-element.6, u8[4,16,1536]{2,1,0:T(8,128)(4,1)S(1)} %get-tuple-element.5), kind=kOutput, calls=%fused_computation.223 | convolution fusion | flops 1263403008 | bytes 23003136 | tf_op jit(solution)/shard_map/rnsf,rfd->nrsd/dot_general | solution.py:156
  150.4 0.9 copy.34
  151.3 4.5 %all-to-all-start.1 = ((bf16[4,8,16,768]{3,2,1,0:T(8,128)(2,1)}), bf16[4,8,16,768]{3,2,1,0:T(8,128)(2,1)S(1)}, u32[]{:S(2)}, u32[]{:S(2)}) async-start(bf16[4,8,16,768]{3,2,1,0:T(8,128)(2,1)} %copy.34), calls=%async_computation.1 | async-start | bytes 1572864 | tf_op jit(solution)/shard_map/all_to_all | solution.py:157
  156.0 0.8 fusion.166
  156.8 9.8 %all-to-all-done.1 = bf16[4,8,16,768]{3,2,1,0:T(8,128)(2,1)S(1)} async-done(((bf16[4,8,16,768]{3,2,1,0:T(8,128)(2,1)}), bf16[4,8,16,768]{3,2,1,0:T(8,128)(2,1)S(1)}, u32[]{:S(2)}, u32[]{:S(2)}) %all-to-all-start.1) | async-done | bytes 786464 | tf_op jit(solution)/shard_map/all_to_all | solution.py:157
  166.6 1.6 fusion.116
  (55 shorter events, 2.3 us)
Async XLA Ops:
  6.5 149.5 %copy-start = (f32[16,768]{1,0:T(8,128)S(1)}, f32[16,768]{1,0:T(8,128)}, u32[]{:S(2)}) copy-start(f32[16,768]{1,0:T(8,128)} %param.18) | copy-start | bytes 147460
  6.5 14.8 %copy-start.3 = (bf16[16,32,768]{2,1,0:T(8,128)(2,1)S(1)}, bf16[16,32,768]{2,1,0:T(8,128)(2,1)}, u32[]{:S(2)}) copy-start(bf16[16,32,768]{2,1,0:T(8,128)(2,1)} %param.11) | copy-start | bytes 2359300
  6.5 55.8 %all-gather.3.cloned.1.call-start = ((), (), s32[]{:S(2)}) async-start(), calls=%async_computation.2 | async-start | bytes 3760128 | tf_op jit(solution)/shard_map/all_gather | solution.py:46
  7.3 94.7 %all-gather.5.cloned.1.call-start = ((), (), s32[]{:S(2)}) async-start(), calls=%async_computation.3 | async-start | bytes 1253376 | tf_op jit(solution)/shard_map/all_gather | solution.py:72
  8.3 13.0 %collective-permute-start = (bf16[7,32,768]{2,1,0:T(8,128)(2,1)S(1)}, bf16[7,32,768]{2,1,0:T(8,128)(2,1)S(1)}, u32[]{:S(2)}, u32[]{:S(2)}) collective-permute-start(bf16[7,32,768]{2,1,0:T(8,128)(2,1)S(1)} %slice.322), channel_id=1, source_target_pairs={{0,4},{4,8},{8,12},{12,0},{1,5},{5,9},{9,13},{13,1},{2,6},{6,10},{... | collective-permute-start | bytes 1032200 | tf_op jit(solution)/shard_map/ppermute | solution.py:16
  15.1 9.3 %copy-start.4 = (f32[24,64,64]{2,1,0:T(8,128)S(1)}, f32[24,64,64]{2,1,0:T(8,128)}, u32[]{:S(2)}) copy-start(f32[24,64,64]{2,1,0:T(8,128)} %param.15) | copy-start | bytes 1179652
  21.4 1.1 copy-start.2
  22.5 15.0 %collective-permute-start.1 = (bf16[23,7,768]{2,1,0:T(8,128)(2,1)S(1)}, bf16[23,7,768]{2,1,0:T(8,128)(2,1)S(1)}, u32[]{:S(2)}, u32[]{:S(2)}) collective-permute-start(bf16[23,7,768]{2,1,0:T(8,128)(2,1)S(1)} %slice.429), channel_id=1, source_target_pairs={{0,1},{1,2},{2,3},{3,0},{4,5},{5,6},{6,7},{7,4},{8,9},{9,10},{10,1... | collective-permute-start | bytes 741896 | tf_op jit(solution)/shard_map/ppermute | solution.py:16
  69.9 1.1 copy-start.5
  84.4 17.6 %copy-start.1 = (bf16[16,32,768]{2,1,0:T(8,128)(2,1)S(1)}, bf16[16,32,768]{2,1,0:T(8,128)(2,1)}, u32[]{:S(2)}) copy-start(bf16[16,32,768]{2,1,0:T(8,128)(2,1)} %get-tuple-element.59) | copy-start | bytes 2359300
  102.0 2.4 %copy-start.6 = (s32[16,32]{1,0:T(8,128)S(1)}, s32[16,32]{1,0:T(8,128)}, u32[]{:S(2)}) copy-start(s32[16,32]{1,0:T(8,128)} %param.19) | copy-start | bytes 6148
  102.0 2.4 %copy-start.7 = (s32[16,32]{1,0:T(8,128)S(1)}, s32[16,32]{1,0:T(8,128)}, u32[]{:S(2)}) copy-start(s32[16,32]{1,0:T(8,128)} %param.20) | copy-start | bytes 6148
  102.0 9.4 %copy-start.10 = (pred[512]{0:T(512)(128)(4,1)S(1)}, pred[512]{0:T(512)(128)(4,1)}, u32[]{:S(2)}) copy-start(pred[512]{0:T(512)(128)(4,1)} %lt.32) | copy-start | bytes 1540
  104.1 5.1 %collective-permute-start.2 = (bf16[4,32,768]{2,1,0:T(8,128)(2,1)S(1)}, bf16[4,32,768]{2,1,0:T(8,128)(2,1)S(1)}, u32[]{:S(2)}, u32[]{:S(2)}) collective-permute-start(bf16[4,32,768]{2,1,0:T(8,128)(2,1)S(1)} %bitcast.75), channel_id=1, source_target_pairs={{0,12},{4,0},{8,4},{12,8},{1,13},{5,1},{9,5},{13,9},{2,14},{6,2},{... | collective-permute-start | bytes 589832 | tf_op jit(solution)/shard_map/ppermute | solution.py:16
  109.3 4.5 %collective-permute-start.3 = (bf16[20,4,768]{2,1,0:T(4,128)(2,1)S(1)}, bf16[20,4,768]{2,1,0:T(4,128)(2,1)S(1)}, u32[]{:S(2)}, u32[]{:S(2)}) collective-permute-start(bf16[20,4,768]{2,1,0:T(4,128)(2,1)S(1)} %pad_maximum_fusion.2), channel_id=1, source_target_pairs={{0,3},{1,0},{2,1},{3,2},{4,7},{5,4},{6,5},{7,6},{8,11},{9,8},{10,9... | collective-permute-start | bytes 368648 | tf_op jit(solution)/shard_map/ppermute | solution.py:16
  150.3 5.5 %copy-start.9 = (pred[16,32]{1,0:T(8,128)(4,1)S(1)}, pred[16,32]{1,0:T(8,128)(4,1)}, u32[]{:S(2)}) copy-start(pred[16,32]{1,0:T(8,128)(4,1)} %get-tuple-element.63) | copy-start | bytes 1540
  150.4 5.5 %copy-start.8 = (s32[16,32]{1,0:T(8,128)S(1)}, s32[16,32]{1,0:T(8,128)}, u32[]{:S(2)}) copy-start(s32[16,32]{1,0:T(8,128)} %param.21) | copy-start | bytes 6148
  151.3 15.3 %all-to-all-start.1 = ((bf16[4,8,16,768]{3,2,1,0:T(8,128)(2,1)}), bf16[4,8,16,768]{3,2,1,0:T(8,128)(2,1)S(1)}, u32[]{:S(2)}, u32[]{:S(2)}) async-start(bf16[4,8,16,768]{3,2,1,0:T(8,128)(2,1)} %copy.34), calls=%async_computation.1 | async-start | bytes 1572864 | tf_op jit(solution)/shard_map/all_to_all | solution.py:157
Sparse Core Ops, SparseCore 0:
  9.7 52.6 all-gather.2
  64.6 37.3 all-gather.4

commit v2 on v1

v2 whole, which is shorter than its diff:
```python
import functools

import jax
import jax.numpy as jnp
from jax import lax
from jax.experimental import pallas as pl
from jax.experimental.pallas import tpu as pltpu
from jax.sharding import PartitionSpec as P

HD = 32
EXPERTS = 32
WIN = 8
SHIFT = 4
KERNEL = 7
CAP = 16
LANES = 128
GROUP = LANES // HD
SPOTS = WIN * WIN
HALO = 8
VMEM = pl.BlockSpec(memory_space=pltpu.VMEM)
SMEM = pl.BlockSpec(memory_space=pltpu.SMEM)
ANY = pl.BlockSpec(memory_space=pl.ANY)
LARGEST = 3.38e38


def shifted(x, axis, by):
    size = lax.axis_size(axis)
    return lax.ppermute(x, axis, [(i, (i + by) % size) for i in range(size)])


def shifted_both(x, by):
    rows, cols = lax.axis_size("gy"), lax.axis_size("gx")
    pairs = [
        (i * cols + j, ((i + by) % rows) * cols + (j + by) % cols)
        for i in range(rows)
        for j in range(cols)
    ]
    return lax.ppermute(x, ("gy", "gx"), pairs)


def exchanged(x, axis, mask):
    size = lax.axis_size(axis)
    return lax.ppermute(x, axis, [(i, i ^ mask) for i in range(size)])


def normalized(values):
    centred = values - jnp.mean(values, axis=-1, keepdims=True)
    spread = jnp.mean(centred * centred, axis=-1, keepdims=True)
    return (centred * lax.rsqrt(spread + 1e-05)).astype(jnp.bfloat16)


def encode_kernel(place, tokens, above, beside, taps, encoded, normed, extended, weights):
    rows, cols, channels = tokens.shape
    reach = KERNEL // 2 + SHIFT
    extended[:, :HALO] = beside[...].astype(jnp.float32)
    extended[:reach, HALO:] = above[...].astype(jnp.float32)
    extended[reach:, HALO:] = tokens[...].astype(jnp.float32)
    weights[...] = taps[...].astype(jnp.float32)
    inner_row = jnp.where(place[0] == 0, 0.0, 1.0)
    first_col = place[1] == 0
    window_cols = cols // WIN
    col = lax.broadcasted_iota(jnp.int32, (WIN, LANES), 0)

    def block(index, _):
        lanes = pl.ds(pl.multiple_of(index * LANES, LANES), LANES)
        for tile in range(window_cols):
            sums = [None] * rows
            for col_off in range(KERNEL):
                column = [
                    jnp.broadcast_to(weights[row_off, pl.ds(col_off, 1), lanes], (WIN, LANES))
                    for row_off in range(KERNEL)
                ]
                if tile == 0:
                    near = (col < SHIFT) == (col + col_off < reach)
                    keep = jnp.where(near | jnp.logical_not(first_col), 1.0, 0.0)
                for row in range(rows + KERNEL - 1):
                    here = extended[row, tile * WIN : tile * WIN + WIN, lanes]
                    after = extended[row, (tile + 1) * WIN : (tile + 2) * WIN, lanes]
                    line = jnp.where(col > col_off, here, after)
                    line = pltpu.roll(line, WIN - 1 - col_off, 0)
                    if tile == 0:
                        line = line * keep
                    cut = line * inner_row if SHIFT <= row < reach + KERNEL // 2 else line
                    for out in range(max(0, row - KERNEL + 1), min(rows, row + 1)):
                        row_off = row - out
                        same = (out < SHIFT) == (row < reach)
                        term = (line if same else cut) * column[row_off]
                        if row_off == KERNEL // 2 and col_off == KERNEL // 2:
                            term = term + line
                        sums[out] = term if sums[out] is None else sums[out] + term
            for window_row in range(rows // WIN):
                stacked = jnp.concatenate(sums[window_row * WIN : (window_row + 1) * WIN], axis=0)
                first = (window_row * window_cols + tile) * SPOTS
                encoded[first : first + SPOTS, lanes] = stacked.astype(jnp.bfloat16)
        return 0

    lax.fori_loop(0, channels // LANES, block, 0)

    def norm(index, _):
        part = pl.ds(pl.multiple_of(index * SPOTS, SPOTS), SPOTS)
        normed[part, :] = normalized(encoded[part, :].astype(jnp.float32))
        return 0

    lax.fori_loop(0, rows * cols // SPOTS, norm, 0)


def encode(place, tokens, above, beside, taps):
    rows, cols, channels = tokens.shape
    flat = jax.ShapeDtypeStruct((rows * cols, channels), jnp.bfloat16)
    reach = KERNEL // 2 + SHIFT
    return pl.pallas_call(
        encode_kernel,
        out_shape=(flat, flat),
        in_specs=[SMEM] + [VMEM] * 4,
        out_specs=(VMEM, VMEM),
        scratch_shapes=[
            pltpu.VMEM((rows + reach, cols + HALO, channels), jnp.float32),
            pltpu.VMEM(taps.shape, jnp.float32),
        ],
        compiler_params=pltpu.CompilerParams(vmem_limit_bytes=12 * 1024 * 1024),
        cost_estimate=pl.CostEstimate(
            flops=2 * rows * cols * channels * KERNEL * KERNEL,
            bytes_accessed=6 * rows * cols * channels,
            transcendentals=0,
        ),
        name="encode",
    )(place, tokens, above, beside, taps)


def fetch(place, grid_cols, pieces, ids, target, sems):
    copies = []
    for piece, parts in zip(pieces, ids, strict=True):
        size = piece.shape[0] // len(parts)
        for at, (mask_row, mask_col) in enumerate(parts):
            if mask_row is None:
                first = 0
            else:
                owner = (place[0] ^ mask_row) * grid_cols + (place[1] ^ mask_col)
                first = pl.multiple_of(owner * size, 16)
            copy = pltpu.make_async_copy(
                piece.at[pl.ds(at * size, size), pl.ds(0, target.shape[1])],
                target.at[pl.ds(first, size), :],
                sems.at[len(copies)],
            )
            copy.start()
            copies.append(copy)
    return copies


def attend_kernel(shape, ids, grid_cols, *refs):
    rows, cols = shape
    place, normed, rel_bias = refs[:3]
    context, weight, mixed, bias, sems = refs[3 + len(ids) :]
    channels = normed.shape[1]
    copies = fetch(place, grid_cols, refs[3 : 3 + len(ids)], ids, weight, sems)
    groups = channels // LANES
    for head in range(rel_bias.shape[0]):
        at = head % GROUP * SPOTS
        bias[head // GROUP, :, at : at + SPOTS] = rel_bias[head]
    for copy in copies:
        copy.wait()
    wide = 2 * LANES

    def project(index, _):
        lanes = pl.ds(pl.multiple_of(index * wide, wide), wide)
        mixed[:, lanes] = jnp.dot(
            normed[...], weight[:, lanes], preferred_element_type=jnp.float32
        ).astype(jnp.bfloat16)
        return 0

    lax.fori_loop(0, 3 * channels // wide, project, 0)

    window_cols = cols // WIN
    keys = GROUP * SPOTS
    query_at = lax.broadcasted_iota(jnp.int32, (SPOTS, keys), 0)
    key_at = lax.broadcasted_iota(jnp.int32, (SPOTS, keys), 1) % SPOTS
    row_differs = (query_at < SPOTS // 2) != (key_at < SPOTS // 2)
    col_differs = (query_at % WIN < SHIFT) != (key_at % WIN < SHIFT)
    lane = lax.broadcasted_iota(jnp.int32, (SPOTS, LANES), 1) // HD
    head_masks = [jnp.where(lane == h, 1.0, 0.0).astype(jnp.bfloat16) for h in range(GROUP)]
    block_row = lax.broadcasted_iota(jnp.int32, (keys, keys), 0) // SPOTS
    block_col = lax.broadcasted_iota(jnp.int32, (keys, keys), 1) // SPOTS
    same_head = jnp.where(block_row == block_col, 1.0, 0.0).astype(jnp.bfloat16)

    def window(index, _):
        part = pl.ds(pl.multiple_of(index * SPOTS, SPOTS), SPOTS)
        cut_rows = jnp.logical_and(place[0] == 0, index < window_cols)
        cut_cols = jnp.logical_and(place[1] == 0, index % window_cols == 0)
        hidden = (row_differs & cut_rows) | (col_differs & cut_cols)
        barrier = jnp.where(hidden, -1e30, 0.0)
        all_weights = []
        for group in range(groups):
            first = group * LANES
            query = mixed[part, first : first + LANES]
            key = mixed[part, channels + first : channels + first + LANES]
            key_all = jnp.concatenate([key * m for m in head_masks], axis=0)
            scores = lax.dot_general(
                query, key_all, (((1,), (1,)), ((), ())), preferred_element_type=jnp.float32
            )
            all_weights.append(jnp.exp(scores * HD ** (-0.5) + (bias[group] + barrier)))
        weights = jnp.concatenate(all_weights, axis=0)
        total = jnp.dot(
            jnp.minimum(weights, LARGEST).astype(jnp.bfloat16),
            same_head,
            preferred_element_type=jnp.float32,
        )
        probs = (weights * pl.reciprocal(total)).astype(jnp.bfloat16)
        for group in range(groups):
            first = group * LANES
            value = mixed[part, 2 * channels + first : 2 * channels + first + LANES]
            value_all = jnp.concatenate([value * m for m in head_masks], axis=0)
            context[part, first : first + LANES] = jnp.dot(
                probs[group * SPOTS : (group + 1) * SPOTS],
                value_all,
                preferred_element_type=jnp.float32,
            ).astype(jnp.bfloat16)
        return 0

    lax.fori_loop(0, rows * cols // SPOTS, window, 0)


def attend(place, shape, normed, rel_bias, pieces, grid_cols):
    rows, cols = shape
    channels = normed.shape[1]
    ids = [p[1] for p in pieces]
    return pl.pallas_call(
        functools.partial(attend_kernel, shape, ids, grid_cols),
        out_shape=jax.ShapeDtypeStruct((rows * cols, channels), jnp.bfloat16),
        in_specs=[SMEM, VMEM, VMEM] + [ANY] * len(pieces),
        out_specs=VMEM,
        scratch_shapes=[
            pltpu.VMEM((channels, 3 * channels), jnp.bfloat16),
            pltpu.VMEM((rows * cols, 3 * channels), jnp.bfloat16),
            pltpu.VMEM((channels // LANES, SPOTS, GROUP * SPOTS), jnp.float32),
            pltpu.SemaphoreType.DMA((sum(len(p) for p in ids),)),
        ],
        compiler_params=pltpu.CompilerParams(vmem_limit_bytes=14 * 1024 * 1024),
        cost_estimate=pl.CostEstimate(
            flops=2 * rows * cols * channels * 4 * channels,
            bytes_accessed=6 * channels * channels,
            transcendentals=rows * cols * SPOTS * channels // HD,
        ),
        name="attend",
    )(place, normed, rel_bias, *[p[0] for p in pieces])


def project_kernel(shape, ids, grid_cols, *refs):
    rows, cols = shape
    place, context, encoded = refs[:3]
    rolled, top, side, corner, weight, sems = refs[3 + len(ids) :]
    channels = context.shape[1]
    for copy in fetch(place, grid_cols, refs[3 : 3 + len(ids)], ids, weight, sems):
        copy.wait()
    window_cols = cols // WIN
    wide = 2 * LANES
    sublane = lax.broadcasted_iota(jnp.int32, (WIN, wide), 0)

    def finish(index, _):
        lanes = pl.ds(pl.multiple_of(index * wide, wide), wide)
        update = jnp.dot(context[...], weight[:, lanes], preferred_element_type=jnp.float32)
        summed = encoded[:, lanes].astype(jnp.float32) + update
        edge = []
        for row in range(rows):
            tiles = []
            for tile in range(window_cols):
                first = (row // WIN * window_cols + tile) * SPOTS + row % WIN * WIN
                tiles.append(summed[first : first + WIN])
            for pair in range(window_cols // 2):
                both = jnp.concatenate(tiles[2 * pair : 2 * pair + 2], axis=0)
                both = both.astype(jnp.bfloat16)
                at = pair * 2 * WIN
                rolled[row, at : at + 2 * WIN, lanes] = both
                if row < SHIFT:
                    top[row, at : at + 2 * WIN, lanes] = both
            edge.append(tiles[0])
        for quad in range(rows // 4):
            halves = [
                jnp.where(
                    sublane < SHIFT,
                    edge[4 * quad + two],
                    pltpu.roll(edge[4 * quad + two + 1], SHIFT, 0),
                )
                for two in (0, 2)
            ]
            packed = jnp.concatenate(halves, axis=0).astype(jnp.bfloat16)
            if quad == 0:
                corner[:, lanes] = packed
            else:
                side[(quad - 1) * 16 : quad * 16, lanes] = packed
        return 0

    lax.fori_loop(0, channels // wide, finish, 0)


def project(place, shape, context, encoded, pieces, grid_cols):
    rows, cols = shape
    channels = context.shape[1]
    bf16 = functools.partial(jax.ShapeDtypeStruct, dtype=jnp.bfloat16)
    ids = [p[1] for p in pieces]
    return pl.pallas_call(
        functools.partial(project_kernel, shape, ids, grid_cols),
        out_shape=(
            bf16((rows, cols, channels)),
            bf16((SHIFT, cols, channels)),
            bf16(((rows - SHIFT) * SHIFT, channels)),
            bf16((SHIFT * SHIFT, channels)),
        ),
        in_specs=[SMEM, VMEM, VMEM] + [ANY] * len(pieces),
        out_specs=(VMEM,) * 4,
        scratch_shapes=[
            pltpu.VMEM((channels, channels), jnp.bfloat16),
            pltpu.SemaphoreType.DMA((sum(len(p) for p in ids),)),
        ],
        compiler_params=pltpu.CompilerParams(vmem_limit_bytes=12 * 1024 * 1024),
        cost_estimate=pl.CostEstimate(
            flops=2 * rows * cols * channels * channels,
            bytes_accessed=2 * channels * channels,
            transcendentals=0,
        ),
        name="project",
    )(place, context, encoded, *[p[0] for p in pieces])


def dispatch_kernel(place, rolled, below, right, corner, position, *refs):
    rows, cols, channels = rolled.shape
    attended, outgoing, normed = refs[0], refs[1:-1], refs[-1]
    sublane = lax.broadcasted_iota(jnp.int32, (WIN, channels), 0)
    for row in range(rows):
        if row < rows - SHIFT:
            line, beside, at = rolled[row + SHIFT], right, row
        else:
            line, beside, at = below[row + SHIFT - rows], corner, row + SHIFT - rows
        line = line.astype(jnp.float32)
        tiles = [
            pltpu.roll(line[tile * WIN : (tile + 1) * WIN], SHIFT, 0) for tile in range(cols // WIN)
        ]
        block = at * SHIFT // 16 * 16
        last = beside[block : block + 16].astype(jnp.float32)
        within = at * SHIFT - block
        last = last[within // WIN * WIN : within // WIN * WIN + WIN]
        tiles.append(last if within % WIN else pltpu.roll(last, SHIFT, 0))
        line = jnp.concatenate(
            [
                jnp.where(sublane < SHIFT, tiles[tile], tiles[tile + 1])
                for tile in range(cols // WIN)
            ],
            axis=0,
        )
        attended[row * cols : (row + 1) * cols] = line.astype(jnp.bfloat16)
        normed[row * cols : (row + 1) * cols] = normalized(line)
    for mask, target in enumerate(outgoing):
        count = target.shape[0]
        spot = lax.broadcasted_iota(jnp.int32, (count, rows * cols), 0)
        spot = spot + (place[0] ^ mask) * count
        chosen = jnp.where(position[...] == spot, 1.0, 0.0).astype(jnp.bfloat16)
        target[...] = jnp.dot(
            chosen, normed[...], preferred_element_type=jnp.float32
        ).astype(jnp.bfloat16)


def dispatch(place, rolled, below, right, corner, position, grid_rows):
    rows, cols, channels = rolled.shape
    bf16 = functools.partial(jax.ShapeDtypeStruct, dtype=jnp.bfloat16)
    slot_rows = EXPERTS * CAP // grid_rows
    return pl.pallas_call(
        dispatch_kernel,
        out_shape=(bf16((rows * cols, channels)),) + (bf16((slot_rows, channels)),) * grid_rows,
        in_specs=[SMEM] + [VMEM] * 5,
        out_specs=(VMEM,) * (grid_rows + 1),
        scratch_shapes=[pltpu.VMEM((rows * cols, channels), jnp.bfloat16)],
        compiler_params=pltpu.CompilerParams(vmem_limit_bytes=24 * 1024 * 1024),
        name="dispatch",
    )(place, rolled, below, right, corner, position)


def expert_kernel(count, *refs):
    incoming, (weight_in, weight_out), results = refs[:count], refs[count : count + 2], refs[count + 2 :]
    rows = jnp.concatenate([ref[...] for ref in incoming], axis=0)
    hidden = lax.dot_general(
        rows, weight_in[0], (((1,), (1,)), ((), ())), preferred_element_type=jnp.float32
    )
    hidden = (0.5 * hidden * (1.0 + lax.erf(hidden * 0.5**0.5))).astype(jnp.bfloat16)
    result = jnp.dot(hidden, weight_out[0], preferred_element_type=jnp.float32)
    result = result.astype(jnp.bfloat16)
    for at, ref in enumerate(results):
        ref[...] = result[at * CAP : (at + 1) * CAP]


def serve(incoming, expert_in, expert_out):
    count = len(incoming)
    experts, hidden, channels = expert_in.shape
    slot = pl.BlockSpec((CAP, channels), lambda e: (e, 0))
    weight = pl.BlockSpec((1, hidden, channels), lambda e: (e, 0, 0))
    return pl.pallas_call(
        functools.partial(expert_kernel, count),
        grid=(experts,),
        out_shape=tuple(jax.ShapeDtypeStruct(x.shape, x.dtype) for x in incoming),
        in_specs=[slot] * count + [weight, weight],
        out_specs=(slot,) * count,
        compiler_params=pltpu.CompilerParams(vmem_limit_bytes=32 * 1024 * 1024),
        cost_estimate=pl.CostEstimate(
            flops=4 * count * CAP * experts * hidden * channels,
            bytes_accessed=4 * experts * hidden * channels,
            transcendentals=count * CAP * experts * hidden,
        ),
        name="experts",
    )(*incoming, expert_in, expert_out)


def combine_kernel(place, attended, position, constant_at, table, *refs):
    results, output = refs[:-1], refs[-1]
    tokens = attended.shape[0]
    total = attended[...].astype(jnp.float32)
    for mask, result in enumerate(results):
        count = result.shape[0]
        spot = lax.broadcasted_iota(jnp.int32, (tokens, count), 1)
        spot = spot + (place[0] ^ mask) * count
        chosen = jnp.where(position[...] == spot, 1.0, 0.0).astype(jnp.bfloat16)
        total = total + jnp.dot(chosen, result[...], preferred_element_type=jnp.float32)
    entries = table.shape[0]
    spot = lax.broadcasted_iota(jnp.int32, (tokens, entries), 1)
    chosen = jnp.where(constant_at[...] == spot, 1.0, 0.0).astype(jnp.bfloat16)
    rest = table[...]
    constant = None
    for _ in range(3):
        part = rest.astype(jnp.bfloat16)
        rest = rest - part.astype(jnp.float32)
        term = jnp.dot(chosen, part, preferred_element_type=jnp.float32)
        constant = term if constant is None else constant + term
    output[...] = (total + constant).astype(jnp.bfloat16)


def combine(place, attended, position, constant_at, table, results):
    return pl.pallas_call(
        combine_kernel,
        out_shape=jax.ShapeDtypeStruct(attended.shape, jnp.bfloat16),
        in_specs=[SMEM] + [VMEM] * (4 + len(results)),
        out_specs=VMEM,
        compiler_params=pltpu.CompilerParams(vmem_limit_bytes=24 * 1024 * 1024),
        name="combine",
    )(place, attended, position, constant_at, table, *results)


def stacked(parts):
    return jnp.concatenate([p[0] for p in parts], axis=0), sum([p[1] for p in parts], [])


def along(part, axis, mask):
    array, ids = part
    change = (mask, 0) if axis == "gy" else (0, mask)
    return exchanged(array, axis, mask), [(a ^ change[0], b ^ change[1]) for a, b in ids]


def held(*values):
    return lax.optimization_barrier(values)


def shards(
    tokens,
    conv_kernel,
    project_in,
    project_out,
    rel_bias,
    expert_in,
    expert_out,
    const_table,
    expert_ids,
    slots,
    const_index,
):
    rows, cols, channels = tokens.shape
    grid_rows, grid_cols = lax.axis_size("gy"), lax.axis_size("gx")
    place = jnp.stack([lax.axis_index("gy"), lax.axis_index("gx")]).astype(jnp.int32)
    reach = KERNEL // 2 + SHIFT
    above = shifted(tokens[rows - reach :], "gy", 1)
    quick = grid_rows == 4 and grid_cols == 4
    if quick:
        own = [(0, 0)]
        line = [exchanged(project_in, "gx", mask) for mask in (3, 2, 1)]
        both = jnp.concatenate([project_in, project_out], axis=1)
        facing = exchanged(both, "gy", 2)
        *line, facing, above = held(*line, facing, above)
    edge = jnp.concatenate([above[:, cols - HALO :], tokens[:, cols - HALO :]], axis=0)
    beside = shifted(edge, "gx", 1)
    if quick:
        line = stacked([(array, [(0, mask)]) for array, mask in zip(line, (3, 2, 1), strict=True)])
        facing = (facing, [(2, 0)])
        pair = stacked([(project_out, own), (facing[0][:, 3 * channels :], facing[1])])
        far = along(line, "gy", 2)
        plane = stacked([pair] + [along(pair, "gx", mask) for mask in (3, 2, 1)])
    else:
        whole = [(None, None)]
        pieces_in = [(lax.all_gather(project_in, ("gy", "gx"), axis=0, tiled=True), whole)]
        pieces_out = [(lax.all_gather(project_out, ("gy", "gx"), axis=0, tiled=True), whole)]
    encoded, normed = encode(place, tokens, above, beside, conv_kernel)
    if quick:
        near = [(project_in, own), line, facing]
        pieces_in = near + [far] + [along(part, "gy", 1) for part in near + [far]]
        pieces_out = [plane, along(plane, "gy", 1)]
    context = attend(place, (rows, cols), normed, rel_bias, pieces_in, grid_cols)
    rolled, top, side, corner = project(
        place, (rows, cols), context, encoded, pieces_out, grid_cols
    )
    below = shifted(top, "gy", -1)
    right = shifted(side, "gx", -1)
    last = shifted_both(corner, -1)
    expert_of, slot_of = expert_ids.reshape(-1), slots.reshape(-1)
    position = jnp.where(expert_of < EXPERTS, expert_of * CAP + slot_of, -1)
    constant_at = jnp.where(expert_of == EXPERTS, const_index.reshape(-1), -1)
    attended, *outgoing = dispatch(
        place, rolled, below, right, last, position[None, :], grid_rows
    )
    incoming = [outgoing[0]] + [exchanged(outgoing[m], "gy", m) for m in range(1, grid_rows)]
    served = serve(incoming, expert_in, expert_out)
    results = [served[0]] + [exchanged(served[m], "gy", m) for m in range(1, grid_rows)]
    output = combine(
        place, attended, position[:, None], constant_at[:, None], const_table, results
    )
    return output.reshape(rows, cols, channels)


def solution(mesh):
    placed = (
        P(("groups", "gy"), "gx", None),
        P(),
        P(("gy", "gx"), None),
        P(("gy", "gx"), None),
        P(),
        P("gy", None, None),
        P("gy", None, None),
        P(),
        P(("groups", "gy"), "gx"),
        P(("groups", "gy"), "gx"),
        P(("groups", "gy"), "gx"),
    )
    return jax.shard_map(
        shards,
        mesh=mesh,
        in_specs=placed,
        out_specs=P(("groups", "gy"), "gx", None),
        check_vma=False,
    )
```

time: 177 us -> 135 us (0.76)
  Pallas kernels: 0 us -> 43.5 us
  matrix products: 37.4 us -> 0 us
  other arithmetic: 31.6 us -> 2.73 us
  blocking collectives: 13.6 us -> 0 us
  between operations: 13.7 us -> 0.24 us
  starting transfers between devices: 10.9 us -> 22.4 us
  local copies, waits for them, and re-layouts: 17.6 us -> 14 us
    ppermute x0 -> x20, waiting for transfers between devices: none -> 51.5 us  [the longest x19 48.5 us: exchanged(): return lax.ppermute(x, axis, [(i, i ^ mask) for i in range(size)])]
    pallas_call x0 -> x6, Pallas kernels: none -> 43.5 us  [the longest x1 13.3 us: serve(): pl.pallas_call(functools.partial(expert_kernel, count), grid=(experts,),...]
    dot_general x9 -> x0, matrix products: 37.4 us -> none  [the longest x1 11.4 us: shards(): jnp.einsum('rnsf,rfd->nrsd', hidden, expert_out, preferred_element_type=j...]
    all_gather x2 -> x0, waiting for transfers between devices: 21.2 us -> none  [the longest x1 16.3 us: attend(): lax.all_gather(project_out, ('gy', 'gx'), axis=0, tiled=True)]
    ppermute x0 -> x20, starting transfers between devices: none -> 18.9 us  [the longest x19 17.7 us: exchanged(): return lax.ppermute(x, axis, [(i, i ^ mask) for i in range(size)])]
    ppermute x4, waiting for transfers between devices: 18.4 us -> 0.01 us  [shifted(): return lax.ppermute(x, axis, [(i, (i + by) % size) for i in range(size)])]
    reduce_sum x4 -> x0, other arithmetic: 17.5 us -> none  [the longest x2 15.7 us: layer_norm(): centred = values - jnp.mean(values, axis=-1, keepdims=True)]
    all_to_all x1 -> x0, blocking collectives: 13.6 us -> none  [shards(): lax.all_to_all(outgoing, 'gy', split_axis=0, concat_axis=0, tiled=True)]
  transfers between devices with their start and end apart: 7 -> 24, of which waited for: 6 -> 10; matrix products, arithmetic and copies ran while one was open for 33% -> 4% of each run, Pallas kernels for 0% -> 16%
where the time goes in v2:
time: 135 us; the launch traced here: 134 us
  waiting for transfers between devices  51.5 us (38%)
  Pallas kernels  43.5 us (32%)
  starting transfers between devices  22.4 us (17%)
  local copies, waits for them, and re-layouts  14 us (10%)
  other arithmetic  2.73 us (2%)
    ppermute x19, waiting for transfers between devices, exchanged(): return lax.ppermute(x, axis, [(i, i ^ mask) for i in range(size)])  48.5 us
    ppermute x19, starting transfers between devices, exchanged(): return lax.ppermute(x, axis, [(i, i ^ mask) for i in range(size)])  17.7 us
    pallas_call x1, Pallas kernels, serve(): pl.pallas_call(functools.partial(expert_kernel, count), grid=(experts,),...  13.3 us
    pallas_call x1, Pallas kernels, attend(): pl.pallas_call(functools.partial(attend_kernel, shape, ids, grid_cols), o...  12.1 us
    unnamed x17, local copies, waits for them, and re-layouts  11.4 us
    pallas_call x1, Pallas kernels, encode(): pl.pallas_call(encode_kernel, out_shape=(flat, flat), in_specs=[SMEM] + [...  9.94 us
    ppermute x4, starting transfers between devices, shifted(): return lax.ppermute(x, axis, [(i, (i + by) % size) for i in range(size)])  3.55 us
    pallas_call x1, Pallas kernels, project(): pl.pallas_call(functools.partial(project_kernel, shape, ids, grid_cols),...  3.48 us
  transfers between devices with their start and end apart: 24, of which 10 were waited for; matrix products, arithmetic and copies ran while one was open for 4% of the time, Pallas kernels for 16%

profile of v2, /device:TPU:1, one launch (start us, length us, event | category | flops | bytes accessed | tf_op | source)
XLA Modules:
  0.0 134.3 jit_solution(7876548224006127655)
XLA Ops:
  0.0 1.0 slice.12
  1.0 2.7 %collective-permute-start.4 = (bf16[7,32,768]{2,1,0:T(8,128)(2,1)S(1)}, bf16[7,32,768]{2,1,0:T(8,128)(2,1)S(1)}, u32[]{:S(2)}, u32[]{:S(2)}) collective-permute-start(bf16[7,32,768]{2,1,0:T(8,128)(2,1)S(1)} %slice.12), channel_id=1, source_target_pairs={{0,4},{4,8},{8,12},{12,0},{1,5},{5,9},{9,13},{13,1},{2,6},{6,10},{... | collective-permute-start | bytes 1032200 | tf_op jit(solution)/shard_map/ppermute | solution.py:28
  3.7 1.0 pad_maximum_fusion
  4.7 3.6 %collective-permute-start = (bf16[48,2304]{1,0:T(8,128)(2,1)}, bf16[48,2304]{1,0:T(8,128)(2,1)S(1)}, u32[]{:S(2)}, u32[]{:S(2)}) collective-permute-start(bf16[48,2304]{1,0:T(8,128)(2,1)} %refs_3_.1), channel_id=1, source_target_pairs={{0,3},{1,2},{2,1},{3,0},{4,7},{5,6},{6,5},{7,4},{8,11},{9,10},{10,... | collective-permute-start | bytes 663560 | tf_op jit(solution)/shard_map/ppermute | solution.py:43
  8.3 0.3 collective-permute-start.2
  8.6 5.5 %collective-permute-done = bf16[48,2304]{1,0:T(8,128)(2,1)S(1)} collective-permute-done((bf16[48,2304]{1,0:T(8,128)(2,1)}, bf16[48,2304]{1,0:T(8,128)(2,1)S(1)}, u32[]{:S(2)}, u32[]{:S(2)}) %collective-permute-start) | collective-permute-done | bytes 221216 | tf_op jit(solution)/shard_map/ppermute | solution.py:43
  14.1 13.2 %collective-permute-done.1 = bf16[48,2304]{1,0:T(8,128)(2,1)S(1)} collective-permute-done((bf16[48,2304]{1,0:T(8,128)(2,1)}, bf16[48,2304]{1,0:T(8,128)(2,1)S(1)}, u32[]{:S(2)}, u32[]{:S(2)}) %collective-permute-start.1) | collective-permute-done | bytes 221216 | tf_op jit(solution)/shard_map/ppermute | solution.py:43
  27.4 1.2 collective-permute-start.6
  28.6 0.9 constant_dynamic-update-slice_fusion.7
  29.5 0.9 pad_maximum_fusion.2
  30.4 2.3 %collective-permute-start.11 = (bf16[96,768]{1,0:T(8,128)(2,1)S(1)}, bf16[96,768]{1,0:T(8,128)(2,1)S(1)}, u32[]{:S(2)}, u32[]{:S(2)}) collective-permute-start(bf16[96,768]{1,0:T(8,128)(2,1)S(1)} %pad_maximum_fusion.2), channel_id=1, source_target_pairs={{0,3},{1,2},{2,1},{3,0},{4,7},{5,6},{6,5},{7,4},{8,11},{9,10},{10,... | collective-permute-start | bytes 442376 | tf_op jit(solution)/shard_map/ppermute | solution.py:43
  32.7 0.9 slice.14
  33.6 1.0 collective-permute-start.8
  34.6 1.4 %collective-permute-start.13 = (bf16[96,768]{1,0:T(8,128)(2,1)S(1)}, bf16[96,768]{1,0:T(8,128)(2,1)S(1)}, u32[]{:S(2)}, u32[]{:S(2)}) collective-permute-start(bf16[96,768]{1,0:T(8,128)(2,1)S(1)} %pad_maximum_fusion.2), channel_id=1, source_target_pairs={{0,1},{1,0},{2,3},{3,2},{4,5},{5,4},{6,7},{7,6},{8,9},{9,8},{10,11... | collective-permute-start | bytes 442376 | tf_op jit(solution)/shard_map/ppermute | solution.py:43
  36.0 1.1 collective-permute-done.11
  37.1 5.8 %collective-permute-done.6.refs_6_ = bf16[144,2304]{1,0:T(8,128)(2,1)S(1)} collective-permute-done((bf16[144,2304]{1,0:T(8,128)(2,1)S(1)}, bf16[144,2304]{1,0:T(8,128)(2,1)S(1)}, u32[]{:S(2)}, u32[]{:S(2)}) %collective-permute-start.6) | collective-permute-done | bytes 663584 | tf_op jit(solution)/shard_map/ppermute | solution.py:43
  42.9 1.9 %collective-permute-start.10 = (bf16[144,2304]{1,0:T(8,128)(2,1)S(1)}, bf16[144,2304]{1,0:T(8,128)(2,1)}, u32[]{:S(2)}, u32[]{:S(2)}) collective-permute-start(bf16[144,2304]{1,0:T(8,128)(2,1)S(1)} %collective-permute-done.6.refs_6_), channel_id=1, source_target_pairs={{0,4},{4,0},{8,12},{12,8},{1,5},{5,1},{9,13},{13,9},{2,6},{6,2},{1... | collective-permute-start | bytes 1990664 | tf_op jit(solution)/shard_map/ppermute | solution.py:43
  44.8 5.9 %collective-permute-done.12 = bf16[96,768]{1,0:T(8,128)(2,1)S(1)} collective-permute-done((bf16[96,768]{1,0:T(8,128)(2,1)S(1)}, bf16[96,768]{1,0:T(8,128)(2,1)S(1)}, u32[]{:S(2)}, u32[]{:S(2)}) %collective-permute-start.12) | collective-permute-done | bytes 147488 | tf_op jit(solution)/shard_map/ppermute | solution.py:43
  50.7 1.2 collective-permute-start.14
  51.9 0.1 collective-permute-start.9
  52.0 0.4 collective-permute-start.7
  52.5 1.1 copy-done.1
  53.6 0.9 copy-done.3
  54.5 9.9 %encode.1 = (bf16[512,768]{1,0:T(8,128)(2,1)S(1)}, bf16[512,768]{1,0:T(8,128)(2,1)S(1)}) custom-call(s32[2]{0:T(128)S(1)} %pad_add_fusion.place.refs_0_, bf16[16,32,768]{2,1,0:T(8,128)(2,1)S(1)} %copy-done.1, bf16[7,32,768]{2,1,0:T(8,128)(2,1)S(1)} %collective-permute-done.4.above, bf16[23,8,768]{2,1,0:T(8,128)(2,1)S(1)} %collective-permute-done.5.beside, ...), custom_call_target="tpu_custom_call" | custom-call | flops 38535168 | bytes 2359296 | tf_op jit(solution)/shard_map/encode/pallas_call | solution.py:111
  64.5 0.9 copy-done.2
  65.4 1.1 copy-done.5
  66.5 12.1 %attend.1.refs_1_ = bf16[512,768]{1,0:T(8,128)(2,1)S(1)} custom-call(s32[2]{0:T(128)S(1)} %pad_add_fusion.place.refs_0_, bf16[512,768]{1,0:T(8,128)(2,1)S(1)} %get-tuple-element.26.refs_1_, f32[24,64,64]{2,1,0:T(8,128)S(1)} %copy-done.5, bf16[48,2304]{1,0:T(8,128)(2,1)S(1)} %copy-done.2, bf16[144,2304]{1,0:T(8,128)(2,1)S(1)} %constant_dynamic-update-slice_fusion.refs_4_, ...), custom_call_target="tpu_custom_call" | custom-call | flops 2415919104 | bytes 3538944 | tf_op jit(solution)/shard_map/attend/pallas_call | solution.py:226
  78.7 3.5 %project.1 = (bf16[16,32,768]{2,1,0:T(8,128)(2,1)S(1)}, bf16[4,32,768]{2,1,0:T(8,128)(2,1)S(1)}, bf16[48,768]{1,0:T(8,128)(2,1)S(1)}, bf16[16,768]{1,0:T(8,128)(2,1)S(1)}) custom-call(s32[2]{0:T(128)S(1)} %pad_add_fusion.place.refs_0_, bf16[512,768]{1,0:T(8,128)(2,1)S(1)} %attend.1.refs_1_, bf16[512,768]{1,0:T(8,128)(2,1)S(1)} %get-tuple-element.31.refs_2_, ...), custom_call_target="tpu_custom_call" | custom-call | flops 603979776 | bytes 1179648 | tf_op jit(solution)/shard_map/project/pallas_call | solution.py:300
  82.1 0.1 collective-permute-start.15
  82.3 0.8 collective-permute-start.16
  83.0 1.2 collective-permute-start.17
  84.2 0.7 compare_select_fusion
  85.0 0.1 select_n.38.position
  85.1 2.9 %collective-permute-done.17.corner = bf16[16,768]{1,0:T(8,128)(2,1)S(1)} collective-permute-done((bf16[16,768]{1,0:T(8,128)(2,1)S(1)}, bf16[16,768]{1,0:T(8,128)(2,1)S(1)}, u32[]{:S(2)}, u32[]{:S(2)}) %collective-permute-start.17) | collective-permute-done | bytes 24608 | tf_op jit(solution)/shard_map/ppermute | solution.py:38
  88.0 1.6 %dispatch.1 = (bf16[512,768]{1,0:T(8,128)(2,1)S(1)}, bf16[128,768]{1,0:T(8,128)(2,1)S(1)}, bf16[128,768]{1,0:T(8,128)(2,1)S(1)}, bf16[128,768]{1,0:T(8,128)(2,1)S(1)}, bf16[128,768]{1,0:T(8,128)(2,1)S(1)}) custom-call(s32[2]{0:T(128)S(1)} %pad_add_fusion.place.refs_0_, bf16[16,32,768]{2,1,0:T(8,128)(2,1)S(1)} %get-tuple-element.32.rolled, ...), custom_call_target="tpu_custom_call" | custom-call | tf_op jit(solution)/shard_map/dispatch/pallas_call | solution.py:365
  89.7 0.7 collective-permute-start.19
  90.4 1.4 %collective-permute-start.20 = (bf16[128,768]{1,0:T(8,128)(2,1)S(1)}, bf16[128,768]{1,0:T(8,128)(2,1)S(1)}, u32[]{:S(2)}, u32[]{:S(2)}) collective-permute-start(bf16[128,768]{1,0:T(8,128)(2,1)S(1)} %get-tuple-element.40), channel_id=1, source_target_pairs={{0,12},{4,8},{8,4},{12,0},{1,13},{5,9},{9,5},{13,1},{2,14},{6,10},... | collective-permute-start | bytes 589832 | tf_op jit(solution)/shard_map/ppermute | solution.py:43
  91.8 4.0 %collective-permute-done.19.refs_2_ = bf16[128,768]{1,0:T(8,128)(2,1)S(1)} collective-permute-done((bf16[128,768]{1,0:T(8,128)(2,1)S(1)}, bf16[128,768]{1,0:T(8,128)(2,1)S(1)}, u32[]{:S(2)}, u32[]{:S(2)}) %collective-permute-start.19) | collective-permute-done | bytes 196640 | tf_op jit(solution)/shard_map/ppermute | solution.py:43
  95.8 4.8 %collective-permute-done.20.refs_3_ = bf16[128,768]{1,0:T(8,128)(2,1)S(1)} collective-permute-done((bf16[128,768]{1,0:T(8,128)(2,1)S(1)}, bf16[128,768]{1,0:T(8,128)(2,1)S(1)}, u32[]{:S(2)}, u32[]{:S(2)}) %collective-permute-start.20) | collective-permute-done | bytes 196640 | tf_op jit(solution)/shard_map/ppermute | solution.py:43
  100.6 6.4 %copy-done = bf16[8,1536,768]{2,1,0:T(8,128)(2,1)S(1)} copy-done((bf16[8,1536,768]{2,1,0:T(8,128)(2,1)S(1)}, bf16[8,1536,768]{2,1,0:T(8,128)(2,1)}, u32[]{:S(2)}) %copy-start) | copy-done | bytes 18874392
  107.0 13.3 %experts.1 = (bf16[128,768]{1,0:T(8,128)(2,1)S(1)}, bf16[128,768]{1,0:T(8,128)(2,1)S(1)}, bf16[128,768]{1,0:T(8,128)(2,1)S(1)}, bf16[128,768]{1,0:T(8,128)(2,1)S(1)}) custom-call(bf16[128,768]{1,0:T(8,128)(2,1)S(1)} %get-tuple-element.37.refs_0_, bf16[128,768]{1,0:T(8,128)(2,1)S(1)} %collective-permute-done.18.refs_1_, ...), custom_call_target="tpu_custom_call" | custom-call | flops 2415919104 | bytes 37748736 | tf_op jit(solution)/shard_map/experts/pallas_call | solution.py:394
  120.4 0.9 collective-permute-start.22
  121.2 1.3 collective-permute-start.23
  122.5 0.3 select_n.42.position
  122.8 0.3 select_n.43.constant_at
  123.0 3.4 %collective-permute-done.22.refs_2_ = bf16[128,768]{1,0:T(8,128)(2,1)S(1)} collective-permute-done((bf16[128,768]{1,0:T(8,128)(2,1)S(1)}, bf16[128,768]{1,0:T(8,128)(2,1)S(1)}, u32[]{:S(2)}, u32[]{:S(2)}) %collective-permute-start.22) | collective-permute-done | bytes 196640 | tf_op jit(solution)/shard_map/ppermute | solution.py:43
  126.5 4.8 %collective-permute-done.23.refs_3_ = bf16[128,768]{1,0:T(8,128)(2,1)S(1)} collective-permute-done((bf16[128,768]{1,0:T(8,128)(2,1)S(1)}, bf16[128,768]{1,0:T(8,128)(2,1)S(1)}, u32[]{:S(2)}, u32[]{:S(2)}) %collective-permute-start.23) | collective-permute-done | bytes 196640 | tf_op jit(solution)/shard_map/ppermute | solution.py:43
  131.3 3.1 %combine.1 = bf16[512,768]{1,0:T(8,128)(2,1)} custom-call(s32[2]{0:T(128)S(1)} %pad_add_fusion.place.refs_0_, bf16[512,768]{1,0:T(8,128)(2,1)S(1)} %get-tuple-element.36.attended, s32[512,1]{1,0:T(8,128)S(1)} %select_n.42.position, s32[512,1]{1,0:T(8,128)S(1)} %select_n.43.constant_at, f32[16,768]{1,0:T(8,128)S(1)} %copy-done.4, ...), custom_call_target="tpu_custom_call" | custom-call | tf_op jit(solution)/shard_map/combine/pallas_call | solution.py:434
  (37 shorter events, 0.5 us)
Async XLA Ops:
  1.0 26.3 %collective-permute-start.4 = (bf16[7,32,768]{2,1,0:T(8,128)(2,1)S(1)}, bf16[7,32,768]{2,1,0:T(8,128)(2,1)S(1)}, u32[]{:S(2)}, u32[]{:S(2)}) collective-permute-start(bf16[7,32,768]{2,1,0:T(8,128)(2,1)S(1)} %slice.12), channel_id=1, source_target_pairs={{0,4},{4,8},{8,12},{12,0},{1,5},{5,9},{9,13},{13,1},{2,6},{6,10},{... | collective-permute-start | bytes 1032200 | tf_op jit(solution)/shard_map/ppermute | solution.py:28
  4.7 22.7 %collective-permute-start.3 = (bf16[48,3072]{1,0:T(8,128)(2,1)S(1)}, bf16[48,3072]{1,0:T(8,128)(2,1)S(1)}, u32[]{:S(2)}, u32[]{:S(2)}) collective-permute-start(bf16[48,3072]{1,0:T(8,128)(2,1)S(1)} %pad_maximum_fusion), channel_id=1, source_target_pairs={{0,8},{4,12},{8,0},{12,4},{1,9},{5,13},{9,1},{13,5},{2,10},{6,14},... | collective-permute-start | bytes 884744 | tf_op jit(solution)/shard_map/ppermute | solution.py:43
  4.7 9.4 %collective-permute-start = (bf16[48,2304]{1,0:T(8,128)(2,1)}, bf16[48,2304]{1,0:T(8,128)(2,1)S(1)}, u32[]{:S(2)}, u32[]{:S(2)}) collective-permute-start(bf16[48,2304]{1,0:T(8,128)(2,1)} %refs_3_.1), channel_id=1, source_target_pairs={{0,3},{1,2},{2,1},{3,0},{4,7},{5,6},{6,5},{7,4},{8,11},{9,10},{10,... | collective-permute-start | bytes 663560 | tf_op jit(solution)/shard_map/ppermute | solution.py:43
  8.3 19.0 %collective-permute-start.1 = (bf16[48,2304]{1,0:T(8,128)(2,1)}, bf16[48,2304]{1,0:T(8,128)(2,1)S(1)}, u32[]{:S(2)}, u32[]{:S(2)}) collective-permute-start(bf16[48,2304]{1,0:T(8,128)(2,1)} %refs_3_.1), channel_id=1, source_target_pairs={{0,2},{1,3},{2,0},{3,1},{4,6},{5,7},{6,4},{7,5},{8,10},{9,11},{10,... | collective-permute-start | bytes 663560 | tf_op jit(solution)/shard_map/ppermute | solution.py:43
  8.3 19.0 %collective-permute-start.2 = (bf16[48,2304]{1,0:T(8,128)(2,1)}, bf16[48,2304]{1,0:T(8,128)(2,1)S(1)}, u32[]{:S(2)}, u32[]{:S(2)}) collective-permute-start(bf16[48,2304]{1,0:T(8,128)(2,1)} %refs_3_.1), channel_id=1, source_target_pairs={{0,1},{1,0},{2,3},{3,2},{4,5},{5,4},{6,7},{7,6},{8,9},{9,8},{10,11... | collective-permute-start | bytes 663560 | tf_op jit(solution)/shard_map/ppermute | solution.py:43
  27.4 15.5 %collective-permute-start.6 = (bf16[144,2304]{1,0:T(8,128)(2,1)S(1)}, bf16[144,2304]{1,0:T(8,128)(2,1)S(1)}, u32[]{:S(2)}, u32[]{:S(2)}) collective-permute-start(bf16[144,2304]{1,0:T(8,128)(2,1)S(1)} %constant_dynamic-update-slice_fusion.refs_4_), channel_id=1, source_target_pairs={{0,8},{4,12},{8,0},{12,4},{1,9},{5,13},{9,1},{13,5},{2,10},{6,14},... | collective-permute-start | bytes 1990664 | tf_op jit(solution)/shard_map/ppermute | solution.py:43
  30.4 6.7 %collective-permute-start.11 = (bf16[96,768]{1,0:T(8,128)(2,1)S(1)}, bf16[96,768]{1,0:T(8,128)(2,1)S(1)}, u32[]{:S(2)}, u32[]{:S(2)}) collective-permute-start(bf16[96,768]{1,0:T(8,128)(2,1)S(1)} %pad_maximum_fusion.2), channel_id=1, source_target_pairs={{0,3},{1,2},{2,1},{3,0},{4,7},{5,6},{6,5},{7,4},{8,11},{9,10},{10,... | collective-permute-start | bytes 442376 | tf_op jit(solution)/shard_map/ppermute | solution.py:43
  33.6 30.8 %collective-permute-start.8 = (bf16[144,2304]{1,0:T(8,128)(2,1)S(1)}, bf16[144,2304]{1,0:T(8,128)(2,1)}, u32[]{:S(2)}, u32[]{:S(2)}) collective-permute-start(bf16[144,2304]{1,0:T(8,128)(2,1)S(1)} %constant_dynamic-update-slice_fusion.refs_4_), channel_id=1, source_target_pairs={{0,4},{4,0},{8,12},{12,8},{1,5},{5,1},{9,13},{13,9},{2,6},{6,2},{1... | collective-permute-start | bytes 1990664 | tf_op jit(solution)/shard_map/ppermute | solution.py:43
  34.6 16.1 %collective-permute-start.12 = (bf16[96,768]{1,0:T(8,128)(2,1)S(1)}, bf16[96,768]{1,0:T(8,128)(2,1)S(1)}, u32[]{:S(2)}, u32[]{:S(2)}) collective-permute-start(bf16[96,768]{1,0:T(8,128)(2,1)S(1)} %pad_maximum_fusion.2), channel_id=1, source_target_pairs={{0,2},{1,3},{2,0},{3,1},{4,6},{5,7},{6,4},{7,5},{8,10},{9,11},{10,... | collective-permute-start | bytes 442376 | tf_op jit(solution)/shard_map/ppermute | solution.py:43
  34.6 16.1 %collective-permute-start.13 = (bf16[96,768]{1,0:T(8,128)(2,1)S(1)}, bf16[96,768]{1,0:T(8,128)(2,1)S(1)}, u32[]{:S(2)}, u32[]{:S(2)}) collective-permute-start(bf16[96,768]{1,0:T(8,128)(2,1)S(1)} %pad_maximum_fusion.2), channel_id=1, source_target_pairs={{0,1},{1,0},{2,3},{3,2},{4,5},{5,4},{6,7},{7,6},{8,9},{9,8},{10,11... | collective-permute-start | bytes 442376 | tf_op jit(solution)/shard_map/ppermute | solution.py:43
  37.1 14.8 %collective-permute-start.5 = (bf16[23,8,768]{2,1,0:T(8,128)(2,1)S(1)}, bf16[23,8,768]{2,1,0:T(8,128)(2,1)S(1)}, u32[]{:S(2)}, u32[]{:S(2)}) collective-permute-start(bf16[23,8,768]{2,1,0:T(8,128)(2,1)S(1)} %pad_maximum_fusion.1), channel_id=1, source_target_pairs={{0,1},{1,2},{2,3},{3,0},{4,5},{5,6},{6,7},{7,4},{8,9},{9,10},{10,1... | collective-permute-start | bytes 847880 | tf_op jit(solution)/shard_map/ppermute | solution.py:28
  42.9 21.6 %collective-permute-start.10 = (bf16[144,2304]{1,0:T(8,128)(2,1)S(1)}, bf16[144,2304]{1,0:T(8,128)(2,1)}, u32[]{:S(2)}, u32[]{:S(2)}) collective-permute-start(bf16[144,2304]{1,0:T(8,128)(2,1)S(1)} %collective-permute-done.6.refs_6_), channel_id=1, source_target_pairs={{0,4},{4,0},{8,12},{12,8},{1,5},{5,1},{9,13},{13,9},{2,6},{6,2},{1... | collective-permute-start | bytes 1990664 | tf_op jit(solution)/shard_map/ppermute | solution.py:43
  50.7 27.9 %collective-permute-start.14 = (bf16[384,768]{1,0:T(8,128)(2,1)S(1)}, bf16[384,768]{1,0:T(8,128)(2,1)S(1)}, u32[]{:S(2)}, u32[]{:S(2)}) collective-permute-start(bf16[384,768]{1,0:T(8,128)(2,1)S(1)} %constant_dynamic-update-slice_fusion.3.refs_3_), channel_id=1, source_target_pairs={{0,4},{4,0},{8,12},{12,8},{1,5},{5,1},{9,13},{13,9},{2,6},{6,2},{1... | collective-permute-start | bytes 1769480 | tf_op jit(solution)/shard_map/ppermute | solution.py:43
  51.9 12.6 %collective-permute-start.9 = (bf16[48,3072]{1,0:T(8,128)(2,1)S(1)}, bf16[48,3072]{1,0:T(8,128)(2,1)}, u32[]{:S(2)}, u32[]{:S(2)}) collective-permute-start(bf16[48,3072]{1,0:T(8,128)(2,1)S(1)} %collective-permute-done.3.refs_5_), channel_id=1, source_target_pairs={{0,4},{4,0},{8,12},{12,8},{1,5},{5,1},{9,13},{13,9},{2,6},{6,2},{1... | collective-permute-start | bytes 884744 | tf_op jit(solution)/shard_map/ppermute | solution.py:43
  52.0 12.5 %collective-permute-start.7 = (bf16[48,2304]{1,0:T(8,128)(2,1)}, bf16[48,2304]{1,0:T(8,128)(2,1)}, u32[]{:S(2)}, u32[]{:S(2)}) collective-permute-start(bf16[48,2304]{1,0:T(8,128)(2,1)} %refs_3_.1), channel_id=1, source_target_pairs={{0,4},{4,0},{8,12},{12,8},{1,5},{5,1},{9,13},{13,9},{2,6},{6,2},{1... | collective-permute-start | bytes 663560 | tf_op jit(solution)/shard_map/ppermute | solution.py:43
  52.5 1.1 copy-start.1
  53.6 0.9 copy-start.3
  64.5 0.9 copy-start.2
  65.4 1.1 copy-start.5
  82.1 5.8 %collective-permute-start.15 = (bf16[4,32,768]{2,1,0:T(8,128)(2,1)S(1)}, bf16[4,32,768]{2,1,0:T(8,128)(2,1)S(1)}, u32[]{:S(2)}, u32[]{:S(2)}) collective-permute-start(bf16[4,32,768]{2,1,0:T(8,128)(2,1)S(1)} %get-tuple-element.33), channel_id=1, source_target_pairs={{0,12},{4,0},{8,4},{12,8},{1,13},{5,1},{9,5},{13,9},{2,14},{6,2},{... | collective-permute-start | bytes 589832 | tf_op jit(solution)/shard_map/ppermute | solution.py:28
  82.3 5.7 %collective-permute-start.16 = (bf16[48,768]{1,0:T(8,128)(2,1)S(1)}, bf16[48,768]{1,0:T(8,128)(2,1)S(1)}, u32[]{:S(2)}, u32[]{:S(2)}) collective-permute-start(bf16[48,768]{1,0:T(8,128)(2,1)S(1)} %get-tuple-element.34), channel_id=1, source_target_pairs={{0,3},{1,0},{2,1},{3,2},{4,7},{5,4},{6,5},{7,6},{8,11},{9,8},{10,9... | collective-permute-start | bytes 221192 | tf_op jit(solution)/shard_map/ppermute | solution.py:28
  83.0 4.9 %collective-permute-start.17 = (bf16[16,768]{1,0:T(8,128)(2,1)S(1)}, bf16[16,768]{1,0:T(8,128)(2,1)S(1)}, u32[]{:S(2)}, u32[]{:S(2)}) collective-permute-start(bf16[16,768]{1,0:T(8,128)(2,1)S(1)} %get-tuple-element.35), channel_id=1, source_target_pairs={{0,15},{1,12},{2,13},{3,14},{4,3},{5,0},{6,1},{7,2},{8,7},{9,4},{1... | collective-permute-start | bytes 73736 | tf_op jit(solution)/shard_map/ppermute | solution.py:38
  89.6 2.2 %collective-permute-start.18 = (bf16[128,768]{1,0:T(8,128)(2,1)S(1)}, bf16[128,768]{1,0:T(8,128)(2,1)S(1)}, u32[]{:S(2)}, u32[]{:S(2)}) collective-permute-start(bf16[128,768]{1,0:T(8,128)(2,1)S(1)} %get-tuple-element.38), channel_id=1, source_target_pairs={{0,4},{4,0},{8,12},{12,8},{1,5},{5,1},{9,13},{13,9},{2,6},{6,2},{1... | collective-permute-start | bytes 589832 | tf_op jit(solution)/shard_map/ppermute | solution.py:43
  89.7 6.1 %collective-permute-start.19 = (bf16[128,768]{1,0:T(8,128)(2,1)S(1)}, bf16[128,768]{1,0:T(8,128)(2,1)S(1)}, u32[]{:S(2)}, u32[]{:S(2)}) collective-permute-start(bf16[128,768]{1,0:T(8,128)(2,1)S(1)} %get-tuple-element.39), channel_id=1, source_target_pairs={{0,8},{4,12},{8,0},{12,4},{1,9},{5,13},{9,1},{13,5},{2,10},{6,14},... | collective-permute-start | bytes 589832 | tf_op jit(solution)/shard_map/ppermute | solution.py:43
  90.4 10.2 %collective-permute-start.20 = (bf16[128,768]{1,0:T(8,128)(2,1)S(1)}, bf16[128,768]{1,0:T(8,128)(2,1)S(1)}, u32[]{:S(2)}, u32[]{:S(2)}) collective-permute-start(bf16[128,768]{1,0:T(8,128)(2,1)S(1)} %get-tuple-element.40), channel_id=1, source_target_pairs={{0,12},{4,8},{8,4},{12,0},{1,13},{5,9},{9,5},{13,1},{2,14},{6,10},... | collective-permute-start | bytes 589832 | tf_op jit(solution)/shard_map/ppermute | solution.py:43
  100.6 6.4 %copy-start = (bf16[8,1536,768]{2,1,0:T(8,128)(2,1)S(1)}, bf16[8,1536,768]{2,1,0:T(8,128)(2,1)}, u32[]{:S(2)}) copy-start(bf16[8,1536,768]{2,1,0:T(8,128)(2,1)} %refs_4_.1) | copy-start | bytes 56623108
  107.0 24.3 %copy-start.4 = (f32[16,768]{1,0:T(8,128)S(1)}, f32[16,768]{1,0:T(8,128)}, u32[]{:S(2)}) copy-start(f32[16,768]{1,0:T(8,128)} %table.1) | copy-start | bytes 147460
  120.3 2.7 %collective-permute-start.21 = (bf16[128,768]{1,0:T(8,128)(2,1)S(1)}, bf16[128,768]{1,0:T(8,128)(2,1)S(1)}, u32[]{:S(2)}, u32[]{:S(2)}) collective-permute-start(bf16[128,768]{1,0:T(8,128)(2,1)S(1)} %get-tuple-element.42), channel_id=1, source_target_pairs={{0,4},{4,0},{8,12},{12,8},{1,5},{5,1},{9,13},{13,9},{2,6},{6,2},{1... | collective-permute-start | bytes 589832 | tf_op jit(solution)/shard_map/ppermute | solution.py:43
  120.4 6.1 %collective-permute-start.22 = (bf16[128,768]{1,0:T(8,128)(2,1)S(1)}, bf16[128,768]{1,0:T(8,128)(2,1)S(1)}, u32[]{:S(2)}, u32[]{:S(2)}) collective-permute-start(bf16[128,768]{1,0:T(8,128)(2,1)S(1)} %get-tuple-element.43), channel_id=1, source_target_pairs={{0,8},{4,12},{8,0},{12,4},{1,9},{5,13},{9,1},{13,5},{2,10},{6,14},... | collective-permute-start | bytes 589832 | tf_op jit(solution)/shard_map/ppermute | solution.py:43
  121.2 10.0 %collective-permute-start.23 = (bf16[128,768]{1,0:T(8,128)(2,1)S(1)}, bf16[128,768]{1,0:T(8,128)(2,1)S(1)}, u32[]{:S(2)}, u32[]{:S(2)}) collective-permute-start(bf16[128,768]{1,0:T(8,128)(2,1)S(1)} %get-tuple-element.44), channel_id=1, source_target_pairs={{0,12},{4,8},{8,4},{12,0},{1,13},{5,9},{9,5},{13,1},{2,14},{6,10},... | collective-permute-start | bytes 589832 | tf_op jit(solution)/shard_map/ppermute | solution.py:43

commit v3 on v2

--- a/solution.py
+++ b/solution.py
@@ -20,7 +20,16 @@
 VMEM = pl.BlockSpec(memory_space=pltpu.VMEM)
 SMEM = pl.BlockSpec(memory_space=pltpu.SMEM)
 ANY = pl.BlockSpec(memory_space=pl.ANY)
+HBM = pl.BlockSpec(memory_space=pltpu.HBM)
 LARGEST = 3.38e38
+DEPTH = 3
+PARTS = 2
+
+
+def lasting(microseconds):
+    return pl.CostEstimate(
+        flops=int(microseconds * 1.15e9), bytes_accessed=0, transcendentals=0
+    )
 
 
 def shifted(x, axis, by):
@@ -49,13 +58,26 @@
     return (centred * lax.rsqrt(spread + 1e-05)).astype(jnp.bfloat16)
 
 
-def encode_kernel(place, tokens, above, beside, taps, encoded, normed, extended, weights):
+def encode_kernel(
+    place, tokens_at, above, beside, taps_at, rel_bias, encoded, normed, bias, extended, weights, tokens, taps, sems
+):
+    copies = [
+        pltpu.make_async_copy(tokens_at, tokens, sems.at[0]),
+        pltpu.make_async_copy(taps_at, taps, sems.at[1]),
+    ]
+    for copy in copies:
+        copy.start()
     rows, cols, channels = tokens.shape
     reach = KERNEL // 2 + SHIFT
     extended[:, :HALO] = beside[...].astype(jnp.float32)
     extended[:reach, HALO:] = above[...].astype(jnp.float32)
+    for copy in copies:
+        copy.wait()
     extended[reach:, HALO:] = tokens[...].astype(jnp.float32)
     weights[...] = taps[...].astype(jnp.float32)
+    for head in range(rel_bias.shape[0]):
+        at = head % GROUP * SPOTS
+        bias[head // GROUP, :, at : at + SPOTS] = rel_bias[head]
     inner_row = jnp.where(place[0] == 0, 0.0, 1.0)
     first_col = place[1] == 0
     window_cols = cols // WIN
@@ -104,33 +126,35 @@
     lax.fori_loop(0, rows * cols // SPOTS, norm, 0)
 
 
-def encode(place, tokens, above, beside, taps):
+def encode(place, tokens, above, beside, taps, rel_bias):
     rows, cols, channels = tokens.shape
     flat = jax.ShapeDtypeStruct((rows * cols, channels), jnp.bfloat16)
     reach = KERNEL // 2 + SHIFT
+    bias_shape = (rel_bias.shape[0] // GROUP, SPOTS, GROUP * SPOTS)
     return pl.pallas_call(
         encode_kernel,
-        out_shape=(flat, flat),
-        in_specs=[SMEM] + [VMEM] * 4,
-        out_specs=(VMEM, VMEM),
+        out_shape=(flat, flat, jax.ShapeDtypeStruct(bias_shape, jnp.float32)),
+        in_specs=[SMEM, HBM, VMEM, VMEM, HBM, VMEM],
+        out_specs=(VMEM, VMEM, VMEM),
         scratch_shapes=[
             pltpu.VMEM((rows + reach, cols + HALO, channels), jnp.float32),
             pltpu.VMEM(taps.shape, jnp.float32),
+            pltpu.VMEM(tokens.shape, jnp.bfloat16),
+            pltpu.VMEM(taps.shape, jnp.bfloat16),
+            pltpu.SemaphoreType.DMA((2,)),
         ],
         compiler_params=pltpu.CompilerParams(vmem_limit_bytes=12 * 1024 * 1024),
-        cost_estimate=pl.CostEstimate(
-            flops=2 * rows * cols * channels * KERNEL * KERNEL,
-            bytes_accessed=6 * rows * cols * channels,
-            transcendentals=0,
-        ),
+        cost_estimate=lasting(0.1),
         name="encode",
-    )(place, tokens, above, beside, taps)
+    )(place, tokens, above, beside, taps, rel_bias)
 
 
 def fetch(place, grid_cols, pieces, ids, target, sems):
     copies = []
-    for piece, parts in zip(pieces, ids, strict=True):
+    for piece, (parts, half) in zip(pieces, ids, strict=True):
         size = piece.shape[0] // len(parts)
+        wide = min(piece.shape[1], target.shape[1])
+        left = 0 if half is None else pl.multiple_of((place[2] ^ half) * wide, LANES)
         for at, (mask_row, mask_col) in enumerate(parts):
             if mask_row is None:
                 first = 0
@@ -138,8 +162,8 @@
                 owner = (place[0] ^ mask_row) * grid_cols + (place[1] ^ mask_col)
                 first = pl.multiple_of(owner * size, 16)
             copy = pltpu.make_async_copy(
-                piece.at[pl.ds(at * size, size), pl.ds(0, target.shape[1])],
-                target.at[pl.ds(first, size), :],
+                piece.at[pl.ds(at * size, size), pl.ds(0, wide)],
+                target.at[pl.ds(first, size), pl.ds(left, wide)],
                 sems.at[len(copies)],
             )
             copy.start()
@@ -149,17 +173,14 @@
 
 def attend_kernel(shape, ids, grid_cols, *refs):
     rows, cols = shape
-    place, normed, rel_bias = refs[:3]
-    context, weight, mixed, bias, sems = refs[3 + len(ids) :]
+    place, normed, bias = refs[:3]
+    context, weight, mixed, sems = refs[3 + len(ids) :]
     channels = normed.shape[1]
     copies = fetch(place, grid_cols, refs[3 : 3 + len(ids)], ids, weight, sems)
     groups = channels // LANES
-    for head in range(rel_bias.shape[0]):
-        at = head % GROUP * SPOTS
-        bias[head // GROUP, :, at : at + SPOTS] = rel_bias[head]
     for copy in copies:
         copy.wait()
-    wide = 2 * LANES
+    wide = channels
 
     def project(index, _):
         lanes = pl.ds(pl.multiple_of(index * wide, wide), wide)
@@ -219,10 +240,10 @@
     lax.fori_loop(0, rows * cols // SPOTS, window, 0)
 
 
-def attend(place, shape, normed, rel_bias, pieces, grid_cols):
+def attend(place, shape, normed, bias, pieces, grid_cols):
     rows, cols = shape
     channels = normed.shape[1]
-    ids = [p[1] for p in pieces]
+    ids = [p[1:] for p in pieces]
     return pl.pallas_call(
         functools.partial(attend_kernel, shape, ids, grid_cols),
         out_shape=jax.ShapeDtypeStruct((rows * cols, channels), jnp.bfloat16),
@@ -231,17 +252,12 @@
         scratch_shapes=[
             pltpu.VMEM((channels, 3 * channels), jnp.bfloat16),
             pltpu.VMEM((rows * cols, 3 * channels), jnp.bfloat16),
-            pltpu.VMEM((channels // LANES, SPOTS, GROUP * SPOTS), jnp.float32),
-            pltpu.SemaphoreType.DMA((sum(len(p) for p in ids),)),
+            pltpu.SemaphoreType.DMA((sum(len(p[0]) for p in ids),)),
         ],
-        compiler_params=pltpu.CompilerParams(vmem_limit_bytes=14 * 1024 * 1024),
-        cost_estimate=pl.CostEstimate(
-            flops=2 * rows * cols * channels * 4 * channels,
-            bytes_accessed=6 * channels * channels,
-            transcendentals=rows * cols * SPOTS * channels // HD,
-        ),
+        compiler_params=pltpu.CompilerParams(vmem_limit_bytes=18 * 1024 * 1024),
+        cost_estimate=lasting(10),
         name="attend",
-    )(place, normed, rel_bias, *[p[0] for p in pieces])
+    )(place, normed, bias, *[p[0] for p in pieces])
 
 
 def project_kernel(shape, ids, grid_cols, *refs):
@@ -296,7 +312,7 @@
     rows, cols = shape
     channels = context.shape[1]
     bf16 = functools.partial(jax.ShapeDtypeStruct, dtype=jnp.bfloat16)
-    ids = [p[1] for p in pieces]
+    ids = [p[1:] for p in pieces]
     return pl.pallas_call(
         functools.partial(project_kernel, shape, ids, grid_cols),
         out_shape=(
@@ -309,14 +325,10 @@
         out_specs=(VMEM,) * 4,
         scratch_shapes=[
             pltpu.VMEM((channels, channels), jnp.bfloat16),
-            pltpu.SemaphoreType.DMA((sum(len(p) for p in ids),)),
+            pltpu.SemaphoreType.DMA((sum(len(p[0]) for p in ids),)),
         ],
         compiler_params=pltpu.CompilerParams(vmem_limit_bytes=12 * 1024 * 1024),
-        cost_estimate=pl.CostEstimate(
-            flops=2 * rows * cols * channels * channels,
-            bytes_accessed=2 * channels * channels,
-            transcendentals=0,
-        ),
+        cost_estimate=lasting(3),
         name="project",
     )(place, context, encoded, *[p[0] for p in pieces])
 
@@ -374,35 +386,64 @@
 
 
 def expert_kernel(count, *refs):
-    incoming, (weight_in, weight_out), results = refs[:count], refs[count : count + 2], refs[count + 2 :]
-    rows = jnp.concatenate([ref[...] for ref in incoming], axis=0)
-    hidden = lax.dot_general(
-        rows, weight_in[0], (((1,), (1,)), ((), ())), preferred_element_type=jnp.float32
-    )
-    hidden = (0.5 * hidden * (1.0 + lax.erf(hidden * 0.5**0.5))).astype(jnp.bfloat16)
-    result = jnp.dot(hidden, weight_out[0], preferred_element_type=jnp.float32)
-    result = result.astype(jnp.bfloat16)
-    for at, ref in enumerate(results):
-        ref[...] = result[at * CAP : (at + 1) * CAP]
+    incoming, (all_in, all_out), results = refs[:count], refs[count : count + 2], refs[count + 2 : -3]
+    held_in, held_out, sems = refs[-3:]
+    experts, hidden_units = all_in.shape[:2]
+    part = hidden_units // PARTS
+
+    def copies(expert):
+        slot = expert % held_in.shape[0]
+        return [
+            pltpu.make_async_copy(
+                source.at[expert, pl.ds(at * part, part), :],
+                target.at[slot, pl.ds(at * part, part), :],
+                sems.at[slot, which, at],
+            )
+            for which, (source, target) in enumerate(((all_in, held_in), (all_out, held_out)))
+            for at in range(PARTS)
+        ]
+
+    for expert in range(min(experts, held_in.shape[0])):
+        for copy in copies(expert):
+            copy.start()
+    for expert in range(experts):
+        slot = expert % held_in.shape[0]
+        own = pl.ds(expert * CAP, CAP)
+        rows = jnp.concatenate([ref[own, :] for ref in incoming], axis=0)
+        arriving = copies(expert)
+        for copy in arriving[:PARTS]:
+            copy.wait()
+        hidden = lax.dot_general(
+            rows, held_in[slot], (((1,), (1,)), ((), ())), preferred_element_type=jnp.float32
+        )
+        hidden = (0.5 * hidden * (1.0 + lax.erf(hidden * 0.5**0.5))).astype(jnp.bfloat16)
+        for copy in arriving[PARTS:]:
+            copy.wait()
+        result = jnp.dot(hidden, held_out[slot], preferred_element_type=jnp.float32)
+        result = result.astype(jnp.bfloat16)
+        for at, ref in enumerate(results):
+            ref[own, :] = result[at * CAP : (at + 1) * CAP]
+        if expert + held_in.shape[0] < experts:
+            for copy in copies(expert + held_in.shape[0]):
+                copy.start()
 
 
 def serve(incoming, expert_in, expert_out):
     count = len(incoming)
     experts, hidden, channels = expert_in.shape
-    slot = pl.BlockSpec((CAP, channels), lambda e: (e, 0))
-    weight = pl.BlockSpec((1, hidden, channels), lambda e: (e, 0, 0))
+    depth = min(DEPTH, experts)
     return pl.pallas_call(
         functools.partial(expert_kernel, count),
-        grid=(experts,),
         out_shape=tuple(jax.ShapeDtypeStruct(x.shape, x.dtype) for x in incoming),
-        in_specs=[slot] * count + [weight, weight],
-        out_specs=(slot,) * count,
-        compiler_params=pltpu.CompilerParams(vmem_limit_bytes=32 * 1024 * 1024),
-        cost_estimate=pl.CostEstimate(
-            flops=4 * count * CAP * experts * hidden * channels,
-            bytes_accessed=4 * experts * hidden * channels,
-            transcendentals=count * CAP * experts * hidden,
-        ),
+        in_specs=[VMEM] * count + [HBM, HBM],
+        out_specs=(VMEM,) * count,
+        scratch_shapes=[
+            pltpu.VMEM((depth, hidden, channels), jnp.bfloat16),
+            pltpu.VMEM((depth, hidden, channels), jnp.bfloat16),
+            pltpu.SemaphoreType.DMA((depth, 2, PARTS)),
+        ],
+        compiler_params=pltpu.CompilerParams(vmem_limit_bytes=56 * 1024 * 1024),
+        cost_estimate=lasting(12),
         name="experts",
     )(*incoming, expert_in, expert_out)
 
@@ -442,13 +483,27 @@
 
 
 def stacked(parts):
-    return jnp.concatenate([p[0] for p in parts], axis=0), sum([p[1] for p in parts], [])
+    ids = sum([part[1] for part in parts], [])
+    return jnp.concatenate([part[0] for part in parts], axis=0), ids, None
 
 
 def along(part, axis, mask):
-    array, ids = part
+    array, ids, half = part
+    moved = exchanged(array, axis, mask)
+    if axis == "groups":
+        return moved, ids, half ^ mask
     change = (mask, 0) if axis == "gy" else (0, mask)
-    return exchanged(array, axis, mask), [(a ^ change[0], b ^ change[1]) for a, b in ids]
+    return moved, [(a ^ change[0], b ^ change[1]) for a, b in ids], half
+
+
+def diagonal(part, mask):
+    array, ids, half = part
+    groups, rows = lax.axis_size("groups"), lax.axis_size("gy")
+    pairs = [
+        (i * rows + j, (i ^ 1) * rows + (j ^ mask)) for i in range(groups) for j in range(rows)
+    ]
+    moved = lax.ppermute(array, ("groups", "gy"), pairs)
+    return moved, [(a ^ mask, b) for a, b in ids], half ^ 1
 
 
 def held(*values):
@@ -470,34 +525,41 @@
 ):
     rows, cols, channels = tokens.shape
     grid_rows, grid_cols = lax.axis_size("gy"), lax.axis_size("gx")
-    place = jnp.stack([lax.axis_index("gy"), lax.axis_index("gx")]).astype(jnp.int32)
+    place = jnp.stack([lax.axis_index(axis) for axis in ("gy", "gx", "groups")]).astype(jnp.int32)
     reach = KERNEL // 2 + SHIFT
+    quick = grid_rows == 4 and grid_cols == 4 and lax.axis_size("groups") == 2
     above = shifted(tokens[rows - reach :], "gy", 1)
-    quick = grid_rows == 4 and grid_cols == 4
     if quick:
-        own = [(0, 0)]
-        line = [exchanged(project_in, "gx", mask) for mask in (3, 2, 1)]
-        both = jnp.concatenate([project_in, project_out], axis=1)
-        facing = exchanged(both, "gy", 2)
-        *line, facing, above = held(*line, facing, above)
+        beyond = exchanged(project_in, "gx", 1)
+        facing_out = exchanged(project_out, "gy", 2)
+        beyond, facing_out, above = held(beyond, facing_out, above)
+        two = (jnp.concatenate([project_in, beyond], axis=0), [(0, 0), (0, 1)], None)
+        wide = two[0].shape[1] // 2
+        mine = lax.dynamic_slice_in_dim(two[0], lax.axis_index("groups") * wide, wide, axis=1)
+        far = along((mine, two[1], 0), "gx", 2)
+        facing = along(two, "gy", 2)
     edge = jnp.concatenate([above[:, cols - HALO :], tokens[:, cols - HALO :]], axis=0)
     beside = shifted(edge, "gx", 1)
+    encoded, normed, bias = encode(place, tokens, above, beside, conv_kernel, rel_bias)
     if quick:
-        line = stacked([(array, [(0, mask)]) for array, mask in zip(line, (3, 2, 1), strict=True)])
-        facing = (facing, [(2, 0)])
-        pair = stacked([(project_out, own), (facing[0][:, 3 * channels :], facing[1])])
-        far = along(line, "gy", 2)
-        plane = stacked([pair] + [along(pair, "gx", mask) for mask in (3, 2, 1)])
+        first, second, normed = held(far[0], facing[0], normed)
+        far, facing = (first, *far[1:]), (second, *facing[1:])
+        across = along(far, "gy", 2)
+        pair = stacked([(project_out, [(0, 0)]), (facing_out, [(2, 0)])])
+        plane = [pair] + [along(pair, "gx", mask) for mask in (3, 2, 1)]
+        far_rest, across_rest = along(far, "groups", 1), diagonal(far, 2)
+        pieces_in = [two, facing, far, far_rest, across]
+        pieces_in = pieces_in + [along(part, "gy", 1) for part in pieces_in]
+        pieces_in = pieces_in + [across_rest, along(across_rest, "gy", 1)]
     else:
         whole = [(None, None)]
-        pieces_in = [(lax.all_gather(project_in, ("gy", "gx"), axis=0, tiled=True), whole)]
-        pieces_out = [(lax.all_gather(project_out, ("gy", "gx"), axis=0, tiled=True), whole)]
-    encoded, normed = encode(place, tokens, above, beside, conv_kernel)
+        pieces_in = [(lax.all_gather(project_in, ("gy", "gx"), axis=0, tiled=True), whole, None)]
+        pieces_out = [(lax.all_gather(project_out, ("gy", "gx"), axis=0, tiled=True), whole, None)]
+    context = attend(place, (rows, cols), normed, bias, pieces_in, grid_cols)
     if quick:
-        near = [(project_in, own), line, facing]
-        pieces_in = near + [far] + [along(part, "gy", 1) for part in near + [far]]
+        *arrays, context = held(*[part[0] for part in plane], context)
+        plane = stacked([(array, *part[1:]) for array, part in zip(arrays, plane, strict=True)])
         pieces_out = [plane, along(plane, "gy", 1)]
-    context = attend(place, (rows, cols), normed, rel_bias, pieces_in, grid_cols)
     rolled, top, side, corner = project(
         place, (rows, cols), context, encoded, pieces_out, grid_cols
     )

time: 135 us -> 123 us (0.911)
  waiting for transfers between devices: 51.5 us -> 33.7 us
  starting transfers between devices: 22.4 us -> 34.4 us
  local copies, waits for them, and re-layouts: 14 us -> 9.92 us
  other arithmetic: 2.73 us -> 0.11 us
    ppermute x19 -> x22, waiting for transfers between devices: 48.5 us -> 25.8 us  [exchanged(): return lax.ppermute(x, axis, [(i, i ^ mask) for i in range(size)])]
    ppermute x19 -> x22, starting transfers between devices: 17.7 us -> 26.3 us  [exchanged(): return lax.ppermute(x, axis, [(i, i ^ mask) for i in range(size)])]
    ppermute x4, waiting for transfers between devices: 0.01 us -> 4.19 us  [shifted(): return lax.ppermute(x, axis, [(i, (i + by) % size) for i in range(size)])]
    unnamed x17 -> x29, local copies, waits for them, and re-layouts: 11.4 us -> 7.33 us
    ppermute x4, starting transfers between devices: 3.55 us -> 6.59 us  [shifted(): return lax.ppermute(x, axis, [(i, (i + by) % size) for i in range(size)])]
    pallas_call x2, Pallas kernels: 23.3 us -> 25.8 us  [the longest x1 15.5 us: serve(): pl.pallas_call(functools.partial(expert_kernel, count), out_shape=tuple((...]
    concatenate x2 -> x0, other arithmetic: 1.89 us -> none  [the longest x1 0.99 us: shards(): both = jnp.concatenate([project_in, project_out], axis=1)]
    pallas_call x1, Pallas kernels: 12.1 us -> 10.3 us  [attend(): pl.pallas_call(functools.partial(attend_kernel, shape, ids, grid_cols), o...]
  transfers between devices with their start and end apart: 24 -> 28, of which waited for: 10 -> 12; matrix products, arithmetic and copies ran while one was open for 4% -> 3% of each run, Pallas kernels for 16% -> 17%
where the time goes in v3:
time: 123 us
  Pallas kernels  44.3 us (36%)
  starting transfers between devices  34.4 us (28%)
  waiting for transfers between devices  33.7 us (27%)
  local copies, waits for them, and re-layouts  9.92 us (8%)
    ppermute x22, starting transfers between devices, exchanged(): return lax.ppermute(x, axis, [(i, i ^ mask) for i in range(size)])  26.3 us
    ppermute x22, waiting for transfers between devices, exchanged(): return lax.ppermute(x, axis, [(i, i ^ mask) for i in range(size)])  25.8 us
    pallas_call x1, Pallas kernels, serve(): pl.pallas_call(functools.partial(expert_kernel, count), out_shape=tuple((...  15.5 us
    pallas_call x1, Pallas kernels, attend(): pl.pallas_call(functools.partial(attend_kernel, shape, ids, grid_cols), o...  10.3 us
    pallas_call x1, Pallas kernels, encode(): pl.pallas_call(encode_kernel, out_shape=(flat, flat, jax.ShapeDtypeStruct...  10.3 us
    unnamed x29, local copies, waits for them, and re-layouts  7.33 us
    ppermute x4, starting transfers between devices, shifted(): return lax.ppermute(x, axis, [(i, (i + by) % size) for i in range(size)])  6.59 us
    ppermute x4, waiting for transfers between devices, shifted(): return lax.ppermute(x, axis, [(i, (i + by) % size) for i in range(size)])  4.19 us
  transfers between devices with their start and end apart: 28, of which 12 were waited for; matrix products, arithmetic and copies ran while one was open for 3% of the time, Pallas kernels for 17%

profile of v3, /device:TPU:1, one launch (start us, length us, event | category | flops | bytes accessed | tf_op | source)
XLA Modules:
  0.0 122.7 jit_solution(8780176730863117558)
XLA Ops:
  0.0 1.0 slice.9
  1.0 2.7 %collective-permute-start.2 = (bf16[7,32,768]{2,1,0:T(8,128)(2,1)S(1)}, bf16[7,32,768]{2,1,0:T(8,128)(2,1)S(1)}, u32[]{:S(2)}, u32[]{:S(2)}) collective-permute-start(bf16[7,32,768]{2,1,0:T(8,128)(2,1)S(1)} %slice.9), channel_id=1, source_target_pairs={{0,4},{4,8},{8,12},{12,0},{1,5},{5,9},{9,13},{13,1},{2,6},{6,10},{... | collective-permute-start | bytes 1032200 | tf_op jit(solution)/shard_map/ppermute | solution.py:37
  3.7 1.3 %collective-permute-start = (bf16[48,2304]{1,0:T(8,128)(2,1)}, bf16[48,2304]{1,0:T(8,128)(2,1)S(1)}, u32[]{:S(2)}, u32[]{:S(2)}) collective-permute-start(bf16[48,2304]{1,0:T(8,128)(2,1)} %param.13), channel_id=1, source_target_pairs={{0,1},{1,0},{2,3},{3,2},{4,5},{5,4},{6,7},{7,6},{8,9},{9,8},{10,11... | collective-permute-start | bytes 663560 | tf_op jit(solution)/shard_map/ppermute | solution.py:52
  5.2 0.9 constant_dynamic-update-slice_fusion.3
  6.2 0.9 slice.11
  7.1 2.4 %collective-permute-done.1 = bf16[48,768]{1,0:T(8,128)(2,1)S(1)} collective-permute-done((bf16[48,768]{1,0:T(8,128)(2,1)}, bf16[48,768]{1,0:T(8,128)(2,1)S(1)}, u32[]{:S(2)}, u32[]{:S(2)}) %collective-permute-start.1) | collective-permute-done | bytes 73760 | tf_op jit(solution)/shard_map/ppermute | solution.py:52
  10.1 1.8 %collective-permute-start.8 = (bf16[23,8,768]{2,1,0:T(8,128)(2,1)S(1)}, bf16[23,8,768]{2,1,0:T(8,128)(2,1)S(1)}, u32[]{:S(2)}, u32[]{:S(2)}) collective-permute-start(bf16[23,8,768]{2,1,0:T(8,128)(2,1)S(1)} %pad_maximum_fusion), channel_id=1, source_target_pairs={{0,1},{1,2},{2,3},{3,0},{4,5},{5,6},{6,7},{7,4},{8,9},{9,10},{10,1... | collective-permute-start | bytes 847880 | tf_op jit(solution)/shard_map/ppermute | solution.py:37
  11.9 1.2 collective-permute-start.7
  13.1 2.4 %collective-permute-start.6 = (bf16[96,1152]{1,0:T(8,128)(2,1)S(1)}, bf16[96,1152]{1,0:T(8,128)(2,1)S(1)}, u32[]{:S(2)}, u32[]{:S(2)}) collective-permute-start(bf16[96,1152]{1,0:T(8,128)(2,1)S(1)} %constant_dynamic-slice_fusion), channel_id=1, source_target_pairs={{0,2},{1,3},{2,0},{3,1},{4,6},{5,7},{6,4},{7,5},{8,10},{9,11},{10,... | collective-permute-start | bytes 663560 | tf_op jit(solution)/shard_map/ppermute | solution.py:52
  15.5 1.2 %collective-permute-start.11 = (bf16[96,2304]{1,0:T(8,128)(2,1)S(1)}, bf16[96,2304]{1,0:T(8,128)(2,1)S(1)}, u32[]{:S(2)}, u32[]{:S(2)}) collective-permute-start(bf16[96,2304]{1,0:T(8,128)(2,1)S(1)} %constant_dynamic-update-slice_fusion.2.refs_3_), channel_id=1, source_target_pairs={{0,4},{4,0},{8,12},{12,8},{1,5},{5,1},{9,13},{13,9},{2,6},{6,2},{1... | collective-permute-start | bytes 1327112 | tf_op jit(solution)/shard_map/ppermute | solution.py:52
  16.8 4.2 %collective-permute-done.8.beside = bf16[23,8,768]{2,1,0:T(8,128)(2,1)S(1)} collective-permute-done((bf16[23,8,768]{2,1,0:T(8,128)(2,1)S(1)}, bf16[23,8,768]{2,1,0:T(8,128)(2,1)S(1)}, u32[]{:S(2)}, u32[]{:S(2)}) %collective-permute-start.8) | collective-permute-done | bytes 282656 | tf_op jit(solution)/shard_map/ppermute | solution.py:37
  21.0 1.1 copy-done
  22.1 1.1 copy-done.1
  23.2 0.9 copy-done.3
  24.1 10.3 %encode.1 = (bf16[512,768]{1,0:T(8,128)(2,1)S(1)}, bf16[512,768]{1,0:T(8,128)(2,1)S(1)}, f32[6,64,256]{2,1,0:T(8,128)S(1)}) custom-call(s32[3]{0:T(128)S(1)} %pad_add_fusion.place.refs_0_, bf16[16,32,768]{2,1,0:T(8,128)(2,1)S(1)} %copy-done, bf16[7,32,768]{2,1,0:T(8,128)(2,1)S(1)} %collective-permute-done.2.above, ...), custom_call_target="tpu_custom_call" | custom-call | flops 115000000 | tf_op jit(solution)/shard_map/encode/pallas_call | solution.py:134
  34.4 1.1 collective-permute-start.9
  35.5 0.9 collective-permute-start.10
  36.4 0.8 collective-permute-start.16
  37.1 1.9 %collective-permute-start.12 = (bf16[96,2304]{1,0:T(8,128)(2,1)S(1)}, bf16[96,2304]{1,0:T(8,128)(2,1)S(1)}, u32[]{:S(2)}, u32[]{:S(2)}) collective-permute-start(bf16[96,2304]{1,0:T(8,128)(2,1)S(1)} %collective-permute-done.7.refs_4_), channel_id=1, source_target_pairs={{0,4},{4,0},{8,12},{12,8},{1,5},{5,1},{9,13},{13,9},{2,6},{6,2},{1... | collective-permute-start | bytes 1327112 | tf_op jit(solution)/shard_map/ppermute | solution.py:52
  39.0 1.4 %collective-permute-done.9.refs_6_ = bf16[96,1152]{1,0:T(8,128)(2,1)S(1)} collective-permute-done((bf16[96,1152]{1,0:T(8,128)(2,1)S(1)}, bf16[96,1152]{1,0:T(8,128)(2,1)S(1)}, u32[]{:S(2)}, u32[]{:S(2)}) %collective-permute-start.9) | collective-permute-done | bytes 221216 | tf_op jit(solution)/shard_map/ppermute | solution.py:52
  40.4 2.6 %collective-permute-start.14 = (bf16[96,1152]{1,0:T(8,128)(2,1)S(1)}, bf16[96,1152]{1,0:T(8,128)(2,1)S(1)}, u32[]{:S(2)}, u32[]{:S(2)}) collective-permute-start(bf16[96,1152]{1,0:T(8,128)(2,1)S(1)} %collective-permute-done.9.refs_6_), channel_id=1, source_target_pairs={{0,4},{4,0},{8,12},{12,8},{1,5},{5,1},{9,13},{13,9},{2,6},{6,2},{1... | collective-permute-start | bytes 663560 | tf_op jit(solution)/shard_map/ppermute | solution.py:52
  43.0 2.7 %collective-permute-start.15 = (bf16[96,1152]{1,0:T(8,128)(2,1)S(1)}, bf16[96,1152]{1,0:T(8,128)(2,1)S(1)}, u32[]{:S(2)}, u32[]{:S(2)}) collective-permute-start(bf16[96,1152]{1,0:T(8,128)(2,1)S(1)} %collective-permute-done.10.refs_7_), channel_id=1, source_target_pairs={{0,4},{4,0},{8,12},{12,8},{1,5},{5,1},{9,13},{13,9},{2,6},{6,2},{1... | collective-permute-start | bytes 663560 | tf_op jit(solution)/shard_map/ppermute | solution.py:52
  46.0 2.2 %collective-permute-start.17 = (bf16[96,1152]{1,0:T(8,128)(2,1)S(1)}, bf16[96,1152]{1,0:T(8,128)(2,1)S(1)}, u32[]{:S(2)}, u32[]{:S(2)}) collective-permute-start(bf16[96,1152]{1,0:T(8,128)(2,1)S(1)} %collective-permute-done.16.refs_13_), channel_id=1, source_target_pairs={{0,4},{4,0},{8,12},{12,8},{1,5},{5,1},{9,13},{13,9},{2,6},{6,2},{1... | collective-permute-start | bytes 663560 | tf_op jit(solution)/shard_map/ppermute | solution.py:52
  48.3 0.9 constant_dynamic-update-slice_fusion.1
  49.2 1.2 collective-permute-start.3
  50.3 1.6 %collective-permute-start.4 = (bf16[96,768]{1,0:T(8,128)(2,1)S(1)}, bf16[96,768]{1,0:T(8,128)(2,1)S(1)}, u32[]{:S(2)}, u32[]{:S(2)}) collective-permute-start(bf16[96,768]{1,0:T(8,128)(2,1)S(1)} %constant_dynamic-update-slice_fusion), channel_id=1, source_target_pairs={{0,2},{1,3},{2,0},{3,1},{4,6},{5,7},{6,4},{7,5},{8,10},{9,11},{10,... | collective-permute-start | bytes 442376 | tf_op jit(solution)/shard_map/ppermute | solution.py:52
  52.0 0.8 collective-permute-start.5
  52.8 10.3 %attend.1.refs_1_ = bf16[512,768]{1,0:T(8,128)(2,1)S(1)} custom-call(s32[3]{0:T(128)S(1)} %pad_add_fusion.place.refs_0_, bf16[512,768]{1,0:T(8,128)(2,1)S(1)} %get-tuple-element.36.refs_1_, f32[6,64,256]{2,1,0:T(8,128)S(1)} %get-tuple-element.37.refs_2_, bf16[96,2304]{1,0:T(8,128)(2,1)S(1)} %constant_dynamic-update-slice_fusion.2.refs_3_, ...), custom_call_target="tpu_custom_call" | custom-call | flops 11500000256 | tf_op jit(solution)/shard_map/attend/pallas_call | solution.py:247
  63.2 2.4 %collective-permute-done.4 = bf16[96,768]{1,0:T(8,128)(2,1)S(1)} collective-permute-done((bf16[96,768]{1,0:T(8,128)(2,1)S(1)}, bf16[96,768]{1,0:T(8,128)(2,1)S(1)}, u32[]{:S(2)}, u32[]{:S(2)}) %collective-permute-start.4) | collective-permute-done | bytes 147488 | tf_op jit(solution)/shard_map/ppermute | solution.py:52
  65.6 0.6 collective-permute-start.18
  66.3 1.6 %collective-permute-done.18.refs_4_ = bf16[384,768]{1,0:T(8,128)(2,1)S(1)} collective-permute-done((bf16[384,768]{1,0:T(8,128)(2,1)S(1)}, bf16[384,768]{1,0:T(8,128)(2,1)S(1)}, u32[]{:S(2)}, u32[]{:S(2)}) %collective-permute-start.18) | collective-permute-done | bytes 589856 | tf_op jit(solution)/shard_map/ppermute | solution.py:52
  67.9 3.5 %project.1 = (bf16[16,32,768]{2,1,0:T(8,128)(2,1)S(1)}, bf16[4,32,768]{2,1,0:T(8,128)(2,1)S(1)}, bf16[48,768]{1,0:T(8,128)(2,1)S(1)}, bf16[16,768]{1,0:T(8,128)(2,1)S(1)}) custom-call(s32[3]{0:T(128)S(1)} %pad_add_fusion.place.refs_0_, bf16[512,768]{1,0:T(8,128)(2,1)S(1)} %attend.1.refs_1_, bf16[512,768]{1,0:T(8,128)(2,1)S(1)} %get-tuple-element.41.refs_2_, ...), custom_call_target="tpu_custom_call" | custom-call | flops 3449999872 | tf_op jit(solution)/shard_map/project/pallas_call | solution.py:316
  71.8 1.7 %collective-permute-start.20 = (bf16[48,768]{1,0:T(8,128)(2,1)S(1)}, bf16[48,768]{1,0:T(8,128)(2,1)S(1)}, u32[]{:S(2)}, u32[]{:S(2)}) collective-permute-start(bf16[48,768]{1,0:T(8,128)(2,1)S(1)} %get-tuple-element.48), channel_id=1, source_target_pairs={{0,3},{1,0},{2,1},{3,2},{4,7},{5,4},{6,5},{7,6},{8,11},{9,8},{10,9... | collective-permute-start | bytes 221192 | tf_op jit(solution)/shard_map/ppermute | solution.py:37
  73.6 0.8 collective-permute-start.21
  74.5 3.4 %collective-permute-done.21.corner = bf16[16,768]{1,0:T(8,128)(2,1)S(1)} collective-permute-done((bf16[16,768]{1,0:T(8,128)(2,1)S(1)}, bf16[16,768]{1,0:T(8,128)(2,1)S(1)}, u32[]{:S(2)}, u32[]{:S(2)}) %collective-permute-start.21) | collective-permute-done | bytes 24608 | tf_op jit(solution)/shard_map/ppermute | solution.py:47
  77.9 1.6 %dispatch.1 = (bf16[512,768]{1,0:T(8,128)(2,1)S(1)}, bf16[128,768]{1,0:T(8,128)(2,1)S(1)}, bf16[128,768]{1,0:T(8,128)(2,1)S(1)}, bf16[128,768]{1,0:T(8,128)(2,1)S(1)}, bf16[128,768]{1,0:T(8,128)(2,1)S(1)}) custom-call(s32[3]{0:T(128)S(1)} %pad_add_fusion.place.refs_0_, bf16[16,32,768]{2,1,0:T(8,128)(2,1)S(1)} %get-tuple-element.46.rolled, ...), custom_call_target="tpu_custom_call" | custom-call | tf_op jit(solution)/shard_map/dispatch/pallas_call | solution.py:377
  79.5 0.7 copy-done.5
  81.1 1.3 %collective-permute-start.24 = (bf16[128,768]{1,0:T(8,128)(2,1)S(1)}, bf16[128,768]{1,0:T(8,128)(2,1)S(1)}, u32[]{:S(2)}, u32[]{:S(2)}) collective-permute-start(bf16[128,768]{1,0:T(8,128)(2,1)S(1)} %get-tuple-element.54), channel_id=1, source_target_pairs={{0,12},{4,8},{8,4},{12,0},{1,13},{5,9},{9,5},{13,1},{2,14},{6,10},... | collective-permute-start | bytes 589832 | tf_op jit(solution)/shard_map/ppermute | solution.py:52
  82.3 4.4 %collective-permute-done.23.refs_2_ = bf16[128,768]{1,0:T(8,128)(2,1)S(1)} collective-permute-done((bf16[128,768]{1,0:T(8,128)(2,1)S(1)}, bf16[128,768]{1,0:T(8,128)(2,1)S(1)}, u32[]{:S(2)}, u32[]{:S(2)}) %collective-permute-start.23) | collective-permute-done | bytes 196640 | tf_op jit(solution)/shard_map/ppermute | solution.py:52
  86.8 4.6 %collective-permute-done.24.refs_3_ = bf16[128,768]{1,0:T(8,128)(2,1)S(1)} collective-permute-done((bf16[128,768]{1,0:T(8,128)(2,1)S(1)}, bf16[128,768]{1,0:T(8,128)(2,1)S(1)}, u32[]{:S(2)}, u32[]{:S(2)}) %collective-permute-start.24) | collective-permute-done | bytes 196640 | tf_op jit(solution)/shard_map/ppermute | solution.py:52
  91.3 0.7 copy-done.11
  92.0 15.5 %experts.1 = (bf16[128,768]{1,0:T(8,128)(2,1)}, bf16[128,768]{1,0:T(8,128)(2,1)}, bf16[128,768]{1,0:T(8,128)(2,1)}, bf16[128,768]{1,0:T(8,128)(2,1)}) custom-call(bf16[128,768]{1,0:T(8,128)(2,1)} %copy-done.5, bf16[128,768]{1,0:T(8,128)(2,1)} %copy-done.9, bf16[128,768]{1,0:T(8,128)(2,1)} %copy-done.10, bf16[128,768]{1,0:T(8,128)(2,1)} %copy-done.11, ...), custom_call_target="tpu_custom_call" | custom-call | flops 13799999488 | tf_op jit(solution)/shard_map/experts/pallas_call | solution.py:435
  107.7 0.6 collective-permute-start.26
  108.3 1.5 %collective-permute-start.27 = (bf16[128,768]{1,0:T(8,128)(2,1)}, bf16[128,768]{1,0:T(8,128)(2,1)S(1)}, u32[]{:S(2)}, u32[]{:S(2)}) collective-permute-start(bf16[128,768]{1,0:T(8,128)(2,1)} %get-tuple-element.58), channel_id=1, source_target_pairs={{0,12},{4,8},{8,4},{12,0},{1,13},{5,9},{9,5},{13,1},{2,14},{6,10},... | collective-permute-start | bytes 589832 | tf_op jit(solution)/shard_map/ppermute | solution.py:52
  110.3 3.7 %collective-permute-done.26.refs_2_ = bf16[128,768]{1,0:T(8,128)(2,1)S(1)} collective-permute-done((bf16[128,768]{1,0:T(8,128)(2,1)}, bf16[128,768]{1,0:T(8,128)(2,1)S(1)}, u32[]{:S(2)}, u32[]{:S(2)}) %collective-permute-start.26) | collective-permute-done | bytes 196640 | tf_op jit(solution)/shard_map/ppermute | solution.py:52
  113.9 4.8 %collective-permute-done.27.refs_3_ = bf16[128,768]{1,0:T(8,128)(2,1)S(1)} collective-permute-done((bf16[128,768]{1,0:T(8,128)(2,1)}, bf16[128,768]{1,0:T(8,128)(2,1)S(1)}, u32[]{:S(2)}, u32[]{:S(2)}) %collective-permute-start.27) | collective-permute-done | bytes 196640 | tf_op jit(solution)/shard_map/ppermute | solution.py:52
  118.7 0.9 copy-done.2
  119.7 3.1 %combine.1 = bf16[512,768]{1,0:T(8,128)(2,1)} custom-call(s32[3]{0:T(128)S(1)} %pad_add_fusion.place.refs_0_, bf16[512,768]{1,0:T(8,128)(2,1)S(1)} %get-tuple-element.50.attended, s32[512,1]{1,0:T(8,128)S(1)} %select_n.46.position, s32[512,1]{1,0:T(8,128)S(1)} %select_n.47.constant_at, f32[16,768]{1,0:T(8,128)S(1)} %copy-done.4, ...), custom_call_target="tpu_custom_call" | custom-call | tf_op jit(solution)/shard_map/combine/pallas_call | solution.py:475
  (56 shorter events, 3.4 us)
Async XLA Ops:
  1.0 9.0 %collective-permute-start.2 = (bf16[7,32,768]{2,1,0:T(8,128)(2,1)S(1)}, bf16[7,32,768]{2,1,0:T(8,128)(2,1)S(1)}, u32[]{:S(2)}, u32[]{:S(2)}) collective-permute-start(bf16[7,32,768]{2,1,0:T(8,128)(2,1)S(1)} %slice.9), channel_id=1, source_target_pairs={{0,4},{4,8},{8,12},{12,0},{1,5},{5,9},{9,13},{13,1},{2,6},{6,10},{... | collective-permute-start | bytes 1032200 | tf_op jit(solution)/shard_map/ppermute | solution.py:37
  3.7 6.4 %collective-permute-start = (bf16[48,2304]{1,0:T(8,128)(2,1)}, bf16[48,2304]{1,0:T(8,128)(2,1)S(1)}, u32[]{:S(2)}, u32[]{:S(2)}) collective-permute-start(bf16[48,2304]{1,0:T(8,128)(2,1)} %param.13), channel_id=1, source_target_pairs={{0,1},{1,0},{2,3},{3,2},{4,5},{5,4},{6,7},{7,6},{8,9},{9,8},{10,11... | collective-permute-start | bytes 663560 | tf_op jit(solution)/shard_map/ppermute | solution.py:52
  5.0 4.6 %collective-permute-start.1 = (bf16[48,768]{1,0:T(8,128)(2,1)}, bf16[48,768]{1,0:T(8,128)(2,1)S(1)}, u32[]{:S(2)}, u32[]{:S(2)}) collective-permute-start(bf16[48,768]{1,0:T(8,128)(2,1)} %param.14), channel_id=1, source_target_pairs={{0,8},{4,12},{8,0},{12,4},{1,9},{5,13},{9,1},{13,5},{2,10},{6,14},... | collective-permute-start | bytes 221192 | tf_op jit(solution)/shard_map/ppermute | solution.py:52
  10.1 10.9 %collective-permute-start.8 = (bf16[23,8,768]{2,1,0:T(8,128)(2,1)S(1)}, bf16[23,8,768]{2,1,0:T(8,128)(2,1)S(1)}, u32[]{:S(2)}, u32[]{:S(2)}) collective-permute-start(bf16[23,8,768]{2,1,0:T(8,128)(2,1)S(1)} %pad_maximum_fusion), channel_id=1, source_target_pairs={{0,1},{1,2},{2,3},{3,0},{4,5},{5,6},{6,7},{7,4},{8,9},{9,10},{10,1... | collective-permute-start | bytes 847880 | tf_op jit(solution)/shard_map/ppermute | solution.py:37
  11.9 22.5 %collective-permute-start.7 = (bf16[96,2304]{1,0:T(8,128)(2,1)S(1)}, bf16[96,2304]{1,0:T(8,128)(2,1)S(1)}, u32[]{:S(2)}, u32[]{:S(2)}) collective-permute-start(bf16[96,2304]{1,0:T(8,128)(2,1)S(1)} %constant_dynamic-update-slice_fusion.2.refs_3_), channel_id=1, source_target_pairs={{0,8},{4,12},{8,0},{12,4},{1,9},{5,13},{9,1},{13,5},{2,10},{6,14},... | collective-permute-start | bytes 1327112 | tf_op jit(solution)/shard_map/ppermute | solution.py:52
  13.1 21.3 %collective-permute-start.6 = (bf16[96,1152]{1,0:T(8,128)(2,1)S(1)}, bf16[96,1152]{1,0:T(8,128)(2,1)S(1)}, u32[]{:S(2)}, u32[]{:S(2)}) collective-permute-start(bf16[96,1152]{1,0:T(8,128)(2,1)S(1)} %constant_dynamic-slice_fusion), channel_id=1, source_target_pairs={{0,2},{1,3},{2,0},{3,1},{4,6},{5,7},{6,4},{7,5},{8,10},{9,11},{10,... | collective-permute-start | bytes 663560 | tf_op jit(solution)/shard_map/ppermute | solution.py:52
  15.5 23.6 %collective-permute-start.11 = (bf16[96,2304]{1,0:T(8,128)(2,1)S(1)}, bf16[96,2304]{1,0:T(8,128)(2,1)S(1)}, u32[]{:S(2)}, u32[]{:S(2)}) collective-permute-start(bf16[96,2304]{1,0:T(8,128)(2,1)S(1)} %constant_dynamic-update-slice_fusion.2.refs_3_), channel_id=1, source_target_pairs={{0,4},{4,0},{8,12},{12,8},{1,5},{5,1},{9,13},{13,9},{2,6},{6,2},{1... | collective-permute-start | bytes 1327112 | tf_op jit(solution)/shard_map/ppermute | solution.py:52
  20.9 1.1 copy-start
  22.1 1.1 copy-start.1
  23.2 0.9 copy-start.3
  34.4 6.0 %collective-permute-start.9 = (bf16[96,1152]{1,0:T(8,128)(2,1)S(1)}, bf16[96,1152]{1,0:T(8,128)(2,1)S(1)}, u32[]{:S(2)}, u32[]{:S(2)}) collective-permute-start(bf16[96,1152]{1,0:T(8,128)(2,1)S(1)} %collective-permute-done.6.refs_5_), channel_id=1, source_target_pairs={{0,16},{16,0},{1,17},{17,1},{2,18},{18,2},{3,19},{19,3},{4,20},{20... | collective-permute-start | bytes 663560 | tf_op jit(solution)/shard_map/ppermute | solution.py:52
  35.5 7.5 %collective-permute-start.10 = (bf16[96,1152]{1,0:T(8,128)(2,1)S(1)}, bf16[96,1152]{1,0:T(8,128)(2,1)S(1)}, u32[]{:S(2)}, u32[]{:S(2)}) collective-permute-start(bf16[96,1152]{1,0:T(8,128)(2,1)S(1)} %collective-permute-done.6.refs_5_), channel_id=1, source_target_pairs={{0,8},{4,12},{8,0},{12,4},{1,9},{5,13},{9,1},{13,5},{2,10},{6,14},... | collective-permute-start | bytes 663560 | tf_op jit(solution)/shard_map/ppermute | solution.py:52
  36.4 9.6 %collective-permute-start.16 = (bf16[96,1152]{1,0:T(8,128)(2,1)S(1)}, bf16[96,1152]{1,0:T(8,128)(2,1)S(1)}, u32[]{:S(2)}, u32[]{:S(2)}) collective-permute-start(bf16[96,1152]{1,0:T(8,128)(2,1)S(1)} %collective-permute-done.6.refs_5_), channel_id=1, source_target_pairs={{0,24},{4,28},{8,16},{12,20},{16,8},{20,12},{24,0},{28,4},{1,25},{... | collective-permute-start | bytes 663560 | tf_op jit(solution)/shard_map/ppermute | solution.py:505
  37.1 15.7 %collective-permute-start.12 = (bf16[96,2304]{1,0:T(8,128)(2,1)S(1)}, bf16[96,2304]{1,0:T(8,128)(2,1)S(1)}, u32[]{:S(2)}, u32[]{:S(2)}) collective-permute-start(bf16[96,2304]{1,0:T(8,128)(2,1)S(1)} %collective-permute-done.7.refs_4_), channel_id=1, source_target_pairs={{0,4},{4,0},{8,12},{12,8},{1,5},{5,1},{9,13},{13,9},{2,6},{6,2},{1... | collective-permute-start | bytes 1327112 | tf_op jit(solution)/shard_map/ppermute | solution.py:52
  39.0 10.1 %collective-permute-start.13 = (bf16[96,1152]{1,0:T(8,128)(2,1)S(1)}, bf16[96,1152]{1,0:T(8,128)(2,1)S(1)}, u32[]{:S(2)}, u32[]{:S(2)}) collective-permute-start(bf16[96,1152]{1,0:T(8,128)(2,1)S(1)} %collective-permute-done.6.refs_5_), channel_id=1, source_target_pairs={{0,4},{4,0},{8,12},{12,8},{1,5},{5,1},{9,13},{13,9},{2,6},{6,2},{1... | collective-permute-start | bytes 663560 | tf_op jit(solution)/shard_map/ppermute | solution.py:52
  40.4 10.0 %collective-permute-start.14 = (bf16[96,1152]{1,0:T(8,128)(2,1)S(1)}, bf16[96,1152]{1,0:T(8,128)(2,1)S(1)}, u32[]{:S(2)}, u32[]{:S(2)}) collective-permute-start(bf16[96,1152]{1,0:T(8,128)(2,1)S(1)} %collective-permute-done.9.refs_6_), channel_id=1, source_target_pairs={{0,4},{4,0},{8,12},{12,8},{1,5},{5,1},{9,13},{13,9},{2,6},{6,2},{1... | collective-permute-start | bytes 663560 | tf_op jit(solution)/shard_map/ppermute | solution.py:52
  43.0 9.0 %collective-permute-start.15 = (bf16[96,1152]{1,0:T(8,128)(2,1)S(1)}, bf16[96,1152]{1,0:T(8,128)(2,1)S(1)}, u32[]{:S(2)}, u32[]{:S(2)}) collective-permute-start(bf16[96,1152]{1,0:T(8,128)(2,1)S(1)} %collective-permute-done.10.refs_7_), channel_id=1, source_target_pairs={{0,4},{4,0},{8,12},{12,8},{1,5},{5,1},{9,13},{13,9},{2,6},{6,2},{1... | collective-permute-start | bytes 663560 | tf_op jit(solution)/shard_map/ppermute | solution.py:52
  46.0 6.8 %collective-permute-start.17 = (bf16[96,1152]{1,0:T(8,128)(2,1)S(1)}, bf16[96,1152]{1,0:T(8,128)(2,1)S(1)}, u32[]{:S(2)}, u32[]{:S(2)}) collective-permute-start(bf16[96,1152]{1,0:T(8,128)(2,1)S(1)} %collective-permute-done.16.refs_13_), channel_id=1, source_target_pairs={{0,4},{4,0},{8,12},{12,8},{1,5},{5,1},{9,13},{13,9},{2,6},{6,2},{1... | collective-permute-start | bytes 663560 | tf_op jit(solution)/shard_map/ppermute | solution.py:52
  49.2 14.0 %collective-permute-start.3 = (bf16[96,768]{1,0:T(8,128)(2,1)S(1)}, bf16[96,768]{1,0:T(8,128)(2,1)S(1)}, u32[]{:S(2)}, u32[]{:S(2)}) collective-permute-start(bf16[96,768]{1,0:T(8,128)(2,1)S(1)} %constant_dynamic-update-slice_fusion), channel_id=1, source_target_pairs={{0,3},{1,2},{2,1},{3,0},{4,7},{5,6},{6,5},{7,4},{8,11},{9,10},{10,... | collective-permute-start | bytes 442376 | tf_op jit(solution)/shard_map/ppermute | solution.py:52
  50.3 15.2 %collective-permute-start.4 = (bf16[96,768]{1,0:T(8,128)(2,1)S(1)}, bf16[96,768]{1,0:T(8,128)(2,1)S(1)}, u32[]{:S(2)}, u32[]{:S(2)}) collective-permute-start(bf16[96,768]{1,0:T(8,128)(2,1)S(1)} %constant_dynamic-update-slice_fusion), channel_id=1, source_target_pairs={{0,2},{1,3},{2,0},{3,1},{4,6},{5,7},{6,4},{7,5},{8,10},{9,11},{10,... | collective-permute-start | bytes 442376 | tf_op jit(solution)/shard_map/ppermute | solution.py:52
  52.0 13.6 %collective-permute-start.5 = (bf16[96,768]{1,0:T(8,128)(2,1)S(1)}, bf16[96,768]{1,0:T(8,128)(2,1)S(1)}, u32[]{:S(2)}, u32[]{:S(2)}) collective-permute-start(bf16[96,768]{1,0:T(8,128)(2,1)S(1)} %constant_dynamic-update-slice_fusion), channel_id=1, source_target_pairs={{0,1},{1,0},{2,3},{3,2},{4,5},{5,4},{6,7},{7,6},{8,9},{9,8},{10,11... | collective-permute-start | bytes 442376 | tf_op jit(solution)/shard_map/ppermute | solution.py:52
  52.8 21.6 %copy-start.6 = (s32[16,32]{1,0:T(8,128)S(1)}, s32[16,32]{1,0:T(8,128)}, u32[]{:S(2)}) copy-start(s32[16,32]{1,0:T(8,128)} %param.21) | copy-start | bytes 6148
  52.8 21.6 %copy-start.7 = (s32[16,32]{1,0:T(8,128)S(1)}, s32[16,32]{1,0:T(8,128)}, u32[]{:S(2)}) copy-start(s32[16,32]{1,0:T(8,128)} %param.19) | copy-start | bytes 6148
  52.8 21.6 %copy-start.8 = (s32[16,32]{1,0:T(8,128)S(1)}, s32[16,32]{1,0:T(8,128)}, u32[]{:S(2)}) copy-start(s32[16,32]{1,0:T(8,128)} %param.20) | copy-start | bytes 6148
  65.6 2.3 %collective-permute-start.18 = (bf16[384,768]{1,0:T(8,128)(2,1)S(1)}, bf16[384,768]{1,0:T(8,128)(2,1)S(1)}, u32[]{:S(2)}, u32[]{:S(2)}) collective-permute-start(bf16[384,768]{1,0:T(8,128)(2,1)S(1)} %constant_dynamic-update-slice_fusion.4.refs_3_), channel_id=1, source_target_pairs={{0,4},{4,0},{8,12},{12,8},{1,5},{5,1},{9,13},{13,9},{2,6},{6,2},{1... | collective-permute-start | bytes 1769480 | tf_op jit(solution)/shard_map/ppermute | solution.py:52
  71.4 6.5 %collective-permute-start.19 = (bf16[4,32,768]{2,1,0:T(8,128)(2,1)S(1)}, bf16[4,32,768]{2,1,0:T(8,128)(2,1)S(1)}, u32[]{:S(2)}, u32[]{:S(2)}) collective-permute-start(bf16[4,32,768]{2,1,0:T(8,128)(2,1)S(1)} %get-tuple-element.47), channel_id=1, source_target_pairs={{0,12},{4,0},{8,4},{12,8},{1,13},{5,1},{9,5},{13,9},{2,14},{6,2},{... | collective-permute-start | bytes 589832 | tf_op jit(solution)/shard_map/ppermute | solution.py:37
  71.8 6.0 %collective-permute-start.20 = (bf16[48,768]{1,0:T(8,128)(2,1)S(1)}, bf16[48,768]{1,0:T(8,128)(2,1)S(1)}, u32[]{:S(2)}, u32[]{:S(2)}) collective-permute-start(bf16[48,768]{1,0:T(8,128)(2,1)S(1)} %get-tuple-element.48), channel_id=1, source_target_pairs={{0,3},{1,0},{2,1},{3,2},{4,7},{5,4},{6,5},{7,6},{8,11},{9,8},{10,9... | collective-permute-start | bytes 221192 | tf_op jit(solution)/shard_map/ppermute | solution.py:37
  73.6 4.3 %collective-permute-start.21 = (bf16[16,768]{1,0:T(8,128)(2,1)S(1)}, bf16[16,768]{1,0:T(8,128)(2,1)S(1)}, u32[]{:S(2)}, u32[]{:S(2)}) collective-permute-start(bf16[16,768]{1,0:T(8,128)(2,1)S(1)} %get-tuple-element.49), channel_id=1, source_target_pairs={{0,15},{1,12},{2,13},{3,14},{4,3},{5,0},{6,1},{7,2},{8,7},{9,4},{1... | collective-permute-start | bytes 73736 | tf_op jit(solution)/shard_map/ppermute | solution.py:47
  79.5 0.7 copy-start.5
  80.2 2.1 %collective-permute-start.22 = (bf16[128,768]{1,0:T(8,128)(2,1)S(1)}, bf16[128,768]{1,0:T(8,128)(2,1)S(1)}, u32[]{:S(2)}, u32[]{:S(2)}) collective-permute-start(bf16[128,768]{1,0:T(8,128)(2,1)S(1)} %get-tuple-element.52), channel_id=1, source_target_pairs={{0,4},{4,0},{8,12},{12,8},{1,5},{5,1},{9,13},{13,9},{2,6},{6,2},{1... | collective-permute-start | bytes 589832 | tf_op jit(solution)/shard_map/ppermute | solution.py:52
  80.5 6.3 %collective-permute-start.23 = (bf16[128,768]{1,0:T(8,128)(2,1)S(1)}, bf16[128,768]{1,0:T(8,128)(2,1)S(1)}, u32[]{:S(2)}, u32[]{:S(2)}) collective-permute-start(bf16[128,768]{1,0:T(8,128)(2,1)S(1)} %get-tuple-element.53), channel_id=1, source_target_pairs={{0,8},{4,12},{8,0},{12,4},{1,9},{5,13},{9,1},{13,5},{2,10},{6,14},... | collective-permute-start | bytes 589832 | tf_op jit(solution)/shard_map/ppermute | solution.py:52
  81.1 10.2 %collective-permute-start.24 = (bf16[128,768]{1,0:T(8,128)(2,1)S(1)}, bf16[128,768]{1,0:T(8,128)(2,1)S(1)}, u32[]{:S(2)}, u32[]{:S(2)}) collective-permute-start(bf16[128,768]{1,0:T(8,128)(2,1)S(1)} %get-tuple-element.54), channel_id=1, source_target_pairs={{0,12},{4,8},{8,4},{12,0},{1,13},{5,9},{9,5},{13,1},{2,14},{6,10},... | collective-permute-start | bytes 589832 | tf_op jit(solution)/shard_map/ppermute | solution.py:52
  82.3 9.0 %copy-start.9 = (bf16[128,768]{1,0:T(8,128)(2,1)}, bf16[128,768]{1,0:T(8,128)(2,1)S(1)}, u32[]{:S(2)}) copy-start(bf16[128,768]{1,0:T(8,128)(2,1)S(1)} %collective-permute-done.22.refs_1_) | copy-start | bytes 589828
  86.7 4.6 %copy-start.10 = (bf16[128,768]{1,0:T(8,128)(2,1)}, bf16[128,768]{1,0:T(8,128)(2,1)S(1)}, u32[]{:S(2)}) copy-start(bf16[128,768]{1,0:T(8,128)(2,1)S(1)} %collective-permute-done.23.refs_2_) | copy-start | bytes 589828
  91.3 0.7 copy-start.11
  92.0 26.8 %copy-start.4 = (f32[16,768]{1,0:T(8,128)S(1)}, f32[16,768]{1,0:T(8,128)}, u32[]{:S(2)}) copy-start(f32[16,768]{1,0:T(8,128)} %table.1) | copy-start | bytes 147460
  107.5 2.7 %collective-permute-start.25 = (bf16[128,768]{1,0:T(8,128)(2,1)}, bf16[128,768]{1,0:T(8,128)(2,1)S(1)}, u32[]{:S(2)}, u32[]{:S(2)}) collective-permute-start(bf16[128,768]{1,0:T(8,128)(2,1)} %get-tuple-element.56), channel_id=1, source_target_pairs={{0,4},{4,0},{8,12},{12,8},{1,5},{5,1},{9,13},{13,9},{2,6},{6,2},{1... | collective-permute-start | bytes 589832 | tf_op jit(solution)/shard_map/ppermute | solution.py:52
  107.7 6.3 %collective-permute-start.26 = (bf16[128,768]{1,0:T(8,128)(2,1)}, bf16[128,768]{1,0:T(8,128)(2,1)S(1)}, u32[]{:S(2)}, u32[]{:S(2)}) collective-permute-start(bf16[128,768]{1,0:T(8,128)(2,1)} %get-tuple-element.57), channel_id=1, source_target_pairs={{0,8},{4,12},{8,0},{12,4},{1,9},{5,13},{9,1},{13,5},{2,10},{6,14},... | collective-permute-start | bytes 589832 | tf_op jit(solution)/shard_map/ppermute | solution.py:52
  108.3 10.4 %collective-permute-start.27 = (bf16[128,768]{1,0:T(8,128)(2,1)}, bf16[128,768]{1,0:T(8,128)(2,1)S(1)}, u32[]{:S(2)}, u32[]{:S(2)}) collective-permute-start(bf16[128,768]{1,0:T(8,128)(2,1)} %get-tuple-element.58), channel_id=1, source_target_pairs={{0,12},{4,8},{8,4},{12,0},{1,13},{5,9},{9,5},{13,1},{2,14},{6,10},... | collective-permute-start | bytes 589832 | tf_op jit(solution)/shard_map/ppermute | solution.py:52
  118.7 0.9 copy-start.2

commit v4 on v3

--- a/solution.py
+++ b/solution.py
@@ -22,8 +22,6 @@
 ANY = pl.BlockSpec(memory_space=pl.ANY)
 HBM = pl.BlockSpec(memory_space=pltpu.HBM)
 LARGEST = 3.38e38
-DEPTH = 3
-PARTS = 2
 
 
 def lasting(microseconds):
@@ -254,7 +252,7 @@
             pltpu.VMEM((rows * cols, 3 * channels), jnp.bfloat16),
             pltpu.SemaphoreType.DMA((sum(len(p[0]) for p in ids),)),
         ],
-        compiler_params=pltpu.CompilerParams(vmem_limit_bytes=18 * 1024 * 1024),
+        compiler_params=pltpu.CompilerParams(vmem_limit_bytes=16 * 1024 * 1024),
         cost_estimate=lasting(10),
         name="attend",
     )(place, normed, bias, *[p[0] for p in pieces])
@@ -327,7 +325,7 @@
             pltpu.VMEM((channels, channels), jnp.bfloat16),
             pltpu.SemaphoreType.DMA((sum(len(p[0]) for p in ids),)),
         ],
-        compiler_params=pltpu.CompilerParams(vmem_limit_bytes=12 * 1024 * 1024),
+        compiler_params=pltpu.CompilerParams(vmem_limit_bytes=10 * 1024 * 1024),
         cost_estimate=lasting(3),
         name="project",
     )(place, context, encoded, *[p[0] for p in pieces])
@@ -360,115 +358,99 @@
         )
         attended[row * cols : (row + 1) * cols] = line.astype(jnp.bfloat16)
         normed[row * cols : (row + 1) * cols] = normalized(line)
-    for mask, target in enumerate(outgoing):
-        count = target.shape[0]
+    for mask in range(len(outgoing) // 2):
+        halves = outgoing[2 * mask : 2 * mask + 2]
+        count = 2 * halves[0].shape[0]
         spot = lax.broadcasted_iota(jnp.int32, (count, rows * cols), 0)
         spot = spot + (place[0] ^ mask) * count
         chosen = jnp.where(position[...] == spot, 1.0, 0.0).astype(jnp.bfloat16)
-        target[...] = jnp.dot(
-            chosen, normed[...], preferred_element_type=jnp.float32
-        ).astype(jnp.bfloat16)
+        slots = jnp.dot(chosen, normed[...], preferred_element_type=jnp.float32)
+        slots = slots.astype(jnp.bfloat16)
+        for at, target in enumerate(halves):
+            target[...] = slots[at * count // 2 : (at + 1) * count // 2]
 
 
 def dispatch(place, rolled, below, right, corner, position, grid_rows):
     rows, cols, channels = rolled.shape
     bf16 = functools.partial(jax.ShapeDtypeStruct, dtype=jnp.bfloat16)
-    slot_rows = EXPERTS * CAP // grid_rows
+    slot_rows = EXPERTS * CAP // grid_rows // 2
     return pl.pallas_call(
         dispatch_kernel,
-        out_shape=(bf16((rows * cols, channels)),) + (bf16((slot_rows, channels)),) * grid_rows,
+        out_shape=(bf16((rows * cols, channels)),) + (bf16((slot_rows, channels)),) * (2 * grid_rows),
         in_specs=[SMEM] + [VMEM] * 5,
-        out_specs=(VMEM,) * (grid_rows + 1),
+        out_specs=(VMEM,) * (2 * grid_rows + 1),
         scratch_shapes=[pltpu.VMEM((rows * cols, channels), jnp.bfloat16)],
-        compiler_params=pltpu.CompilerParams(vmem_limit_bytes=24 * 1024 * 1024),
+        compiler_params=pltpu.CompilerParams(vmem_limit_bytes=10 * 1024 * 1024),
         name="dispatch",
     )(place, rolled, below, right, corner, position)
 
 
-def expert_kernel(count, *refs):
-    incoming, (all_in, all_out), results = refs[:count], refs[count : count + 2], refs[count + 2 : -3]
-    held_in, held_out, sems = refs[-3:]
-    experts, hidden_units = all_in.shape[:2]
-    part = hidden_units // PARTS
-
-    def copies(expert):
-        slot = expert % held_in.shape[0]
-        return [
-            pltpu.make_async_copy(
-                source.at[expert, pl.ds(at * part, part), :],
-                target.at[slot, pl.ds(at * part, part), :],
-                sems.at[slot, which, at],
-            )
-            for which, (source, target) in enumerate(((all_in, held_in), (all_out, held_out)))
-            for at in range(PARTS)
+def expert_kernel(count, first, *refs):
+    incoming, sources = refs[:count], refs[count : count + 2]
+    results, (held_in, held_out, sems) = refs[-3 - count : -3], refs[-3:]
+    copies = [
+        [
+            pltpu.make_async_copy(source.at[first + slot], target.at[slot], sems.at[slot, which])
+            for which, (source, target) in enumerate(zip(sources, (held_in, held_out), strict=True))
         ]
-
-    for expert in range(min(experts, held_in.shape[0])):
-        for copy in copies(expert):
+        for slot in range(held_in.shape[0])
+    ]
+    for pair in copies:
+        for copy in pair:
             copy.start()
-    for expert in range(experts):
-        slot = expert % held_in.shape[0]
-        own = pl.ds(expert * CAP, CAP)
+    for slot, (copy_in, copy_out) in enumerate(copies):
+        own = pl.ds(slot * CAP, CAP)
         rows = jnp.concatenate([ref[own, :] for ref in incoming], axis=0)
-        arriving = copies(expert)
-        for copy in arriving[:PARTS]:
-            copy.wait()
+        copy_in.wait()
         hidden = lax.dot_general(
             rows, held_in[slot], (((1,), (1,)), ((), ())), preferred_element_type=jnp.float32
         )
         hidden = (0.5 * hidden * (1.0 + lax.erf(hidden * 0.5**0.5))).astype(jnp.bfloat16)
-        for copy in arriving[PARTS:]:
-            copy.wait()
+        copy_out.wait()
         result = jnp.dot(hidden, held_out[slot], preferred_element_type=jnp.float32)
         result = result.astype(jnp.bfloat16)
         for at, ref in enumerate(results):
             ref[own, :] = result[at * CAP : (at + 1) * CAP]
-        if expert + held_in.shape[0] < experts:
-            for copy in copies(expert + held_in.shape[0]):
-                copy.start()
-
-
-def serve(incoming, expert_in, expert_out):
+
+
+def serve(incoming, weights, first, number):
     count = len(incoming)
-    experts, hidden, channels = expert_in.shape
-    depth = min(DEPTH, experts)
+    shape = (number, *weights[0].shape[1:])
     return pl.pallas_call(
-        functools.partial(expert_kernel, count),
+        functools.partial(expert_kernel, count, first),
         out_shape=tuple(jax.ShapeDtypeStruct(x.shape, x.dtype) for x in incoming),
         in_specs=[VMEM] * count + [HBM, HBM],
         out_specs=(VMEM,) * count,
         scratch_shapes=[
-            pltpu.VMEM((depth, hidden, channels), jnp.bfloat16),
-            pltpu.VMEM((depth, hidden, channels), jnp.bfloat16),
-            pltpu.SemaphoreType.DMA((depth, 2, PARTS)),
+            pltpu.VMEM(shape, jnp.bfloat16),
+            pltpu.VMEM(shape, jnp.bfloat16),
+            pltpu.SemaphoreType.DMA((number, 2)),
         ],
-        compiler_params=pltpu.CompilerParams(vmem_limit_bytes=56 * 1024 * 1024),
-        cost_estimate=lasting(12),
+        compiler_params=pltpu.CompilerParams(vmem_limit_bytes=52 * 1024 * 1024),
+        cost_estimate=lasting(7),
         name="experts",
-    )(*incoming, expert_in, expert_out)
+    )(*incoming, *weights)
 
 
 def combine_kernel(place, attended, position, constant_at, table, *refs):
     results, output = refs[:-1], refs[-1]
     tokens = attended.shape[0]
-    total = attended[...].astype(jnp.float32)
-    for mask, result in enumerate(results):
-        count = result.shape[0]
-        spot = lax.broadcasted_iota(jnp.int32, (tokens, count), 1)
-        spot = spot + (place[0] ^ mask) * count
-        chosen = jnp.where(position[...] == spot, 1.0, 0.0).astype(jnp.bfloat16)
-        total = total + jnp.dot(chosen, result[...], preferred_element_type=jnp.float32)
+    rows = jnp.concatenate([result[...] for result in results], axis=0)
+    total, count = rows.shape[0], 2 * results[0].shape[0]
+    spot = lax.broadcasted_iota(jnp.int32, (tokens, total), 1)
+    spot = (spot // count ^ place[0]) * count + spot % count
+    chosen = jnp.where(position[...] == spot, 1.0, 0.0).astype(jnp.bfloat16)
     entries = table.shape[0]
-    spot = lax.broadcasted_iota(jnp.int32, (tokens, entries), 1)
-    chosen = jnp.where(constant_at[...] == spot, 1.0, 0.0).astype(jnp.bfloat16)
-    rest = table[...]
-    constant = None
+    spot = lax.broadcasted_iota(jnp.int32, (tokens, 3 * entries), 1) % entries
+    constant = jnp.where(constant_at[...] == spot, 1.0, 0.0).astype(jnp.bfloat16)
+    parts, rest = [], table[...]
     for _ in range(3):
-        part = rest.astype(jnp.bfloat16)
-        rest = rest - part.astype(jnp.float32)
-        term = jnp.dot(chosen, part, preferred_element_type=jnp.float32)
-        constant = term if constant is None else constant + term
-    output[...] = (total + constant).astype(jnp.bfloat16)
+        parts.append(rest.astype(jnp.bfloat16))
+        rest = rest - parts[-1].astype(jnp.float32)
+    parts = jnp.concatenate(parts, axis=0)
+    mixture = jnp.dot(chosen, rows, preferred_element_type=jnp.float32)
+    mixture = mixture + jnp.dot(constant, parts, preferred_element_type=jnp.float32)
+    output[...] = (attended[...].astype(jnp.float32) + mixture).astype(jnp.bfloat16)
 
 
 def combine(place, attended, position, constant_at, table, results):
@@ -477,7 +459,7 @@
         out_shape=jax.ShapeDtypeStruct(attended.shape, jnp.bfloat16),
         in_specs=[SMEM] + [VMEM] * (4 + len(results)),
         out_specs=VMEM,
-        compiler_params=pltpu.CompilerParams(vmem_limit_bytes=24 * 1024 * 1024),
+        compiler_params=pltpu.CompilerParams(vmem_limit_bytes=12 * 1024 * 1024),
         name="combine",
     )(place, attended, position, constant_at, table, *results)
 
@@ -572,9 +554,18 @@
     attended, *outgoing = dispatch(
         place, rolled, below, right, last, position[None, :], grid_rows
     )
-    incoming = [outgoing[0]] + [exchanged(outgoing[m], "gy", m) for m in range(1, grid_rows)]
-    served = serve(incoming, expert_in, expert_out)
-    results = [served[0]] + [exchanged(served[m], "gy", m) for m in range(1, grid_rows)]
+    half, results = expert_in.shape[0] // 2, [None] * len(outgoing)
+    incoming = [
+        [
+            exchanged(outgoing[2 * mask + h], "gy", mask) if mask else outgoing[h]
+            for mask in range(grid_rows)
+        ]
+        for h in range(2)
+    ]
+    for h, arrived in enumerate(incoming):
+        served = serve(arrived, (expert_in, expert_out), h * half, half)
+        for mask, array in enumerate(served):
+            results[2 * mask + h] = exchanged(array, "gy", mask) if mask else array
     output = combine(
         place, attended, position[:, None], constant_at[:, None], const_table, results
     )

time: 123 us -> 114 us (0.927)
  waiting for transfers between devices: 33.7 us -> 23.6 us
  starting transfers between devices: 34.4 us -> 38.8 us
  local copies, waits for them, and re-layouts: 9.92 us -> 7.64 us
    ppermute x22 -> x28, waiting for transfers between devices: 25.8 us -> 15.6 us  [exchanged(): return lax.ppermute(x, axis, [(i, i ^ mask) for i in range(size)])]
    ppermute x22 -> x28, starting transfers between devices: 26.3 us -> 30.7 us  [exchanged(): return lax.ppermute(x, axis, [(i, i ^ mask) for i in range(size)])]
    unnamed x29 -> x19, local copies, waits for them, and re-layouts: 7.33 us -> 5.05 us
    pallas_call x1 -> x2, Pallas kernels: 15.5 us -> 15.1 us  [serve(): pl.pallas_call(functools.partial(expert_kernel, count, first), out_shape=...]
  transfers between devices with their start and end apart: 28 -> 34, of which waited for: 12 -> 12; matrix products, arithmetic and copies ran while one was open for 3% -> 3% of each run, Pallas kernels for 17% -> 32%
where the time goes in v4:
time: 114 us
  Pallas kernels  43.1 us (38%)
  starting transfers between devices  38.8 us (34%)
  waiting for transfers between devices  23.6 us (21%)
  local copies, waits for them, and re-layouts  7.64 us (7%)
    ppermute x28, starting transfers between devices, exchanged(): return lax.ppermute(x, axis, [(i, i ^ mask) for i in range(size)])  30.7 us
    ppermute x28, waiting for transfers between devices, exchanged(): return lax.ppermute(x, axis, [(i, i ^ mask) for i in range(size)])  15.6 us
    pallas_call x2, Pallas kernels, serve(): pl.pallas_call(functools.partial(expert_kernel, count, first), out_shape=...  15.1 us
    pallas_call x1, Pallas kernels, attend(): pl.pallas_call(functools.partial(attend_kernel, shape, ids, grid_cols), o...  10.3 us
    pallas_call x1, Pallas kernels, encode(): pl.pallas_call(encode_kernel, out_shape=(flat, flat, jax.ShapeDtypeStruct...  10.3 us
    ppermute x4, starting transfers between devices, shifted(): return lax.ppermute(x, axis, [(i, (i + by) % size) for i in range(size)])  6.59 us
    unnamed x19, local copies, waits for them, and re-layouts  5.05 us
    ppermute x4, waiting for transfers between devices, shifted(): return lax.ppermute(x, axis, [(i, (i + by) % size) for i in range(size)])  4.19 us
  transfers between devices with their start and end apart: 34, of which 12 were waited for; matrix products, arithmetic and copies ran while one was open for 3% of the time, Pallas kernels for 32%

profile of v4, /device:TPU:1, one launch (start us, length us, event | category | flops | bytes accessed | tf_op | source)
XLA Modules:
  0.0 113.5 jit_solution(160845077883592957)
XLA Ops:
  0.0 1.0 slice.9
  1.0 2.7 %collective-permute-start.2 = (bf16[7,32,768]{2,1,0:T(8,128)(2,1)S(1)}, bf16[7,32,768]{2,1,0:T(8,128)(2,1)S(1)}, u32[]{:S(2)}, u32[]{:S(2)}) collective-permute-start(bf16[7,32,768]{2,1,0:T(8,128)(2,1)S(1)} %slice.9), channel_id=1, source_target_pairs={{0,4},{4,8},{8,12},{12,0},{1,5},{5,9},{9,13},{13,1},{2,6},{6,10},{... | collective-permute-start | bytes 1032200 | tf_op jit(solution)/shard_map/ppermute | solution.py:35
  3.7 1.3 %collective-permute-start = (bf16[48,2304]{1,0:T(8,128)(2,1)}, bf16[48,2304]{1,0:T(8,128)(2,1)S(1)}, u32[]{:S(2)}, u32[]{:S(2)}) collective-permute-start(bf16[48,2304]{1,0:T(8,128)(2,1)} %param.13), channel_id=1, source_target_pairs={{0,1},{1,0},{2,3},{3,2},{4,5},{5,4},{6,7},{7,6},{8,9},{9,8},{10,11... | collective-permute-start | bytes 663560 | tf_op jit(solution)/shard_map/ppermute | solution.py:50
  5.2 0.9 constant_dynamic-update-slice_fusion.3
  6.2 0.9 slice.11
  7.1 2.4 %collective-permute-done.1 = bf16[48,768]{1,0:T(8,128)(2,1)S(1)} collective-permute-done((bf16[48,768]{1,0:T(8,128)(2,1)}, bf16[48,768]{1,0:T(8,128)(2,1)S(1)}, u32[]{:S(2)}, u32[]{:S(2)}) %collective-permute-start.1) | collective-permute-done | bytes 73760 | tf_op jit(solution)/shard_map/ppermute | solution.py:50
  10.1 1.8 %collective-permute-start.8 = (bf16[23,8,768]{2,1,0:T(8,128)(2,1)S(1)}, bf16[23,8,768]{2,1,0:T(8,128)(2,1)S(1)}, u32[]{:S(2)}, u32[]{:S(2)}) collective-permute-start(bf16[23,8,768]{2,1,0:T(8,128)(2,1)S(1)} %pad_maximum_fusion), channel_id=1, source_target_pairs={{0,1},{1,2},{2,3},{3,0},{4,5},{5,6},{6,7},{7,4},{8,9},{9,10},{10,1... | collective-permute-start | bytes 847880 | tf_op jit(solution)/shard_map/ppermute | solution.py:35
  11.9 1.2 %collective-permute-start.7 = (bf16[96,2304]{1,0:T(8,128)(2,1)S(1)}, bf16[96,2304]{1,0:T(8,128)(2,1)S(1)}, u32[]{:S(2)}, u32[]{:S(2)}) collective-permute-start(bf16[96,2304]{1,0:T(8,128)(2,1)S(1)} %constant_dynamic-update-slice_fusion.2.refs_3_), channel_id=1, source_target_pairs={{0,8},{4,12},{8,0},{12,4},{1,9},{5,13},{9,1},{13,5},{2,10},{6,14},... | collective-permute-start | bytes 1327112 | tf_op jit(solution)/shard_map/ppermute | solution.py:50
  13.1 2.4 %collective-permute-start.6 = (bf16[96,1152]{1,0:T(8,128)(2,1)S(1)}, bf16[96,1152]{1,0:T(8,128)(2,1)S(1)}, u32[]{:S(2)}, u32[]{:S(2)}) collective-permute-start(bf16[96,1152]{1,0:T(8,128)(2,1)S(1)} %constant_dynamic-slice_fusion), channel_id=1, source_target_pairs={{0,2},{1,3},{2,0},{3,1},{4,6},{5,7},{6,4},{7,5},{8,10},{9,11},{10,... | collective-permute-start | bytes 663560 | tf_op jit(solution)/shard_map/ppermute | solution.py:50
  15.5 1.2 %collective-permute-start.11 = (bf16[96,2304]{1,0:T(8,128)(2,1)S(1)}, bf16[96,2304]{1,0:T(8,128)(2,1)S(1)}, u32[]{:S(2)}, u32[]{:S(2)}) collective-permute-start(bf16[96,2304]{1,0:T(8,128)(2,1)S(1)} %constant_dynamic-update-slice_fusion.2.refs_3_), channel_id=1, source_target_pairs={{0,4},{4,0},{8,12},{12,8},{1,5},{5,1},{9,13},{13,9},{2,6},{6,2},{1... | collective-permute-start | bytes 1327112 | tf_op jit(solution)/shard_map/ppermute | solution.py:50
  16.8 4.2 %collective-permute-done.8.beside = bf16[23,8,768]{2,1,0:T(8,128)(2,1)S(1)} collective-permute-done((bf16[23,8,768]{2,1,0:T(8,128)(2,1)S(1)}, bf16[23,8,768]{2,1,0:T(8,128)(2,1)S(1)}, u32[]{:S(2)}, u32[]{:S(2)}) %collective-permute-start.8) | collective-permute-done | bytes 282656 | tf_op jit(solution)/shard_map/ppermute | solution.py:35
  21.0 1.1 copy-done
  22.1 1.1 copy-done.1
  23.2 0.9 copy-done.2
  24.1 10.3 %encode.1 = (bf16[512,768]{1,0:T(8,128)(2,1)S(1)}, bf16[512,768]{1,0:T(8,128)(2,1)S(1)}, f32[6,64,256]{2,1,0:T(8,128)S(1)}) custom-call(s32[3]{0:T(128)S(1)} %pad_add_fusion.place.refs_0_, bf16[16,32,768]{2,1,0:T(8,128)(2,1)S(1)} %copy-done, bf16[7,32,768]{2,1,0:T(8,128)(2,1)S(1)} %collective-permute-done.2.above, ...), custom_call_target="tpu_custom_call" | custom-call | flops 115000000 | tf_op jit(solution)/shard_map/encode/pallas_call | solution.py:132
  34.4 1.1 collective-permute-start.9
  35.5 0.9 collective-permute-start.10
  36.4 0.8 collective-permute-start.16
  37.1 1.9 %collective-permute-start.12 = (bf16[96,2304]{1,0:T(8,128)(2,1)S(1)}, bf16[96,2304]{1,0:T(8,128)(2,1)S(1)}, u32[]{:S(2)}, u32[]{:S(2)}) collective-permute-start(bf16[96,2304]{1,0:T(8,128)(2,1)S(1)} %collective-permute-done.7.refs_4_), channel_id=1, source_target_pairs={{0,4},{4,0},{8,12},{12,8},{1,5},{5,1},{9,13},{13,9},{2,6},{6,2},{1... | collective-permute-start | bytes 1327112 | tf_op jit(solution)/shard_map/ppermute | solution.py:50
  39.0 1.4 %collective-permute-done.9.refs_6_ = bf16[96,1152]{1,0:T(8,128)(2,1)S(1)} collective-permute-done((bf16[96,1152]{1,0:T(8,128)(2,1)S(1)}, bf16[96,1152]{1,0:T(8,128)(2,1)S(1)}, u32[]{:S(2)}, u32[]{:S(2)}) %collective-permute-start.9) | collective-permute-done | bytes 221216 | tf_op jit(solution)/shard_map/ppermute | solution.py:50
  40.4 2.6 %collective-permute-start.14 = (bf16[96,1152]{1,0:T(8,128)(2,1)S(1)}, bf16[96,1152]{1,0:T(8,128)(2,1)S(1)}, u32[]{:S(2)}, u32[]{:S(2)}) collective-permute-start(bf16[96,1152]{1,0:T(8,128)(2,1)S(1)} %collective-permute-done.9.refs_6_), channel_id=1, source_target_pairs={{0,4},{4,0},{8,12},{12,8},{1,5},{5,1},{9,13},{13,9},{2,6},{6,2},{1... | collective-permute-start | bytes 663560 | tf_op jit(solution)/shard_map/ppermute | solution.py:50
  43.0 2.7 %collective-permute-start.15 = (bf16[96,1152]{1,0:T(8,128)(2,1)S(1)}, bf16[96,1152]{1,0:T(8,128)(2,1)S(1)}, u32[]{:S(2)}, u32[]{:S(2)}) collective-permute-start(bf16[96,1152]{1,0:T(8,128)(2,1)S(1)} %collective-permute-done.10.refs_7_), channel_id=1, source_target_pairs={{0,4},{4,0},{8,12},{12,8},{1,5},{5,1},{9,13},{13,9},{2,6},{6,2},{1... | collective-permute-start | bytes 663560 | tf_op jit(solution)/shard_map/ppermute | solution.py:50
  46.0 2.2 %collective-permute-start.17 = (bf16[96,1152]{1,0:T(8,128)(2,1)S(1)}, bf16[96,1152]{1,0:T(8,128)(2,1)S(1)}, u32[]{:S(2)}, u32[]{:S(2)}) collective-permute-start(bf16[96,1152]{1,0:T(8,128)(2,1)S(1)} %collective-permute-done.16.refs_13_), channel_id=1, source_target_pairs={{0,4},{4,0},{8,12},{12,8},{1,5},{5,1},{9,13},{13,9},{2,6},{6,2},{1... | collective-permute-start | bytes 663560 | tf_op jit(solution)/shard_map/ppermute | solution.py:50
  48.3 0.9 constant_dynamic-update-slice_fusion.1
  49.2 1.2 %collective-permute-start.3 = (bf16[96,768]{1,0:T(8,128)(2,1)S(1)}, bf16[96,768]{1,0:T(8,128)(2,1)S(1)}, u32[]{:S(2)}, u32[]{:S(2)}) collective-permute-start(bf16[96,768]{1,0:T(8,128)(2,1)S(1)} %constant_dynamic-update-slice_fusion), channel_id=1, source_target_pairs={{0,3},{1,2},{2,1},{3,0},{4,7},{5,6},{6,5},{7,4},{8,11},{9,10},{10,... | collective-permute-start | bytes 442376 | tf_op jit(solution)/shard_map/ppermute | solution.py:50
  50.3 1.6 %collective-permute-start.4 = (bf16[96,768]{1,0:T(8,128)(2,1)S(1)}, bf16[96,768]{1,0:T(8,128)(2,1)S(1)}, u32[]{:S(2)}, u32[]{:S(2)}) collective-permute-start(bf16[96,768]{1,0:T(8,128)(2,1)S(1)} %constant_dynamic-update-slice_fusion), channel_id=1, source_target_pairs={{0,2},{1,3},{2,0},{3,1},{4,6},{5,7},{6,4},{7,5},{8,10},{9,11},{10,... | collective-permute-start | bytes 442376 | tf_op jit(solution)/shard_map/ppermute | solution.py:50
  52.0 0.8 collective-permute-start.5
  52.8 10.3 %attend.1.refs_1_ = bf16[512,768]{1,0:T(8,128)(2,1)S(1)} custom-call(s32[3]{0:T(128)S(1)} %pad_add_fusion.place.refs_0_, bf16[512,768]{1,0:T(8,128)(2,1)S(1)} %get-tuple-element.44.refs_1_, f32[6,64,256]{2,1,0:T(8,128)S(1)} %get-tuple-element.45.refs_2_, bf16[96,2304]{1,0:T(8,128)(2,1)S(1)} %constant_dynamic-update-slice_fusion.2.refs_3_, ...), custom_call_target="tpu_custom_call" | custom-call | flops 11500000256 | tf_op jit(solution)/shard_map/attend/pallas_call | solution.py:245
  63.2 2.4 %collective-permute-done.4 = bf16[96,768]{1,0:T(8,128)(2,1)S(1)} collective-permute-done((bf16[96,768]{1,0:T(8,128)(2,1)S(1)}, bf16[96,768]{1,0:T(8,128)(2,1)S(1)}, u32[]{:S(2)}, u32[]{:S(2)}) %collective-permute-start.4) | collective-permute-done | bytes 147488 | tf_op jit(solution)/shard_map/ppermute | solution.py:50
  66.3 1.6 %collective-permute-done.18.refs_4_ = bf16[384,768]{1,0:T(8,128)(2,1)S(1)} collective-permute-done((bf16[384,768]{1,0:T(8,128)(2,1)S(1)}, bf16[384,768]{1,0:T(8,128)(2,1)S(1)}, u32[]{:S(2)}, u32[]{:S(2)}) %collective-permute-start.18) | collective-permute-done | bytes 589856 | tf_op jit(solution)/shard_map/ppermute | solution.py:50
  67.9 3.5 %project.1 = (bf16[16,32,768]{2,1,0:T(8,128)(2,1)S(1)}, bf16[4,32,768]{2,1,0:T(8,128)(2,1)S(1)}, bf16[48,768]{1,0:T(8,128)(2,1)S(1)}, bf16[16,768]{1,0:T(8,128)(2,1)S(1)}) custom-call(s32[3]{0:T(128)S(1)} %pad_add_fusion.place.refs_0_, bf16[512,768]{1,0:T(8,128)(2,1)S(1)} %attend.1.refs_1_, bf16[512,768]{1,0:T(8,128)(2,1)S(1)} %get-tuple-element.49.refs_2_, ...), custom_call_target="tpu_custom_call" | custom-call | flops 3449999872 | tf_op jit(solution)/shard_map/project/pallas_call | solution.py:314
  71.8 1.7 %collective-permute-start.20 = (bf16[48,768]{1,0:T(8,128)(2,1)S(1)}, bf16[48,768]{1,0:T(8,128)(2,1)S(1)}, u32[]{:S(2)}, u32[]{:S(2)}) collective-permute-start(bf16[48,768]{1,0:T(8,128)(2,1)S(1)} %get-tuple-element.56), channel_id=1, source_target_pairs={{0,3},{1,0},{2,1},{3,2},{4,7},{5,4},{6,5},{7,6},{8,11},{9,8},{10,9... | collective-permute-start | bytes 221192 | tf_op jit(solution)/shard_map/ppermute | solution.py:35
  73.6 0.8 collective-permute-start.21
  74.5 3.4 %collective-permute-done.21.corner = bf16[16,768]{1,0:T(8,128)(2,1)S(1)} collective-permute-done((bf16[16,768]{1,0:T(8,128)(2,1)S(1)}, bf16[16,768]{1,0:T(8,128)(2,1)S(1)}, u32[]{:S(2)}, u32[]{:S(2)}) %collective-permute-start.21) | collective-permute-done | bytes 24608 | tf_op jit(solution)/shard_map/ppermute | solution.py:45
  77.9 1.6 %dispatch.1 = (bf16[512,768]{1,0:T(8,128)(2,1)S(1)}, bf16[64,768]{1,0:T(8,128)(2,1)S(1)}, bf16[64,768]{1,0:T(8,128)(2,1)S(1)}, bf16[64,768]{1,0:T(8,128)(2,1)S(1...) custom-call(s32[3]{0:T(128)S(1)} %pad_add_fusion.place.refs_0_, ...), custom_call_target="tpu_custom_call" | custom-call | tf_op jit(solution)/shard_map/dispatch/pallas_call | solution.py:377
  80.5 1.2 %collective-permute-start.27 = (bf16[64,768]{1,0:T(8,128)(2,1)S(1)}, bf16[64,768]{1,0:T(8,128)(2,1)S(1)}, u32[]{:S(2)}, u32[]{:S(2)}) collective-permute-start(bf16[64,768]{1,0:T(8,128)(2,1)S(1)} %get-tuple-element.67), channel_id=1, source_target_pairs={{0,12},{4,8},{8,4},{12,0},{1,13},{5,9},{9,5},{13,1},{2,14},{6,10},... | collective-permute-start | bytes 294920 | tf_op jit(solution)/shard_map/ppermute | solution.py:50
  81.7 0.9 collective-permute-start.23
  82.6 1.3 %collective-permute-start.24 = (bf16[64,768]{1,0:T(8,128)(2,1)S(1)}, bf16[64,768]{1,0:T(8,128)(2,1)S(1)}, u32[]{:S(2)}, u32[]{:S(2)}) collective-permute-start(bf16[64,768]{1,0:T(8,128)(2,1)S(1)} %get-tuple-element.62), channel_id=1, source_target_pairs={{0,12},{4,8},{8,4},{12,0},{1,13},{5,9},{9,5},{13,1},{2,14},{6,10},... | collective-permute-start | bytes 294920 | tf_op jit(solution)/shard_map/ppermute | solution.py:50
  84.0 3.1 %collective-permute-done.27.refs_3_ = bf16[64,768]{1,0:T(8,128)(2,1)S(1)} collective-permute-done((bf16[64,768]{1,0:T(8,128)(2,1)S(1)}, bf16[64,768]{1,0:T(8,128)(2,1)S(1)}, u32[]{:S(2)}, u32[]{:S(2)}) %collective-permute-start.27) | collective-permute-done | bytes 98336 | tf_op jit(solution)/shard_map/ppermute | solution.py:50
  87.1 7.6 %experts.3 = (bf16[64,768]{1,0:T(8,128)(2,1)S(1)}, bf16[64,768]{1,0:T(8,128)(2,1)S(1)}, bf16[64,768]{1,0:T(8,128)(2,1)S(1)}, bf16[64,768]{1,0:T(8,128)(2,1)S(1)}) custom-call(bf16[64,768]{1,0:T(8,128)(2,1)S(1)} %get-tuple-element.64.refs_0_, bf16[64,768]{1,0:T(8,128)(2,1)S(1)} %collective-permute-done.25.refs_1_, ...), custom_call_target="tpu_custom_call" | custom-call | flops 8049999872 | tf_op jit(solution)/shard_map/experts/pallas_call | solution.py:419
  94.8 1.0 collective-permute-start.31
  95.8 1.1 %collective-permute-start.33 = (bf16[64,768]{1,0:T(8,128)(2,1)S(1)}, bf16[64,768]{1,0:T(8,128)(2,1)S(1)}, u32[]{:S(2)}, u32[]{:S(2)}) collective-permute-start(bf16[64,768]{1,0:T(8,128)(2,1)S(1)} %get-tuple-element.74), channel_id=1, source_target_pairs={{0,12},{4,8},{8,4},{12,0},{1,13},{5,9},{9,5},{13,1},{2,14},{6,10},... | collective-permute-start | bytes 294920 | tf_op jit(solution)/shard_map/ppermute | solution.py:50
  96.9 7.6 %experts.2 = (bf16[64,768]{1,0:T(8,128)(2,1)S(1)}, bf16[64,768]{1,0:T(8,128)(2,1)S(1)}, bf16[64,768]{1,0:T(8,128)(2,1)S(1)}, bf16[64,768]{1,0:T(8,128)(2,1)S(1)}) custom-call(bf16[64,768]{1,0:T(8,128)(2,1)S(1)} %get-tuple-element.59.refs_0_, bf16[64,768]{1,0:T(8,128)(2,1)S(1)} %collective-permute-done.22.refs_1_, ...), custom_call_target="tpu_custom_call" | custom-call | flops 8049999872 | tf_op jit(solution)/shard_map/experts/pallas_call | solution.py:419
  104.6 1.0 collective-permute-start.30
  105.6 1.1 %collective-permute-start.32 = (bf16[64,768]{1,0:T(8,128)(2,1)S(1)}, bf16[64,768]{1,0:T(8,128)(2,1)S(1)}, u32[]{:S(2)}, u32[]{:S(2)}) collective-permute-start(bf16[64,768]{1,0:T(8,128)(2,1)S(1)} %get-tuple-element.73), channel_id=1, source_target_pairs={{0,12},{4,8},{8,4},{12,0},{1,13},{5,9},{9,5},{13,1},{2,14},{6,10},... | collective-permute-start | bytes 294920 | tf_op jit(solution)/shard_map/ppermute | solution.py:50
  107.3 1.3 %collective-permute-done.30.refs_4_ = bf16[64,768]{1,0:T(8,128)(2,1)S(1)} collective-permute-done((bf16[64,768]{1,0:T(8,128)(2,1)S(1)}, bf16[64,768]{1,0:T(8,128)(2,1)S(1)}, u32[]{:S(2)}, u32[]{:S(2)}) %collective-permute-start.30) | collective-permute-done | bytes 98336 | tf_op jit(solution)/shard_map/ppermute | solution.py:50
  108.6 2.7 %collective-permute-done.32.refs_6_ = bf16[64,768]{1,0:T(8,128)(2,1)S(1)} collective-permute-done((bf16[64,768]{1,0:T(8,128)(2,1)S(1)}, bf16[64,768]{1,0:T(8,128)(2,1)S(1)}, u32[]{:S(2)}, u32[]{:S(2)}) %collective-permute-start.32) | collective-permute-done | bytes 98336 | tf_op jit(solution)/shard_map/ppermute | solution.py:50
  111.3 2.3 %combine.1 = bf16[512,768]{1,0:T(8,128)(2,1)} custom-call(s32[3]{0:T(128)S(1)} %pad_add_fusion.place.refs_0_, bf16[512,768]{1,0:T(8,128)(2,1)S(1)} %get-tuple-element.58.attended, s32[512,1]{1,0:T(8,128)S(1)} %select_n.46.position, s32[512,1]{1,0:T(8,128)S(1)} %select_n.47.constant_at, f32[16,768]{1,0:T(8,128)S(1)} %copy-done.3, ...), custom_call_target="tpu_custom_call" | custom-call | tf_op jit(solution)/shard_map/combine/pallas_call | solution.py:457
  (59 shorter events, 4.4 us)
Async XLA Ops:
  1.0 9.0 %collective-permute-start.2 = (bf16[7,32,768]{2,1,0:T(8,128)(2,1)S(1)}, bf16[7,32,768]{2,1,0:T(8,128)(2,1)S(1)}, u32[]{:S(2)}, u32[]{:S(2)}) collective-permute-start(bf16[7,32,768]{2,1,0:T(8,128)(2,1)S(1)} %slice.9), channel_id=1, source_target_pairs={{0,4},{4,8},{8,12},{12,0},{1,5},{5,9},{9,13},{13,1},{2,6},{6,10},{... | collective-permute-start | bytes 1032200 | tf_op jit(solution)/shard_map/ppermute | solution.py:35
  3.7 6.4 %collective-permute-start = (bf16[48,2304]{1,0:T(8,128)(2,1)}, bf16[48,2304]{1,0:T(8,128)(2,1)S(1)}, u32[]{:S(2)}, u32[]{:S(2)}) collective-permute-start(bf16[48,2304]{1,0:T(8,128)(2,1)} %param.13), channel_id=1, source_target_pairs={{0,1},{1,0},{2,3},{3,2},{4,5},{5,4},{6,7},{7,6},{8,9},{9,8},{10,11... | collective-permute-start | bytes 663560 | tf_op jit(solution)/shard_map/ppermute | solution.py:50
  5.0 4.6 %collective-permute-start.1 = (bf16[48,768]{1,0:T(8,128)(2,1)}, bf16[48,768]{1,0:T(8,128)(2,1)S(1)}, u32[]{:S(2)}, u32[]{:S(2)}) collective-permute-start(bf16[48,768]{1,0:T(8,128)(2,1)} %param.14), channel_id=1, source_target_pairs={{0,8},{4,12},{8,0},{12,4},{1,9},{5,13},{9,1},{13,5},{2,10},{6,14},... | collective-permute-start | bytes 221192 | tf_op jit(solution)/shard_map/ppermute | solution.py:50
  10.1 10.9 %collective-permute-start.8 = (bf16[23,8,768]{2,1,0:T(8,128)(2,1)S(1)}, bf16[23,8,768]{2,1,0:T(8,128)(2,1)S(1)}, u32[]{:S(2)}, u32[]{:S(2)}) collective-permute-start(bf16[23,8,768]{2,1,0:T(8,128)(2,1)S(1)} %pad_maximum_fusion), channel_id=1, source_target_pairs={{0,1},{1,2},{2,3},{3,0},{4,5},{5,6},{6,7},{7,4},{8,9},{9,10},{10,1... | collective-permute-start | bytes 847880 | tf_op jit(solution)/shard_map/ppermute | solution.py:35
  11.9 22.5 %collective-permute-start.7 = (bf16[96,2304]{1,0:T(8,128)(2,1)S(1)}, bf16[96,2304]{1,0:T(8,128)(2,1)S(1)}, u32[]{:S(2)}, u32[]{:S(2)}) collective-permute-start(bf16[96,2304]{1,0:T(8,128)(2,1)S(1)} %constant_dynamic-update-slice_fusion.2.refs_3_), channel_id=1, source_target_pairs={{0,8},{4,12},{8,0},{12,4},{1,9},{5,13},{9,1},{13,5},{2,10},{6,14},... | collective-permute-start | bytes 1327112 | tf_op jit(solution)/shard_map/ppermute | solution.py:50
  13.1 21.3 %collective-permute-start.6 = (bf16[96,1152]{1,0:T(8,128)(2,1)S(1)}, bf16[96,1152]{1,0:T(8,128)(2,1)S(1)}, u32[]{:S(2)}, u32[]{:S(2)}) collective-permute-start(bf16[96,1152]{1,0:T(8,128)(2,1)S(1)} %constant_dynamic-slice_fusion), channel_id=1, source_target_pairs={{0,2},{1,3},{2,0},{3,1},{4,6},{5,7},{6,4},{7,5},{8,10},{9,11},{10,... | collective-permute-start | bytes 663560 | tf_op jit(solution)/shard_map/ppermute | solution.py:50
  15.5 23.6 %collective-permute-start.11 = (bf16[96,2304]{1,0:T(8,128)(2,1)S(1)}, bf16[96,2304]{1,0:T(8,128)(2,1)S(1)}, u32[]{:S(2)}, u32[]{:S(2)}) collective-permute-start(bf16[96,2304]{1,0:T(8,128)(2,1)S(1)} %constant_dynamic-update-slice_fusion.2.refs_3_), channel_id=1, source_target_pairs={{0,4},{4,0},{8,12},{12,8},{1,5},{5,1},{9,13},{13,9},{2,6},{6,2},{1... | collective-permute-start | bytes 1327112 | tf_op jit(solution)/shard_map/ppermute | solution.py:50
  20.9 1.1 copy-start
  22.1 1.1 copy-start.1
  23.2 0.9 copy-start.2
  34.4 6.0 %collective-permute-start.9 = (bf16[96,1152]{1,0:T(8,128)(2,1)S(1)}, bf16[96,1152]{1,0:T(8,128)(2,1)S(1)}, u32[]{:S(2)}, u32[]{:S(2)}) collective-permute-start(bf16[96,1152]{1,0:T(8,128)(2,1)S(1)} %collective-permute-done.6.refs_5_), channel_id=1, source_target_pairs={{0,16},{16,0},{1,17},{17,1},{2,18},{18,2},{3,19},{19,3},{4,20},{20... | collective-permute-start | bytes 663560 | tf_op jit(solution)/shard_map/ppermute | solution.py:50
  35.5 7.5 %collective-permute-start.10 = (bf16[96,1152]{1,0:T(8,128)(2,1)S(1)}, bf16[96,1152]{1,0:T(8,128)(2,1)S(1)}, u32[]{:S(2)}, u32[]{:S(2)}) collective-permute-start(bf16[96,1152]{1,0:T(8,128)(2,1)S(1)} %collective-permute-done.6.refs_5_), channel_id=1, source_target_pairs={{0,8},{4,12},{8,0},{12,4},{1,9},{5,13},{9,1},{13,5},{2,10},{6,14},... | collective-permute-start | bytes 663560 | tf_op jit(solution)/shard_map/ppermute | solution.py:50
  36.4 9.6 %collective-permute-start.16 = (bf16[96,1152]{1,0:T(8,128)(2,1)S(1)}, bf16[96,1152]{1,0:T(8,128)(2,1)S(1)}, u32[]{:S(2)}, u32[]{:S(2)}) collective-permute-start(bf16[96,1152]{1,0:T(8,128)(2,1)S(1)} %collective-permute-done.6.refs_5_), channel_id=1, source_target_pairs={{0,24},{4,28},{8,16},{12,20},{16,8},{20,12},{24,0},{28,4},{1,25},{... | collective-permute-start | bytes 663560 | tf_op jit(solution)/shard_map/ppermute | solution.py:487
  37.1 15.7 %collective-permute-start.12 = (bf16[96,2304]{1,0:T(8,128)(2,1)S(1)}, bf16[96,2304]{1,0:T(8,128)(2,1)S(1)}, u32[]{:S(2)}, u32[]{:S(2)}) collective-permute-start(bf16[96,2304]{1,0:T(8,128)(2,1)S(1)} %collective-permute-done.7.refs_4_), channel_id=1, source_target_pairs={{0,4},{4,0},{8,12},{12,8},{1,5},{5,1},{9,13},{13,9},{2,6},{6,2},{1... | collective-permute-start | bytes 1327112 | tf_op jit(solution)/shard_map/ppermute | solution.py:50
  39.0 10.1 %collective-permute-start.13 = (bf16[96,1152]{1,0:T(8,128)(2,1)S(1)}, bf16[96,1152]{1,0:T(8,128)(2,1)S(1)}, u32[]{:S(2)}, u32[]{:S(2)}) collective-permute-start(bf16[96,1152]{1,0:T(8,128)(2,1)S(1)} %collective-permute-done.6.refs_5_), channel_id=1, source_target_pairs={{0,4},{4,0},{8,12},{12,8},{1,5},{5,1},{9,13},{13,9},{2,6},{6,2},{1... | collective-permute-start | bytes 663560 | tf_op jit(solution)/shard_map/ppermute | solution.py:50
  40.4 10.0 %collective-permute-start.14 = (bf16[96,1152]{1,0:T(8,128)(2,1)S(1)}, bf16[96,1152]{1,0:T(8,128)(2,1)S(1)}, u32[]{:S(2)}, u32[]{:S(2)}) collective-permute-start(bf16[96,1152]{1,0:T(8,128)(2,1)S(1)} %collective-permute-done.9.refs_6_), channel_id=1, source_target_pairs={{0,4},{4,0},{8,12},{12,8},{1,5},{5,1},{9,13},{13,9},{2,6},{6,2},{1... | collective-permute-start | bytes 663560 | tf_op jit(solution)/shard_map/ppermute | solution.py:50
  43.0 9.0 %collective-permute-start.15 = (bf16[96,1152]{1,0:T(8,128)(2,1)S(1)}, bf16[96,1152]{1,0:T(8,128)(2,1)S(1)}, u32[]{:S(2)}, u32[]{:S(2)}) collective-permute-start(bf16[96,1152]{1,0:T(8,128)(2,1)S(1)} %collective-permute-done.10.refs_7_), channel_id=1, source_target_pairs={{0,4},{4,0},{8,12},{12,8},{1,5},{5,1},{9,13},{13,9},{2,6},{6,2},{1... | collective-permute-start | bytes 663560 | tf_op jit(solution)/shard_map/ppermute | solution.py:50
  46.0 6.8 %collective-permute-start.17 = (bf16[96,1152]{1,0:T(8,128)(2,1)S(1)}, bf16[96,1152]{1,0:T(8,128)(2,1)S(1)}, u32[]{:S(2)}, u32[]{:S(2)}) collective-permute-start(bf16[96,1152]{1,0:T(8,128)(2,1)S(1)} %collective-permute-done.16.refs_13_), channel_id=1, source_target_pairs={{0,4},{4,0},{8,12},{12,8},{1,5},{5,1},{9,13},{13,9},{2,6},{6,2},{1... | collective-permute-start | bytes 663560 | tf_op jit(solution)/shard_map/ppermute | solution.py:50
  49.2 14.0 %collective-permute-start.3 = (bf16[96,768]{1,0:T(8,128)(2,1)S(1)}, bf16[96,768]{1,0:T(8,128)(2,1)S(1)}, u32[]{:S(2)}, u32[]{:S(2)}) collective-permute-start(bf16[96,768]{1,0:T(8,128)(2,1)S(1)} %constant_dynamic-update-slice_fusion), channel_id=1, source_target_pairs={{0,3},{1,2},{2,1},{3,0},{4,7},{5,6},{6,5},{7,4},{8,11},{9,10},{10,... | collective-permute-start | bytes 442376 | tf_op jit(solution)/shard_map/ppermute | solution.py:50
  50.3 15.2 %collective-permute-start.4 = (bf16[96,768]{1,0:T(8,128)(2,1)S(1)}, bf16[96,768]{1,0:T(8,128)(2,1)S(1)}, u32[]{:S(2)}, u32[]{:S(2)}) collective-permute-start(bf16[96,768]{1,0:T(8,128)(2,1)S(1)} %constant_dynamic-update-slice_fusion), channel_id=1, source_target_pairs={{0,2},{1,3},{2,0},{3,1},{4,6},{5,7},{6,4},{7,5},{8,10},{9,11},{10,... | collective-permute-start | bytes 442376 | tf_op jit(solution)/shard_map/ppermute | solution.py:50
  52.0 13.6 %collective-permute-start.5 = (bf16[96,768]{1,0:T(8,128)(2,1)S(1)}, bf16[96,768]{1,0:T(8,128)(2,1)S(1)}, u32[]{:S(2)}, u32[]{:S(2)}) collective-permute-start(bf16[96,768]{1,0:T(8,128)(2,1)S(1)} %constant_dynamic-update-slice_fusion), channel_id=1, source_target_pairs={{0,1},{1,0},{2,3},{3,2},{4,5},{5,4},{6,7},{7,6},{8,9},{9,8},{10,11... | collective-permute-start | bytes 442376 | tf_op jit(solution)/shard_map/ppermute | solution.py:50
  52.8 21.6 %copy-start.4 = (s32[16,32]{1,0:T(8,128)S(1)}, s32[16,32]{1,0:T(8,128)}, u32[]{:S(2)}) copy-start(s32[16,32]{1,0:T(8,128)} %param.21) | copy-start | bytes 6148
  52.8 21.6 %copy-start.5 = (s32[16,32]{1,0:T(8,128)S(1)}, s32[16,32]{1,0:T(8,128)}, u32[]{:S(2)}) copy-start(s32[16,32]{1,0:T(8,128)} %param.19) | copy-start | bytes 6148
  52.8 21.6 %copy-start.6 = (s32[16,32]{1,0:T(8,128)S(1)}, s32[16,32]{1,0:T(8,128)}, u32[]{:S(2)}) copy-start(s32[16,32]{1,0:T(8,128)} %param.20) | copy-start | bytes 6148
  65.6 2.3 %collective-permute-start.18 = (bf16[384,768]{1,0:T(8,128)(2,1)S(1)}, bf16[384,768]{1,0:T(8,128)(2,1)S(1)}, u32[]{:S(2)}, u32[]{:S(2)}) collective-permute-start(bf16[384,768]{1,0:T(8,128)(2,1)S(1)} %constant_dynamic-update-slice_fusion.4.refs_3_), channel_id=1, source_target_pairs={{0,4},{4,0},{8,12},{12,8},{1,5},{5,1},{9,13},{13,9},{2,6},{6,2},{1... | collective-permute-start | bytes 1769480 | tf_op jit(solution)/shard_map/ppermute | solution.py:50
  71.4 6.5 %collective-permute-start.19 = (bf16[4,32,768]{2,1,0:T(8,128)(2,1)S(1)}, bf16[4,32,768]{2,1,0:T(8,128)(2,1)S(1)}, u32[]{:S(2)}, u32[]{:S(2)}) collective-permute-start(bf16[4,32,768]{2,1,0:T(8,128)(2,1)S(1)} %get-tuple-element.55), channel_id=1, source_target_pairs={{0,12},{4,0},{8,4},{12,8},{1,13},{5,1},{9,5},{13,9},{2,14},{6,2},{... | collective-permute-start | bytes 589832 | tf_op jit(solution)/shard_map/ppermute | solution.py:35
  71.8 6.0 %collective-permute-start.20 = (bf16[48,768]{1,0:T(8,128)(2,1)S(1)}, bf16[48,768]{1,0:T(8,128)(2,1)S(1)}, u32[]{:S(2)}, u32[]{:S(2)}) collective-permute-start(bf16[48,768]{1,0:T(8,128)(2,1)S(1)} %get-tuple-element.56), channel_id=1, source_target_pairs={{0,3},{1,0},{2,1},{3,2},{4,7},{5,4},{6,5},{7,6},{8,11},{9,8},{10,9... | collective-permute-start | bytes 221192 | tf_op jit(solution)/shard_map/ppermute | solution.py:35
  73.6 4.3 %collective-permute-start.21 = (bf16[16,768]{1,0:T(8,128)(2,1)S(1)}, bf16[16,768]{1,0:T(8,128)(2,1)S(1)}, u32[]{:S(2)}, u32[]{:S(2)}) collective-permute-start(bf16[16,768]{1,0:T(8,128)(2,1)S(1)} %get-tuple-element.57), channel_id=1, source_target_pairs={{0,15},{1,12},{2,13},{3,14},{4,3},{5,0},{6,1},{7,2},{8,7},{9,4},{1... | collective-permute-start | bytes 73736 | tf_op jit(solution)/shard_map/ppermute | solution.py:45
  79.5 3.1 %collective-permute-start.25 = (bf16[64,768]{1,0:T(8,128)(2,1)S(1)}, bf16[64,768]{1,0:T(8,128)(2,1)S(1)}, u32[]{:S(2)}, u32[]{:S(2)}) collective-permute-start(bf16[64,768]{1,0:T(8,128)(2,1)S(1)} %get-tuple-element.65), channel_id=1, source_target_pairs={{0,4},{4,0},{8,12},{12,8},{1,5},{5,1},{9,13},{13,9},{2,6},{6,2},{1... | collective-permute-start | bytes 294920 | tf_op jit(solution)/shard_map/ppermute | solution.py:50
  79.9 4.2 %collective-permute-start.26 = (bf16[64,768]{1,0:T(8,128)(2,1)S(1)}, bf16[64,768]{1,0:T(8,128)(2,1)S(1)}, u32[]{:S(2)}, u32[]{:S(2)}) collective-permute-start(bf16[64,768]{1,0:T(8,128)(2,1)S(1)} %get-tuple-element.66), channel_id=1, source_target_pairs={{0,8},{4,12},{8,0},{12,4},{1,9},{5,13},{9,1},{13,5},{2,10},{6,14},... | collective-permute-start | bytes 294920 | tf_op jit(solution)/shard_map/ppermute | solution.py:50
  80.5 6.6 %collective-permute-start.27 = (bf16[64,768]{1,0:T(8,128)(2,1)S(1)}, bf16[64,768]{1,0:T(8,128)(2,1)S(1)}, u32[]{:S(2)}, u32[]{:S(2)}) collective-permute-start(bf16[64,768]{1,0:T(8,128)(2,1)S(1)} %get-tuple-element.67), channel_id=1, source_target_pairs={{0,12},{4,8},{8,4},{12,0},{1,13},{5,9},{9,5},{13,1},{2,14},{6,10},... | collective-permute-start | bytes 294920 | tf_op jit(solution)/shard_map/ppermute | solution.py:50
  81.7 14.0 %collective-permute-start.22 = (bf16[64,768]{1,0:T(8,128)(2,1)S(1)}, bf16[64,768]{1,0:T(8,128)(2,1)S(1)}, u32[]{:S(2)}, u32[]{:S(2)}) collective-permute-start(bf16[64,768]{1,0:T(8,128)(2,1)S(1)} %get-tuple-element.60), channel_id=1, source_target_pairs={{0,4},{4,0},{8,12},{12,8},{1,5},{5,1},{9,13},{13,9},{2,6},{6,2},{1... | collective-permute-start | bytes 294920 | tf_op jit(solution)/shard_map/ppermute | solution.py:50
  81.7 15.2 %collective-permute-start.23 = (bf16[64,768]{1,0:T(8,128)(2,1)S(1)}, bf16[64,768]{1,0:T(8,128)(2,1)S(1)}, u32[]{:S(2)}, u32[]{:S(2)}) collective-permute-start(bf16[64,768]{1,0:T(8,128)(2,1)S(1)} %get-tuple-element.61), channel_id=1, source_target_pairs={{0,8},{4,12},{8,0},{12,4},{1,9},{5,13},{9,1},{13,5},{2,10},{6,14},... | collective-permute-start | bytes 294920 | tf_op jit(solution)/shard_map/ppermute | solution.py:50
  82.6 14.3 %collective-permute-start.24 = (bf16[64,768]{1,0:T(8,128)(2,1)S(1)}, bf16[64,768]{1,0:T(8,128)(2,1)S(1)}, u32[]{:S(2)}, u32[]{:S(2)}) collective-permute-start(bf16[64,768]{1,0:T(8,128)(2,1)S(1)} %get-tuple-element.62), channel_id=1, source_target_pairs={{0,12},{4,8},{8,4},{12,0},{1,13},{5,9},{9,5},{13,1},{2,14},{6,10},... | collective-permute-start | bytes 294920 | tf_op jit(solution)/shard_map/ppermute | solution.py:50
  94.7 10.9 %collective-permute-start.29 = (bf16[64,768]{1,0:T(8,128)(2,1)S(1)}, bf16[64,768]{1,0:T(8,128)(2,1)S(1)}, u32[]{:S(2)}, u32[]{:S(2)}) collective-permute-start(bf16[64,768]{1,0:T(8,128)(2,1)S(1)} %get-tuple-element.70), channel_id=1, source_target_pairs={{0,4},{4,0},{8,12},{12,8},{1,5},{5,1},{9,13},{13,9},{2,6},{6,2},{1... | collective-permute-start | bytes 294920 | tf_op jit(solution)/shard_map/ppermute | solution.py:50
  94.8 12.5 %collective-permute-start.31 = (bf16[64,768]{1,0:T(8,128)(2,1)S(1)}, bf16[64,768]{1,0:T(8,128)(2,1)S(1)}, u32[]{:S(2)}, u32[]{:S(2)}) collective-permute-start(bf16[64,768]{1,0:T(8,128)(2,1)S(1)} %get-tuple-element.72), channel_id=1, source_target_pairs={{0,8},{4,12},{8,0},{12,4},{1,9},{5,13},{9,1},{13,5},{2,10},{6,14},... | collective-permute-start | bytes 294920 | tf_op jit(solution)/shard_map/ppermute | solution.py:50
  95.8 11.5 %collective-permute-start.33 = (bf16[64,768]{1,0:T(8,128)(2,1)S(1)}, bf16[64,768]{1,0:T(8,128)(2,1)S(1)}, u32[]{:S(2)}, u32[]{:S(2)}) collective-permute-start(bf16[64,768]{1,0:T(8,128)(2,1)S(1)} %get-tuple-element.74), channel_id=1, source_target_pairs={{0,12},{4,8},{8,4},{12,0},{1,13},{5,9},{9,5},{13,1},{2,14},{6,10},... | collective-permute-start | bytes 294920 | tf_op jit(solution)/shard_map/ppermute | solution.py:50
  96.9 14.4 %copy-start.3 = (f32[16,768]{1,0:T(8,128)S(1)}, f32[16,768]{1,0:T(8,128)}, u32[]{:S(2)}) copy-start(f32[16,768]{1,0:T(8,128)} %table.1) | copy-start | bytes 147460
  104.5 2.8 %collective-permute-start.28 = (bf16[64,768]{1,0:T(8,128)(2,1)S(1)}, bf16[64,768]{1,0:T(8,128)(2,1)S(1)}, u32[]{:S(2)}, u32[]{:S(2)}) collective-permute-start(bf16[64,768]{1,0:T(8,128)(2,1)S(1)} %get-tuple-element.69), channel_id=1, source_target_pairs={{0,4},{4,0},{8,12},{12,8},{1,5},{5,1},{9,13},{13,9},{2,6},{6,2},{1... | collective-permute-start | bytes 294920 | tf_op jit(solution)/shard_map/ppermute | solution.py:50
  104.6 4.0 %collective-permute-start.30 = (bf16[64,768]{1,0:T(8,128)(2,1)S(1)}, bf16[64,768]{1,0:T(8,128)(2,1)S(1)}, u32[]{:S(2)}, u32[]{:S(2)}) collective-permute-start(bf16[64,768]{1,0:T(8,128)(2,1)S(1)} %get-tuple-element.71), channel_id=1, source_target_pairs={{0,8},{4,12},{8,0},{12,4},{1,9},{5,13},{9,1},{13,5},{2,10},{6,14},... | collective-permute-start | bytes 294920 | tf_op jit(solution)/shard_map/ppermute | solution.py:50
  105.6 5.7 %collective-permute-start.32 = (bf16[64,768]{1,0:T(8,128)(2,1)S(1)}, bf16[64,768]{1,0:T(8,128)(2,1)S(1)}, u32[]{:S(2)}, u32[]{:S(2)}) collective-permute-start(bf16[64,768]{1,0:T(8,128)(2,1)S(1)} %get-tuple-element.73), channel_id=1, source_target_pairs={{0,12},{4,8},{8,4},{12,0},{1,13},{5,9},{9,5},{13,1},{2,14},{6,10},... | collective-permute-start | bytes 294920 | tf_op jit(solution)/shard_map/ppermute | solution.py:50

commit v5 on v4

--- a/solution.py
+++ b/solution.py
@@ -56,30 +56,48 @@
     return (centred * lax.rsqrt(spread + 1e-05)).astype(jnp.bfloat16)
 
 
-def encode_kernel(
-    place, tokens_at, above, beside, taps_at, rel_bias, encoded, normed, bias, extended, weights, tokens, taps, sems
-):
-    copies = [
-        pltpu.make_async_copy(tokens_at, tokens, sems.at[0]),
-        pltpu.make_async_copy(taps_at, taps, sems.at[1]),
-    ]
-    for copy in copies:
-        copy.start()
-    rows, cols, channels = tokens.shape
-    reach = KERNEL // 2 + SHIFT
-    extended[:, :HALO] = beside[...].astype(jnp.float32)
-    extended[:reach, HALO:] = above[...].astype(jnp.float32)
-    for copy in copies:
-        copy.wait()
-    extended[reach:, HALO:] = tokens[...].astype(jnp.float32)
+def prepare_kernel(tokens, taps, rel_bias, kept, weights, bias):
+    kept[...] = tokens[...].astype(jnp.float32)
     weights[...] = taps[...].astype(jnp.float32)
     for head in range(rel_bias.shape[0]):
         at = head % GROUP * SPOTS
         bias[head // GROUP, :, at : at + SPOTS] = rel_bias[head]
+
+
+def prepare(tokens, taps, rel_bias):
+    bias_shape = (rel_bias.shape[0] // GROUP, SPOTS, GROUP * SPOTS)
+    return pl.pallas_call(
+        prepare_kernel,
+        out_shape=(
+            jax.ShapeDtypeStruct(tokens.shape, jnp.float32),
+            jax.ShapeDtypeStruct(taps.shape, jnp.float32),
+            jax.ShapeDtypeStruct(bias_shape, jnp.float32),
+        ),
+        in_specs=[VMEM] * 3,
+        out_specs=(VMEM,) * 3,
+        compiler_params=pltpu.CompilerParams(vmem_limit_bytes=8 * 1024 * 1024),
+        cost_estimate=lasting(3),
+        name="prepare",
+    )(tokens, taps, rel_bias)
+
+
+def encode_kernel(place, tokens, above, beside, weights, encoded, normed, upper, left):
+    rows, cols, channels = tokens.shape
+    reach = KERNEL // 2 + SHIFT
+    upper[:, :HALO] = beside[:reach].astype(jnp.float32)
+    upper[:, HALO:] = above[...].astype(jnp.float32)
+    left[...] = beside[reach:].astype(jnp.float32)
     inner_row = jnp.where(place[0] == 0, 0.0, 1.0)
     first_col = place[1] == 0
     window_cols = cols // WIN
     col = lax.broadcasted_iota(jnp.int32, (WIN, LANES), 0)
+
+    def extended(row, tile, lanes):
+        if row < reach:
+            return upper[row, tile * WIN : (tile + 1) * WIN, lanes]
+        if tile == 0:
+            return left[row - reach, :, lanes]
+        return tokens[row - reach, (tile - 1) * WIN : tile * WIN, lanes]
 
     def block(index, _):
         lanes = pl.ds(pl.multiple_of(index * LANES, LANES), LANES)
@@ -94,9 +112,9 @@
                     near = (col < SHIFT) == (col + col_off < reach)
                     keep = jnp.where(near | jnp.logical_not(first_col), 1.0, 0.0)
                 for row in range(rows + KERNEL - 1):
-                    here = extended[row, tile * WIN : tile * WIN + WIN, lanes]
-                    after = extended[row, (tile + 1) * WIN : (tile + 2) * WIN, lanes]
-                    line = jnp.where(col > col_off, here, after)
+                    line = jnp.where(
+                        col > col_off, extended(row, tile, lanes), extended(row, tile + 1, lanes)
+                    )
                     line = pltpu.roll(line, WIN - 1 - col_off, 0)
                     if tile == 0:
                         line = line * keep
@@ -124,27 +142,23 @@
     lax.fori_loop(0, rows * cols // SPOTS, norm, 0)
 
 
-def encode(place, tokens, above, beside, taps, rel_bias):
+def encode(place, tokens, above, beside, weights):
     rows, cols, channels = tokens.shape
     flat = jax.ShapeDtypeStruct((rows * cols, channels), jnp.bfloat16)
     reach = KERNEL // 2 + SHIFT
-    bias_shape = (rel_bias.shape[0] // GROUP, SPOTS, GROUP * SPOTS)
     return pl.pallas_call(
         encode_kernel,
-        out_shape=(flat, flat, jax.ShapeDtypeStruct(bias_shape, jnp.float32)),
-        in_specs=[SMEM, HBM, VMEM, VMEM, HBM, VMEM],
-        out_specs=(VMEM, VMEM, VMEM),
+        out_shape=(flat, flat),
+        in_specs=[SMEM] + [VMEM] * 4,
+        out_specs=(VMEM, VMEM),
         scratch_shapes=[
-            pltpu.VMEM((rows + reach, cols + HALO, channels), jnp.float32),
-            pltpu.VMEM(taps.shape, jnp.float32),
-            pltpu.VMEM(tokens.shape, jnp.bfloat16),
-            pltpu.VMEM(taps.shape, jnp.bfloat16),
-            pltpu.SemaphoreType.DMA((2,)),
+            pltpu.VMEM((reach, cols + HALO, channels), jnp.float32),
+            pltpu.VMEM((rows, HALO, channels), jnp.float32),
         ],
         compiler_params=pltpu.CompilerParams(vmem_limit_bytes=12 * 1024 * 1024),
         cost_estimate=lasting(0.1),
         name="encode",
-    )(place, tokens, above, beside, taps, rel_bias)
+    )(place, tokens, above, beside, weights)
 
 
 def fetch(place, grid_cols, pieces, ids, target, sems):
@@ -512,23 +526,26 @@
     quick = grid_rows == 4 and grid_cols == 4 and lax.axis_size("groups") == 2
     above = shifted(tokens[rows - reach :], "gy", 1)
     if quick:
-        beyond = exchanged(project_in, "gx", 1)
-        facing_out = exchanged(project_out, "gy", 2)
-        beyond, facing_out, above = held(beyond, facing_out, above)
-        two = (jnp.concatenate([project_in, beyond], axis=0), [(0, 0), (0, 1)], None)
+        pair = [(0, 0), (0, 1)]
+        beyond, beyond_out = exchanged(project_in, "gx", 1), exchanged(project_out, "gx", 1)
+        beyond, beyond_out, above = held(beyond, beyond_out, above)
+        two = (jnp.concatenate([project_in, beyond], axis=0), pair, None)
+        two_out = (jnp.concatenate([project_out, beyond_out], axis=0), pair, None)
         wide = two[0].shape[1] // 2
         mine = lax.dynamic_slice_in_dim(two[0], lax.axis_index("groups") * wide, wide, axis=1)
         far = along((mine, two[1], 0), "gx", 2)
         facing = along(two, "gy", 2)
+        far_out = along(two_out, "gx", 2)
     edge = jnp.concatenate([above[:, cols - HALO :], tokens[:, cols - HALO :]], axis=0)
     beside = shifted(edge, "gx", 1)
-    encoded, normed, bias = encode(place, tokens, above, beside, conv_kernel, rel_bias)
+    kept, weights, bias = prepare(tokens, conv_kernel, rel_bias)
+    encoded, normed = encode(place, kept, above, beside, weights)
     if quick:
         first, second, normed = held(far[0], facing[0], normed)
         far, facing = (first, *far[1:]), (second, *facing[1:])
         across = along(far, "gy", 2)
-        pair = stacked([(project_out, [(0, 0)]), (facing_out, [(2, 0)])])
-        plane = [pair] + [along(pair, "gx", mask) for mask in (3, 2, 1)]
+        four_out = stacked([two_out, far_out])
+        across_out = along(four_out, "gy", 2)
         far_rest, across_rest = along(far, "groups", 1), diagonal(far, 2)
         pieces_in = [two, facing, far, far_rest, across]
         pieces_in = pieces_in + [along(part, "gy", 1) for part in pieces_in]
@@ -539,9 +556,9 @@
         pieces_out = [(lax.all_gather(project_out, ("gy", "gx"), axis=0, tiled=True), whole, None)]
     context = attend(place, (rows, cols), normed, bias, pieces_in, grid_cols)
     if quick:
-        *arrays, context = held(*[part[0] for part in plane], context)
-        plane = stacked([(array, *part[1:]) for array, part in zip(arrays, plane, strict=True)])
-        pieces_out = [plane, along(plane, "gy", 1)]
+        array, context = held(across_out[0], context)
+        pieces_out = [four_out, across_out, along(four_out, "gy", 1)]
+        pieces_out = pieces_out + [along((array, *across_out[1:]), "gy", 1)]
     rolled, top, side, corner = project(
         place, (rows, cols), context, encoded, pieces_out, grid_cols
     )

time: 114 us -> 112 us (0.982)
  starting transfers between devices: 38.8 us -> 34.3 us
  local copies, waits for them, and re-layouts: 7.64 us -> 10.9 us
  other arithmetic: 0.11 us -> 2.37 us
  waiting for transfers between devices: 23.6 us -> 21.4 us
    ppermute x28, starting transfers between devices: 30.7 us -> 23.3 us  [exchanged(): return lax.ppermute(x, axis, [(i, i ^ mask) for i in range(size)])]
    ppermute x4, waiting for transfers between devices: 4.19 us -> 0.54 us  [shifted(): return lax.ppermute(x, axis, [(i, (i + by) % size) for i in range(size)])]
    ppermute x1, starting transfers between devices: 0.83 us -> 4.3 us  [shifted_both(): return lax.ppermute(x, ('gy', 'gx'), pairs)]
    ppermute x28, waiting for transfers between devices: 15.6 us -> 18.3 us  [exchanged(): return lax.ppermute(x, axis, [(i, i ^ mask) for i in range(size)])]
    ppermute x1, waiting for transfers between devices: 3.38 us -> 0.94 us  [shifted_both(): return lax.ppermute(x, ('gy', 'gx'), pairs)]
    unnamed x19 -> x21, local copies, waits for them, and re-layouts: 5.05 us -> 6.74 us
    concatenate x0 -> x1, other arithmetic: none -> 1.54 us  [shards(): two_out = (jnp.concatenate([project_out, beyond_out], axis=0), pair, None)]
    ppermute x1, waiting for transfers between devices: 0.38 us -> 1.67 us  [diagonal(): moved = lax.ppermute(array, ('groups', 'gy'), pairs)]
  transfers between devices with their start and end apart: 34 -> 34, of which waited for: 12 -> 12; matrix products, arithmetic and copies ran while one was open for 3% -> 7% of each run, Pallas kernels for 32% -> 31%
where the time goes in v5:
time: 112 us
  Pallas kernels  42.4 us (38%)
  starting transfers between devices  34.3 us (31%)
  waiting for transfers between devices  21.4 us (19%)
  local copies, waits for them, and re-layouts  10.9 us (10%)
  other arithmetic  2.37 us (2%)
    ppermute x28, starting transfers between devices, exchanged(): return lax.ppermute(x, axis, [(i, i ^ mask) for i in range(size)])  23.3 us
    ppermute x28, waiting for transfers between devices, exchanged(): return lax.ppermute(x, axis, [(i, i ^ mask) for i in range(size)])  18.3 us
    pallas_call x2, Pallas kernels, serve(): pl.pallas_call(functools.partial(expert_kernel, count, first), out_shape=...  15.1 us
    pallas_call x1, Pallas kernels, attend(): pl.pallas_call(functools.partial(attend_kernel, shape, ids, grid_cols), o...  9.87 us
    pallas_call x1, Pallas kernels, encode(): pl.pallas_call(encode_kernel, out_shape=(flat, flat), in_specs=[SMEM] + [...  9.82 us
    unnamed x21, local copies, waits for them, and re-layouts  6.74 us
    ppermute x4, starting transfers between devices, shifted(): return lax.ppermute(x, axis, [(i, (i + by) % size) for i in range(size)])  5.39 us
    ppermute x1, starting transfers between devices, shifted_both(): return lax.ppermute(x, ('gy', 'gx'), pairs)  4.3 us
  transfers between devices with their start and end apart: 34, of which 12 were waited for; matrix products, arithmetic and copies ran while one was open for 7% of the time, Pallas kernels for 31%

profile of v5, /device:TPU:1, one launch (start us, length us, event | category | flops | bytes accessed | tf_op | source)
XLA Modules:
  0.0 111.6 jit_solution(9190018284876885453)
XLA Ops:
  0.0 1.0 slice.9
  1.0 2.7 %collective-permute-start.2 = (bf16[7,32,768]{2,1,0:T(8,128)(2,1)S(1)}, bf16[7,32,768]{2,1,0:T(8,128)(2,1)S(1)}, u32[]{:S(2)}, u32[]{:S(2)}) collective-permute-start(bf16[7,32,768]{2,1,0:T(8,128)(2,1)S(1)} %slice.9), channel_id=1, source_target_pairs={{0,4},{4,8},{8,12},{12,0},{1,5},{5,9},{9,13},{13,1},{2,6},{6,10},{... | collective-permute-start | bytes 1032200 | tf_op jit(solution)/shard_map/ppermute | solution.py:35
  3.7 1.3 %collective-permute-start = (bf16[48,2304]{1,0:T(8,128)(2,1)}, bf16[48,2304]{1,0:T(8,128)(2,1)S(1)}, u32[]{:S(2)}, u32[]{:S(2)}) collective-permute-start(bf16[48,2304]{1,0:T(8,128)(2,1)} %param.13), channel_id=1, source_target_pairs={{0,1},{1,0},{2,3},{3,2},{4,5},{5,4},{6,7},{7,6},{8,9},{9,8},{10,11... | collective-permute-start | bytes 663560 | tf_op jit(solution)/shard_map/ppermute | solution.py:50
  5.1 0.9 constant_dynamic-update-slice_fusion.4
  6.1 0.9 slice.11
  7.0 4.6 %collective-permute-done.1 = bf16[48,768]{1,0:T(8,128)(2,1)S(1)} collective-permute-done((bf16[48,768]{1,0:T(8,128)(2,1)}, bf16[48,768]{1,0:T(8,128)(2,1)S(1)}, u32[]{:S(2)}, u32[]{:S(2)}) %collective-permute-start.1) | collective-permute-done | bytes 73760 | tf_op jit(solution)/shard_map/ppermute | solution.py:50
  11.6 0.9 collective-permute-start.6
  12.6 1.2 %collective-permute-start.10 = (bf16[96,2304]{1,0:T(8,128)(2,1)S(1)}, bf16[96,2304]{1,0:T(8,128)(2,1)}, u32[]{:S(2)}, u32[]{:S(2)}) collective-permute-start(bf16[96,2304]{1,0:T(8,128)(2,1)S(1)} %constant_dynamic-update-slice_fusion.3.refs_3_), channel_id=1, source_target_pairs={{0,4},{4,0},{8,12},{12,8},{1,5},{5,1},{9,13},{13,9},{2,6},{6,2},{1... | collective-permute-start | bytes 1327112 | tf_op jit(solution)/shard_map/ppermute | solution.py:50
  13.8 0.7 pad_maximum_fusion
  14.5 1.5 %collective-permute-start.7 = (bf16[23,8,768]{2,1,0:T(8,128)(2,1)}, bf16[23,8,768]{2,1,0:T(8,128)(2,1)S(1)}, u32[]{:S(2)}, u32[]{:S(2)}) collective-permute-start(bf16[23,8,768]{2,1,0:T(8,128)(2,1)} %pad_maximum_fusion), channel_id=1, source_target_pairs={{0,1},{1,2},{2,3},{3,0},{4,5},{5,6},{6,7},{7,4},{8,9},{9,10},{10,1... | collective-permute-start | bytes 847880 | tf_op jit(solution)/shard_map/ppermute | solution.py:35
  16.0 0.7 constant_dynamic-slice_fusion
  16.7 2.3 %collective-permute-start.5 = (bf16[96,1152]{1,0:T(8,128)(2,1)}, bf16[96,1152]{1,0:T(8,128)(2,1)S(1)}, u32[]{:S(2)}, u32[]{:S(2)}) collective-permute-start(bf16[96,1152]{1,0:T(8,128)(2,1)} %constant_dynamic-slice_fusion), channel_id=1, source_target_pairs={{0,2},{1,3},{2,0},{3,1},{4,6},{5,7},{6,4},{7,5},{8,10},{9,11},{10,... | collective-permute-start | bytes 663560 | tf_op jit(solution)/shard_map/ppermute | solution.py:50
  19.0 1.5 %pad_maximum_fusion.1 = bf16[96,768]{1,0:T(8,128)(2,1)} fusion(bf16[48,768]{1,0:T(8,128)(2,1)S(1)} %collective-permute-done.1, bf16[48,768]{1,0:T(8,128)(2,1)} %param.14), kind=kLoop, calls=%fused_computation.1 | loop fusion | flops 294912 | bytes 294912 | tf_op jit(solution)/shard_map/concatenate | solution.py:533
  20.6 1.1 %copy-done = bf16[16,32,768]{2,1,0:T(8,128)(2,1)S(1)} copy-done((bf16[16,32,768]{2,1,0:T(8,128)(2,1)S(1)}, bf16[16,32,768]{2,1,0:T(8,128)(2,1)}, u32[]{:S(2)}) %copy-start) | copy-done | bytes 786456
  21.7 1.1 %copy-done.2 = f32[24,64,64]{2,1,0:T(8,128)S(1)} copy-done((f32[24,64,64]{2,1,0:T(8,128)S(1)}, f32[24,64,64]{2,1,0:T(8,128)}, u32[]{:S(2)}) %copy-start.2) | copy-done | bytes 393240
  22.9 0.9 copy-done.3
  24.0 0.7 copy-done.4
  25.3 9.8 %encode.1 = (bf16[512,768]{1,0:T(8,128)(2,1)S(1)}, bf16[512,768]{1,0:T(8,128)(2,1)S(1)}) custom-call(s32[3]{0:T(128)S(1)} %pad_add_fusion.place.refs_0_, f32[16,32,768]{2,1,0:T(8,128)S(1)} %get-tuple-element.41.tokens, bf16[7,32,768]{2,1,0:T(8,128)(2,1)S(1)} %collective-permute-done.2.above, bf16[23,8,768]{2,1,0:T(8,128)(2,1)S(1)} %collective-permute-done.7.beside, ...), custom_call_target="tpu_custom_call" | custom-call | flops 115000000 | tf_op jit(solution)/shard_map/encode/pallas_call | solution.py:149
  35.1 2.9 %collective-permute-done.5.refs_5_ = bf16[96,1152]{1,0:T(8,128)(2,1)S(1)} collective-permute-done((bf16[96,1152]{1,0:T(8,128)(2,1)}, bf16[96,1152]{1,0:T(8,128)(2,1)S(1)}, u32[]{:S(2)}, u32[]{:S(2)}) %collective-permute-start.5) | collective-permute-done | bytes 221216 | tf_op jit(solution)/shard_map/ppermute | solution.py:50
  38.1 1.2 %collective-permute-start.8 = (bf16[96,1152]{1,0:T(8,128)(2,1)S(1)}, bf16[96,1152]{1,0:T(8,128)(2,1)S(1)}, u32[]{:S(2)}, u32[]{:S(2)}) collective-permute-start(bf16[96,1152]{1,0:T(8,128)(2,1)S(1)} %collective-permute-done.5.refs_5_), channel_id=1, source_target_pairs={{0,16},{16,0},{1,17},{17,1},{2,18},{18,2},{3,19},{19,3},{4,20},{20... | collective-permute-start | bytes 663560 | tf_op jit(solution)/shard_map/ppermute | solution.py:50
  39.5 1.3 %collective-permute-start.15 = (bf16[96,1152]{1,0:T(8,128)(2,1)S(1)}, bf16[96,1152]{1,0:T(8,128)(2,1)S(1)}, u32[]{:S(2)}, u32[]{:S(2)}) collective-permute-start(bf16[96,1152]{1,0:T(8,128)(2,1)S(1)} %collective-permute-done.5.refs_5_), channel_id=1, source_target_pairs={{0,24},{4,28},{8,16},{12,20},{16,8},{20,12},{24,0},{28,4},{1,25},{... | collective-permute-start | bytes 663560 | tf_op jit(solution)/shard_map/ppermute | solution.py:501
  40.7 0.6 collective-permute-done.3
  41.3 0.8 collective-permute-start.11
  42.1 0.9 constant_dynamic-update-slice_fusion.2
  43.1 1.5 %collective-permute-done.8.refs_6_ = bf16[96,1152]{1,0:T(8,128)(2,1)S(1)} collective-permute-done((bf16[96,1152]{1,0:T(8,128)(2,1)S(1)}, bf16[96,1152]{1,0:T(8,128)(2,1)S(1)}, u32[]{:S(2)}, u32[]{:S(2)}) %collective-permute-start.8) | collective-permute-done | bytes 221216 | tf_op jit(solution)/shard_map/ppermute | solution.py:50
  44.5 1.5 %collective-permute-start.13 = (bf16[96,1152]{1,0:T(8,128)(2,1)S(1)}, bf16[96,1152]{1,0:T(8,128)(2,1)S(1)}, u32[]{:S(2)}, u32[]{:S(2)}) collective-permute-start(bf16[96,1152]{1,0:T(8,128)(2,1)S(1)} %collective-permute-done.8.refs_6_), channel_id=1, source_target_pairs={{0,4},{4,0},{8,12},{12,8},{1,5},{5,1},{9,13},{13,9},{2,6},{6,2},{1... | collective-permute-start | bytes 663560 | tf_op jit(solution)/shard_map/ppermute | solution.py:50
  46.1 2.4 %collective-permute-start.14 = (bf16[96,1152]{1,0:T(8,128)(2,1)S(1)}, bf16[96,1152]{1,0:T(8,128)(2,1)S(1)}, u32[]{:S(2)}, u32[]{:S(2)}) collective-permute-start(bf16[96,1152]{1,0:T(8,128)(2,1)S(1)} %collective-permute-done.9.refs_7_), channel_id=1, source_target_pairs={{0,4},{4,0},{8,12},{12,8},{1,5},{5,1},{9,13},{13,9},{2,6},{6,2},{1... | collective-permute-start | bytes 663560 | tf_op jit(solution)/shard_map/ppermute | solution.py:50
  48.5 1.7 %collective-permute-done.15.refs_13_ = bf16[96,1152]{1,0:T(8,128)(2,1)S(1)} collective-permute-done((bf16[96,1152]{1,0:T(8,128)(2,1)S(1)}, bf16[96,1152]{1,0:T(8,128)(2,1)S(1)}, u32[]{:S(2)}, u32[]{:S(2)}) %collective-permute-start.15) | collective-permute-done | bytes 221216 | tf_op jit(solution)/shard_map/ppermute | solution.py:501
  50.1 1.7 %collective-permute-start.16 = (bf16[96,1152]{1,0:T(8,128)(2,1)S(1)}, bf16[96,1152]{1,0:T(8,128)(2,1)S(1)}, u32[]{:S(2)}, u32[]{:S(2)}) collective-permute-start(bf16[96,1152]{1,0:T(8,128)(2,1)S(1)} %collective-permute-done.15.refs_13_), channel_id=1, source_target_pairs={{0,4},{4,0},{8,12},{12,8},{1,5},{5,1},{9,13},{13,9},{2,6},{6,2},{1... | collective-permute-start | bytes 663560 | tf_op jit(solution)/shard_map/ppermute | solution.py:50
  51.9 0.9 constant_dynamic-update-slice_fusion.refs_3_
  53.3 1.0 copy-done.5
  54.3 9.9 %attend.1.refs_1_ = bf16[512,768]{1,0:T(8,128)(2,1)S(1)} custom-call(s32[3]{0:T(128)S(1)} %pad_add_fusion.place.refs_0_, bf16[512,768]{1,0:T(8,128)(2,1)S(1)} %get-tuple-element.45.refs_1_, f32[6,64,256]{2,1,0:T(8,128)S(1)} %copy-done.5, bf16[96,2304]{1,0:T(8,128)(2,1)S(1)} %constant_dynamic-update-slice_fusion.3.refs_3_, ...), custom_call_target="tpu_custom_call" | custom-call | flops 11500000256 | tf_op jit(solution)/shard_map/attend/pallas_call | solution.py:259
  64.5 1.4 %collective-permute-done.18.refs_6_ = bf16[192,768]{1,0:T(8,128)(2,1)S(1)} collective-permute-done((bf16[192,768]{1,0:T(8,128)(2,1)S(1)}, bf16[192,768]{1,0:T(8,128)(2,1)S(1)}, u32[]{:S(2)}, u32[]{:S(2)}) %collective-permute-start.18) | collective-permute-done | bytes 294944 | tf_op jit(solution)/shard_map/ppermute | solution.py:50
  65.9 3.5 %project.1 = (bf16[16,32,768]{2,1,0:T(8,128)(2,1)S(1)}, bf16[4,32,768]{2,1,0:T(8,128)(2,1)S(1)}, bf16[48,768]{1,0:T(8,128)(2,1)S(1)}, bf16[16,768]{1,0:T(8,128)(2,1)S(1)}) custom-call(s32[3]{0:T(128)S(1)} %pad_add_fusion.place.refs_0_, bf16[512,768]{1,0:T(8,128)(2,1)S(1)} %attend.1.refs_1_, bf16[512,768]{1,0:T(8,128)(2,1)S(1)} %get-tuple-element.50.refs_2_, ...), custom_call_target="tpu_custom_call" | custom-call | flops 3449999872 | tf_op jit(solution)/shard_map/project/pallas_call | solution.py:328
  69.6 1.0 collective-permute-start.20
  70.6 4.3 %collective-permute-start.21 = (bf16[16,768]{1,0:T(8,128)(2,1)S(1)}, bf16[16,768]{1,0:T(8,128)(2,1)S(1)}, u32[]{:S(2)}, u32[]{:S(2)}) collective-permute-start(bf16[16,768]{1,0:T(8,128)(2,1)S(1)} %get-tuple-element.55), channel_id=1, source_target_pairs={{0,15},{1,12},{2,13},{3,14},{4,3},{5,0},{6,1},{7,2},{8,7},{9,4},{1... | collective-permute-start | bytes 73736 | tf_op jit(solution)/shard_map/ppermute | solution.py:45
  75.0 0.9 collective-permute-done.21.corner
  76.0 1.6 %dispatch.1 = (bf16[512,768]{1,0:T(8,128)(2,1)S(1)}, bf16[64,768]{1,0:T(8,128)(2,1)S(1)}, bf16[64,768]{1,0:T(8,128)(2,1)S(1)}, bf16[64,768]{1,0:T(8,128)(2,1)S(1...) custom-call(s32[3]{0:T(128)S(1)} %pad_add_fusion.place.refs_0_, ...), custom_call_target="tpu_custom_call" | custom-call | tf_op jit(solution)/shard_map/dispatch/pallas_call | solution.py:391
  78.3 1.5 %collective-permute-start.27 = (bf16[64,768]{1,0:T(8,128)(2,1)S(1)}, bf16[64,768]{1,0:T(8,128)(2,1)S(1)}, u32[]{:S(2)}, u32[]{:S(2)}) collective-permute-start(bf16[64,768]{1,0:T(8,128)(2,1)S(1)} %get-tuple-element.65), channel_id=1, source_target_pairs={{0,12},{4,8},{8,4},{12,0},{1,13},{5,9},{9,5},{13,1},{2,14},{6,10},... | collective-permute-start | bytes 294920 | tf_op jit(solution)/shard_map/ppermute | solution.py:50
  80.3 1.6 %collective-permute-start.24 = (bf16[64,768]{1,0:T(8,128)(2,1)S(1)}, bf16[64,768]{1,0:T(8,128)(2,1)S(1)}, u32[]{:S(2)}, u32[]{:S(2)}) collective-permute-start(bf16[64,768]{1,0:T(8,128)(2,1)S(1)} %get-tuple-element.60), channel_id=1, source_target_pairs={{0,12},{4,8},{8,4},{12,0},{1,13},{5,9},{9,5},{13,1},{2,14},{6,10},... | collective-permute-start | bytes 294920 | tf_op jit(solution)/shard_map/ppermute | solution.py:50
  82.1 3.1 %collective-permute-done.27.refs_3_ = bf16[64,768]{1,0:T(8,128)(2,1)S(1)} collective-permute-done((bf16[64,768]{1,0:T(8,128)(2,1)S(1)}, bf16[64,768]{1,0:T(8,128)(2,1)S(1)}, u32[]{:S(2)}, u32[]{:S(2)}) %collective-permute-start.27) | collective-permute-done | bytes 98336 | tf_op jit(solution)/shard_map/ppermute | solution.py:50
  85.2 7.6 %experts.3 = (bf16[64,768]{1,0:T(8,128)(2,1)S(1)}, bf16[64,768]{1,0:T(8,128)(2,1)S(1)}, bf16[64,768]{1,0:T(8,128)(2,1)S(1)}, bf16[64,768]{1,0:T(8,128)(2,1)S(1)}) custom-call(bf16[64,768]{1,0:T(8,128)(2,1)S(1)} %get-tuple-element.62.refs_0_, bf16[64,768]{1,0:T(8,128)(2,1)S(1)} %collective-permute-done.25.refs_1_, ...), custom_call_target="tpu_custom_call" | custom-call | flops 8049999872 | tf_op jit(solution)/shard_map/experts/pallas_call | solution.py:433
  93.3 1.7 %collective-permute-start.33 = (bf16[64,768]{1,0:T(8,128)(2,1)S(1)}, bf16[64,768]{1,0:T(8,128)(2,1)S(1)}, u32[]{:S(2)}, u32[]{:S(2)}) collective-permute-start(bf16[64,768]{1,0:T(8,128)(2,1)S(1)} %get-tuple-element.72), channel_id=1, source_target_pairs={{0,12},{4,8},{8,4},{12,0},{1,13},{5,9},{9,5},{13,1},{2,14},{6,10},... | collective-permute-start | bytes 294920 | tf_op jit(solution)/shard_map/ppermute | solution.py:50
  95.0 7.6 %experts.2 = (bf16[64,768]{1,0:T(8,128)(2,1)S(1)}, bf16[64,768]{1,0:T(8,128)(2,1)S(1)}, bf16[64,768]{1,0:T(8,128)(2,1)S(1)}, bf16[64,768]{1,0:T(8,128)(2,1)S(1)}) custom-call(bf16[64,768]{1,0:T(8,128)(2,1)S(1)} %get-tuple-element.57.refs_0_, bf16[64,768]{1,0:T(8,128)(2,1)S(1)} %collective-permute-done.22.refs_1_, ...), custom_call_target="tpu_custom_call" | custom-call | flops 8049999872 | tf_op jit(solution)/shard_map/experts/pallas_call | solution.py:433
  103.1 1.7 %collective-permute-start.32 = (bf16[64,768]{1,0:T(8,128)(2,1)S(1)}, bf16[64,768]{1,0:T(8,128)(2,1)S(1)}, u32[]{:S(2)}, u32[]{:S(2)}) collective-permute-start(bf16[64,768]{1,0:T(8,128)(2,1)S(1)} %get-tuple-element.71), channel_id=1, source_target_pairs={{0,12},{4,8},{8,4},{12,0},{1,13},{5,9},{9,5},{13,1},{2,14},{6,10},... | collective-permute-start | bytes 294920 | tf_op jit(solution)/shard_map/ppermute | solution.py:50
  105.3 1.3 %collective-permute-done.30.refs_4_ = bf16[64,768]{1,0:T(8,128)(2,1)S(1)} collective-permute-done((bf16[64,768]{1,0:T(8,128)(2,1)S(1)}, bf16[64,768]{1,0:T(8,128)(2,1)S(1)}, u32[]{:S(2)}, u32[]{:S(2)}) %collective-permute-start.30) | collective-permute-done | bytes 98336 | tf_op jit(solution)/shard_map/ppermute | solution.py:50
  106.7 2.7 %collective-permute-done.32.refs_6_ = bf16[64,768]{1,0:T(8,128)(2,1)S(1)} collective-permute-done((bf16[64,768]{1,0:T(8,128)(2,1)S(1)}, bf16[64,768]{1,0:T(8,128)(2,1)S(1)}, u32[]{:S(2)}, u32[]{:S(2)}) %collective-permute-start.32) | collective-permute-done | bytes 98336 | tf_op jit(solution)/shard_map/ppermute | solution.py:50
  109.4 2.3 %combine.1 = bf16[512,768]{1,0:T(8,128)(2,1)} custom-call(s32[3]{0:T(128)S(1)} %pad_add_fusion.place.refs_0_, bf16[512,768]{1,0:T(8,128)(2,1)S(1)} %get-tuple-element.56.attended, s32[512,1]{1,0:T(8,128)S(1)} %select_n.46.position, s32[512,1]{1,0:T(8,128)S(1)} %select_n.47.constant_at, f32[16,768]{1,0:T(8,128)S(1)} %copy-done.1, ...), custom_call_target="tpu_custom_call" | custom-call | tf_op jit(solution)/shard_map/combine/pallas_call | solution.py:471
  (62 shorter events, 5.5 us)
Async XLA Ops:
  1.0 10.6 %collective-permute-start.2 = (bf16[7,32,768]{2,1,0:T(8,128)(2,1)S(1)}, bf16[7,32,768]{2,1,0:T(8,128)(2,1)S(1)}, u32[]{:S(2)}, u32[]{:S(2)}) collective-permute-start(bf16[7,32,768]{2,1,0:T(8,128)(2,1)S(1)} %slice.9), channel_id=1, source_target_pairs={{0,4},{4,8},{8,12},{12,0},{1,5},{5,9},{9,13},{13,1},{2,6},{6,10},{... | collective-permute-start | bytes 1032200 | tf_op jit(solution)/shard_map/ppermute | solution.py:35
  3.7 7.9 %collective-permute-start = (bf16[48,2304]{1,0:T(8,128)(2,1)}, bf16[48,2304]{1,0:T(8,128)(2,1)S(1)}, u32[]{:S(2)}, u32[]{:S(2)}) collective-permute-start(bf16[48,2304]{1,0:T(8,128)(2,1)} %param.13), channel_id=1, source_target_pairs={{0,1},{1,0},{2,3},{3,2},{4,5},{5,4},{6,7},{7,6},{8,9},{9,8},{10,11... | collective-permute-start | bytes 663560 | tf_op jit(solution)/shard_map/ppermute | solution.py:50
  5.0 6.6 %collective-permute-start.1 = (bf16[48,768]{1,0:T(8,128)(2,1)}, bf16[48,768]{1,0:T(8,128)(2,1)S(1)}, u32[]{:S(2)}, u32[]{:S(2)}) collective-permute-start(bf16[48,768]{1,0:T(8,128)(2,1)} %param.14), channel_id=1, source_target_pairs={{0,1},{1,0},{2,3},{3,2},{4,5},{5,4},{6,7},{7,6},{8,9},{9,8},{10,11... | collective-permute-start | bytes 221192 | tf_op jit(solution)/shard_map/ppermute | solution.py:50
  11.6 26.5 %collective-permute-start.6 = (bf16[96,2304]{1,0:T(8,128)(2,1)S(1)}, bf16[96,2304]{1,0:T(8,128)(2,1)S(1)}, u32[]{:S(2)}, u32[]{:S(2)}) collective-permute-start(bf16[96,2304]{1,0:T(8,128)(2,1)S(1)} %constant_dynamic-update-slice_fusion.3.refs_3_), channel_id=1, source_target_pairs={{0,8},{4,12},{8,0},{12,4},{1,9},{5,13},{9,1},{13,5},{2,10},{6,14},... | collective-permute-start | bytes 1327112 | tf_op jit(solution)/shard_map/ppermute | solution.py:50
  12.6 30.4 %collective-permute-start.10 = (bf16[96,2304]{1,0:T(8,128)(2,1)S(1)}, bf16[96,2304]{1,0:T(8,128)(2,1)}, u32[]{:S(2)}, u32[]{:S(2)}) collective-permute-start(bf16[96,2304]{1,0:T(8,128)(2,1)S(1)} %constant_dynamic-update-slice_fusion.3.refs_3_), channel_id=1, source_target_pairs={{0,4},{4,0},{8,12},{12,8},{1,5},{5,1},{9,13},{13,9},{2,6},{6,2},{1... | collective-permute-start | bytes 1327112 | tf_op jit(solution)/shard_map/ppermute | solution.py:50
  14.5 10.8 %collective-permute-start.7 = (bf16[23,8,768]{2,1,0:T(8,128)(2,1)}, bf16[23,8,768]{2,1,0:T(8,128)(2,1)S(1)}, u32[]{:S(2)}, u32[]{:S(2)}) collective-permute-start(bf16[23,8,768]{2,1,0:T(8,128)(2,1)} %pad_maximum_fusion), channel_id=1, source_target_pairs={{0,1},{1,2},{2,3},{3,0},{4,5},{5,6},{6,7},{7,4},{8,9},{9,10},{10,1... | collective-permute-start | bytes 847880 | tf_op jit(solution)/shard_map/ppermute | solution.py:35
  16.7 21.4 %collective-permute-start.5 = (bf16[96,1152]{1,0:T(8,128)(2,1)}, bf16[96,1152]{1,0:T(8,128)(2,1)S(1)}, u32[]{:S(2)}, u32[]{:S(2)}) collective-permute-start(bf16[96,1152]{1,0:T(8,128)(2,1)} %constant_dynamic-slice_fusion), channel_id=1, source_target_pairs={{0,2},{1,3},{2,0},{3,1},{4,6},{5,7},{6,4},{7,5},{8,10},{9,11},{10,... | collective-permute-start | bytes 663560 | tf_op jit(solution)/shard_map/ppermute | solution.py:50
  20.5 20.8 %collective-permute-start.3 = (bf16[96,768]{1,0:T(8,128)(2,1)}, bf16[96,768]{1,0:T(8,128)(2,1)}, u32[]{:S(2)}, u32[]{:S(2)}) collective-permute-start(bf16[96,768]{1,0:T(8,128)(2,1)} %pad_maximum_fusion.1), channel_id=1, source_target_pairs={{0,2},{1,3},{2,0},{3,1},{4,6},{5,7},{6,4},{7,5},{8,10},{9,11},{10,... | collective-permute-start | bytes 442376 | tf_op jit(solution)/shard_map/ppermute | solution.py:50
  20.6 1.1 %copy-start = (bf16[16,32,768]{2,1,0:T(8,128)(2,1)S(1)}, bf16[16,32,768]{2,1,0:T(8,128)(2,1)}, u32[]{:S(2)}) copy-start(bf16[16,32,768]{2,1,0:T(8,128)(2,1)} %tokens.1) | copy-start | bytes 2359300
  21.7 1.1 %copy-start.2 = (f32[24,64,64]{2,1,0:T(8,128)S(1)}, f32[24,64,64]{2,1,0:T(8,128)}, u32[]{:S(2)}) copy-start(f32[24,64,64]{2,1,0:T(8,128)} %rel_bias.1) | copy-start | bytes 1179652
  22.9 0.9 copy-start.3
  24.0 0.7 copy-start.4
  38.1 6.5 %collective-permute-start.8 = (bf16[96,1152]{1,0:T(8,128)(2,1)S(1)}, bf16[96,1152]{1,0:T(8,128)(2,1)S(1)}, u32[]{:S(2)}, u32[]{:S(2)}) collective-permute-start(bf16[96,1152]{1,0:T(8,128)(2,1)S(1)} %collective-permute-done.5.refs_5_), channel_id=1, source_target_pairs={{0,16},{16,0},{1,17},{17,1},{2,18},{18,2},{3,19},{19,3},{4,20},{20... | collective-permute-start | bytes 663560 | tf_op jit(solution)/shard_map/ppermute | solution.py:50
  39.3 6.7 %collective-permute-start.9 = (bf16[96,1152]{1,0:T(8,128)(2,1)S(1)}, bf16[96,1152]{1,0:T(8,128)(2,1)S(1)}, u32[]{:S(2)}, u32[]{:S(2)}) collective-permute-start(bf16[96,1152]{1,0:T(8,128)(2,1)S(1)} %collective-permute-done.5.refs_5_), channel_id=1, source_target_pairs={{0,8},{4,12},{8,0},{12,4},{1,9},{5,13},{9,1},{13,5},{2,10},{6,14},... | collective-permute-start | bytes 663560 | tf_op jit(solution)/shard_map/ppermute | solution.py:50
  39.5 10.7 %collective-permute-start.15 = (bf16[96,1152]{1,0:T(8,128)(2,1)S(1)}, bf16[96,1152]{1,0:T(8,128)(2,1)S(1)}, u32[]{:S(2)}, u32[]{:S(2)}) collective-permute-start(bf16[96,1152]{1,0:T(8,128)(2,1)S(1)} %collective-permute-done.5.refs_5_), channel_id=1, source_target_pairs={{0,24},{4,28},{8,16},{12,20},{16,8},{20,12},{24,0},{28,4},{1,25},{... | collective-permute-start | bytes 663560 | tf_op jit(solution)/shard_map/ppermute | solution.py:501
  41.3 12.0 %collective-permute-start.11 = (bf16[96,2304]{1,0:T(8,128)(2,1)S(1)}, bf16[96,2304]{1,0:T(8,128)(2,1)S(1)}, u32[]{:S(2)}, u32[]{:S(2)}) collective-permute-start(bf16[96,2304]{1,0:T(8,128)(2,1)S(1)} %collective-permute-done.6.refs_4_), channel_id=1, source_target_pairs={{0,4},{4,0},{8,12},{12,8},{1,5},{5,1},{9,13},{13,9},{2,6},{6,2},{1... | collective-permute-start | bytes 1327112 | tf_op jit(solution)/shard_map/ppermute | solution.py:50
  43.0 9.8 %collective-permute-start.12 = (bf16[96,1152]{1,0:T(8,128)(2,1)S(1)}, bf16[96,1152]{1,0:T(8,128)(2,1)S(1)}, u32[]{:S(2)}, u32[]{:S(2)}) collective-permute-start(bf16[96,1152]{1,0:T(8,128)(2,1)S(1)} %collective-permute-done.5.refs_5_), channel_id=1, source_target_pairs={{0,4},{4,0},{8,12},{12,8},{1,5},{5,1},{9,13},{13,9},{2,6},{6,2},{1... | collective-permute-start | bytes 663560 | tf_op jit(solution)/shard_map/ppermute | solution.py:50
  44.5 8.5 %collective-permute-start.13 = (bf16[96,1152]{1,0:T(8,128)(2,1)S(1)}, bf16[96,1152]{1,0:T(8,128)(2,1)S(1)}, u32[]{:S(2)}, u32[]{:S(2)}) collective-permute-start(bf16[96,1152]{1,0:T(8,128)(2,1)S(1)} %collective-permute-done.8.refs_6_), channel_id=1, source_target_pairs={{0,4},{4,0},{8,12},{12,8},{1,5},{5,1},{9,13},{13,9},{2,6},{6,2},{1... | collective-permute-start | bytes 663560 | tf_op jit(solution)/shard_map/ppermute | solution.py:50
  46.1 7.3 %collective-permute-start.14 = (bf16[96,1152]{1,0:T(8,128)(2,1)S(1)}, bf16[96,1152]{1,0:T(8,128)(2,1)S(1)}, u32[]{:S(2)}, u32[]{:S(2)}) collective-permute-start(bf16[96,1152]{1,0:T(8,128)(2,1)S(1)} %collective-permute-done.9.refs_7_), channel_id=1, source_target_pairs={{0,4},{4,0},{8,12},{12,8},{1,5},{5,1},{9,13},{13,9},{2,6},{6,2},{1... | collective-permute-start | bytes 663560 | tf_op jit(solution)/shard_map/ppermute | solution.py:50
  50.1 3.2 %collective-permute-start.16 = (bf16[96,1152]{1,0:T(8,128)(2,1)S(1)}, bf16[96,1152]{1,0:T(8,128)(2,1)S(1)}, u32[]{:S(2)}, u32[]{:S(2)}) collective-permute-start(bf16[96,1152]{1,0:T(8,128)(2,1)S(1)} %collective-permute-done.15.refs_13_), channel_id=1, source_target_pairs={{0,4},{4,0},{8,12},{12,8},{1,5},{5,1},{9,13},{13,9},{2,6},{6,2},{1... | collective-permute-start | bytes 663560 | tf_op jit(solution)/shard_map/ppermute | solution.py:50
  52.8 11.4 %collective-permute-start.4 = (bf16[192,768]{1,0:T(8,128)(2,1)S(1)}, bf16[192,768]{1,0:T(8,128)(2,1)S(1)}, u32[]{:S(2)}, u32[]{:S(2)}) collective-permute-start(bf16[192,768]{1,0:T(8,128)(2,1)S(1)} %constant_dynamic-update-slice_fusion.refs_3_), channel_id=1, source_target_pairs={{0,8},{4,12},{8,0},{12,4},{1,9},{5,13},{9,1},{13,5},{2,10},{6,14},... | collective-permute-start | bytes 884744 | tf_op jit(solution)/shard_map/ppermute | solution.py:50
  53.0 11.5 %collective-permute-start.17 = (bf16[192,768]{1,0:T(8,128)(2,1)S(1)}, bf16[192,768]{1,0:T(8,128)(2,1)S(1)}, u32[]{:S(2)}, u32[]{:S(2)}) collective-permute-start(bf16[192,768]{1,0:T(8,128)(2,1)S(1)} %constant_dynamic-update-slice_fusion.refs_3_), channel_id=1, source_target_pairs={{0,4},{4,0},{8,12},{12,8},{1,5},{5,1},{9,13},{13,9},{2,6},{6,2},{1... | collective-permute-start | bytes 884744 | tf_op jit(solution)/shard_map/ppermute | solution.py:50
  53.3 1.0 copy-start.5
  54.3 20.6 %copy-start.6 = (s32[16,32]{1,0:T(8,128)S(1)}, s32[16,32]{1,0:T(8,128)}, u32[]{:S(2)}) copy-start(s32[16,32]{1,0:T(8,128)} %param.21) | copy-start | bytes 6148
  54.3 20.6 %copy-start.7 = (s32[16,32]{1,0:T(8,128)S(1)}, s32[16,32]{1,0:T(8,128)}, u32[]{:S(2)}) copy-start(s32[16,32]{1,0:T(8,128)} %param.19) | copy-start | bytes 6148
  54.3 20.6 %copy-start.8 = (s32[16,32]{1,0:T(8,128)S(1)}, s32[16,32]{1,0:T(8,128)}, u32[]{:S(2)}) copy-start(s32[16,32]{1,0:T(8,128)} %param.20) | copy-start | bytes 6148
  64.2 1.6 %collective-permute-start.18 = (bf16[192,768]{1,0:T(8,128)(2,1)S(1)}, bf16[192,768]{1,0:T(8,128)(2,1)S(1)}, u32[]{:S(2)}, u32[]{:S(2)}) collective-permute-start(bf16[192,768]{1,0:T(8,128)(2,1)S(1)} %collective-permute-done.4.refs_4_), channel_id=1, source_target_pairs={{0,4},{4,0},{8,12},{12,8},{1,5},{5,1},{9,13},{13,9},{2,6},{6,2},{1... | collective-permute-start | bytes 884744 | tf_op jit(solution)/shard_map/ppermute | solution.py:50
  69.3 6.6 %collective-permute-start.19 = (bf16[4,32,768]{2,1,0:T(8,128)(2,1)S(1)}, bf16[4,32,768]{2,1,0:T(8,128)(2,1)S(1)}, u32[]{:S(2)}, u32[]{:S(2)}) collective-permute-start(bf16[4,32,768]{2,1,0:T(8,128)(2,1)S(1)} %get-tuple-element.53), channel_id=1, source_target_pairs={{0,12},{4,0},{8,4},{12,8},{1,13},{5,1},{9,5},{13,9},{2,14},{6,2},{... | collective-permute-start | bytes 589832 | tf_op jit(solution)/shard_map/ppermute | solution.py:35
  69.6 6.3 %collective-permute-start.20 = (bf16[48,768]{1,0:T(8,128)(2,1)S(1)}, bf16[48,768]{1,0:T(8,128)(2,1)S(1)}, u32[]{:S(2)}, u32[]{:S(2)}) collective-permute-start(bf16[48,768]{1,0:T(8,128)(2,1)S(1)} %get-tuple-element.54), channel_id=1, source_target_pairs={{0,3},{1,0},{2,1},{3,2},{4,7},{5,4},{6,5},{7,6},{8,11},{9,8},{10,9... | collective-permute-start | bytes 221192 | tf_op jit(solution)/shard_map/ppermute | solution.py:35
  70.6 5.3 %collective-permute-start.21 = (bf16[16,768]{1,0:T(8,128)(2,1)S(1)}, bf16[16,768]{1,0:T(8,128)(2,1)S(1)}, u32[]{:S(2)}, u32[]{:S(2)}) collective-permute-start(bf16[16,768]{1,0:T(8,128)(2,1)S(1)} %get-tuple-element.55), channel_id=1, source_target_pairs={{0,15},{1,12},{2,13},{3,14},{4,3},{5,0},{6,1},{7,2},{8,7},{9,4},{1... | collective-permute-start | bytes 73736 | tf_op jit(solution)/shard_map/ppermute | solution.py:45
  77.6 2.7 %collective-permute-start.25 = (bf16[64,768]{1,0:T(8,128)(2,1)S(1)}, bf16[64,768]{1,0:T(8,128)(2,1)S(1)}, u32[]{:S(2)}, u32[]{:S(2)}) collective-permute-start(bf16[64,768]{1,0:T(8,128)(2,1)S(1)} %get-tuple-element.63), channel_id=1, source_target_pairs={{0,4},{4,0},{8,12},{12,8},{1,5},{5,1},{9,13},{13,9},{2,6},{6,2},{1... | collective-permute-start | bytes 294920 | tf_op jit(solution)/shard_map/ppermute | solution.py:50
  78.0 4.2 %collective-permute-start.26 = (bf16[64,768]{1,0:T(8,128)(2,1)S(1)}, bf16[64,768]{1,0:T(8,128)(2,1)S(1)}, u32[]{:S(2)}, u32[]{:S(2)}) collective-permute-start(bf16[64,768]{1,0:T(8,128)(2,1)S(1)} %get-tuple-element.64), channel_id=1, source_target_pairs={{0,8},{4,12},{8,0},{12,4},{1,9},{5,13},{9,1},{13,5},{2,10},{6,14},... | collective-permute-start | bytes 294920 | tf_op jit(solution)/shard_map/ppermute | solution.py:50
  78.3 6.9 %collective-permute-start.27 = (bf16[64,768]{1,0:T(8,128)(2,1)S(1)}, bf16[64,768]{1,0:T(8,128)(2,1)S(1)}, u32[]{:S(2)}, u32[]{:S(2)}) collective-permute-start(bf16[64,768]{1,0:T(8,128)(2,1)S(1)} %get-tuple-element.65), channel_id=1, source_target_pairs={{0,12},{4,8},{8,4},{12,0},{1,13},{5,9},{9,5},{13,1},{2,14},{6,10},... | collective-permute-start | bytes 294920 | tf_op jit(solution)/shard_map/ppermute | solution.py:50
  79.8 13.5 %collective-permute-start.22 = (bf16[64,768]{1,0:T(8,128)(2,1)S(1)}, bf16[64,768]{1,0:T(8,128)(2,1)S(1)}, u32[]{:S(2)}, u32[]{:S(2)}) collective-permute-start(bf16[64,768]{1,0:T(8,128)(2,1)S(1)} %get-tuple-element.58), channel_id=1, source_target_pairs={{0,4},{4,0},{8,12},{12,8},{1,5},{5,1},{9,13},{13,9},{2,6},{6,2},{1... | collective-permute-start | bytes 294920 | tf_op jit(solution)/shard_map/ppermute | solution.py:50
  79.8 15.2 %collective-permute-start.23 = (bf16[64,768]{1,0:T(8,128)(2,1)S(1)}, bf16[64,768]{1,0:T(8,128)(2,1)S(1)}, u32[]{:S(2)}, u32[]{:S(2)}) collective-permute-start(bf16[64,768]{1,0:T(8,128)(2,1)S(1)} %get-tuple-element.59), channel_id=1, source_target_pairs={{0,8},{4,12},{8,0},{12,4},{1,9},{5,13},{9,1},{13,5},{2,10},{6,14},... | collective-permute-start | bytes 294920 | tf_op jit(solution)/shard_map/ppermute | solution.py:50
  80.3 14.7 %collective-permute-start.24 = (bf16[64,768]{1,0:T(8,128)(2,1)S(1)}, bf16[64,768]{1,0:T(8,128)(2,1)S(1)}, u32[]{:S(2)}, u32[]{:S(2)}) collective-permute-start(bf16[64,768]{1,0:T(8,128)(2,1)S(1)} %get-tuple-element.60), channel_id=1, source_target_pairs={{0,12},{4,8},{8,4},{12,0},{1,13},{5,9},{9,5},{13,1},{2,14},{6,10},... | collective-permute-start | bytes 294920 | tf_op jit(solution)/shard_map/ppermute | solution.py:50
  92.8 10.3 %collective-permute-start.29 = (bf16[64,768]{1,0:T(8,128)(2,1)S(1)}, bf16[64,768]{1,0:T(8,128)(2,1)S(1)}, u32[]{:S(2)}, u32[]{:S(2)}) collective-permute-start(bf16[64,768]{1,0:T(8,128)(2,1)S(1)} %get-tuple-element.68), channel_id=1, source_target_pairs={{0,4},{4,0},{8,12},{12,8},{1,5},{5,1},{9,13},{13,9},{2,6},{6,2},{1... | collective-permute-start | bytes 294920 | tf_op jit(solution)/shard_map/ppermute | solution.py:50
  92.8 12.5 %collective-permute-start.31 = (bf16[64,768]{1,0:T(8,128)(2,1)S(1)}, bf16[64,768]{1,0:T(8,128)(2,1)S(1)}, u32[]{:S(2)}, u32[]{:S(2)}) collective-permute-start(bf16[64,768]{1,0:T(8,128)(2,1)S(1)} %get-tuple-element.70), channel_id=1, source_target_pairs={{0,8},{4,12},{8,0},{12,4},{1,9},{5,13},{9,1},{13,5},{2,10},{6,14},... | collective-permute-start | bytes 294920 | tf_op jit(solution)/shard_map/ppermute | solution.py:50
  93.3 12.1 %collective-permute-start.33 = (bf16[64,768]{1,0:T(8,128)(2,1)S(1)}, bf16[64,768]{1,0:T(8,128)(2,1)S(1)}, u32[]{:S(2)}, u32[]{:S(2)}) collective-permute-start(bf16[64,768]{1,0:T(8,128)(2,1)S(1)} %get-tuple-element.72), channel_id=1, source_target_pairs={{0,12},{4,8},{8,4},{12,0},{1,13},{5,9},{9,5},{13,1},{2,14},{6,10},... | collective-permute-start | bytes 294920 | tf_op jit(solution)/shard_map/ppermute | solution.py:50
  95.0 14.4 %copy-start.1 = (f32[16,768]{1,0:T(8,128)S(1)}, f32[16,768]{1,0:T(8,128)}, u32[]{:S(2)}) copy-start(f32[16,768]{1,0:T(8,128)} %table.1) | copy-start | bytes 147460
  102.6 2.8 %collective-permute-start.28 = (bf16[64,768]{1,0:T(8,128)(2,1)S(1)}, bf16[64,768]{1,0:T(8,128)(2,1)S(1)}, u32[]{:S(2)}, u32[]{:S(2)}) collective-permute-start(bf16[64,768]{1,0:T(8,128)(2,1)S(1)} %get-tuple-element.67), channel_id=1, source_target_pairs={{0,4},{4,0},{8,12},{12,8},{1,5},{5,1},{9,13},{13,9},{2,6},{6,2},{1... | collective-permute-start | bytes 294920 | tf_op jit(solution)/shard_map/ppermute | solution.py:50
  102.7 4.0 %collective-permute-start.30 = (bf16[64,768]{1,0:T(8,128)(2,1)S(1)}, bf16[64,768]{1,0:T(8,128)(2,1)S(1)}, u32[]{:S(2)}, u32[]{:S(2)}) collective-permute-start(bf16[64,768]{1,0:T(8,128)(2,1)S(1)} %get-tuple-element.69), channel_id=1, source_target_pairs={{0,8},{4,12},{8,0},{12,4},{1,9},{5,13},{9,1},{13,5},{2,10},{6,14},... | collective-permute-start | bytes 294920 | tf_op jit(solution)/shard_map/ppermute | solution.py:50
  103.1 6.3 %collective-permute-start.32 = (bf16[64,768]{1,0:T(8,128)(2,1)S(1)}, bf16[64,768]{1,0:T(8,128)(2,1)S(1)}, u32[]{:S(2)}, u32[]{:S(2)}) collective-permute-start(bf16[64,768]{1,0:T(8,128)(2,1)S(1)} %get-tuple-element.71), channel_id=1, source_target_pairs={{0,12},{4,8},{8,4},{12,0},{1,13},{5,9},{9,5},{13,1},{2,14},{6,10},... | collective-permute-start | bytes 294920 | tf_op jit(solution)/shard_map/ppermute | solution.py:50

commit v6 on v5

--- a/solution.py
+++ b/solution.py
@@ -56,15 +56,21 @@
     return (centred * lax.rsqrt(spread + 1e-05)).astype(jnp.bfloat16)
 
 
-def prepare_kernel(tokens, taps, rel_bias, kept, weights, bias):
+def prepare_kernel(tokens, taps, rel_bias, *refs):
+    count = (len(refs) - 4) // 2
+    sources, (kept, weights, bias, edge), copies = refs[:count], refs[count : count + 4], refs[count + 4 :]
     kept[...] = tokens[...].astype(jnp.float32)
     weights[...] = taps[...].astype(jnp.float32)
+    edge[...] = tokens[:, tokens.shape[1] - HALO :]
     for head in range(rel_bias.shape[0]):
         at = head % GROUP * SPOTS
         bias[head // GROUP, :, at : at + SPOTS] = rel_bias[head]
-
-
-def prepare(tokens, taps, rel_bias):
+    for source, copy in zip(sources, copies, strict=True):
+        copy[...] = source[...]
+
+
+def prepare(tokens, taps, rel_bias, *others):
+    rows, _, channels = tokens.shape
     bias_shape = (rel_bias.shape[0] // GROUP, SPOTS, GROUP * SPOTS)
     return pl.pallas_call(
         prepare_kernel,
@@ -72,13 +78,47 @@
             jax.ShapeDtypeStruct(tokens.shape, jnp.float32),
             jax.ShapeDtypeStruct(taps.shape, jnp.float32),
             jax.ShapeDtypeStruct(bias_shape, jnp.float32),
+            jax.ShapeDtypeStruct((rows, HALO, channels), jnp.bfloat16),
+            *[jax.ShapeDtypeStruct(x.shape, x.dtype) for x in others],
         ),
-        in_specs=[VMEM] * 3,
-        out_specs=(VMEM,) * 3,
+        in_specs=[VMEM] * (3 + len(others)),
+        out_specs=(VMEM,) * (4 + len(others)),
         compiler_params=pltpu.CompilerParams(vmem_limit_bytes=8 * 1024 * 1024),
         cost_estimate=lasting(3),
         name="prepare",
-    )(tokens, taps, rel_bias)
+    )(tokens, taps, rel_bias, *others)
+
+
+def join_kernel(place, own_in, beyond_in, own_out, beyond_out, above, edge, two, mine, two_out, column):
+    size, half = own_in.shape[0], mine.shape[1]
+    lanes = pl.ds(pl.multiple_of(place[2] * half, LANES), half)
+    for at, (part_in, part_out) in enumerate(((own_in, own_out), (beyond_in, beyond_out))):
+        rows = slice(at * size, (at + 1) * size)
+        two[rows, :] = part_in[...]
+        mine[rows, :] = part_in[:, lanes]
+        two_out[rows, :] = part_out[...]
+    reach = above.shape[0]
+    column[:reach] = above[:, above.shape[1] - HALO :]
+    column[reach:] = edge[...]
+
+
+def join(place, own_in, beyond_in, own_out, beyond_out, above, edge):
+    bf16 = functools.partial(jax.ShapeDtypeStruct, dtype=jnp.bfloat16)
+    size, wide = own_in.shape
+    return pl.pallas_call(
+        join_kernel,
+        out_shape=(
+            bf16((2 * size, wide)),
+            bf16((2 * size, wide // 2)),
+            bf16((2 * size, own_out.shape[1])),
+            bf16((above.shape[0] + edge.shape[0], *edge.shape[1:])),
+        ),
+        in_specs=[SMEM] + [VMEM] * 6,
+        out_specs=(VMEM,) * 4,
+        compiler_params=pltpu.CompilerParams(vmem_limit_bytes=8 * 1024 * 1024),
+        cost_estimate=lasting(1),
+        name="join",
+    )(place, own_in, beyond_in, own_out, beyond_out, above, edge)
 
 
 def encode_kernel(place, tokens, above, beside, weights, encoded, normed, upper, left):
@@ -139,7 +179,7 @@
         normed[part, :] = normalized(encoded[part, :].astype(jnp.float32))
         return 0
 
-    lax.fori_loop(0, rows * cols // SPOTS, norm, 0)
+    lax.fori_loop(0, rows * cols // SPOTS, norm, 0, unroll=4)
 
 
 def encode(place, tokens, above, beside, weights):
@@ -192,7 +232,7 @@
     groups = channels // LANES
     for copy in copies:
         copy.wait()
-    wide = channels
+    wide = 3 * channels
 
     def project(index, _):
         lanes = pl.ds(pl.multiple_of(index * wide, wide), wide)
@@ -249,7 +289,7 @@
             ).astype(jnp.bfloat16)
         return 0
 
-    lax.fori_loop(0, rows * cols // SPOTS, window, 0)
+    lax.fori_loop(0, rows * cols // SPOTS, window, 0, unroll=4)
 
 
 def attend(place, shape, normed, bias, pieces, grid_cols):
@@ -280,7 +320,7 @@
     for copy in fetch(place, grid_cols, refs[3 : 3 + len(ids)], ids, weight, sems):
         copy.wait()
     window_cols = cols // WIN
-    wide = 2 * LANES
+    wide = channels
     sublane = lax.broadcasted_iota(jnp.int32, (WIN, wide), 0)
 
     def finish(index, _):
@@ -528,17 +568,18 @@
     if quick:
         pair = [(0, 0), (0, 1)]
         beyond, beyond_out = exchanged(project_in, "gx", 1), exchanged(project_out, "gx", 1)
-        beyond, beyond_out, above = held(beyond, beyond_out, above)
-        two = (jnp.concatenate([project_in, beyond], axis=0), pair, None)
-        two_out = (jnp.concatenate([project_out, beyond_out], axis=0), pair, None)
-        wide = two[0].shape[1] // 2
-        mine = lax.dynamic_slice_in_dim(two[0], lax.axis_index("groups") * wide, wide, axis=1)
-        far = along((mine, two[1], 0), "gx", 2)
+        kept, weights, bias, edge, own_in, own_out = prepare(
+            tokens, conv_kernel, rel_bias, project_in, project_out
+        )
+        two, mine, two_out, column = join(place, own_in, beyond, own_out, beyond_out, above, edge)
+        two, two_out = (two, pair, None), (two_out, pair, None)
+        far = along((mine, pair, 0), "gx", 2)
         facing = along(two, "gy", 2)
         far_out = along(two_out, "gx", 2)
-    edge = jnp.concatenate([above[:, cols - HALO :], tokens[:, cols - HALO :]], axis=0)
-    beside = shifted(edge, "gx", 1)
-    kept, weights, bias = prepare(tokens, conv_kernel, rel_bias)
+    else:
+        kept, weights, bias, edge = prepare(tokens, conv_kernel, rel_bias)
+        column = jnp.concatenate([above[:, cols - HALO :], edge], axis=0)
+    beside = shifted(column, "gx", 1)
     encoded, normed = encode(place, kept, above, beside, weights)
     if quick:
         first, second, normed = held(far[0], facing[0], normed)

time: 112 us -> 108 us (0.964)
  local copies, waits for them, and re-layouts: 10.9 us -> 7.33 us
  waiting for transfers between devices: 21.4 us -> 24.1 us
  other arithmetic: 2.37 us -> 0.08 us
  Pallas kernels: 42.4 us -> 40.8 us
    ppermute x4, waiting for transfers between devices: 0.54 us -> 4.19 us  [shifted(): return lax.ppermute(x, axis, [(i, (i + by) % size) for i in range(size)])]
    concatenate x2 -> x0, other arithmetic: 2.29 us -> none  [the longest x1 1.54 us: shards(): two_out = (jnp.concatenate([project_out, beyond_out], axis=0), pair, None)]
    ppermute x28, starting transfers between devices: 23.3 us -> 25.3 us  [exchanged(): return lax.ppermute(x, axis, [(i, i ^ mask) for i in range(size)])]
    unnamed x21 -> x19, local copies, waits for them, and re-layouts: 6.74 us -> 5 us
  transfers between devices with their start and end apart: 34 -> 34, of which waited for: 12 -> 13; matrix products, arithmetic and copies ran while one was open for 7% -> 1% of each run, Pallas kernels for 31% -> 31%
where the time goes in v6:
time: 108 us
  Pallas kernels  40.8 us (38%)
  starting transfers between devices  35.4 us (33%)
  waiting for transfers between devices  24.1 us (22%)
  local copies, waits for them, and re-layouts  7.33 us (7%)
    ppermute x28, starting transfers between devices, exchanged(): return lax.ppermute(x, axis, [(i, i ^ mask) for i in range(size)])  25.3 us
    ppermute x28, waiting for transfers between devices, exchanged(): return lax.ppermute(x, axis, [(i, i ^ mask) for i in range(size)])  17.4 us
    pallas_call x2, Pallas kernels, serve(): pl.pallas_call(functools.partial(expert_kernel, count, first), out_shape=...  15.1 us
    pallas_call x1, Pallas kernels, attend(): pl.pallas_call(functools.partial(attend_kernel, shape, ids, grid_cols), o...  9.02 us
    pallas_call x1, Pallas kernels, encode(): pl.pallas_call(encode_kernel, out_shape=(flat, flat), in_specs=[SMEM] + [...  8.73 us
    ppermute x4, starting transfers between devices, shifted(): return lax.ppermute(x, axis, [(i, (i + by) % size) for i in range(size)])  5.06 us
    unnamed x19, local copies, waits for them, and re-layouts  5 us
    ppermute x1, starting transfers between devices, shifted_both(): return lax.ppermute(x, ('gy', 'gx'), pairs)  4.24 us
  transfers between devices with their start and end apart: 34, of which 13 were waited for; matrix products, arithmetic and copies ran while one was open for 1% of the time, Pallas kernels for 31%

profile of v6, /device:TPU:1, one launch (start us, length us, event | category | flops | bytes accessed | tf_op | source)
XLA Modules:
  0.0 107.9 jit_solution(7239844851330853902)
XLA Ops:
  0.0 1.7 %slice.3 = bf16[7,32,768]{2,1,0:T(8,128)(2,1)} slice(bf16[16,32,768]{2,1,0:T(8,128)(2,1)} %tokens.1), slice={[9:16], [0:32], [0:768]} | slice | bytes 688128 | tf_op jit(solution)/shard_map/slice | solution.py:567
  1.7 2.6 %collective-permute-start.2 = (bf16[7,32,768]{2,1,0:T(8,128)(2,1)}, bf16[7,32,768]{2,1,0:T(8,128)(2,1)S(1)}, u32[]{:S(2)}, u32[]{:S(2)}) collective-permute-start(bf16[7,32,768]{2,1,0:T(8,128)(2,1)} %slice.3), channel_id=1, source_target_pairs={{0,4},{4,8},{8,12},{12,0},{1,5},{5,9},{9,13},{13,1},{2,6},{6,10},{... | collective-permute-start | bytes 1032200 | tf_op jit(solution)/shard_map/ppermute | solution.py:35
  4.3 1.3 %collective-permute-start = (bf16[48,2304]{1,0:T(8,128)(2,1)}, bf16[48,2304]{1,0:T(8,128)(2,1)S(1)}, u32[]{:S(2)}, u32[]{:S(2)}) collective-permute-start(bf16[48,2304]{1,0:T(8,128)(2,1)} %refs_0_.1), channel_id=1, source_target_pairs={{0,1},{1,0},{2,3},{3,2},{4,5},{5,4},{6,7},{7,6},{8,9},{9,8},{10,11... | collective-permute-start | bytes 663560 | tf_op jit(solution)/shard_map/ppermute | solution.py:50
  5.8 1.1 %copy-done = bf16[16,32,768]{2,1,0:T(8,128)(2,1)S(1)} copy-done((bf16[16,32,768]{2,1,0:T(8,128)(2,1)S(1)}, bf16[16,32,768]{2,1,0:T(8,128)(2,1)}, u32[]{:S(2)}) %copy-start) | copy-done | bytes 786456
  6.9 1.1 %copy-done.2 = f32[24,64,64]{2,1,0:T(8,128)S(1)} copy-done((f32[24,64,64]{2,1,0:T(8,128)S(1)}, f32[24,64,64]{2,1,0:T(8,128)}, u32[]{:S(2)}) %copy-start.2) | copy-done | bytes 393240
  8.1 0.9 copy-done.3
  9.0 0.9 copy-done.4
  9.9 0.9 copy-done.5
  11.1 1.1 %collective-permute-done.1.beyond_out = bf16[48,768]{1,0:T(8,128)(2,1)S(1)} collective-permute-done((bf16[48,768]{1,0:T(8,128)(2,1)}, bf16[48,768]{1,0:T(8,128)(2,1)S(1)}, u32[]{:S(2)}, u32[]{:S(2)}) %collective-permute-start.1) | collective-permute-done | bytes 73760 | tf_op jit(solution)/shard_map/ppermute | solution.py:50
  12.2 0.6 join.1
  12.8 1.1 %collective-permute-start.6 = (bf16[96,2304]{1,0:T(8,128)(2,1)S(1)}, bf16[96,2304]{1,0:T(8,128)(2,1)S(1)}, u32[]{:S(2)}, u32[]{:S(2)}) collective-permute-start(bf16[96,2304]{1,0:T(8,128)(2,1)S(1)} %get-tuple-element.48.refs_3_), channel_id=1, source_target_pairs={{0,8},{4,12},{8,0},{12,4},{1,9},{5,13},{9,1},{13,5},{2,10},{6,14},... | collective-permute-start | bytes 1327112 | tf_op jit(solution)/shard_map/ppermute | solution.py:50
  13.9 1.6 %collective-permute-start.7 = (bf16[23,8,768]{2,1,0:T(8,128)(2,1)S(1)}, bf16[23,8,768]{2,1,0:T(8,128)(2,1)S(1)}, u32[]{:S(2)}, u32[]{:S(2)}) collective-permute-start(bf16[23,8,768]{2,1,0:T(8,128)(2,1)S(1)} %get-tuple-element.50), channel_id=1, source_target_pairs={{0,1},{1,2},{2,3},{3,0},{4,5},{5,6},{6,7},{7,4},{8,9},{9,10},{10,1... | collective-permute-start | bytes 847880 | tf_op jit(solution)/shard_map/ppermute | solution.py:35
  15.5 2.3 %collective-permute-start.5 = (bf16[96,1152]{1,0:T(8,128)(2,1)S(1)}, bf16[96,1152]{1,0:T(8,128)(2,1)S(1)}, u32[]{:S(2)}, u32[]{:S(2)}) collective-permute-start(bf16[96,1152]{1,0:T(8,128)(2,1)S(1)} %get-tuple-element.47), channel_id=1, source_target_pairs={{0,2},{1,3},{2,0},{3,1},{4,6},{5,7},{6,4},{7,5},{8,10},{9,11},{10,... | collective-permute-start | bytes 663560 | tf_op jit(solution)/shard_map/ppermute | solution.py:50
  17.8 1.6 %collective-permute-start.10 = (bf16[96,2304]{1,0:T(8,128)(2,1)S(1)}, bf16[96,2304]{1,0:T(8,128)(2,1)S(1)}, u32[]{:S(2)}, u32[]{:S(2)}) collective-permute-start(bf16[96,2304]{1,0:T(8,128)(2,1)S(1)} %get-tuple-element.48.refs_3_), channel_id=1, source_target_pairs={{0,4},{4,0},{8,12},{12,8},{1,5},{5,1},{9,13},{13,9},{2,6},{6,2},{1... | collective-permute-start | bytes 1327112 | tf_op jit(solution)/shard_map/ppermute | solution.py:50
  19.4 4.2 %collective-permute-done.7.beside = bf16[23,8,768]{2,1,0:T(8,128)(2,1)S(1)} collective-permute-done((bf16[23,8,768]{2,1,0:T(8,128)(2,1)S(1)}, bf16[23,8,768]{2,1,0:T(8,128)(2,1)S(1)}, u32[]{:S(2)}, u32[]{:S(2)}) %collective-permute-start.7) | collective-permute-done | bytes 282656 | tf_op jit(solution)/shard_map/ppermute | solution.py:35
  23.6 8.7 %encode.1 = (bf16[512,768]{1,0:T(8,128)(2,1)S(1)}, bf16[512,768]{1,0:T(8,128)(2,1)S(1)}) custom-call(s32[3]{0:T(128)S(1)} %pad_add_fusion.place.refs_0_, f32[16,32,768]{2,1,0:T(8,128)S(1)} %get-tuple-element.49.tokens, bf16[7,32,768]{2,1,0:T(8,128)(2,1)S(1)} %collective-permute-done.2.above, bf16[23,8,768]{2,1,0:T(8,128)(2,1)S(1)} %collective-permute-done.7.beside, ...), custom_call_target="tpu_custom_call" | custom-call | flops 115000000 | tf_op jit(solution)/shard_map/encode/pallas_call | solution.py:189
  32.3 5.0 %collective-permute-done.5.refs_5_ = bf16[96,1152]{1,0:T(8,128)(2,1)S(1)} collective-permute-done((bf16[96,1152]{1,0:T(8,128)(2,1)S(1)}, bf16[96,1152]{1,0:T(8,128)(2,1)S(1)}, u32[]{:S(2)}, u32[]{:S(2)}) %collective-permute-start.5) | collective-permute-done | bytes 221216 | tf_op jit(solution)/shard_map/ppermute | solution.py:50
  37.4 1.2 %collective-permute-start.8 = (bf16[96,1152]{1,0:T(8,128)(2,1)S(1)}, bf16[96,1152]{1,0:T(8,128)(2,1)S(1)}, u32[]{:S(2)}, u32[]{:S(2)}) collective-permute-start(bf16[96,1152]{1,0:T(8,128)(2,1)S(1)} %collective-permute-done.5.refs_5_), channel_id=1, source_target_pairs={{0,16},{16,0},{1,17},{17,1},{2,18},{18,2},{3,19},{19,3},{4,20},{20... | collective-permute-start | bytes 663560 | tf_op jit(solution)/shard_map/ppermute | solution.py:50
  38.6 0.6 collective-permute-start.9
  39.2 0.8 collective-permute-start.15
  40.0 0.5 collective-permute-done.3
  40.5 0.9 collective-permute-start.11
  41.5 2.2 %collective-permute-done.8.refs_6_ = bf16[96,1152]{1,0:T(8,128)(2,1)S(1)} collective-permute-done((bf16[96,1152]{1,0:T(8,128)(2,1)S(1)}, bf16[96,1152]{1,0:T(8,128)(2,1)S(1)}, u32[]{:S(2)}, u32[]{:S(2)}) %collective-permute-start.8) | collective-permute-done | bytes 221216 | tf_op jit(solution)/shard_map/ppermute | solution.py:50
  43.8 1.6 %collective-permute-start.13 = (bf16[96,1152]{1,0:T(8,128)(2,1)S(1)}, bf16[96,1152]{1,0:T(8,128)(2,1)S(1)}, u32[]{:S(2)}, u32[]{:S(2)}) collective-permute-start(bf16[96,1152]{1,0:T(8,128)(2,1)S(1)} %collective-permute-done.8.refs_6_), channel_id=1, source_target_pairs={{0,4},{4,0},{8,12},{12,8},{1,5},{5,1},{9,13},{13,9},{2,6},{6,2},{1... | collective-permute-start | bytes 663560 | tf_op jit(solution)/shard_map/ppermute | solution.py:50
  45.4 2.4 %collective-permute-start.14 = (bf16[96,1152]{1,0:T(8,128)(2,1)S(1)}, bf16[96,1152]{1,0:T(8,128)(2,1)S(1)}, u32[]{:S(2)}, u32[]{:S(2)}) collective-permute-start(bf16[96,1152]{1,0:T(8,128)(2,1)S(1)} %collective-permute-done.9.refs_7_), channel_id=1, source_target_pairs={{0,4},{4,0},{8,12},{12,8},{1,5},{5,1},{9,13},{13,9},{2,6},{6,2},{1... | collective-permute-start | bytes 663560 | tf_op jit(solution)/shard_map/ppermute | solution.py:50
  47.8 1.5 %collective-permute-done.15.refs_13_ = bf16[96,1152]{1,0:T(8,128)(2,1)S(1)} collective-permute-done((bf16[96,1152]{1,0:T(8,128)(2,1)S(1)}, bf16[96,1152]{1,0:T(8,128)(2,1)S(1)}, u32[]{:S(2)}, u32[]{:S(2)}) %collective-permute-start.15) | collective-permute-done | bytes 221216 | tf_op jit(solution)/shard_map/ppermute | solution.py:541
  49.4 1.8 %collective-permute-start.16 = (bf16[96,1152]{1,0:T(8,128)(2,1)S(1)}, bf16[96,1152]{1,0:T(8,128)(2,1)S(1)}, u32[]{:S(2)}, u32[]{:S(2)}) collective-permute-start(bf16[96,1152]{1,0:T(8,128)(2,1)S(1)} %collective-permute-done.15.refs_13_), channel_id=1, source_target_pairs={{0,4},{4,0},{8,12},{12,8},{1,5},{5,1},{9,13},{13,9},{2,6},{6,2},{1... | collective-permute-start | bytes 663560 | tf_op jit(solution)/shard_map/ppermute | solution.py:50
  51.2 0.7 collective-permute-start.4
  52.2 9.0 %attend.1.refs_1_ = bf16[512,768]{1,0:T(8,128)(2,1)S(1)} custom-call(s32[3]{0:T(128)S(1)} %pad_add_fusion.place.refs_0_, bf16[512,768]{1,0:T(8,128)(2,1)S(1)} %get-tuple-element.53.refs_1_, f32[6,64,256]{2,1,0:T(8,128)S(1)} %get-tuple-element.54.refs_2_, bf16[96,2304]{1,0:T(8,128)(2,1)S(1)} %get-tuple-element.48.refs_3_, ...), custom_call_target="tpu_custom_call" | custom-call | flops 11500000256 | tf_op jit(solution)/shard_map/attend/pallas_call | solution.py:299
  61.7 1.2 %collective-permute-done.18.refs_6_ = bf16[192,768]{1,0:T(8,128)(2,1)S(1)} collective-permute-done((bf16[192,768]{1,0:T(8,128)(2,1)S(1)}, bf16[192,768]{1,0:T(8,128)(2,1)S(1)}, u32[]{:S(2)}, u32[]{:S(2)}) %collective-permute-start.18) | collective-permute-done | bytes 294944 | tf_op jit(solution)/shard_map/ppermute | solution.py:50
  62.9 3.1 %project.1 = (bf16[16,32,768]{2,1,0:T(8,128)(2,1)S(1)}, bf16[4,32,768]{2,1,0:T(8,128)(2,1)S(1)}, bf16[48,768]{1,0:T(8,128)(2,1)S(1)}, bf16[16,768]{1,0:T(8,128)(2,1)S(1)}) custom-call(s32[3]{0:T(128)S(1)} %pad_add_fusion.place.refs_0_, bf16[512,768]{1,0:T(8,128)(2,1)S(1)} %attend.1.refs_1_, bf16[512,768]{1,0:T(8,128)(2,1)S(1)} %get-tuple-element.58.refs_2_, ...), custom_call_target="tpu_custom_call" | custom-call | flops 3449999872 | tf_op jit(solution)/shard_map/project/pallas_call | solution.py:368
  67.0 4.2 %collective-permute-start.21 = (bf16[16,768]{1,0:T(8,128)(2,1)S(1)}, bf16[16,768]{1,0:T(8,128)(2,1)S(1)}, u32[]{:S(2)}, u32[]{:S(2)}) collective-permute-start(bf16[16,768]{1,0:T(8,128)(2,1)S(1)} %get-tuple-element.63), channel_id=1, source_target_pairs={{0,15},{1,12},{2,13},{3,14},{4,3},{5,0},{6,1},{7,2},{8,7},{9,4},{1... | collective-permute-start | bytes 73736 | tf_op jit(solution)/shard_map/ppermute | solution.py:45
  71.3 0.9 collective-permute-done.21.corner
  72.3 1.6 %dispatch.1 = (bf16[512,768]{1,0:T(8,128)(2,1)S(1)}, bf16[64,768]{1,0:T(8,128)(2,1)S(1)}, bf16[64,768]{1,0:T(8,128)(2,1)S(1)}, bf16[64,768]{1,0:T(8,128)(2,1)S(1...) custom-call(s32[3]{0:T(128)S(1)} %pad_add_fusion.place.refs_0_, ...), custom_call_target="tpu_custom_call" | custom-call | tf_op jit(solution)/shard_map/dispatch/pallas_call | solution.py:431
  74.3 0.8 collective-permute-start.26
  75.0 1.0 collective-permute-start.27
  76.1 0.8 collective-permute-start.23
  76.9 1.3 %collective-permute-start.24 = (bf16[64,768]{1,0:T(8,128)(2,1)S(1)}, bf16[64,768]{1,0:T(8,128)(2,1)S(1)}, u32[]{:S(2)}, u32[]{:S(2)}) collective-permute-start(bf16[64,768]{1,0:T(8,128)(2,1)S(1)} %get-tuple-element.68), channel_id=1, source_target_pairs={{0,12},{4,8},{8,4},{12,0},{1,13},{5,9},{9,5},{13,1},{2,14},{6,10},... | collective-permute-start | bytes 294920 | tf_op jit(solution)/shard_map/ppermute | solution.py:50
  78.5 3.0 %collective-permute-done.27.refs_3_ = bf16[64,768]{1,0:T(8,128)(2,1)S(1)} collective-permute-done((bf16[64,768]{1,0:T(8,128)(2,1)S(1)}, bf16[64,768]{1,0:T(8,128)(2,1)S(1)}, u32[]{:S(2)}, u32[]{:S(2)}) %collective-permute-start.27) | collective-permute-done | bytes 98336 | tf_op jit(solution)/shard_map/ppermute | solution.py:50
  81.5 7.6 %experts.3 = (bf16[64,768]{1,0:T(8,128)(2,1)S(1)}, bf16[64,768]{1,0:T(8,128)(2,1)S(1)}, bf16[64,768]{1,0:T(8,128)(2,1)S(1)}, bf16[64,768]{1,0:T(8,128)(2,1)S(1)}) custom-call(bf16[64,768]{1,0:T(8,128)(2,1)S(1)} %get-tuple-element.70.refs_0_, bf16[64,768]{1,0:T(8,128)(2,1)S(1)} %collective-permute-done.25.refs_1_, ...), custom_call_target="tpu_custom_call" | custom-call | flops 8049999872 | tf_op jit(solution)/shard_map/experts/pallas_call | solution.py:473
  89.1 0.7 collective-permute-start.31
  89.8 1.4 %collective-permute-start.33 = (bf16[64,768]{1,0:T(8,128)(2,1)S(1)}, bf16[64,768]{1,0:T(8,128)(2,1)S(1)}, u32[]{:S(2)}, u32[]{:S(2)}) collective-permute-start(bf16[64,768]{1,0:T(8,128)(2,1)S(1)} %get-tuple-element.80), channel_id=1, source_target_pairs={{0,12},{4,8},{8,4},{12,0},{1,13},{5,9},{9,5},{13,1},{2,14},{6,10},... | collective-permute-start | bytes 294920 | tf_op jit(solution)/shard_map/ppermute | solution.py:50
  91.3 7.6 %experts.2 = (bf16[64,768]{1,0:T(8,128)(2,1)S(1)}, bf16[64,768]{1,0:T(8,128)(2,1)S(1)}, bf16[64,768]{1,0:T(8,128)(2,1)S(1)}, bf16[64,768]{1,0:T(8,128)(2,1)S(1)}) custom-call(bf16[64,768]{1,0:T(8,128)(2,1)S(1)} %get-tuple-element.65.refs_0_, bf16[64,768]{1,0:T(8,128)(2,1)S(1)} %collective-permute-done.22.refs_1_, ...), custom_call_target="tpu_custom_call" | custom-call | flops 8049999872 | tf_op jit(solution)/shard_map/experts/pallas_call | solution.py:473
  99.0 0.7 collective-permute-start.30
  99.7 1.4 %collective-permute-start.32 = (bf16[64,768]{1,0:T(8,128)(2,1)S(1)}, bf16[64,768]{1,0:T(8,128)(2,1)S(1)}, u32[]{:S(2)}, u32[]{:S(2)}) collective-permute-start(bf16[64,768]{1,0:T(8,128)(2,1)S(1)} %get-tuple-element.79), channel_id=1, source_target_pairs={{0,12},{4,8},{8,4},{12,0},{1,13},{5,9},{9,5},{13,1},{2,14},{6,10},... | collective-permute-start | bytes 294920 | tf_op jit(solution)/shard_map/ppermute | solution.py:50
  101.6 1.3 %collective-permute-done.30.refs_4_ = bf16[64,768]{1,0:T(8,128)(2,1)S(1)} collective-permute-done((bf16[64,768]{1,0:T(8,128)(2,1)S(1)}, bf16[64,768]{1,0:T(8,128)(2,1)S(1)}, u32[]{:S(2)}, u32[]{:S(2)}) %collective-permute-start.30) | collective-permute-done | bytes 98336 | tf_op jit(solution)/shard_map/ppermute | solution.py:50
  103.0 2.7 %collective-permute-done.32.refs_6_ = bf16[64,768]{1,0:T(8,128)(2,1)S(1)} collective-permute-done((bf16[64,768]{1,0:T(8,128)(2,1)S(1)}, bf16[64,768]{1,0:T(8,128)(2,1)S(1)}, u32[]{:S(2)}, u32[]{:S(2)}) %collective-permute-start.32) | collective-permute-done | bytes 98336 | tf_op jit(solution)/shard_map/ppermute | solution.py:50
  105.7 2.3 %combine.1 = bf16[512,768]{1,0:T(8,128)(2,1)} custom-call(s32[3]{0:T(128)S(1)} %pad_add_fusion.place.refs_0_, bf16[512,768]{1,0:T(8,128)(2,1)S(1)} %get-tuple-element.64.attended, s32[512,1]{1,0:T(8,128)S(1)} %select_n.42.position, s32[512,1]{1,0:T(8,128)S(1)} %select_n.43.constant_at, f32[16,768]{1,0:T(8,128)S(1)} %copy-done.1, ...), custom_call_target="tpu_custom_call" | custom-call | tf_op jit(solution)/shard_map/combine/pallas_call | solution.py:511
  (55 shorter events, 3.8 us)
Async XLA Ops:
  1.7 10.5 %collective-permute-start.2 = (bf16[7,32,768]{2,1,0:T(8,128)(2,1)}, bf16[7,32,768]{2,1,0:T(8,128)(2,1)S(1)}, u32[]{:S(2)}, u32[]{:S(2)}) collective-permute-start(bf16[7,32,768]{2,1,0:T(8,128)(2,1)} %slice.3), channel_id=1, source_target_pairs={{0,4},{4,8},{8,12},{12,0},{1,5},{5,9},{9,13},{13,1},{2,6},{6,10},{... | collective-permute-start | bytes 1032200 | tf_op jit(solution)/shard_map/ppermute | solution.py:35
  4.3 7.9 %collective-permute-start = (bf16[48,2304]{1,0:T(8,128)(2,1)}, bf16[48,2304]{1,0:T(8,128)(2,1)S(1)}, u32[]{:S(2)}, u32[]{:S(2)}) collective-permute-start(bf16[48,2304]{1,0:T(8,128)(2,1)} %refs_0_.1), channel_id=1, source_target_pairs={{0,1},{1,0},{2,3},{3,2},{4,5},{5,4},{6,7},{7,6},{8,9},{9,8},{10,11... | collective-permute-start | bytes 663560 | tf_op jit(solution)/shard_map/ppermute | solution.py:50
  5.6 6.6 %collective-permute-start.1 = (bf16[48,768]{1,0:T(8,128)(2,1)}, bf16[48,768]{1,0:T(8,128)(2,1)S(1)}, u32[]{:S(2)}, u32[]{:S(2)}) collective-permute-start(bf16[48,768]{1,0:T(8,128)(2,1)} %refs_1_.1), channel_id=1, source_target_pairs={{0,1},{1,0},{2,3},{3,2},{4,5},{5,4},{6,7},{7,6},{8,9},{9,8},{10,11... | collective-permute-start | bytes 221192 | tf_op jit(solution)/shard_map/ppermute | solution.py:50
  5.8 1.1 %copy-start = (bf16[16,32,768]{2,1,0:T(8,128)(2,1)S(1)}, bf16[16,32,768]{2,1,0:T(8,128)(2,1)}, u32[]{:S(2)}) copy-start(bf16[16,32,768]{2,1,0:T(8,128)(2,1)} %tokens.1) | copy-start | bytes 2359300
  6.9 1.1 %copy-start.2 = (f32[24,64,64]{2,1,0:T(8,128)S(1)}, f32[24,64,64]{2,1,0:T(8,128)}, u32[]{:S(2)}) copy-start(f32[24,64,64]{2,1,0:T(8,128)} %rel_bias.1) | copy-start | bytes 1179652
  8.1 0.9 copy-start.3
  9.0 0.9 copy-start.4
  9.9 0.9 copy-start.5
  12.8 24.5 %collective-permute-start.6 = (bf16[96,2304]{1,0:T(8,128)(2,1)S(1)}, bf16[96,2304]{1,0:T(8,128)(2,1)S(1)}, u32[]{:S(2)}, u32[]{:S(2)}) collective-permute-start(bf16[96,2304]{1,0:T(8,128)(2,1)S(1)} %get-tuple-element.48.refs_3_), channel_id=1, source_target_pairs={{0,8},{4,12},{8,0},{12,4},{1,9},{5,13},{9,1},{13,5},{2,10},{6,14},... | collective-permute-start | bytes 1327112 | tf_op jit(solution)/shard_map/ppermute | solution.py:50
  13.9 9.7 %collective-permute-start.7 = (bf16[23,8,768]{2,1,0:T(8,128)(2,1)S(1)}, bf16[23,8,768]{2,1,0:T(8,128)(2,1)S(1)}, u32[]{:S(2)}, u32[]{:S(2)}) collective-permute-start(bf16[23,8,768]{2,1,0:T(8,128)(2,1)S(1)} %get-tuple-element.50), channel_id=1, source_target_pairs={{0,1},{1,2},{2,3},{3,0},{4,5},{5,6},{6,7},{7,4},{8,9},{9,10},{10,1... | collective-permute-start | bytes 847880 | tf_op jit(solution)/shard_map/ppermute | solution.py:35
  15.5 21.9 %collective-permute-start.5 = (bf16[96,1152]{1,0:T(8,128)(2,1)S(1)}, bf16[96,1152]{1,0:T(8,128)(2,1)S(1)}, u32[]{:S(2)}, u32[]{:S(2)}) collective-permute-start(bf16[96,1152]{1,0:T(8,128)(2,1)S(1)} %get-tuple-element.47), channel_id=1, source_target_pairs={{0,2},{1,3},{2,0},{3,1},{4,6},{5,7},{6,4},{7,5},{8,10},{9,11},{10,... | collective-permute-start | bytes 663560 | tf_op jit(solution)/shard_map/ppermute | solution.py:50
  17.8 23.6 %collective-permute-start.10 = (bf16[96,2304]{1,0:T(8,128)(2,1)S(1)}, bf16[96,2304]{1,0:T(8,128)(2,1)S(1)}, u32[]{:S(2)}, u32[]{:S(2)}) collective-permute-start(bf16[96,2304]{1,0:T(8,128)(2,1)S(1)} %get-tuple-element.48.refs_3_), channel_id=1, source_target_pairs={{0,4},{4,0},{8,12},{12,8},{1,5},{5,1},{9,13},{13,9},{2,6},{6,2},{1... | collective-permute-start | bytes 1327112 | tf_op jit(solution)/shard_map/ppermute | solution.py:50
  19.4 21.2 %collective-permute-start.3 = (bf16[96,768]{1,0:T(8,128)(2,1)S(1)}, bf16[96,768]{1,0:T(8,128)(2,1)S(1)}, u32[]{:S(2)}, u32[]{:S(2)}) collective-permute-start(bf16[96,768]{1,0:T(8,128)(2,1)S(1)} %get-tuple-element.46), channel_id=1, source_target_pairs={{0,2},{1,3},{2,0},{3,1},{4,6},{5,7},{6,4},{7,5},{8,10},{9,11},{10,... | collective-permute-start | bytes 442376 | tf_op jit(solution)/shard_map/ppermute | solution.py:50
  37.4 6.4 %collective-permute-start.8 = (bf16[96,1152]{1,0:T(8,128)(2,1)S(1)}, bf16[96,1152]{1,0:T(8,128)(2,1)S(1)}, u32[]{:S(2)}, u32[]{:S(2)}) collective-permute-start(bf16[96,1152]{1,0:T(8,128)(2,1)S(1)} %collective-permute-done.5.refs_5_), channel_id=1, source_target_pairs={{0,16},{16,0},{1,17},{17,1},{2,18},{18,2},{3,19},{19,3},{4,20},{20... | collective-permute-start | bytes 663560 | tf_op jit(solution)/shard_map/ppermute | solution.py:50
  38.6 6.8 %collective-permute-start.9 = (bf16[96,1152]{1,0:T(8,128)(2,1)S(1)}, bf16[96,1152]{1,0:T(8,128)(2,1)S(1)}, u32[]{:S(2)}, u32[]{:S(2)}) collective-permute-start(bf16[96,1152]{1,0:T(8,128)(2,1)S(1)} %collective-permute-done.5.refs_5_), channel_id=1, source_target_pairs={{0,8},{4,12},{8,0},{12,4},{1,9},{5,13},{9,1},{13,5},{2,10},{6,14},... | collective-permute-start | bytes 663560 | tf_op jit(solution)/shard_map/ppermute | solution.py:50
  39.2 10.1 %collective-permute-start.15 = (bf16[96,1152]{1,0:T(8,128)(2,1)S(1)}, bf16[96,1152]{1,0:T(8,128)(2,1)S(1)}, u32[]{:S(2)}, u32[]{:S(2)}) collective-permute-start(bf16[96,1152]{1,0:T(8,128)(2,1)S(1)} %collective-permute-done.5.refs_5_), channel_id=1, source_target_pairs={{0,24},{4,28},{8,16},{12,20},{16,8},{20,12},{24,0},{28,4},{1,25},{... | collective-permute-start | bytes 663560 | tf_op jit(solution)/shard_map/ppermute | solution.py:541
  40.5 11.7 %collective-permute-start.11 = (bf16[96,2304]{1,0:T(8,128)(2,1)S(1)}, bf16[96,2304]{1,0:T(8,128)(2,1)S(1)}, u32[]{:S(2)}, u32[]{:S(2)}) collective-permute-start(bf16[96,2304]{1,0:T(8,128)(2,1)S(1)} %collective-permute-done.6.refs_4_), channel_id=1, source_target_pairs={{0,4},{4,0},{8,12},{12,8},{1,5},{5,1},{9,13},{13,9},{2,6},{6,2},{1... | collective-permute-start | bytes 1327112 | tf_op jit(solution)/shard_map/ppermute | solution.py:50
  41.5 9.7 %collective-permute-start.12 = (bf16[96,1152]{1,0:T(8,128)(2,1)S(1)}, bf16[96,1152]{1,0:T(8,128)(2,1)S(1)}, u32[]{:S(2)}, u32[]{:S(2)}) collective-permute-start(bf16[96,1152]{1,0:T(8,128)(2,1)S(1)} %collective-permute-done.5.refs_5_), channel_id=1, source_target_pairs={{0,4},{4,0},{8,12},{12,8},{1,5},{5,1},{9,13},{13,9},{2,6},{6,2},{1... | collective-permute-start | bytes 663560 | tf_op jit(solution)/shard_map/ppermute | solution.py:50
  43.8 8.1 %collective-permute-start.13 = (bf16[96,1152]{1,0:T(8,128)(2,1)S(1)}, bf16[96,1152]{1,0:T(8,128)(2,1)S(1)}, u32[]{:S(2)}, u32[]{:S(2)}) collective-permute-start(bf16[96,1152]{1,0:T(8,128)(2,1)S(1)} %collective-permute-done.8.refs_6_), channel_id=1, source_target_pairs={{0,4},{4,0},{8,12},{12,8},{1,5},{5,1},{9,13},{13,9},{2,6},{6,2},{1... | collective-permute-start | bytes 663560 | tf_op jit(solution)/shard_map/ppermute | solution.py:50
  45.4 6.8 %collective-permute-start.14 = (bf16[96,1152]{1,0:T(8,128)(2,1)S(1)}, bf16[96,1152]{1,0:T(8,128)(2,1)S(1)}, u32[]{:S(2)}, u32[]{:S(2)}) collective-permute-start(bf16[96,1152]{1,0:T(8,128)(2,1)S(1)} %collective-permute-done.9.refs_7_), channel_id=1, source_target_pairs={{0,4},{4,0},{8,12},{12,8},{1,5},{5,1},{9,13},{13,9},{2,6},{6,2},{1... | collective-permute-start | bytes 663560 | tf_op jit(solution)/shard_map/ppermute | solution.py:50
  49.4 2.9 %collective-permute-start.16 = (bf16[96,1152]{1,0:T(8,128)(2,1)S(1)}, bf16[96,1152]{1,0:T(8,128)(2,1)S(1)}, u32[]{:S(2)}, u32[]{:S(2)}) collective-permute-start(bf16[96,1152]{1,0:T(8,128)(2,1)S(1)} %collective-permute-done.15.refs_13_), channel_id=1, source_target_pairs={{0,4},{4,0},{8,12},{12,8},{1,5},{5,1},{9,13},{13,9},{2,6},{6,2},{1... | collective-permute-start | bytes 663560 | tf_op jit(solution)/shard_map/ppermute | solution.py:50
  51.2 10.1 %collective-permute-start.4 = (bf16[192,768]{1,0:T(8,128)(2,1)S(1)}, bf16[192,768]{1,0:T(8,128)(2,1)S(1)}, u32[]{:S(2)}, u32[]{:S(2)}) collective-permute-start(bf16[192,768]{1,0:T(8,128)(2,1)S(1)} %constant_dynamic-update-slice_fusion.refs_3_), channel_id=1, source_target_pairs={{0,8},{4,12},{8,0},{12,4},{1,9},{5,13},{9,1},{13,5},{2,10},{6,14},... | collective-permute-start | bytes 884744 | tf_op jit(solution)/shard_map/ppermute | solution.py:50
  51.9 9.8 %collective-permute-start.17 = (bf16[192,768]{1,0:T(8,128)(2,1)S(1)}, bf16[192,768]{1,0:T(8,128)(2,1)S(1)}, u32[]{:S(2)}, u32[]{:S(2)}) collective-permute-start(bf16[192,768]{1,0:T(8,128)(2,1)S(1)} %constant_dynamic-update-slice_fusion.refs_3_), channel_id=1, source_target_pairs={{0,4},{4,0},{8,12},{12,8},{1,5},{5,1},{9,13},{13,9},{2,6},{6,2},{1... | collective-permute-start | bytes 884744 | tf_op jit(solution)/shard_map/ppermute | solution.py:50
  52.2 19.0 %copy-start.6 = (s32[16,32]{1,0:T(8,128)S(1)}, s32[16,32]{1,0:T(8,128)}, u32[]{:S(2)}) copy-start(s32[16,32]{1,0:T(8,128)} %param.21) | copy-start | bytes 6148
  52.2 19.0 %copy-start.7 = (s32[16,32]{1,0:T(8,128)S(1)}, s32[16,32]{1,0:T(8,128)}, u32[]{:S(2)}) copy-start(s32[16,32]{1,0:T(8,128)} %param.19) | copy-start | bytes 6148
  52.2 19.0 %copy-start.8 = (s32[16,32]{1,0:T(8,128)S(1)}, s32[16,32]{1,0:T(8,128)}, u32[]{:S(2)}) copy-start(s32[16,32]{1,0:T(8,128)} %param.20) | copy-start | bytes 6148
  61.3 1.6 %collective-permute-start.18 = (bf16[192,768]{1,0:T(8,128)(2,1)S(1)}, bf16[192,768]{1,0:T(8,128)(2,1)S(1)}, u32[]{:S(2)}, u32[]{:S(2)}) collective-permute-start(bf16[192,768]{1,0:T(8,128)(2,1)S(1)} %collective-permute-done.4.refs_4_), channel_id=1, source_target_pairs={{0,4},{4,0},{8,12},{12,8},{1,5},{5,1},{9,13},{13,9},{2,6},{6,2},{1... | collective-permute-start | bytes 884744 | tf_op jit(solution)/shard_map/ppermute | solution.py:50
  66.1 6.2 %collective-permute-start.19 = (bf16[4,32,768]{2,1,0:T(8,128)(2,1)S(1)}, bf16[4,32,768]{2,1,0:T(8,128)(2,1)S(1)}, u32[]{:S(2)}, u32[]{:S(2)}) collective-permute-start(bf16[4,32,768]{2,1,0:T(8,128)(2,1)S(1)} %get-tuple-element.61), channel_id=1, source_target_pairs={{0,12},{4,0},{8,4},{12,8},{1,13},{5,1},{9,5},{13,9},{2,14},{6,2},{... | collective-permute-start | bytes 589832 | tf_op jit(solution)/shard_map/ppermute | solution.py:35
  66.5 5.7 %collective-permute-start.20 = (bf16[48,768]{1,0:T(8,128)(2,1)S(1)}, bf16[48,768]{1,0:T(8,128)(2,1)S(1)}, u32[]{:S(2)}, u32[]{:S(2)}) collective-permute-start(bf16[48,768]{1,0:T(8,128)(2,1)S(1)} %get-tuple-element.62), channel_id=1, source_target_pairs={{0,3},{1,0},{2,1},{3,2},{4,7},{5,4},{6,5},{7,6},{8,11},{9,8},{10,9... | collective-permute-start | bytes 221192 | tf_op jit(solution)/shard_map/ppermute | solution.py:35
  67.0 5.3 %collective-permute-start.21 = (bf16[16,768]{1,0:T(8,128)(2,1)S(1)}, bf16[16,768]{1,0:T(8,128)(2,1)S(1)}, u32[]{:S(2)}, u32[]{:S(2)}) collective-permute-start(bf16[16,768]{1,0:T(8,128)(2,1)S(1)} %get-tuple-element.63), channel_id=1, source_target_pairs={{0,15},{1,12},{2,13},{3,14},{4,3},{5,0},{6,1},{7,2},{8,7},{9,4},{1... | collective-permute-start | bytes 73736 | tf_op jit(solution)/shard_map/ppermute | solution.py:45
  73.9 3.0 %collective-permute-start.25 = (bf16[64,768]{1,0:T(8,128)(2,1)S(1)}, bf16[64,768]{1,0:T(8,128)(2,1)S(1)}, u32[]{:S(2)}, u32[]{:S(2)}) collective-permute-start(bf16[64,768]{1,0:T(8,128)(2,1)S(1)} %get-tuple-element.71), channel_id=1, source_target_pairs={{0,4},{4,0},{8,12},{12,8},{1,5},{5,1},{9,13},{13,9},{2,6},{6,2},{1... | collective-permute-start | bytes 294920 | tf_op jit(solution)/shard_map/ppermute | solution.py:50
  74.3 4.2 %collective-permute-start.26 = (bf16[64,768]{1,0:T(8,128)(2,1)S(1)}, bf16[64,768]{1,0:T(8,128)(2,1)S(1)}, u32[]{:S(2)}, u32[]{:S(2)}) collective-permute-start(bf16[64,768]{1,0:T(8,128)(2,1)S(1)} %get-tuple-element.72), channel_id=1, source_target_pairs={{0,8},{4,12},{8,0},{12,4},{1,9},{5,13},{9,1},{13,5},{2,10},{6,14},... | collective-permute-start | bytes 294920 | tf_op jit(solution)/shard_map/ppermute | solution.py:50
  75.0 6.5 %collective-permute-start.27 = (bf16[64,768]{1,0:T(8,128)(2,1)S(1)}, bf16[64,768]{1,0:T(8,128)(2,1)S(1)}, u32[]{:S(2)}, u32[]{:S(2)}) collective-permute-start(bf16[64,768]{1,0:T(8,128)(2,1)S(1)} %get-tuple-element.73), channel_id=1, source_target_pairs={{0,12},{4,8},{8,4},{12,0},{1,13},{5,9},{9,5},{13,1},{2,14},{6,10},... | collective-permute-start | bytes 294920 | tf_op jit(solution)/shard_map/ppermute | solution.py:50
  76.1 13.8 %collective-permute-start.22 = (bf16[64,768]{1,0:T(8,128)(2,1)S(1)}, bf16[64,768]{1,0:T(8,128)(2,1)S(1)}, u32[]{:S(2)}, u32[]{:S(2)}) collective-permute-start(bf16[64,768]{1,0:T(8,128)(2,1)S(1)} %get-tuple-element.66), channel_id=1, source_target_pairs={{0,4},{4,0},{8,12},{12,8},{1,5},{5,1},{9,13},{13,9},{2,6},{6,2},{1... | collective-permute-start | bytes 294920 | tf_op jit(solution)/shard_map/ppermute | solution.py:50
  76.1 15.2 %collective-permute-start.23 = (bf16[64,768]{1,0:T(8,128)(2,1)S(1)}, bf16[64,768]{1,0:T(8,128)(2,1)S(1)}, u32[]{:S(2)}, u32[]{:S(2)}) collective-permute-start(bf16[64,768]{1,0:T(8,128)(2,1)S(1)} %get-tuple-element.67), channel_id=1, source_target_pairs={{0,8},{4,12},{8,0},{12,4},{1,9},{5,13},{9,1},{13,5},{2,10},{6,14},... | collective-permute-start | bytes 294920 | tf_op jit(solution)/shard_map/ppermute | solution.py:50
  76.9 14.4 %collective-permute-start.24 = (bf16[64,768]{1,0:T(8,128)(2,1)S(1)}, bf16[64,768]{1,0:T(8,128)(2,1)S(1)}, u32[]{:S(2)}, u32[]{:S(2)}) collective-permute-start(bf16[64,768]{1,0:T(8,128)(2,1)S(1)} %get-tuple-element.68), channel_id=1, source_target_pairs={{0,12},{4,8},{8,4},{12,0},{1,13},{5,9},{9,5},{13,1},{2,14},{6,10},... | collective-permute-start | bytes 294920 | tf_op jit(solution)/shard_map/ppermute | solution.py:50
  89.1 10.6 %collective-permute-start.29 = (bf16[64,768]{1,0:T(8,128)(2,1)S(1)}, bf16[64,768]{1,0:T(8,128)(2,1)S(1)}, u32[]{:S(2)}, u32[]{:S(2)}) collective-permute-start(bf16[64,768]{1,0:T(8,128)(2,1)S(1)} %get-tuple-element.76), channel_id=1, source_target_pairs={{0,4},{4,0},{8,12},{12,8},{1,5},{5,1},{9,13},{13,9},{2,6},{6,2},{1... | collective-permute-start | bytes 294920 | tf_op jit(solution)/shard_map/ppermute | solution.py:50
  89.1 12.5 %collective-permute-start.31 = (bf16[64,768]{1,0:T(8,128)(2,1)S(1)}, bf16[64,768]{1,0:T(8,128)(2,1)S(1)}, u32[]{:S(2)}, u32[]{:S(2)}) collective-permute-start(bf16[64,768]{1,0:T(8,128)(2,1)S(1)} %get-tuple-element.78), channel_id=1, source_target_pairs={{0,8},{4,12},{8,0},{12,4},{1,9},{5,13},{9,1},{13,5},{2,10},{6,14},... | collective-permute-start | bytes 294920 | tf_op jit(solution)/shard_map/ppermute | solution.py:50
  89.8 11.8 %collective-permute-start.33 = (bf16[64,768]{1,0:T(8,128)(2,1)S(1)}, bf16[64,768]{1,0:T(8,128)(2,1)S(1)}, u32[]{:S(2)}, u32[]{:S(2)}) collective-permute-start(bf16[64,768]{1,0:T(8,128)(2,1)S(1)} %get-tuple-element.80), channel_id=1, source_target_pairs={{0,12},{4,8},{8,4},{12,0},{1,13},{5,9},{9,5},{13,1},{2,14},{6,10},... | collective-permute-start | bytes 294920 | tf_op jit(solution)/shard_map/ppermute | solution.py:50
  91.3 14.4 %copy-start.1 = (f32[16,768]{1,0:T(8,128)S(1)}, f32[16,768]{1,0:T(8,128)}, u32[]{:S(2)}) copy-start(f32[16,768]{1,0:T(8,128)} %table.1) | copy-start | bytes 147460
  98.9 2.8 %collective-permute-start.28 = (bf16[64,768]{1,0:T(8,128)(2,1)S(1)}, bf16[64,768]{1,0:T(8,128)(2,1)S(1)}, u32[]{:S(2)}, u32[]{:S(2)}) collective-permute-start(bf16[64,768]{1,0:T(8,128)(2,1)S(1)} %get-tuple-element.75), channel_id=1, source_target_pairs={{0,4},{4,0},{8,12},{12,8},{1,5},{5,1},{9,13},{13,9},{2,6},{6,2},{1... | collective-permute-start | bytes 294920 | tf_op jit(solution)/shard_map/ppermute | solution.py:50
  99.0 4.0 %collective-permute-start.30 = (bf16[64,768]{1,0:T(8,128)(2,1)S(1)}, bf16[64,768]{1,0:T(8,128)(2,1)S(1)}, u32[]{:S(2)}, u32[]{:S(2)}) collective-permute-start(bf16[64,768]{1,0:T(8,128)(2,1)S(1)} %get-tuple-element.77), channel_id=1, source_target_pairs={{0,8},{4,12},{8,0},{12,4},{1,9},{5,13},{9,1},{13,5},{2,10},{6,14},... | collective-permute-start | bytes 294920 | tf_op jit(solution)/shard_map/ppermute | solution.py:50
  99.7 6.0 %collective-permute-start.32 = (bf16[64,768]{1,0:T(8,128)(2,1)S(1)}, bf16[64,768]{1,0:T(8,128)(2,1)S(1)}, u32[]{:S(2)}, u32[]{:S(2)}) collective-permute-start(bf16[64,768]{1,0:T(8,128)(2,1)S(1)} %get-tuple-element.79), channel_id=1, source_target_pairs={{0,12},{4,8},{8,4},{12,0},{1,13},{5,9},{9,5},{13,1},{2,14},{6,10},... | collective-permute-start | bytes 294920 | tf_op jit(solution)/shard_map/ppermute | solution.py:50

commit v7 on v6

--- a/solution.py
+++ b/solution.py
@@ -89,36 +89,34 @@
     )(tokens, taps, rel_bias, *others)
 
 
-def join_kernel(place, own_in, beyond_in, own_out, beyond_out, above, edge, two, mine, two_out, column):
-    size, half = own_in.shape[0], mine.shape[1]
+def join_kernel(place, own, beyond, above, edge, two, mine, column):
+    size, half = own.shape[0], mine.shape[1]
     lanes = pl.ds(pl.multiple_of(place[2] * half, LANES), half)
-    for at, (part_in, part_out) in enumerate(((own_in, own_out), (beyond_in, beyond_out))):
+    for at, part in enumerate((own, beyond)):
         rows = slice(at * size, (at + 1) * size)
-        two[rows, :] = part_in[...]
-        mine[rows, :] = part_in[:, lanes]
-        two_out[rows, :] = part_out[...]
+        two[rows, :] = part[...]
+        mine[rows, :] = part[:, lanes]
     reach = above.shape[0]
     column[:reach] = above[:, above.shape[1] - HALO :]
     column[reach:] = edge[...]
 
 
-def join(place, own_in, beyond_in, own_out, beyond_out, above, edge):
+def join(place, own, beyond, above, edge):
     bf16 = functools.partial(jax.ShapeDtypeStruct, dtype=jnp.bfloat16)
-    size, wide = own_in.shape
+    size, wide = own.shape
     return pl.pallas_call(
         join_kernel,
         out_shape=(
             bf16((2 * size, wide)),
             bf16((2 * size, wide // 2)),
-            bf16((2 * size, own_out.shape[1])),
             bf16((above.shape[0] + edge.shape[0], *edge.shape[1:])),
         ),
-        in_specs=[SMEM] + [VMEM] * 6,
-        out_specs=(VMEM,) * 4,
+        in_specs=[SMEM] + [VMEM] * 4,
+        out_specs=(VMEM,) * 3,
         compiler_params=pltpu.CompilerParams(vmem_limit_bytes=8 * 1024 * 1024),
         cost_estimate=lasting(1),
         name="join",
-    )(place, own_in, beyond_in, own_out, beyond_out, above, edge)
+    )(place, own, beyond, above, edge)
 
 
 def encode_kernel(place, tokens, above, beside, weights, encoded, normed, upper, left):
@@ -568,18 +566,19 @@
     if quick:
         pair = [(0, 0), (0, 1)]
         beyond, beyond_out = exchanged(project_in, "gx", 1), exchanged(project_out, "gx", 1)
-        kept, weights, bias, edge, own_in, own_out = prepare(
-            tokens, conv_kernel, rel_bias, project_in, project_out
-        )
-        two, mine, two_out, column = join(place, own_in, beyond, own_out, beyond_out, above, edge)
-        two, two_out = (two, pair, None), (two_out, pair, None)
+        kept, weights, bias, edge, own = prepare(tokens, conv_kernel, rel_bias, project_in)
+        two, mine, column = join(place, own, beyond, above, edge)
+        two = (two, pair, None)
         far = along((mine, pair, 0), "gx", 2)
         facing = along(two, "gy", 2)
-        far_out = along(two_out, "gx", 2)
     else:
         kept, weights, bias, edge = prepare(tokens, conv_kernel, rel_bias)
         column = jnp.concatenate([above[:, cols - HALO :], edge], axis=0)
     beside = shifted(column, "gx", 1)
+    if quick:
+        own_out, beyond_out, beside = held(project_out, beyond_out, beside)
+        two_out = (jnp.concatenate([own_out, beyond_out], axis=0), pair, None)
+        far_out = along(two_out, "gx", 2)
     encoded, normed = encode(place, kept, above, beside, weights)
     if quick:
         first, second, normed = held(far[0], facing[0], normed)

time: 108 us -> 106 us (0.981)
  local copies, waits for them, and re-layouts: 7.33 us -> 5.76 us
  waiting for transfers between devices: 24.1 us -> 22.8 us
    ppermute x4, waiting for transfers between devices: 4.19 us -> 0.01 us  [shifted(): return lax.ppermute(x, axis, [(i, (i + by) % size) for i in range(size)])]
    ppermute x28, waiting for transfers between devices: 17.4 us -> 19.8 us  [exchanged(): return lax.ppermute(x, axis, [(i, i ^ mask) for i in range(size)])]
    ppermute x4, starting transfers between devices: 5.06 us -> 6.29 us  [shifted(): return lax.ppermute(x, axis, [(i, (i + by) % size) for i in range(size)])]
    ppermute x1, starting transfers between devices: 4.24 us -> 3.07 us  [shifted_both(): return lax.ppermute(x, ('gy', 'gx'), pairs)]
    unnamed x19 -> x20, local copies, waits for them, and re-layouts: 5 us -> 4.13 us
  transfers between devices with their start and end apart: 34 -> 34, of which waited for: 13 -> 11; matrix products, arithmetic and copies ran while one was open for 1% -> 2% of each run, Pallas kernels for 31% -> 31%
where the time goes in v7:
time: 106 us; the launch traced here: 105 us
  Pallas kernels  40.7 us (38%)
  starting transfers between devices  34.8 us (33%)
  waiting for transfers between devices  22.8 us (22%)
  local copies, waits for them, and re-layouts  5.76 us (5%)
    ppermute x28, starting transfers between devices, exchanged(): return lax.ppermute(x, axis, [(i, i ^ mask) for i in range(size)])  24.8 us
    ppermute x28, waiting for transfers between devices, exchanged(): return lax.ppermute(x, axis, [(i, i ^ mask) for i in range(size)])  19.8 us
    pallas_call x2, Pallas kernels, serve(): pl.pallas_call(functools.partial(expert_kernel, count, first), out_shape=...  15.1 us
    pallas_call x1, Pallas kernels, attend(): pl.pallas_call(functools.partial(attend_kernel, shape, ids, grid_cols), o...  9 us
    pallas_call x1, Pallas kernels, encode(): pl.pallas_call(encode_kernel, out_shape=(flat, flat), in_specs=[SMEM] + [...  8.74 us
    ppermute x4, starting transfers between devices, shifted(): return lax.ppermute(x, axis, [(i, (i + by) % size) for i in range(size)])  6.29 us
    unnamed x20, local copies, waits for them, and re-layouts  4.13 us
    pallas_call x1, Pallas kernels, project(): pl.pallas_call(functools.partial(project_kernel, shape, ids, grid_cols),...  3.12 us
  transfers between devices with their start and end apart: 34, of which 11 were waited for; matrix products, arithmetic and copies ran while one was open for 2% of the time, Pallas kernels for 31%

profile of v7, /device:TPU:1, one launch (start us, length us, event | category | flops | bytes accessed | tf_op | source)
XLA Modules:
  0.0 105.3 jit_solution(1145077286422701271)
XLA Ops:
  0.0 1.0 slice.3
  1.0 2.7 %collective-permute-start.2 = (bf16[7,32,768]{2,1,0:T(8,128)(2,1)S(1)}, bf16[7,32,768]{2,1,0:T(8,128)(2,1)S(1)}, u32[]{:S(2)}, u32[]{:S(2)}) collective-permute-start(bf16[7,32,768]{2,1,0:T(8,128)(2,1)S(1)} %slice.3), channel_id=1, source_target_pairs={{0,4},{4,8},{8,12},{12,0},{1,5},{5,9},{9,13},{13,1},{2,6},{6,10},{... | collective-permute-start | bytes 1032200 | tf_op jit(solution)/shard_map/ppermute | solution.py:35
  3.7 1.3 %collective-permute-start.1 = (bf16[48,2304]{1,0:T(8,128)(2,1)}, bf16[48,2304]{1,0:T(8,128)(2,1)S(1)}, u32[]{:S(2)}, u32[]{:S(2)}) collective-permute-start(bf16[48,2304]{1,0:T(8,128)(2,1)} %refs_0_.1), channel_id=1, source_target_pairs={{0,1},{1,0},{2,3},{3,2},{4,5},{5,4},{6,7},{7,6},{8,9},{9,8},{10,11... | collective-permute-start | bytes 663560 | tf_op jit(solution)/shard_map/ppermute | solution.py:50
  5.1 1.1 %copy-done = bf16[16,32,768]{2,1,0:T(8,128)(2,1)S(1)} copy-done((bf16[16,32,768]{2,1,0:T(8,128)(2,1)S(1)}, bf16[16,32,768]{2,1,0:T(8,128)(2,1)}, u32[]{:S(2)}) %copy-start) | copy-done | bytes 786456
  6.2 1.1 %copy-done.2 = f32[24,64,64]{2,1,0:T(8,128)S(1)} copy-done((f32[24,64,64]{2,1,0:T(8,128)S(1)}, f32[24,64,64]{2,1,0:T(8,128)}, u32[]{:S(2)}) %copy-start.2) | copy-done | bytes 393240
  7.3 0.9 copy-done.3
  8.3 0.9 copy-done.4
  9.4 0.6 collective-permute-done.1.beyond
  10.1 0.6 join.1
  10.7 1.8 %collective-permute-start.3 = (bf16[23,8,768]{2,1,0:T(8,128)(2,1)S(1)}, bf16[23,8,768]{2,1,0:T(8,128)(2,1)S(1)}, u32[]{:S(2)}, u32[]{:S(2)}) collective-permute-start(bf16[23,8,768]{2,1,0:T(8,128)(2,1)S(1)} %get-tuple-element.46), channel_id=1, source_target_pairs={{0,1},{1,2},{2,3},{3,0},{4,5},{5,6},{6,7},{7,4},{8,9},{9,10},{10,1... | collective-permute-start | bytes 847880 | tf_op jit(solution)/shard_map/ppermute | solution.py:35
  12.5 0.8 collective-permute-start.7
  13.3 1.3 %collective-permute-start = (bf16[48,768]{1,0:T(8,128)(2,1)}, bf16[48,768]{1,0:T(8,128)(2,1)S(1)}, u32[]{:S(2)}, u32[]{:S(2)}) collective-permute-start(bf16[48,768]{1,0:T(8,128)(2,1)} %param.14), channel_id=1, source_target_pairs={{0,1},{1,0},{2,3},{3,2},{4,5},{5,4},{6,7},{7,6},{8,9},{9,8},{10,11... | collective-permute-start | bytes 221192 | tf_op jit(solution)/shard_map/ppermute | solution.py:50
  14.6 1.5 %collective-permute-start.10 = (bf16[96,2304]{1,0:T(8,128)(2,1)S(1)}, bf16[96,2304]{1,0:T(8,128)(2,1)S(1)}, u32[]{:S(2)}, u32[]{:S(2)}) collective-permute-start(bf16[96,2304]{1,0:T(8,128)(2,1)S(1)} %get-tuple-element.50.refs_3_), channel_id=1, source_target_pairs={{0,4},{4,0},{8,12},{12,8},{1,5},{5,1},{9,13},{13,9},{2,6},{6,2},{1... | collective-permute-start | bytes 1327112 | tf_op jit(solution)/shard_map/ppermute | solution.py:50
  16.1 0.8 collective-permute-start.6
  16.9 8.1 %collective-permute-done = bf16[48,768]{1,0:T(8,128)(2,1)S(1)} collective-permute-done((bf16[48,768]{1,0:T(8,128)(2,1)}, bf16[48,768]{1,0:T(8,128)(2,1)S(1)}, u32[]{:S(2)}, u32[]{:S(2)}) %collective-permute-start) | collective-permute-done | bytes 73760 | tf_op jit(solution)/shard_map/ppermute | solution.py:50
  25.0 0.9 pad_maximum_fusion
  26.0 8.7 %encode.1 = (bf16[512,768]{1,0:T(8,128)(2,1)S(1)}, bf16[512,768]{1,0:T(8,128)(2,1)S(1)}) custom-call(s32[3]{0:T(128)S(1)} %pad_add_fusion.place.refs_0_, f32[16,32,768]{2,1,0:T(8,128)S(1)} %get-tuple-element.51.tokens, bf16[7,32,768]{2,1,0:T(8,128)(2,1)S(1)} %collective-permute-done.2.above, bf16[23,8,768]{2,1,0:T(8,128)(2,1)S(1)} %collective-permute-done.3.beside, ...), custom_call_target="tpu_custom_call" | custom-call | flops 115000000 | tf_op jit(solution)/shard_map/encode/pallas_call | solution.py:187
  34.7 1.3 %collective-permute-start.8 = (bf16[96,1152]{1,0:T(8,128)(2,1)S(1)}, bf16[96,1152]{1,0:T(8,128)(2,1)S(1)}, u32[]{:S(2)}, u32[]{:S(2)}) collective-permute-start(bf16[96,1152]{1,0:T(8,128)(2,1)S(1)} %collective-permute-done.6.refs_5_), channel_id=1, source_target_pairs={{0,16},{16,0},{1,17},{17,1},{2,18},{18,2},{3,19},{19,3},{4,20},{20... | collective-permute-start | bytes 663560 | tf_op jit(solution)/shard_map/ppermute | solution.py:50
  36.0 0.7 collective-permute-start.9
  36.7 0.7 collective-permute-start.15
  37.6 1.2 %collective-permute-start.11 = (bf16[96,2304]{1,0:T(8,128)(2,1)S(1)}, bf16[96,2304]{1,0:T(8,128)(2,1)S(1)}, u32[]{:S(2)}, u32[]{:S(2)}) collective-permute-start(bf16[96,2304]{1,0:T(8,128)(2,1)S(1)} %collective-permute-done.7.refs_4_), channel_id=1, source_target_pairs={{0,4},{4,0},{8,12},{12,8},{1,5},{5,1},{9,13},{13,9},{2,6},{6,2},{1... | collective-permute-start | bytes 1327112 | tf_op jit(solution)/shard_map/ppermute | solution.py:50
  38.9 2.4 %collective-permute-done.8.refs_6_ = bf16[96,1152]{1,0:T(8,128)(2,1)S(1)} collective-permute-done((bf16[96,1152]{1,0:T(8,128)(2,1)S(1)}, bf16[96,1152]{1,0:T(8,128)(2,1)S(1)}, u32[]{:S(2)}, u32[]{:S(2)}) %collective-permute-start.8) | collective-permute-done | bytes 221216 | tf_op jit(solution)/shard_map/ppermute | solution.py:50
  41.3 1.4 %collective-permute-start.13 = (bf16[96,1152]{1,0:T(8,128)(2,1)S(1)}, bf16[96,1152]{1,0:T(8,128)(2,1)S(1)}, u32[]{:S(2)}, u32[]{:S(2)}) collective-permute-start(bf16[96,1152]{1,0:T(8,128)(2,1)S(1)} %collective-permute-done.8.refs_6_), channel_id=1, source_target_pairs={{0,4},{4,0},{8,12},{12,8},{1,5},{5,1},{9,13},{13,9},{2,6},{6,2},{1... | collective-permute-start | bytes 663560 | tf_op jit(solution)/shard_map/ppermute | solution.py:50
  42.7 2.4 %collective-permute-start.14 = (bf16[96,1152]{1,0:T(8,128)(2,1)S(1)}, bf16[96,1152]{1,0:T(8,128)(2,1)S(1)}, u32[]{:S(2)}, u32[]{:S(2)}) collective-permute-start(bf16[96,1152]{1,0:T(8,128)(2,1)S(1)} %collective-permute-done.9.refs_7_), channel_id=1, source_target_pairs={{0,4},{4,0},{8,12},{12,8},{1,5},{5,1},{9,13},{13,9},{2,6},{6,2},{1... | collective-permute-start | bytes 663560 | tf_op jit(solution)/shard_map/ppermute | solution.py:50
  45.1 1.8 %collective-permute-done.15.refs_13_ = bf16[96,1152]{1,0:T(8,128)(2,1)S(1)} collective-permute-done((bf16[96,1152]{1,0:T(8,128)(2,1)S(1)}, bf16[96,1152]{1,0:T(8,128)(2,1)S(1)}, u32[]{:S(2)}, u32[]{:S(2)}) %collective-permute-start.15) | collective-permute-done | bytes 221216 | tf_op jit(solution)/shard_map/ppermute | solution.py:539
  46.9 1.7 %collective-permute-start.16 = (bf16[96,1152]{1,0:T(8,128)(2,1)S(1)}, bf16[96,1152]{1,0:T(8,128)(2,1)S(1)}, u32[]{:S(2)}, u32[]{:S(2)}) collective-permute-start(bf16[96,1152]{1,0:T(8,128)(2,1)S(1)} %collective-permute-done.15.refs_13_), channel_id=1, source_target_pairs={{0,4},{4,0},{8,12},{12,8},{1,5},{5,1},{9,13},{13,9},{2,6},{6,2},{1... | collective-permute-start | bytes 663560 | tf_op jit(solution)/shard_map/ppermute | solution.py:50
  48.6 0.8 collective-permute-start.5
  49.7 9.0 %attend.1.refs_1_ = bf16[512,768]{1,0:T(8,128)(2,1)S(1)} custom-call(s32[3]{0:T(128)S(1)} %pad_add_fusion.place.refs_0_, bf16[512,768]{1,0:T(8,128)(2,1)S(1)} %get-tuple-element.55.refs_1_, f32[6,64,256]{2,1,0:T(8,128)S(1)} %get-tuple-element.56.refs_2_, bf16[96,2304]{1,0:T(8,128)(2,1)S(1)} %get-tuple-element.50.refs_3_, ...), custom_call_target="tpu_custom_call" | custom-call | flops 11500000256 | tf_op jit(solution)/shard_map/attend/pallas_call | solution.py:297
  59.1 1.2 %collective-permute-done.18.refs_6_ = bf16[192,768]{1,0:T(8,128)(2,1)S(1)} collective-permute-done((bf16[192,768]{1,0:T(8,128)(2,1)S(1)}, bf16[192,768]{1,0:T(8,128)(2,1)S(1)}, u32[]{:S(2)}, u32[]{:S(2)}) %collective-permute-start.18) | collective-permute-done | bytes 294944 | tf_op jit(solution)/shard_map/ppermute | solution.py:50
  60.4 3.1 %project.1 = (bf16[16,32,768]{2,1,0:T(8,128)(2,1)S(1)}, bf16[4,32,768]{2,1,0:T(8,128)(2,1)S(1)}, bf16[48,768]{1,0:T(8,128)(2,1)S(1)}, bf16[16,768]{1,0:T(8,128)(2,1)S(1)}) custom-call(s32[3]{0:T(128)S(1)} %pad_add_fusion.place.refs_0_, bf16[512,768]{1,0:T(8,128)(2,1)S(1)} %attend.1.refs_1_, bf16[512,768]{1,0:T(8,128)(2,1)S(1)} %get-tuple-element.60.refs_2_, ...), custom_call_target="tpu_custom_call" | custom-call | flops 3449999872 | tf_op jit(solution)/shard_map/project/pallas_call | solution.py:366
  63.9 1.4 %collective-permute-start.20 = (bf16[48,768]{1,0:T(8,128)(2,1)S(1)}, bf16[48,768]{1,0:T(8,128)(2,1)S(1)}, u32[]{:S(2)}, u32[]{:S(2)}) collective-permute-start(bf16[48,768]{1,0:T(8,128)(2,1)S(1)} %get-tuple-element.64), channel_id=1, source_target_pairs={{0,3},{1,0},{2,1},{3,2},{4,7},{5,4},{6,5},{7,6},{8,11},{9,8},{10,9... | collective-permute-start | bytes 221192 | tf_op jit(solution)/shard_map/ppermute | solution.py:35
  65.3 3.1 %collective-permute-start.21 = (bf16[16,768]{1,0:T(8,128)(2,1)S(1)}, bf16[16,768]{1,0:T(8,128)(2,1)S(1)}, u32[]{:S(2)}, u32[]{:S(2)}) collective-permute-start(bf16[16,768]{1,0:T(8,128)(2,1)S(1)} %get-tuple-element.65), channel_id=1, source_target_pairs={{0,15},{1,12},{2,13},{3,14},{4,3},{5,0},{6,1},{7,2},{8,7},{9,4},{1... | collective-permute-start | bytes 73736 | tf_op jit(solution)/shard_map/ppermute | solution.py:45
  68.5 1.1 %collective-permute-done.21.corner = bf16[16,768]{1,0:T(8,128)(2,1)S(1)} collective-permute-done((bf16[16,768]{1,0:T(8,128)(2,1)S(1)}, bf16[16,768]{1,0:T(8,128)(2,1)S(1)}, u32[]{:S(2)}, u32[]{:S(2)}) %collective-permute-start.21) | collective-permute-done | bytes 24608 | tf_op jit(solution)/shard_map/ppermute | solution.py:45
  69.7 1.6 %dispatch.1 = (bf16[512,768]{1,0:T(8,128)(2,1)S(1)}, bf16[64,768]{1,0:T(8,128)(2,1)S(1)}, bf16[64,768]{1,0:T(8,128)(2,1)S(1)}, bf16[64,768]{1,0:T(8,128)(2,1)S(1...) custom-call(s32[3]{0:T(128)S(1)} %pad_add_fusion.place.refs_0_, ...), custom_call_target="tpu_custom_call" | custom-call | tf_op jit(solution)/shard_map/dispatch/pallas_call | solution.py:429
  71.6 0.6 collective-permute-start.26
  72.2 1.3 %collective-permute-start.27 = (bf16[64,768]{1,0:T(8,128)(2,1)S(1)}, bf16[64,768]{1,0:T(8,128)(2,1)S(1)}, u32[]{:S(2)}, u32[]{:S(2)}) collective-permute-start(bf16[64,768]{1,0:T(8,128)(2,1)S(1)} %get-tuple-element.75), channel_id=1, source_target_pairs={{0,12},{4,8},{8,4},{12,0},{1,13},{5,9},{9,5},{13,1},{2,14},{6,10},... | collective-permute-start | bytes 294920 | tf_op jit(solution)/shard_map/ppermute | solution.py:50
  73.5 0.7 collective-permute-start.23
  74.2 1.5 %collective-permute-start.24 = (bf16[64,768]{1,0:T(8,128)(2,1)S(1)}, bf16[64,768]{1,0:T(8,128)(2,1)S(1)}, u32[]{:S(2)}, u32[]{:S(2)}) collective-permute-start(bf16[64,768]{1,0:T(8,128)(2,1)S(1)} %get-tuple-element.70), channel_id=1, source_target_pairs={{0,12},{4,8},{8,4},{12,0},{1,13},{5,9},{9,5},{13,1},{2,14},{6,10},... | collective-permute-start | bytes 294920 | tf_op jit(solution)/shard_map/ppermute | solution.py:50
  75.7 3.2 %collective-permute-done.27.refs_3_ = bf16[64,768]{1,0:T(8,128)(2,1)S(1)} collective-permute-done((bf16[64,768]{1,0:T(8,128)(2,1)S(1)}, bf16[64,768]{1,0:T(8,128)(2,1)S(1)}, u32[]{:S(2)}, u32[]{:S(2)}) %collective-permute-start.27) | collective-permute-done | bytes 98336 | tf_op jit(solution)/shard_map/ppermute | solution.py:50
  78.9 7.6 %experts.3 = (bf16[64,768]{1,0:T(8,128)(2,1)S(1)}, bf16[64,768]{1,0:T(8,128)(2,1)S(1)}, bf16[64,768]{1,0:T(8,128)(2,1)S(1)}, bf16[64,768]{1,0:T(8,128)(2,1)S(1)}) custom-call(bf16[64,768]{1,0:T(8,128)(2,1)S(1)} %get-tuple-element.72.refs_0_, bf16[64,768]{1,0:T(8,128)(2,1)S(1)} %collective-permute-done.25.refs_1_, ...), custom_call_target="tpu_custom_call" | custom-call | flops 8049999872 | tf_op jit(solution)/shard_map/experts/pallas_call | solution.py:471
  86.6 0.8 collective-permute-start.31
  87.3 1.4 %collective-permute-start.33 = (bf16[64,768]{1,0:T(8,128)(2,1)S(1)}, bf16[64,768]{1,0:T(8,128)(2,1)S(1)}, u32[]{:S(2)}, u32[]{:S(2)}) collective-permute-start(bf16[64,768]{1,0:T(8,128)(2,1)S(1)} %get-tuple-element.82), channel_id=1, source_target_pairs={{0,12},{4,8},{8,4},{12,0},{1,13},{5,9},{9,5},{13,1},{2,14},{6,10},... | collective-permute-start | bytes 294920 | tf_op jit(solution)/shard_map/ppermute | solution.py:50
  88.7 7.6 %experts.2 = (bf16[64,768]{1,0:T(8,128)(2,1)S(1)}, bf16[64,768]{1,0:T(8,128)(2,1)S(1)}, bf16[64,768]{1,0:T(8,128)(2,1)S(1)}, bf16[64,768]{1,0:T(8,128)(2,1)S(1)}) custom-call(bf16[64,768]{1,0:T(8,128)(2,1)S(1)} %get-tuple-element.67.refs_0_, bf16[64,768]{1,0:T(8,128)(2,1)S(1)} %collective-permute-done.22.refs_1_, ...), custom_call_target="tpu_custom_call" | custom-call | flops 8049999872 | tf_op jit(solution)/shard_map/experts/pallas_call | solution.py:471
  96.4 0.8 collective-permute-start.30
  97.1 1.4 %collective-permute-start.32 = (bf16[64,768]{1,0:T(8,128)(2,1)S(1)}, bf16[64,768]{1,0:T(8,128)(2,1)S(1)}, u32[]{:S(2)}, u32[]{:S(2)}) collective-permute-start(bf16[64,768]{1,0:T(8,128)(2,1)S(1)} %get-tuple-element.81), channel_id=1, source_target_pairs={{0,12},{4,8},{8,4},{12,0},{1,13},{5,9},{9,5},{13,1},{2,14},{6,10},... | collective-permute-start | bytes 294920 | tf_op jit(solution)/shard_map/ppermute | solution.py:50
  99.1 1.3 %collective-permute-done.30.refs_4_ = bf16[64,768]{1,0:T(8,128)(2,1)S(1)} collective-permute-done((bf16[64,768]{1,0:T(8,128)(2,1)S(1)}, bf16[64,768]{1,0:T(8,128)(2,1)S(1)}, u32[]{:S(2)}, u32[]{:S(2)}) %collective-permute-start.30) | collective-permute-done | bytes 98336 | tf_op jit(solution)/shard_map/ppermute | solution.py:50
  100.4 2.7 %collective-permute-done.32.refs_6_ = bf16[64,768]{1,0:T(8,128)(2,1)S(1)} collective-permute-done((bf16[64,768]{1,0:T(8,128)(2,1)S(1)}, bf16[64,768]{1,0:T(8,128)(2,1)S(1)}, u32[]{:S(2)}, u32[]{:S(2)}) %collective-permute-start.32) | collective-permute-done | bytes 98336 | tf_op jit(solution)/shard_map/ppermute | solution.py:50
  103.1 2.3 %combine.1 = bf16[512,768]{1,0:T(8,128)(2,1)} custom-call(s32[3]{0:T(128)S(1)} %pad_add_fusion.place.refs_0_, bf16[512,768]{1,0:T(8,128)(2,1)S(1)} %get-tuple-element.66.attended, s32[512,1]{1,0:T(8,128)S(1)} %select_n.42.position, s32[512,1]{1,0:T(8,128)S(1)} %select_n.43.constant_at, f32[16,768]{1,0:T(8,128)S(1)} %copy-done.1, ...), custom_call_target="tpu_custom_call" | custom-call | tf_op jit(solution)/shard_map/combine/pallas_call | solution.py:509
  (57 shorter events, 3.0 us)
Async XLA Ops:
  0.0 38.8 %copy-start.5 = (bf16[48,768]{1,0:T(8,128)(2,1)S(1)}, bf16[48,768]{1,0:T(8,128)(2,1)}, u32[]{:S(2)}) copy-start(bf16[48,768]{1,0:T(8,128)(2,1)} %param.14) | copy-start | bytes 221188
  1.0 9.0 %collective-permute-start.2 = (bf16[7,32,768]{2,1,0:T(8,128)(2,1)S(1)}, bf16[7,32,768]{2,1,0:T(8,128)(2,1)S(1)}, u32[]{:S(2)}, u32[]{:S(2)}) collective-permute-start(bf16[7,32,768]{2,1,0:T(8,128)(2,1)S(1)} %slice.3), channel_id=1, source_target_pairs={{0,4},{4,8},{8,12},{12,0},{1,5},{5,9},{9,13},{13,1},{2,6},{6,10},{... | collective-permute-start | bytes 1032200 | tf_op jit(solution)/shard_map/ppermute | solution.py:35
  3.7 6.4 %collective-permute-start.1 = (bf16[48,2304]{1,0:T(8,128)(2,1)}, bf16[48,2304]{1,0:T(8,128)(2,1)S(1)}, u32[]{:S(2)}, u32[]{:S(2)}) collective-permute-start(bf16[48,2304]{1,0:T(8,128)(2,1)} %refs_0_.1), channel_id=1, source_target_pairs={{0,1},{1,0},{2,3},{3,2},{4,5},{5,4},{6,7},{7,6},{8,9},{9,8},{10,11... | collective-permute-start | bytes 663560 | tf_op jit(solution)/shard_map/ppermute | solution.py:50
  5.1 1.1 %copy-start = (bf16[16,32,768]{2,1,0:T(8,128)(2,1)S(1)}, bf16[16,32,768]{2,1,0:T(8,128)(2,1)}, u32[]{:S(2)}) copy-start(bf16[16,32,768]{2,1,0:T(8,128)(2,1)} %tokens.1) | copy-start | bytes 2359300
  6.2 1.1 %copy-start.2 = (f32[24,64,64]{2,1,0:T(8,128)S(1)}, f32[24,64,64]{2,1,0:T(8,128)}, u32[]{:S(2)}) copy-start(f32[24,64,64]{2,1,0:T(8,128)} %rel_bias.1) | copy-start | bytes 1179652
  7.3 0.9 copy-start.3
  8.3 0.9 copy-start.4
  10.7 14.3 %collective-permute-start.3 = (bf16[23,8,768]{2,1,0:T(8,128)(2,1)S(1)}, bf16[23,8,768]{2,1,0:T(8,128)(2,1)S(1)}, u32[]{:S(2)}, u32[]{:S(2)}) collective-permute-start(bf16[23,8,768]{2,1,0:T(8,128)(2,1)S(1)} %get-tuple-element.46), channel_id=1, source_target_pairs={{0,1},{1,2},{2,3},{3,0},{4,5},{5,6},{6,7},{7,4},{8,9},{9,10},{10,1... | collective-permute-start | bytes 847880 | tf_op jit(solution)/shard_map/ppermute | solution.py:35
  12.5 22.3 %collective-permute-start.7 = (bf16[96,2304]{1,0:T(8,128)(2,1)S(1)}, bf16[96,2304]{1,0:T(8,128)(2,1)S(1)}, u32[]{:S(2)}, u32[]{:S(2)}) collective-permute-start(bf16[96,2304]{1,0:T(8,128)(2,1)S(1)} %get-tuple-element.50.refs_3_), channel_id=1, source_target_pairs={{0,8},{4,12},{8,0},{12,4},{1,9},{5,13},{9,1},{13,5},{2,10},{6,14},... | collective-permute-start | bytes 1327112 | tf_op jit(solution)/shard_map/ppermute | solution.py:50
  13.3 11.7 %collective-permute-start = (bf16[48,768]{1,0:T(8,128)(2,1)}, bf16[48,768]{1,0:T(8,128)(2,1)S(1)}, u32[]{:S(2)}, u32[]{:S(2)}) collective-permute-start(bf16[48,768]{1,0:T(8,128)(2,1)} %param.14), channel_id=1, source_target_pairs={{0,1},{1,0},{2,3},{3,2},{4,5},{5,4},{6,7},{7,6},{8,9},{9,8},{10,11... | collective-permute-start | bytes 221192 | tf_op jit(solution)/shard_map/ppermute | solution.py:50
  14.6 24.2 %collective-permute-start.10 = (bf16[96,2304]{1,0:T(8,128)(2,1)S(1)}, bf16[96,2304]{1,0:T(8,128)(2,1)S(1)}, u32[]{:S(2)}, u32[]{:S(2)}) collective-permute-start(bf16[96,2304]{1,0:T(8,128)(2,1)S(1)} %get-tuple-element.50.refs_3_), channel_id=1, source_target_pairs={{0,4},{4,0},{8,12},{12,8},{1,5},{5,1},{9,13},{13,9},{2,6},{6,2},{1... | collective-permute-start | bytes 1327112 | tf_op jit(solution)/shard_map/ppermute | solution.py:50
  16.1 18.6 %collective-permute-start.6 = (bf16[96,1152]{1,0:T(8,128)(2,1)S(1)}, bf16[96,1152]{1,0:T(8,128)(2,1)S(1)}, u32[]{:S(2)}, u32[]{:S(2)}) collective-permute-start(bf16[96,1152]{1,0:T(8,128)(2,1)S(1)} %get-tuple-element.49), channel_id=1, source_target_pairs={{0,2},{1,3},{2,0},{3,1},{4,6},{5,7},{6,4},{7,5},{8,10},{9,11},{10,... | collective-permute-start | bytes 663560 | tf_op jit(solution)/shard_map/ppermute | solution.py:50
  25.9 11.7 %collective-permute-start.4 = (bf16[96,768]{1,0:T(8,128)(2,1)S(1)}, bf16[96,768]{1,0:T(8,128)(2,1)S(1)}, u32[]{:S(2)}, u32[]{:S(2)}) collective-permute-start(bf16[96,768]{1,0:T(8,128)(2,1)S(1)} %pad_maximum_fusion), channel_id=1, source_target_pairs={{0,2},{1,3},{2,0},{3,1},{4,6},{5,7},{6,4},{7,5},{8,10},{9,11},{10,... | collective-permute-start | bytes 442376 | tf_op jit(solution)/shard_map/ppermute | solution.py:50
  34.7 6.6 %collective-permute-start.8 = (bf16[96,1152]{1,0:T(8,128)(2,1)S(1)}, bf16[96,1152]{1,0:T(8,128)(2,1)S(1)}, u32[]{:S(2)}, u32[]{:S(2)}) collective-permute-start(bf16[96,1152]{1,0:T(8,128)(2,1)S(1)} %collective-permute-done.6.refs_5_), channel_id=1, source_target_pairs={{0,16},{16,0},{1,17},{17,1},{2,18},{18,2},{3,19},{19,3},{4,20},{20... | collective-permute-start | bytes 663560 | tf_op jit(solution)/shard_map/ppermute | solution.py:50
  36.0 6.7 %collective-permute-start.9 = (bf16[96,1152]{1,0:T(8,128)(2,1)S(1)}, bf16[96,1152]{1,0:T(8,128)(2,1)S(1)}, u32[]{:S(2)}, u32[]{:S(2)}) collective-permute-start(bf16[96,1152]{1,0:T(8,128)(2,1)S(1)} %collective-permute-done.6.refs_5_), channel_id=1, source_target_pairs={{0,8},{4,12},{8,0},{12,4},{1,9},{5,13},{9,1},{13,5},{2,10},{6,14},... | collective-permute-start | bytes 663560 | tf_op jit(solution)/shard_map/ppermute | solution.py:50
  36.7 10.2 %collective-permute-start.15 = (bf16[96,1152]{1,0:T(8,128)(2,1)S(1)}, bf16[96,1152]{1,0:T(8,128)(2,1)S(1)}, u32[]{:S(2)}, u32[]{:S(2)}) collective-permute-start(bf16[96,1152]{1,0:T(8,128)(2,1)S(1)} %collective-permute-done.6.refs_5_), channel_id=1, source_target_pairs={{0,24},{4,28},{8,16},{12,20},{16,8},{20,12},{24,0},{28,4},{1,25},{... | collective-permute-start | bytes 663560 | tf_op jit(solution)/shard_map/ppermute | solution.py:539
  37.6 12.1 %collective-permute-start.11 = (bf16[96,2304]{1,0:T(8,128)(2,1)S(1)}, bf16[96,2304]{1,0:T(8,128)(2,1)S(1)}, u32[]{:S(2)}, u32[]{:S(2)}) collective-permute-start(bf16[96,2304]{1,0:T(8,128)(2,1)S(1)} %collective-permute-done.7.refs_4_), channel_id=1, source_target_pairs={{0,4},{4,0},{8,12},{12,8},{1,5},{5,1},{9,13},{13,9},{2,6},{6,2},{1... | collective-permute-start | bytes 1327112 | tf_op jit(solution)/shard_map/ppermute | solution.py:50
  38.8 9.8 %collective-permute-start.12 = (bf16[96,1152]{1,0:T(8,128)(2,1)S(1)}, bf16[96,1152]{1,0:T(8,128)(2,1)S(1)}, u32[]{:S(2)}, u32[]{:S(2)}) collective-permute-start(bf16[96,1152]{1,0:T(8,128)(2,1)S(1)} %collective-permute-done.6.refs_5_), channel_id=1, source_target_pairs={{0,4},{4,0},{8,12},{12,8},{1,5},{5,1},{9,13},{13,9},{2,6},{6,2},{1... | collective-permute-start | bytes 663560 | tf_op jit(solution)/shard_map/ppermute | solution.py:50
  41.3 8.1 %collective-permute-start.13 = (bf16[96,1152]{1,0:T(8,128)(2,1)S(1)}, bf16[96,1152]{1,0:T(8,128)(2,1)S(1)}, u32[]{:S(2)}, u32[]{:S(2)}) collective-permute-start(bf16[96,1152]{1,0:T(8,128)(2,1)S(1)} %collective-permute-done.8.refs_6_), channel_id=1, source_target_pairs={{0,4},{4,0},{8,12},{12,8},{1,5},{5,1},{9,13},{13,9},{2,6},{6,2},{1... | collective-permute-start | bytes 663560 | tf_op jit(solution)/shard_map/ppermute | solution.py:50
  42.7 6.9 %collective-permute-start.14 = (bf16[96,1152]{1,0:T(8,128)(2,1)S(1)}, bf16[96,1152]{1,0:T(8,128)(2,1)S(1)}, u32[]{:S(2)}, u32[]{:S(2)}) collective-permute-start(bf16[96,1152]{1,0:T(8,128)(2,1)S(1)} %collective-permute-done.9.refs_7_), channel_id=1, source_target_pairs={{0,4},{4,0},{8,12},{12,8},{1,5},{5,1},{9,13},{13,9},{2,6},{6,2},{1... | collective-permute-start | bytes 663560 | tf_op jit(solution)/shard_map/ppermute | solution.py:50
  46.9 2.8 %collective-permute-start.16 = (bf16[96,1152]{1,0:T(8,128)(2,1)S(1)}, bf16[96,1152]{1,0:T(8,128)(2,1)S(1)}, u32[]{:S(2)}, u32[]{:S(2)}) collective-permute-start(bf16[96,1152]{1,0:T(8,128)(2,1)S(1)} %collective-permute-done.15.refs_13_), channel_id=1, source_target_pairs={{0,4},{4,0},{8,12},{12,8},{1,5},{5,1},{9,13},{13,9},{2,6},{6,2},{1... | collective-permute-start | bytes 663560 | tf_op jit(solution)/shard_map/ppermute | solution.py:50
  48.6 10.1 %collective-permute-start.5 = (bf16[192,768]{1,0:T(8,128)(2,1)S(1)}, bf16[192,768]{1,0:T(8,128)(2,1)S(1)}, u32[]{:S(2)}, u32[]{:S(2)}) collective-permute-start(bf16[192,768]{1,0:T(8,128)(2,1)S(1)} %constant_dynamic-update-slice_fusion.refs_3_), channel_id=1, source_target_pairs={{0,8},{4,12},{8,0},{12,4},{1,9},{5,13},{9,1},{13,5},{2,10},{6,14},... | collective-permute-start | bytes 884744 | tf_op jit(solution)/shard_map/ppermute | solution.py:50
  49.4 9.8 %collective-permute-start.17 = (bf16[192,768]{1,0:T(8,128)(2,1)S(1)}, bf16[192,768]{1,0:T(8,128)(2,1)S(1)}, u32[]{:S(2)}, u32[]{:S(2)}) collective-permute-start(bf16[192,768]{1,0:T(8,128)(2,1)S(1)} %constant_dynamic-update-slice_fusion.refs_3_), channel_id=1, source_target_pairs={{0,4},{4,0},{8,12},{12,8},{1,5},{5,1},{9,13},{13,9},{2,6},{6,2},{1... | collective-permute-start | bytes 884744 | tf_op jit(solution)/shard_map/ppermute | solution.py:50
  49.7 18.7 %copy-start.6 = (s32[16,32]{1,0:T(8,128)S(1)}, s32[16,32]{1,0:T(8,128)}, u32[]{:S(2)}) copy-start(s32[16,32]{1,0:T(8,128)} %param.21) | copy-start | bytes 6148
  49.7 18.7 %copy-start.7 = (s32[16,32]{1,0:T(8,128)S(1)}, s32[16,32]{1,0:T(8,128)}, u32[]{:S(2)}) copy-start(s32[16,32]{1,0:T(8,128)} %param.19) | copy-start | bytes 6148
  49.7 18.7 %copy-start.8 = (s32[16,32]{1,0:T(8,128)S(1)}, s32[16,32]{1,0:T(8,128)}, u32[]{:S(2)}) copy-start(s32[16,32]{1,0:T(8,128)} %param.20) | copy-start | bytes 6148
  58.7 1.6 %collective-permute-start.18 = (bf16[192,768]{1,0:T(8,128)(2,1)S(1)}, bf16[192,768]{1,0:T(8,128)(2,1)S(1)}, u32[]{:S(2)}, u32[]{:S(2)}) collective-permute-start(bf16[192,768]{1,0:T(8,128)(2,1)S(1)} %collective-permute-done.5.refs_4_), channel_id=1, source_target_pairs={{0,4},{4,0},{8,12},{12,8},{1,5},{5,1},{9,13},{13,9},{2,6},{6,2},{1... | collective-permute-start | bytes 884744 | tf_op jit(solution)/shard_map/ppermute | solution.py:50
  63.5 6.2 %collective-permute-start.19 = (bf16[4,32,768]{2,1,0:T(8,128)(2,1)S(1)}, bf16[4,32,768]{2,1,0:T(8,128)(2,1)S(1)}, u32[]{:S(2)}, u32[]{:S(2)}) collective-permute-start(bf16[4,32,768]{2,1,0:T(8,128)(2,1)S(1)} %get-tuple-element.63), channel_id=1, source_target_pairs={{0,12},{4,0},{8,4},{12,8},{1,13},{5,1},{9,5},{13,9},{2,14},{6,2},{... | collective-permute-start | bytes 589832 | tf_op jit(solution)/shard_map/ppermute | solution.py:35
  63.9 5.8 %collective-permute-start.20 = (bf16[48,768]{1,0:T(8,128)(2,1)S(1)}, bf16[48,768]{1,0:T(8,128)(2,1)S(1)}, u32[]{:S(2)}, u32[]{:S(2)}) collective-permute-start(bf16[48,768]{1,0:T(8,128)(2,1)S(1)} %get-tuple-element.64), channel_id=1, source_target_pairs={{0,3},{1,0},{2,1},{3,2},{4,7},{5,4},{6,5},{7,6},{8,11},{9,8},{10,9... | collective-permute-start | bytes 221192 | tf_op jit(solution)/shard_map/ppermute | solution.py:35
  65.3 4.3 %collective-permute-start.21 = (bf16[16,768]{1,0:T(8,128)(2,1)S(1)}, bf16[16,768]{1,0:T(8,128)(2,1)S(1)}, u32[]{:S(2)}, u32[]{:S(2)}) collective-permute-start(bf16[16,768]{1,0:T(8,128)(2,1)S(1)} %get-tuple-element.65), channel_id=1, source_target_pairs={{0,15},{1,12},{2,13},{3,14},{4,3},{5,0},{6,1},{7,2},{8,7},{9,4},{1... | collective-permute-start | bytes 73736 | tf_op jit(solution)/shard_map/ppermute | solution.py:45
  71.3 2.9 %collective-permute-start.25 = (bf16[64,768]{1,0:T(8,128)(2,1)S(1)}, bf16[64,768]{1,0:T(8,128)(2,1)S(1)}, u32[]{:S(2)}, u32[]{:S(2)}) collective-permute-start(bf16[64,768]{1,0:T(8,128)(2,1)S(1)} %get-tuple-element.73), channel_id=1, source_target_pairs={{0,4},{4,0},{8,12},{12,8},{1,5},{5,1},{9,13},{13,9},{2,6},{6,2},{1... | collective-permute-start | bytes 294920 | tf_op jit(solution)/shard_map/ppermute | solution.py:50
  71.6 4.1 %collective-permute-start.26 = (bf16[64,768]{1,0:T(8,128)(2,1)S(1)}, bf16[64,768]{1,0:T(8,128)(2,1)S(1)}, u32[]{:S(2)}, u32[]{:S(2)}) collective-permute-start(bf16[64,768]{1,0:T(8,128)(2,1)S(1)} %get-tuple-element.74), channel_id=1, source_target_pairs={{0,8},{4,12},{8,0},{12,4},{1,9},{5,13},{9,1},{13,5},{2,10},{6,14},... | collective-permute-start | bytes 294920 | tf_op jit(solution)/shard_map/ppermute | solution.py:50
  72.2 6.7 %collective-permute-start.27 = (bf16[64,768]{1,0:T(8,128)(2,1)S(1)}, bf16[64,768]{1,0:T(8,128)(2,1)S(1)}, u32[]{:S(2)}, u32[]{:S(2)}) collective-permute-start(bf16[64,768]{1,0:T(8,128)(2,1)S(1)} %get-tuple-element.75), channel_id=1, source_target_pairs={{0,12},{4,8},{8,4},{12,0},{1,13},{5,9},{9,5},{13,1},{2,14},{6,10},... | collective-permute-start | bytes 294920 | tf_op jit(solution)/shard_map/ppermute | solution.py:50
  73.5 13.8 %collective-permute-start.22 = (bf16[64,768]{1,0:T(8,128)(2,1)S(1)}, bf16[64,768]{1,0:T(8,128)(2,1)S(1)}, u32[]{:S(2)}, u32[]{:S(2)}) collective-permute-start(bf16[64,768]{1,0:T(8,128)(2,1)S(1)} %get-tuple-element.68), channel_id=1, source_target_pairs={{0,4},{4,0},{8,12},{12,8},{1,5},{5,1},{9,13},{13,9},{2,6},{6,2},{1... | collective-permute-start | bytes 294920 | tf_op jit(solution)/shard_map/ppermute | solution.py:50
  73.5 15.2 %collective-permute-start.23 = (bf16[64,768]{1,0:T(8,128)(2,1)S(1)}, bf16[64,768]{1,0:T(8,128)(2,1)S(1)}, u32[]{:S(2)}, u32[]{:S(2)}) collective-permute-start(bf16[64,768]{1,0:T(8,128)(2,1)S(1)} %get-tuple-element.69), channel_id=1, source_target_pairs={{0,8},{4,12},{8,0},{12,4},{1,9},{5,13},{9,1},{13,5},{2,10},{6,14},... | collective-permute-start | bytes 294920 | tf_op jit(solution)/shard_map/ppermute | solution.py:50
  74.2 14.5 %collective-permute-start.24 = (bf16[64,768]{1,0:T(8,128)(2,1)S(1)}, bf16[64,768]{1,0:T(8,128)(2,1)S(1)}, u32[]{:S(2)}, u32[]{:S(2)}) collective-permute-start(bf16[64,768]{1,0:T(8,128)(2,1)S(1)} %get-tuple-element.70), channel_id=1, source_target_pairs={{0,12},{4,8},{8,4},{12,0},{1,13},{5,9},{9,5},{13,1},{2,14},{6,10},... | collective-permute-start | bytes 294920 | tf_op jit(solution)/shard_map/ppermute | solution.py:50
  86.5 10.6 %collective-permute-start.29 = (bf16[64,768]{1,0:T(8,128)(2,1)S(1)}, bf16[64,768]{1,0:T(8,128)(2,1)S(1)}, u32[]{:S(2)}, u32[]{:S(2)}) collective-permute-start(bf16[64,768]{1,0:T(8,128)(2,1)S(1)} %get-tuple-element.78), channel_id=1, source_target_pairs={{0,4},{4,0},{8,12},{12,8},{1,5},{5,1},{9,13},{13,9},{2,6},{6,2},{1... | collective-permute-start | bytes 294920 | tf_op jit(solution)/shard_map/ppermute | solution.py:50
  86.6 12.5 %collective-permute-start.31 = (bf16[64,768]{1,0:T(8,128)(2,1)S(1)}, bf16[64,768]{1,0:T(8,128)(2,1)S(1)}, u32[]{:S(2)}, u32[]{:S(2)}) collective-permute-start(bf16[64,768]{1,0:T(8,128)(2,1)S(1)} %get-tuple-element.80), channel_id=1, source_target_pairs={{0,8},{4,12},{8,0},{12,4},{1,9},{5,13},{9,1},{13,5},{2,10},{6,14},... | collective-permute-start | bytes 294920 | tf_op jit(solution)/shard_map/ppermute | solution.py:50
  87.3 11.7 %collective-permute-start.33 = (bf16[64,768]{1,0:T(8,128)(2,1)S(1)}, bf16[64,768]{1,0:T(8,128)(2,1)S(1)}, u32[]{:S(2)}, u32[]{:S(2)}) collective-permute-start(bf16[64,768]{1,0:T(8,128)(2,1)S(1)} %get-tuple-element.82), channel_id=1, source_target_pairs={{0,12},{4,8},{8,4},{12,0},{1,13},{5,9},{9,5},{13,1},{2,14},{6,10},... | collective-permute-start | bytes 294920 | tf_op jit(solution)/shard_map/ppermute | solution.py:50
  88.7 14.4 %copy-start.1 = (f32[16,768]{1,0:T(8,128)S(1)}, f32[16,768]{1,0:T(8,128)}, u32[]{:S(2)}) copy-start(f32[16,768]{1,0:T(8,128)} %table.1) | copy-start | bytes 147460
  96.3 2.8 %collective-permute-start.28 = (bf16[64,768]{1,0:T(8,128)(2,1)S(1)}, bf16[64,768]{1,0:T(8,128)(2,1)S(1)}, u32[]{:S(2)}, u32[]{:S(2)}) collective-permute-start(bf16[64,768]{1,0:T(8,128)(2,1)S(1)} %get-tuple-element.77), channel_id=1, source_target_pairs={{0,4},{4,0},{8,12},{12,8},{1,5},{5,1},{9,13},{13,9},{2,6},{6,2},{1... | collective-permute-start | bytes 294920 | tf_op jit(solution)/shard_map/ppermute | solution.py:50
  96.4 4.0 %collective-permute-start.30 = (bf16[64,768]{1,0:T(8,128)(2,1)S(1)}, bf16[64,768]{1,0:T(8,128)(2,1)S(1)}, u32[]{:S(2)}, u32[]{:S(2)}) collective-permute-start(bf16[64,768]{1,0:T(8,128)(2,1)S(1)} %get-tuple-element.79), channel_id=1, source_target_pairs={{0,8},{4,12},{8,0},{12,4},{1,9},{5,13},{9,1},{13,5},{2,10},{6,14},... | collective-permute-start | bytes 294920 | tf_op jit(solution)/shard_map/ppermute | solution.py:50
  97.1 5.9 %collective-permute-start.32 = (bf16[64,768]{1,0:T(8,128)(2,1)S(1)}, bf16[64,768]{1,0:T(8,128)(2,1)S(1)}, u32[]{:S(2)}, u32[]{:S(2)}) collective-permute-start(bf16[64,768]{1,0:T(8,128)(2,1)S(1)} %get-tuple-element.81), channel_id=1, source_target_pairs={{0,12},{4,8},{8,4},{12,0},{1,13},{5,9},{9,5},{13,1},{2,14},{6,10},... | collective-permute-start | bytes 294920 | tf_op jit(solution)/shard_map/ppermute | solution.py:50

commit v8 on v7

--- a/solution.py
+++ b/solution.py
@@ -177,7 +177,7 @@
         normed[part, :] = normalized(encoded[part, :].astype(jnp.float32))
         return 0
 
-    lax.fori_loop(0, rows * cols // SPOTS, norm, 0, unroll=4)
+    lax.fori_loop(0, rows * cols // SPOTS, norm, 0, unroll=8)
 
 
 def encode(place, tokens, above, beside, weights):
@@ -287,7 +287,7 @@
             ).astype(jnp.bfloat16)
         return 0
 
-    lax.fori_loop(0, rows * cols // SPOTS, window, 0, unroll=4)
+    lax.fori_loop(0, rows * cols // SPOTS, window, 0, unroll=8)
 
 
 def attend(place, shape, normed, bias, pieces, grid_cols):

time: 106 us -> 105 us (level)
  no operation moved by 1% of the time
where the time goes in v8:
time: 105 us
  Pallas kernels  40.2 us (38%)
  starting transfers between devices  34.7 us (33%)
  waiting for transfers between devices  22.9 us (22%)
  local copies, waits for them, and re-layouts  5.76 us (5%)
    ppermute x28, starting transfers between devices, exchanged(): return lax.ppermute(x, axis, [(i, i ^ mask) for i in range(size)])  24.6 us
    ppermute x28, waiting for transfers between devices, exchanged(): return lax.ppermute(x, axis, [(i, i ^ mask) for i in range(size)])  19.9 us
    pallas_call x2, Pallas kernels, serve(): pl.pallas_call(functools.partial(expert_kernel, count, first), out_shape=...  15.1 us
    pallas_call x1, Pallas kernels, encode(): pl.pallas_call(encode_kernel, out_shape=(flat, flat), in_specs=[SMEM] + [...  8.62 us
    pallas_call x1, Pallas kernels, attend(): pl.pallas_call(functools.partial(attend_kernel, shape, ids, grid_cols), o...  8.59 us
    ppermute x4, starting transfers between devices, shifted(): return lax.ppermute(x, axis, [(i, (i + by) % size) for i in range(size)])  6.28 us
    unnamed x20, local copies, waits for them, and re-layouts  4.13 us
    pallas_call x1, Pallas kernels, project(): pl.pallas_call(functools.partial(project_kernel, shape, ids, grid_cols),...  3.12 us
  transfers between devices with their start and end apart: 34, of which 11 were waited for; matrix products, arithmetic and copies ran while one was open for 2% of the time, Pallas kernels for 31%

profile of v8, /device:TPU:1, one launch (start us, length us, event | category | flops | bytes accessed | tf_op | source)
XLA Modules:
  0.0 104.8 jit_solution(6914171564152943094)
XLA Ops:
  0.0 1.0 slice.3
  1.0 2.7 %collective-permute-start.2 = (bf16[7,32,768]{2,1,0:T(8,128)(2,1)S(1)}, bf16[7,32,768]{2,1,0:T(8,128)(2,1)S(1)}, u32[]{:S(2)}, u32[]{:S(2)}) collective-permute-start(bf16[7,32,768]{2,1,0:T(8,128)(2,1)S(1)} %slice.3), channel_id=1, source_target_pairs={{0,4},{4,8},{8,12},{12,0},{1,5},{5,9},{9,13},{13,1},{2,6},{6,10},{... | collective-permute-start | bytes 1032200 | tf_op jit(solution)/shard_map/ppermute | solution.py:35
  3.7 1.3 %collective-permute-start.1 = (bf16[48,2304]{1,0:T(8,128)(2,1)}, bf16[48,2304]{1,0:T(8,128)(2,1)S(1)}, u32[]{:S(2)}, u32[]{:S(2)}) collective-permute-start(bf16[48,2304]{1,0:T(8,128)(2,1)} %refs_0_.1), channel_id=1, source_target_pairs={{0,1},{1,0},{2,3},{3,2},{4,5},{5,4},{6,7},{7,6},{8,9},{9,8},{10,11... | collective-permute-start | bytes 663560 | tf_op jit(solution)/shard_map/ppermute | solution.py:50
  5.1 1.1 %copy-done = bf16[16,32,768]{2,1,0:T(8,128)(2,1)S(1)} copy-done((bf16[16,32,768]{2,1,0:T(8,128)(2,1)S(1)}, bf16[16,32,768]{2,1,0:T(8,128)(2,1)}, u32[]{:S(2)}) %copy-start) | copy-done | bytes 786456
  6.2 1.1 %copy-done.2 = f32[24,64,64]{2,1,0:T(8,128)S(1)} copy-done((f32[24,64,64]{2,1,0:T(8,128)S(1)}, f32[24,64,64]{2,1,0:T(8,128)}, u32[]{:S(2)}) %copy-start.2) | copy-done | bytes 393240
  7.3 0.9 copy-done.3
  8.3 0.9 copy-done.4
  9.4 0.6 collective-permute-done.1.beyond
  10.1 0.6 join.1
  10.7 1.8 %collective-permute-start.3 = (bf16[23,8,768]{2,1,0:T(8,128)(2,1)S(1)}, bf16[23,8,768]{2,1,0:T(8,128)(2,1)S(1)}, u32[]{:S(2)}, u32[]{:S(2)}) collective-permute-start(bf16[23,8,768]{2,1,0:T(8,128)(2,1)S(1)} %get-tuple-element.46), channel_id=1, source_target_pairs={{0,1},{1,2},{2,3},{3,0},{4,5},{5,6},{6,7},{7,4},{8,9},{9,10},{10,1... | collective-permute-start | bytes 847880 | tf_op jit(solution)/shard_map/ppermute | solution.py:35
  12.5 0.8 collective-permute-start.7
  13.3 1.3 %collective-permute-start = (bf16[48,768]{1,0:T(8,128)(2,1)}, bf16[48,768]{1,0:T(8,128)(2,1)S(1)}, u32[]{:S(2)}, u32[]{:S(2)}) collective-permute-start(bf16[48,768]{1,0:T(8,128)(2,1)} %param.14), channel_id=1, source_target_pairs={{0,1},{1,0},{2,3},{3,2},{4,5},{5,4},{6,7},{7,6},{8,9},{9,8},{10,11... | collective-permute-start | bytes 221192 | tf_op jit(solution)/shard_map/ppermute | solution.py:50
  14.6 1.5 %collective-permute-start.10 = (bf16[96,2304]{1,0:T(8,128)(2,1)S(1)}, bf16[96,2304]{1,0:T(8,128)(2,1)S(1)}, u32[]{:S(2)}, u32[]{:S(2)}) collective-permute-start(bf16[96,2304]{1,0:T(8,128)(2,1)S(1)} %get-tuple-element.50.refs_3_), channel_id=1, source_target_pairs={{0,4},{4,0},{8,12},{12,8},{1,5},{5,1},{9,13},{13,9},{2,6},{6,2},{1... | collective-permute-start | bytes 1327112 | tf_op jit(solution)/shard_map/ppermute | solution.py:50
  16.1 0.8 collective-permute-start.6
  16.9 8.1 %collective-permute-done = bf16[48,768]{1,0:T(8,128)(2,1)S(1)} collective-permute-done((bf16[48,768]{1,0:T(8,128)(2,1)}, bf16[48,768]{1,0:T(8,128)(2,1)S(1)}, u32[]{:S(2)}, u32[]{:S(2)}) %collective-permute-start) | collective-permute-done | bytes 73760 | tf_op jit(solution)/shard_map/ppermute | solution.py:50
  25.0 0.9 pad_maximum_fusion
  26.0 8.6 %encode.1 = (bf16[512,768]{1,0:T(8,128)(2,1)S(1)}, bf16[512,768]{1,0:T(8,128)(2,1)S(1)}) custom-call(s32[3]{0:T(128)S(1)} %pad_add_fusion.place.refs_0_, f32[16,32,768]{2,1,0:T(8,128)S(1)} %get-tuple-element.51.tokens, bf16[7,32,768]{2,1,0:T(8,128)(2,1)S(1)} %collective-permute-done.2.above, bf16[23,8,768]{2,1,0:T(8,128)(2,1)S(1)} %collective-permute-done.3.beside, ...), custom_call_target="tpu_custom_call" | custom-call | flops 115000000 | tf_op jit(solution)/shard_map/encode/pallas_call | solution.py:187
  34.6 1.3 %collective-permute-start.8 = (bf16[96,1152]{1,0:T(8,128)(2,1)S(1)}, bf16[96,1152]{1,0:T(8,128)(2,1)S(1)}, u32[]{:S(2)}, u32[]{:S(2)}) collective-permute-start(bf16[96,1152]{1,0:T(8,128)(2,1)S(1)} %collective-permute-done.6.refs_5_), channel_id=1, source_target_pairs={{0,16},{16,0},{1,17},{17,1},{2,18},{18,2},{3,19},{19,3},{4,20},{20... | collective-permute-start | bytes 663560 | tf_op jit(solution)/shard_map/ppermute | solution.py:50
  35.9 0.7 collective-permute-start.9
  36.6 0.7 collective-permute-start.15
  37.6 1.1 %collective-permute-start.11 = (bf16[96,2304]{1,0:T(8,128)(2,1)S(1)}, bf16[96,2304]{1,0:T(8,128)(2,1)S(1)}, u32[]{:S(2)}, u32[]{:S(2)}) collective-permute-start(bf16[96,2304]{1,0:T(8,128)(2,1)S(1)} %collective-permute-done.7.refs_4_), channel_id=1, source_target_pairs={{0,4},{4,0},{8,12},{12,8},{1,5},{5,1},{9,13},{13,9},{2,6},{6,2},{1... | collective-permute-start | bytes 1327112 | tf_op jit(solution)/shard_map/ppermute | solution.py:50
  38.8 2.4 %collective-permute-done.8.refs_6_ = bf16[96,1152]{1,0:T(8,128)(2,1)S(1)} collective-permute-done((bf16[96,1152]{1,0:T(8,128)(2,1)S(1)}, bf16[96,1152]{1,0:T(8,128)(2,1)S(1)}, u32[]{:S(2)}, u32[]{:S(2)}) %collective-permute-start.8) | collective-permute-done | bytes 221216 | tf_op jit(solution)/shard_map/ppermute | solution.py:50
  41.2 1.4 %collective-permute-start.13 = (bf16[96,1152]{1,0:T(8,128)(2,1)S(1)}, bf16[96,1152]{1,0:T(8,128)(2,1)S(1)}, u32[]{:S(2)}, u32[]{:S(2)}) collective-permute-start(bf16[96,1152]{1,0:T(8,128)(2,1)S(1)} %collective-permute-done.8.refs_6_), channel_id=1, source_target_pairs={{0,4},{4,0},{8,12},{12,8},{1,5},{5,1},{9,13},{13,9},{2,6},{6,2},{1... | collective-permute-start | bytes 663560 | tf_op jit(solution)/shard_map/ppermute | solution.py:50
  42.6 2.4 %collective-permute-start.14 = (bf16[96,1152]{1,0:T(8,128)(2,1)S(1)}, bf16[96,1152]{1,0:T(8,128)(2,1)S(1)}, u32[]{:S(2)}, u32[]{:S(2)}) collective-permute-start(bf16[96,1152]{1,0:T(8,128)(2,1)S(1)} %collective-permute-done.9.refs_7_), channel_id=1, source_target_pairs={{0,4},{4,0},{8,12},{12,8},{1,5},{5,1},{9,13},{13,9},{2,6},{6,2},{1... | collective-permute-start | bytes 663560 | tf_op jit(solution)/shard_map/ppermute | solution.py:50
  45.0 1.8 %collective-permute-done.15.refs_13_ = bf16[96,1152]{1,0:T(8,128)(2,1)S(1)} collective-permute-done((bf16[96,1152]{1,0:T(8,128)(2,1)S(1)}, bf16[96,1152]{1,0:T(8,128)(2,1)S(1)}, u32[]{:S(2)}, u32[]{:S(2)}) %collective-permute-start.15) | collective-permute-done | bytes 221216 | tf_op jit(solution)/shard_map/ppermute | solution.py:539
  46.8 1.7 %collective-permute-start.16 = (bf16[96,1152]{1,0:T(8,128)(2,1)S(1)}, bf16[96,1152]{1,0:T(8,128)(2,1)S(1)}, u32[]{:S(2)}, u32[]{:S(2)}) collective-permute-start(bf16[96,1152]{1,0:T(8,128)(2,1)S(1)} %collective-permute-done.15.refs_13_), channel_id=1, source_target_pairs={{0,4},{4,0},{8,12},{12,8},{1,5},{5,1},{9,13},{13,9},{2,6},{6,2},{1... | collective-permute-start | bytes 663560 | tf_op jit(solution)/shard_map/ppermute | solution.py:50
  48.5 0.8 collective-permute-start.5
  49.6 8.6 %attend.1.refs_1_ = bf16[512,768]{1,0:T(8,128)(2,1)S(1)} custom-call(s32[3]{0:T(128)S(1)} %pad_add_fusion.place.refs_0_, bf16[512,768]{1,0:T(8,128)(2,1)S(1)} %get-tuple-element.55.refs_1_, f32[6,64,256]{2,1,0:T(8,128)S(1)} %get-tuple-element.56.refs_2_, bf16[96,2304]{1,0:T(8,128)(2,1)S(1)} %get-tuple-element.50.refs_3_, ...), custom_call_target="tpu_custom_call" | custom-call | flops 11500000256 | tf_op jit(solution)/shard_map/attend/pallas_call | solution.py:297
  58.6 1.2 %collective-permute-done.18.refs_6_ = bf16[192,768]{1,0:T(8,128)(2,1)S(1)} collective-permute-done((bf16[192,768]{1,0:T(8,128)(2,1)S(1)}, bf16[192,768]{1,0:T(8,128)(2,1)S(1)}, u32[]{:S(2)}, u32[]{:S(2)}) %collective-permute-start.18) | collective-permute-done | bytes 294944 | tf_op jit(solution)/shard_map/ppermute | solution.py:50
  59.9 3.1 %project.1 = (bf16[16,32,768]{2,1,0:T(8,128)(2,1)S(1)}, bf16[4,32,768]{2,1,0:T(8,128)(2,1)S(1)}, bf16[48,768]{1,0:T(8,128)(2,1)S(1)}, bf16[16,768]{1,0:T(8,128)(2,1)S(1)}) custom-call(s32[3]{0:T(128)S(1)} %pad_add_fusion.place.refs_0_, bf16[512,768]{1,0:T(8,128)(2,1)S(1)} %attend.1.refs_1_, bf16[512,768]{1,0:T(8,128)(2,1)S(1)} %get-tuple-element.60.refs_2_, ...), custom_call_target="tpu_custom_call" | custom-call | flops 3449999872 | tf_op jit(solution)/shard_map/project/pallas_call | solution.py:366
  63.4 1.4 %collective-permute-start.20 = (bf16[48,768]{1,0:T(8,128)(2,1)S(1)}, bf16[48,768]{1,0:T(8,128)(2,1)S(1)}, u32[]{:S(2)}, u32[]{:S(2)}) collective-permute-start(bf16[48,768]{1,0:T(8,128)(2,1)S(1)} %get-tuple-element.64), channel_id=1, source_target_pairs={{0,3},{1,0},{2,1},{3,2},{4,7},{5,4},{6,5},{7,6},{8,11},{9,8},{10,9... | collective-permute-start | bytes 221192 | tf_op jit(solution)/shard_map/ppermute | solution.py:35
  64.8 3.1 %collective-permute-start.21 = (bf16[16,768]{1,0:T(8,128)(2,1)S(1)}, bf16[16,768]{1,0:T(8,128)(2,1)S(1)}, u32[]{:S(2)}, u32[]{:S(2)}) collective-permute-start(bf16[16,768]{1,0:T(8,128)(2,1)S(1)} %get-tuple-element.65), channel_id=1, source_target_pairs={{0,15},{1,12},{2,13},{3,14},{4,3},{5,0},{6,1},{7,2},{8,7},{9,4},{1... | collective-permute-start | bytes 73736 | tf_op jit(solution)/shard_map/ppermute | solution.py:45
  68.0 1.1 %collective-permute-done.21.corner = bf16[16,768]{1,0:T(8,128)(2,1)S(1)} collective-permute-done((bf16[16,768]{1,0:T(8,128)(2,1)S(1)}, bf16[16,768]{1,0:T(8,128)(2,1)S(1)}, u32[]{:S(2)}, u32[]{:S(2)}) %collective-permute-start.21) | collective-permute-done | bytes 24608 | tf_op jit(solution)/shard_map/ppermute | solution.py:45
  69.1 1.6 %dispatch.1 = (bf16[512,768]{1,0:T(8,128)(2,1)S(1)}, bf16[64,768]{1,0:T(8,128)(2,1)S(1)}, bf16[64,768]{1,0:T(8,128)(2,1)S(1)}, bf16[64,768]{1,0:T(8,128)(2,1)S(1...) custom-call(s32[3]{0:T(128)S(1)} %pad_add_fusion.place.refs_0_, ...), custom_call_target="tpu_custom_call" | custom-call | tf_op jit(solution)/shard_map/dispatch/pallas_call | solution.py:429
  71.1 0.6 collective-permute-start.26
  71.7 1.2 %collective-permute-start.27 = (bf16[64,768]{1,0:T(8,128)(2,1)S(1)}, bf16[64,768]{1,0:T(8,128)(2,1)S(1)}, u32[]{:S(2)}, u32[]{:S(2)}) collective-permute-start(bf16[64,768]{1,0:T(8,128)(2,1)S(1)} %get-tuple-element.75), channel_id=1, source_target_pairs={{0,12},{4,8},{8,4},{12,0},{1,13},{5,9},{9,5},{13,1},{2,14},{6,10},... | collective-permute-start | bytes 294920 | tf_op jit(solution)/shard_map/ppermute | solution.py:50
  73.0 0.7 collective-permute-start.23
  73.7 1.4 %collective-permute-start.24 = (bf16[64,768]{1,0:T(8,128)(2,1)S(1)}, bf16[64,768]{1,0:T(8,128)(2,1)S(1)}, u32[]{:S(2)}, u32[]{:S(2)}) collective-permute-start(bf16[64,768]{1,0:T(8,128)(2,1)S(1)} %get-tuple-element.70), channel_id=1, source_target_pairs={{0,12},{4,8},{8,4},{12,0},{1,13},{5,9},{9,5},{13,1},{2,14},{6,10},... | collective-permute-start | bytes 294920 | tf_op jit(solution)/shard_map/ppermute | solution.py:50
  75.2 3.2 %collective-permute-done.27.refs_3_ = bf16[64,768]{1,0:T(8,128)(2,1)S(1)} collective-permute-done((bf16[64,768]{1,0:T(8,128)(2,1)S(1)}, bf16[64,768]{1,0:T(8,128)(2,1)S(1)}, u32[]{:S(2)}, u32[]{:S(2)}) %collective-permute-start.27) | collective-permute-done | bytes 98336 | tf_op jit(solution)/shard_map/ppermute | solution.py:50
  78.4 7.6 %experts.3 = (bf16[64,768]{1,0:T(8,128)(2,1)S(1)}, bf16[64,768]{1,0:T(8,128)(2,1)S(1)}, bf16[64,768]{1,0:T(8,128)(2,1)S(1)}, bf16[64,768]{1,0:T(8,128)(2,1)S(1)}) custom-call(bf16[64,768]{1,0:T(8,128)(2,1)S(1)} %get-tuple-element.72.refs_0_, bf16[64,768]{1,0:T(8,128)(2,1)S(1)} %collective-permute-done.25.refs_1_, ...), custom_call_target="tpu_custom_call" | custom-call | flops 8049999872 | tf_op jit(solution)/shard_map/experts/pallas_call | solution.py:471
  86.0 0.8 collective-permute-start.31
  86.8 1.4 %collective-permute-start.33 = (bf16[64,768]{1,0:T(8,128)(2,1)S(1)}, bf16[64,768]{1,0:T(8,128)(2,1)S(1)}, u32[]{:S(2)}, u32[]{:S(2)}) collective-permute-start(bf16[64,768]{1,0:T(8,128)(2,1)S(1)} %get-tuple-element.82), channel_id=1, source_target_pairs={{0,12},{4,8},{8,4},{12,0},{1,13},{5,9},{9,5},{13,1},{2,14},{6,10},... | collective-permute-start | bytes 294920 | tf_op jit(solution)/shard_map/ppermute | solution.py:50
  88.2 7.6 %experts.2 = (bf16[64,768]{1,0:T(8,128)(2,1)S(1)}, bf16[64,768]{1,0:T(8,128)(2,1)S(1)}, bf16[64,768]{1,0:T(8,128)(2,1)S(1)}, bf16[64,768]{1,0:T(8,128)(2,1)S(1)}) custom-call(bf16[64,768]{1,0:T(8,128)(2,1)S(1)} %get-tuple-element.67.refs_0_, bf16[64,768]{1,0:T(8,128)(2,1)S(1)} %collective-permute-done.22.refs_1_, ...), custom_call_target="tpu_custom_call" | custom-call | flops 8049999872 | tf_op jit(solution)/shard_map/experts/pallas_call | solution.py:471
  95.8 0.8 collective-permute-start.30
  96.6 1.4 %collective-permute-start.32 = (bf16[64,768]{1,0:T(8,128)(2,1)S(1)}, bf16[64,768]{1,0:T(8,128)(2,1)S(1)}, u32[]{:S(2)}, u32[]{:S(2)}) collective-permute-start(bf16[64,768]{1,0:T(8,128)(2,1)S(1)} %get-tuple-element.81), channel_id=1, source_target_pairs={{0,12},{4,8},{8,4},{12,0},{1,13},{5,9},{9,5},{13,1},{2,14},{6,10},... | collective-permute-start | bytes 294920 | tf_op jit(solution)/shard_map/ppermute | solution.py:50
  98.5 1.3 %collective-permute-done.30.refs_4_ = bf16[64,768]{1,0:T(8,128)(2,1)S(1)} collective-permute-done((bf16[64,768]{1,0:T(8,128)(2,1)S(1)}, bf16[64,768]{1,0:T(8,128)(2,1)S(1)}, u32[]{:S(2)}, u32[]{:S(2)}) %collective-permute-start.30) | collective-permute-done | bytes 98336 | tf_op jit(solution)/shard_map/ppermute | solution.py:50
  99.8 2.7 %collective-permute-done.32.refs_6_ = bf16[64,768]{1,0:T(8,128)(2,1)S(1)} collective-permute-done((bf16[64,768]{1,0:T(8,128)(2,1)S(1)}, bf16[64,768]{1,0:T(8,128)(2,1)S(1)}, u32[]{:S(2)}, u32[]{:S(2)}) %collective-permute-start.32) | collective-permute-done | bytes 98336 | tf_op jit(solution)/shard_map/ppermute | solution.py:50
  102.5 2.3 %combine.1 = bf16[512,768]{1,0:T(8,128)(2,1)} custom-call(s32[3]{0:T(128)S(1)} %pad_add_fusion.place.refs_0_, bf16[512,768]{1,0:T(8,128)(2,1)S(1)} %get-tuple-element.66.attended, s32[512,1]{1,0:T(8,128)S(1)} %select_n.42.position, s32[512,1]{1,0:T(8,128)S(1)} %select_n.43.constant_at, f32[16,768]{1,0:T(8,128)S(1)} %copy-done.1, ...), custom_call_target="tpu_custom_call" | custom-call | tf_op jit(solution)/shard_map/combine/pallas_call | solution.py:509
  (57 shorter events, 3.1 us)
Async XLA Ops:
  0.0 38.7 %copy-start.5 = (bf16[48,768]{1,0:T(8,128)(2,1)S(1)}, bf16[48,768]{1,0:T(8,128)(2,1)}, u32[]{:S(2)}) copy-start(bf16[48,768]{1,0:T(8,128)(2,1)} %param.14) | copy-start | bytes 221188
  1.0 9.0 %collective-permute-start.2 = (bf16[7,32,768]{2,1,0:T(8,128)(2,1)S(1)}, bf16[7,32,768]{2,1,0:T(8,128)(2,1)S(1)}, u32[]{:S(2)}, u32[]{:S(2)}) collective-permute-start(bf16[7,32,768]{2,1,0:T(8,128)(2,1)S(1)} %slice.3), channel_id=1, source_target_pairs={{0,4},{4,8},{8,12},{12,0},{1,5},{5,9},{9,13},{13,1},{2,6},{6,10},{... | collective-permute-start | bytes 1032200 | tf_op jit(solution)/shard_map/ppermute | solution.py:35
  3.7 6.4 %collective-permute-start.1 = (bf16[48,2304]{1,0:T(8,128)(2,1)}, bf16[48,2304]{1,0:T(8,128)(2,1)S(1)}, u32[]{:S(2)}, u32[]{:S(2)}) collective-permute-start(bf16[48,2304]{1,0:T(8,128)(2,1)} %refs_0_.1), channel_id=1, source_target_pairs={{0,1},{1,0},{2,3},{3,2},{4,5},{5,4},{6,7},{7,6},{8,9},{9,8},{10,11... | collective-permute-start | bytes 663560 | tf_op jit(solution)/shard_map/ppermute | solution.py:50
  5.1 1.1 %copy-start = (bf16[16,32,768]{2,1,0:T(8,128)(2,1)S(1)}, bf16[16,32,768]{2,1,0:T(8,128)(2,1)}, u32[]{:S(2)}) copy-start(bf16[16,32,768]{2,1,0:T(8,128)(2,1)} %tokens.1) | copy-start | bytes 2359300
  6.2 1.1 %copy-start.2 = (f32[24,64,64]{2,1,0:T(8,128)S(1)}, f32[24,64,64]{2,1,0:T(8,128)}, u32[]{:S(2)}) copy-start(f32[24,64,64]{2,1,0:T(8,128)} %rel_bias.1) | copy-start | bytes 1179652
  7.3 0.9 copy-start.3
  8.3 0.9 copy-start.4
  10.7 14.3 %collective-permute-start.3 = (bf16[23,8,768]{2,1,0:T(8,128)(2,1)S(1)}, bf16[23,8,768]{2,1,0:T(8,128)(2,1)S(1)}, u32[]{:S(2)}, u32[]{:S(2)}) collective-permute-start(bf16[23,8,768]{2,1,0:T(8,128)(2,1)S(1)} %get-tuple-element.46), channel_id=1, source_target_pairs={{0,1},{1,2},{2,3},{3,0},{4,5},{5,6},{6,7},{7,4},{8,9},{9,10},{10,1... | collective-permute-start | bytes 847880 | tf_op jit(solution)/shard_map/ppermute | solution.py:35
  12.5 22.2 %collective-permute-start.7 = (bf16[96,2304]{1,0:T(8,128)(2,1)S(1)}, bf16[96,2304]{1,0:T(8,128)(2,1)S(1)}, u32[]{:S(2)}, u32[]{:S(2)}) collective-permute-start(bf16[96,2304]{1,0:T(8,128)(2,1)S(1)} %get-tuple-element.50.refs_3_), channel_id=1, source_target_pairs={{0,8},{4,12},{8,0},{12,4},{1,9},{5,13},{9,1},{13,5},{2,10},{6,14},... | collective-permute-start | bytes 1327112 | tf_op jit(solution)/shard_map/ppermute | solution.py:50
  13.3 11.7 %collective-permute-start = (bf16[48,768]{1,0:T(8,128)(2,1)}, bf16[48,768]{1,0:T(8,128)(2,1)S(1)}, u32[]{:S(2)}, u32[]{:S(2)}) collective-permute-start(bf16[48,768]{1,0:T(8,128)(2,1)} %param.14), channel_id=1, source_target_pairs={{0,1},{1,0},{2,3},{3,2},{4,5},{5,4},{6,7},{7,6},{8,9},{9,8},{10,11... | collective-permute-start | bytes 221192 | tf_op jit(solution)/shard_map/ppermute | solution.py:50
  14.6 24.1 %collective-permute-start.10 = (bf16[96,2304]{1,0:T(8,128)(2,1)S(1)}, bf16[96,2304]{1,0:T(8,128)(2,1)S(1)}, u32[]{:S(2)}, u32[]{:S(2)}) collective-permute-start(bf16[96,2304]{1,0:T(8,128)(2,1)S(1)} %get-tuple-element.50.refs_3_), channel_id=1, source_target_pairs={{0,4},{4,0},{8,12},{12,8},{1,5},{5,1},{9,13},{13,9},{2,6},{6,2},{1... | collective-permute-start | bytes 1327112 | tf_op jit(solution)/shard_map/ppermute | solution.py:50
  16.1 18.5 %collective-permute-start.6 = (bf16[96,1152]{1,0:T(8,128)(2,1)S(1)}, bf16[96,1152]{1,0:T(8,128)(2,1)S(1)}, u32[]{:S(2)}, u32[]{:S(2)}) collective-permute-start(bf16[96,1152]{1,0:T(8,128)(2,1)S(1)} %get-tuple-element.49), channel_id=1, source_target_pairs={{0,2},{1,3},{2,0},{3,1},{4,6},{5,7},{6,4},{7,5},{8,10},{9,11},{10,... | collective-permute-start | bytes 663560 | tf_op jit(solution)/shard_map/ppermute | solution.py:50
  25.9 11.7 %collective-permute-start.4 = (bf16[96,768]{1,0:T(8,128)(2,1)S(1)}, bf16[96,768]{1,0:T(8,128)(2,1)S(1)}, u32[]{:S(2)}, u32[]{:S(2)}) collective-permute-start(bf16[96,768]{1,0:T(8,128)(2,1)S(1)} %pad_maximum_fusion), channel_id=1, source_target_pairs={{0,2},{1,3},{2,0},{3,1},{4,6},{5,7},{6,4},{7,5},{8,10},{9,11},{10,... | collective-permute-start | bytes 442376 | tf_op jit(solution)/shard_map/ppermute | solution.py:50
  34.6 6.6 %collective-permute-start.8 = (bf16[96,1152]{1,0:T(8,128)(2,1)S(1)}, bf16[96,1152]{1,0:T(8,128)(2,1)S(1)}, u32[]{:S(2)}, u32[]{:S(2)}) collective-permute-start(bf16[96,1152]{1,0:T(8,128)(2,1)S(1)} %collective-permute-done.6.refs_5_), channel_id=1, source_target_pairs={{0,16},{16,0},{1,17},{17,1},{2,18},{18,2},{3,19},{19,3},{4,20},{20... | collective-permute-start | bytes 663560 | tf_op jit(solution)/shard_map/ppermute | solution.py:50
  35.9 6.7 %collective-permute-start.9 = (bf16[96,1152]{1,0:T(8,128)(2,1)S(1)}, bf16[96,1152]{1,0:T(8,128)(2,1)S(1)}, u32[]{:S(2)}, u32[]{:S(2)}) collective-permute-start(bf16[96,1152]{1,0:T(8,128)(2,1)S(1)} %collective-permute-done.6.refs_5_), channel_id=1, source_target_pairs={{0,8},{4,12},{8,0},{12,4},{1,9},{5,13},{9,1},{13,5},{2,10},{6,14},... | collective-permute-start | bytes 663560 | tf_op jit(solution)/shard_map/ppermute | solution.py:50
  36.6 10.2 %collective-permute-start.15 = (bf16[96,1152]{1,0:T(8,128)(2,1)S(1)}, bf16[96,1152]{1,0:T(8,128)(2,1)S(1)}, u32[]{:S(2)}, u32[]{:S(2)}) collective-permute-start(bf16[96,1152]{1,0:T(8,128)(2,1)S(1)} %collective-permute-done.6.refs_5_), channel_id=1, source_target_pairs={{0,24},{4,28},{8,16},{12,20},{16,8},{20,12},{24,0},{28,4},{1,25},{... | collective-permute-start | bytes 663560 | tf_op jit(solution)/shard_map/ppermute | solution.py:539
  37.6 12.0 %collective-permute-start.11 = (bf16[96,2304]{1,0:T(8,128)(2,1)S(1)}, bf16[96,2304]{1,0:T(8,128)(2,1)S(1)}, u32[]{:S(2)}, u32[]{:S(2)}) collective-permute-start(bf16[96,2304]{1,0:T(8,128)(2,1)S(1)} %collective-permute-done.7.refs_4_), channel_id=1, source_target_pairs={{0,4},{4,0},{8,12},{12,8},{1,5},{5,1},{9,13},{13,9},{2,6},{6,2},{1... | collective-permute-start | bytes 1327112 | tf_op jit(solution)/shard_map/ppermute | solution.py:50
  38.7 9.8 %collective-permute-start.12 = (bf16[96,1152]{1,0:T(8,128)(2,1)S(1)}, bf16[96,1152]{1,0:T(8,128)(2,1)S(1)}, u32[]{:S(2)}, u32[]{:S(2)}) collective-permute-start(bf16[96,1152]{1,0:T(8,128)(2,1)S(1)} %collective-permute-done.6.refs_5_), channel_id=1, source_target_pairs={{0,4},{4,0},{8,12},{12,8},{1,5},{5,1},{9,13},{13,9},{2,6},{6,2},{1... | collective-permute-start | bytes 663560 | tf_op jit(solution)/shard_map/ppermute | solution.py:50
  41.2 8.1 %collective-permute-start.13 = (bf16[96,1152]{1,0:T(8,128)(2,1)S(1)}, bf16[96,1152]{1,0:T(8,128)(2,1)S(1)}, u32[]{:S(2)}, u32[]{:S(2)}) collective-permute-start(bf16[96,1152]{1,0:T(8,128)(2,1)S(1)} %collective-permute-done.8.refs_6_), channel_id=1, source_target_pairs={{0,4},{4,0},{8,12},{12,8},{1,5},{5,1},{9,13},{13,9},{2,6},{6,2},{1... | collective-permute-start | bytes 663560 | tf_op jit(solution)/shard_map/ppermute | solution.py:50
  42.6 6.9 %collective-permute-start.14 = (bf16[96,1152]{1,0:T(8,128)(2,1)S(1)}, bf16[96,1152]{1,0:T(8,128)(2,1)S(1)}, u32[]{:S(2)}, u32[]{:S(2)}) collective-permute-start(bf16[96,1152]{1,0:T(8,128)(2,1)S(1)} %collective-permute-done.9.refs_7_), channel_id=1, source_target_pairs={{0,4},{4,0},{8,12},{12,8},{1,5},{5,1},{9,13},{13,9},{2,6},{6,2},{1... | collective-permute-start | bytes 663560 | tf_op jit(solution)/shard_map/ppermute | solution.py:50
  46.8 2.8 %collective-permute-start.16 = (bf16[96,1152]{1,0:T(8,128)(2,1)S(1)}, bf16[96,1152]{1,0:T(8,128)(2,1)S(1)}, u32[]{:S(2)}, u32[]{:S(2)}) collective-permute-start(bf16[96,1152]{1,0:T(8,128)(2,1)S(1)} %collective-permute-done.15.refs_13_), channel_id=1, source_target_pairs={{0,4},{4,0},{8,12},{12,8},{1,5},{5,1},{9,13},{13,9},{2,6},{6,2},{1... | collective-permute-start | bytes 663560 | tf_op jit(solution)/shard_map/ppermute | solution.py:50
  48.5 9.7 %collective-permute-start.5 = (bf16[192,768]{1,0:T(8,128)(2,1)S(1)}, bf16[192,768]{1,0:T(8,128)(2,1)S(1)}, u32[]{:S(2)}, u32[]{:S(2)}) collective-permute-start(bf16[192,768]{1,0:T(8,128)(2,1)S(1)} %constant_dynamic-update-slice_fusion.refs_3_), channel_id=1, source_target_pairs={{0,8},{4,12},{8,0},{12,4},{1,9},{5,13},{9,1},{13,5},{2,10},{6,14},... | collective-permute-start | bytes 884744 | tf_op jit(solution)/shard_map/ppermute | solution.py:50
  49.3 9.4 %collective-permute-start.17 = (bf16[192,768]{1,0:T(8,128)(2,1)S(1)}, bf16[192,768]{1,0:T(8,128)(2,1)S(1)}, u32[]{:S(2)}, u32[]{:S(2)}) collective-permute-start(bf16[192,768]{1,0:T(8,128)(2,1)S(1)} %constant_dynamic-update-slice_fusion.refs_3_), channel_id=1, source_target_pairs={{0,4},{4,0},{8,12},{12,8},{1,5},{5,1},{9,13},{13,9},{2,6},{6,2},{1... | collective-permute-start | bytes 884744 | tf_op jit(solution)/shard_map/ppermute | solution.py:50
  49.6 18.3 %copy-start.6 = (s32[16,32]{1,0:T(8,128)S(1)}, s32[16,32]{1,0:T(8,128)}, u32[]{:S(2)}) copy-start(s32[16,32]{1,0:T(8,128)} %param.21) | copy-start | bytes 6148
  49.6 18.3 %copy-start.7 = (s32[16,32]{1,0:T(8,128)S(1)}, s32[16,32]{1,0:T(8,128)}, u32[]{:S(2)}) copy-start(s32[16,32]{1,0:T(8,128)} %param.19) | copy-start | bytes 6148
  49.6 18.3 %copy-start.8 = (s32[16,32]{1,0:T(8,128)S(1)}, s32[16,32]{1,0:T(8,128)}, u32[]{:S(2)}) copy-start(s32[16,32]{1,0:T(8,128)} %param.20) | copy-start | bytes 6148
  58.2 1.6 %collective-permute-start.18 = (bf16[192,768]{1,0:T(8,128)(2,1)S(1)}, bf16[192,768]{1,0:T(8,128)(2,1)S(1)}, u32[]{:S(2)}, u32[]{:S(2)}) collective-permute-start(bf16[192,768]{1,0:T(8,128)(2,1)S(1)} %collective-permute-done.5.refs_4_), channel_id=1, source_target_pairs={{0,4},{4,0},{8,12},{12,8},{1,5},{5,1},{9,13},{13,9},{2,6},{6,2},{1... | collective-permute-start | bytes 884744 | tf_op jit(solution)/shard_map/ppermute | solution.py:50
  63.0 6.2 %collective-permute-start.19 = (bf16[4,32,768]{2,1,0:T(8,128)(2,1)S(1)}, bf16[4,32,768]{2,1,0:T(8,128)(2,1)S(1)}, u32[]{:S(2)}, u32[]{:S(2)}) collective-permute-start(bf16[4,32,768]{2,1,0:T(8,128)(2,1)S(1)} %get-tuple-element.63), channel_id=1, source_target_pairs={{0,12},{4,0},{8,4},{12,8},{1,13},{5,1},{9,5},{13,9},{2,14},{6,2},{... | collective-permute-start | bytes 589832 | tf_op jit(solution)/shard_map/ppermute | solution.py:35
  63.4 5.7 %collective-permute-start.20 = (bf16[48,768]{1,0:T(8,128)(2,1)S(1)}, bf16[48,768]{1,0:T(8,128)(2,1)S(1)}, u32[]{:S(2)}, u32[]{:S(2)}) collective-permute-start(bf16[48,768]{1,0:T(8,128)(2,1)S(1)} %get-tuple-element.64), channel_id=1, source_target_pairs={{0,3},{1,0},{2,1},{3,2},{4,7},{5,4},{6,5},{7,6},{8,11},{9,8},{10,9... | collective-permute-start | bytes 221192 | tf_op jit(solution)/shard_map/ppermute | solution.py:35
  64.8 4.3 %collective-permute-start.21 = (bf16[16,768]{1,0:T(8,128)(2,1)S(1)}, bf16[16,768]{1,0:T(8,128)(2,1)S(1)}, u32[]{:S(2)}, u32[]{:S(2)}) collective-permute-start(bf16[16,768]{1,0:T(8,128)(2,1)S(1)} %get-tuple-element.65), channel_id=1, source_target_pairs={{0,15},{1,12},{2,13},{3,14},{4,3},{5,0},{6,1},{7,2},{8,7},{9,4},{1... | collective-permute-start | bytes 73736 | tf_op jit(solution)/shard_map/ppermute | solution.py:45
  70.8 2.9 %collective-permute-start.25 = (bf16[64,768]{1,0:T(8,128)(2,1)S(1)}, bf16[64,768]{1,0:T(8,128)(2,1)S(1)}, u32[]{:S(2)}, u32[]{:S(2)}) collective-permute-start(bf16[64,768]{1,0:T(8,128)(2,1)S(1)} %get-tuple-element.73), channel_id=1, source_target_pairs={{0,4},{4,0},{8,12},{12,8},{1,5},{5,1},{9,13},{13,9},{2,6},{6,2},{1... | collective-permute-start | bytes 294920 | tf_op jit(solution)/shard_map/ppermute | solution.py:50
  71.1 4.1 %collective-permute-start.26 = (bf16[64,768]{1,0:T(8,128)(2,1)S(1)}, bf16[64,768]{1,0:T(8,128)(2,1)S(1)}, u32[]{:S(2)}, u32[]{:S(2)}) collective-permute-start(bf16[64,768]{1,0:T(8,128)(2,1)S(1)} %get-tuple-element.74), channel_id=1, source_target_pairs={{0,8},{4,12},{8,0},{12,4},{1,9},{5,13},{9,1},{13,5},{2,10},{6,14},... | collective-permute-start | bytes 294920 | tf_op jit(solution)/shard_map/ppermute | solution.py:50
  71.7 6.7 %collective-permute-start.27 = (bf16[64,768]{1,0:T(8,128)(2,1)S(1)}, bf16[64,768]{1,0:T(8,128)(2,1)S(1)}, u32[]{:S(2)}, u32[]{:S(2)}) collective-permute-start(bf16[64,768]{1,0:T(8,128)(2,1)S(1)} %get-tuple-element.75), channel_id=1, source_target_pairs={{0,12},{4,8},{8,4},{12,0},{1,13},{5,9},{9,5},{13,1},{2,14},{6,10},... | collective-permute-start | bytes 294920 | tf_op jit(solution)/shard_map/ppermute | solution.py:50
  73.0 13.8 %collective-permute-start.22 = (bf16[64,768]{1,0:T(8,128)(2,1)S(1)}, bf16[64,768]{1,0:T(8,128)(2,1)S(1)}, u32[]{:S(2)}, u32[]{:S(2)}) collective-permute-start(bf16[64,768]{1,0:T(8,128)(2,1)S(1)} %get-tuple-element.68), channel_id=1, source_target_pairs={{0,4},{4,0},{8,12},{12,8},{1,5},{5,1},{9,13},{13,9},{2,6},{6,2},{1... | collective-permute-start | bytes 294920 | tf_op jit(solution)/shard_map/ppermute | solution.py:50
  73.0 15.2 %collective-permute-start.23 = (bf16[64,768]{1,0:T(8,128)(2,1)S(1)}, bf16[64,768]{1,0:T(8,128)(2,1)S(1)}, u32[]{:S(2)}, u32[]{:S(2)}) collective-permute-start(bf16[64,768]{1,0:T(8,128)(2,1)S(1)} %get-tuple-element.69), channel_id=1, source_target_pairs={{0,8},{4,12},{8,0},{12,4},{1,9},{5,13},{9,1},{13,5},{2,10},{6,14},... | collective-permute-start | bytes 294920 | tf_op jit(solution)/shard_map/ppermute | solution.py:50
  73.7 14.5 %collective-permute-start.24 = (bf16[64,768]{1,0:T(8,128)(2,1)S(1)}, bf16[64,768]{1,0:T(8,128)(2,1)S(1)}, u32[]{:S(2)}, u32[]{:S(2)}) collective-permute-start(bf16[64,768]{1,0:T(8,128)(2,1)S(1)} %get-tuple-element.70), channel_id=1, source_target_pairs={{0,12},{4,8},{8,4},{12,0},{1,13},{5,9},{9,5},{13,1},{2,14},{6,10},... | collective-permute-start | bytes 294920 | tf_op jit(solution)/shard_map/ppermute | solution.py:50
  86.0 10.7 %collective-permute-start.29 = (bf16[64,768]{1,0:T(8,128)(2,1)S(1)}, bf16[64,768]{1,0:T(8,128)(2,1)S(1)}, u32[]{:S(2)}, u32[]{:S(2)}) collective-permute-start(bf16[64,768]{1,0:T(8,128)(2,1)S(1)} %get-tuple-element.78), channel_id=1, source_target_pairs={{0,4},{4,0},{8,12},{12,8},{1,5},{5,1},{9,13},{13,9},{2,6},{6,2},{1... | collective-permute-start | bytes 294920 | tf_op jit(solution)/shard_map/ppermute | solution.py:50
  86.0 12.5 %collective-permute-start.31 = (bf16[64,768]{1,0:T(8,128)(2,1)S(1)}, bf16[64,768]{1,0:T(8,128)(2,1)S(1)}, u32[]{:S(2)}, u32[]{:S(2)}) collective-permute-start(bf16[64,768]{1,0:T(8,128)(2,1)S(1)} %get-tuple-element.80), channel_id=1, source_target_pairs={{0,8},{4,12},{8,0},{12,4},{1,9},{5,13},{9,1},{13,5},{2,10},{6,14},... | collective-permute-start | bytes 294920 | tf_op jit(solution)/shard_map/ppermute | solution.py:50
  86.8 11.7 %collective-permute-start.33 = (bf16[64,768]{1,0:T(8,128)(2,1)S(1)}, bf16[64,768]{1,0:T(8,128)(2,1)S(1)}, u32[]{:S(2)}, u32[]{:S(2)}) collective-permute-start(bf16[64,768]{1,0:T(8,128)(2,1)S(1)} %get-tuple-element.82), channel_id=1, source_target_pairs={{0,12},{4,8},{8,4},{12,0},{1,13},{5,9},{9,5},{13,1},{2,14},{6,10},... | collective-permute-start | bytes 294920 | tf_op jit(solution)/shard_map/ppermute | solution.py:50
  88.2 14.4 %copy-start.1 = (f32[16,768]{1,0:T(8,128)S(1)}, f32[16,768]{1,0:T(8,128)}, u32[]{:S(2)}) copy-start(f32[16,768]{1,0:T(8,128)} %table.1) | copy-start | bytes 147460
  95.8 2.8 %collective-permute-start.28 = (bf16[64,768]{1,0:T(8,128)(2,1)S(1)}, bf16[64,768]{1,0:T(8,128)(2,1)S(1)}, u32[]{:S(2)}, u32[]{:S(2)}) collective-permute-start(bf16[64,768]{1,0:T(8,128)(2,1)S(1)} %get-tuple-element.77), channel_id=1, source_target_pairs={{0,4},{4,0},{8,12},{12,8},{1,5},{5,1},{9,13},{13,9},{2,6},{6,2},{1... | collective-permute-start | bytes 294920 | tf_op jit(solution)/shard_map/ppermute | solution.py:50
  95.8 4.0 %collective-permute-start.30 = (bf16[64,768]{1,0:T(8,128)(2,1)S(1)}, bf16[64,768]{1,0:T(8,128)(2,1)S(1)}, u32[]{:S(2)}, u32[]{:S(2)}) collective-permute-start(bf16[64,768]{1,0:T(8,128)(2,1)S(1)} %get-tuple-element.79), channel_id=1, source_target_pairs={{0,8},{4,12},{8,0},{12,4},{1,9},{5,13},{9,1},{13,5},{2,10},{6,14},... | collective-permute-start | bytes 294920 | tf_op jit(solution)/shard_map/ppermute | solution.py:50
  96.6 5.9 %collective-permute-start.32 = (bf16[64,768]{1,0:T(8,128)(2,1)S(1)}, bf16[64,768]{1,0:T(8,128)(2,1)S(1)}, u32[]{:S(2)}, u32[]{:S(2)}) collective-permute-start(bf16[64,768]{1,0:T(8,128)(2,1)S(1)} %get-tuple-element.81), channel_id=1, source_target_pairs={{0,12},{4,8},{8,4},{12,0},{1,13},{5,9},{9,5},{13,1},{2,14},{6,10},... | collective-permute-start | bytes 294920 | tf_op jit(solution)/shard_map/ppermute | solution.py:50

commit v9 on v8

--- a/solution.py
+++ b/solution.py
@@ -576,7 +576,7 @@
         column = jnp.concatenate([above[:, cols - HALO :], edge], axis=0)
     beside = shifted(column, "gx", 1)
     if quick:
-        own_out, beyond_out, beside = held(project_out, beyond_out, beside)
+        own_out, beside = held(project_out, beside)
         two_out = (jnp.concatenate([own_out, beyond_out], axis=0), pair, None)
         far_out = along(two_out, "gx", 2)
     encoded, normed = encode(place, kept, above, beside, weights)

time: 105 us -> 105 us (level)
    ppermute x4, waiting for transfers between devices: 0.01 us -> 4.68 us  [shifted(): return lax.ppermute(x, axis, [(i, (i + by) % size) for i in range(size)])]
    ppermute x28, waiting for transfers between devices: 19.9 us -> 15.3 us  [exchanged(): return lax.ppermute(x, axis, [(i, i ^ mask) for i in range(size)])]
  transfers between devices with their start and end apart: 34 -> 34, of which waited for: 11 -> 12; matrix products, arithmetic and copies ran while one was open for 2% -> 2% of each run, Pallas kernels for 31% -> 31%
where the time goes in v9:
time: 105 us
  Pallas kernels  40.2 us (38%)
  starting transfers between devices  34.7 us (33%)
  waiting for transfers between devices  22.9 us (22%)
  local copies, waits for them, and re-layouts  5.76 us (5%)
    ppermute x28, starting transfers between devices, exchanged(): return lax.ppermute(x, axis, [(i, i ^ mask) for i in range(size)])  24.6 us
    ppermute x28, waiting for transfers between devices, exchanged(): return lax.ppermute(x, axis, [(i, i ^ mask) for i in range(size)])  15.3 us
    pallas_call x2, Pallas kernels, serve(): pl.pallas_call(functools.partial(expert_kernel, count, first), out_shape=...  15.1 us
    pallas_call x1, Pallas kernels, encode(): pl.pallas_call(encode_kernel, out_shape=(flat, flat), in_specs=[SMEM] + [...  8.62 us
    pallas_call x1, Pallas kernels, attend(): pl.pallas_call(functools.partial(attend_kernel, shape, ids, grid_cols), o...  8.59 us
    ppermute x4, starting transfers between devices, shifted(): return lax.ppermute(x, axis, [(i, (i + by) % size) for i in range(size)])  6.29 us
    ppermute x4, waiting for transfers between devices, shifted(): return lax.ppermute(x, axis, [(i, (i + by) % size) for i in range(size)])  4.68 us
    unnamed x20, local copies, waits for them, and re-layouts  4.13 us
  transfers between devices with their start and end apart: 34, of which 12 were waited for; matrix products, arithmetic and copies ran while one was open for 2% of the time, Pallas kernels for 31%

profile of v9, /device:TPU:1, one launch (start us, length us, event | category | flops | bytes accessed | tf_op | source)
XLA Modules:
  0.0 104.8 jit_solution(17402166548772035363)
XLA Ops:
  0.0 1.0 slice.3
  1.0 2.7 %collective-permute-start.1 = (bf16[7,32,768]{2,1,0:T(8,128)(2,1)S(1)}, bf16[7,32,768]{2,1,0:T(8,128)(2,1)S(1)}, u32[]{:S(2)}, u32[]{:S(2)}) collective-permute-start(bf16[7,32,768]{2,1,0:T(8,128)(2,1)S(1)} %slice.3), channel_id=1, source_target_pairs={{0,4},{4,8},{8,12},{12,0},{1,5},{5,9},{9,13},{13,1},{2,6},{6,10},{... | collective-permute-start | bytes 1032200 | tf_op jit(solution)/shard_map/ppermute | solution.py:35
  3.7 1.3 %collective-permute-start = (bf16[48,2304]{1,0:T(8,128)(2,1)}, bf16[48,2304]{1,0:T(8,128)(2,1)S(1)}, u32[]{:S(2)}, u32[]{:S(2)}) collective-permute-start(bf16[48,2304]{1,0:T(8,128)(2,1)} %refs_0_.1), channel_id=1, source_target_pairs={{0,1},{1,0},{2,3},{3,2},{4,5},{5,4},{6,7},{7,6},{8,9},{9,8},{10,11... | collective-permute-start | bytes 663560 | tf_op jit(solution)/shard_map/ppermute | solution.py:50
  5.1 1.1 %copy-done = bf16[16,32,768]{2,1,0:T(8,128)(2,1)S(1)} copy-done((bf16[16,32,768]{2,1,0:T(8,128)(2,1)S(1)}, bf16[16,32,768]{2,1,0:T(8,128)(2,1)}, u32[]{:S(2)}) %copy-start) | copy-done | bytes 786456
  6.2 1.1 %copy-done.2 = f32[24,64,64]{2,1,0:T(8,128)S(1)} copy-done((f32[24,64,64]{2,1,0:T(8,128)S(1)}, f32[24,64,64]{2,1,0:T(8,128)}, u32[]{:S(2)}) %copy-start.2) | copy-done | bytes 393240
  7.3 0.9 copy-done.3
  8.3 0.9 copy-done.4
  9.4 0.6 collective-permute-done.beyond
  10.7 1.8 %collective-permute-start.2 = (bf16[23,8,768]{2,1,0:T(8,128)(2,1)S(1)}, bf16[23,8,768]{2,1,0:T(8,128)(2,1)S(1)}, u32[]{:S(2)}, u32[]{:S(2)}) collective-permute-start(bf16[23,8,768]{2,1,0:T(8,128)(2,1)S(1)} %get-tuple-element.45), channel_id=1, source_target_pairs={{0,1},{1,2},{2,3},{3,0},{4,5},{5,6},{6,7},{7,4},{8,9},{9,10},{10,1... | collective-permute-start | bytes 847880 | tf_op jit(solution)/shard_map/ppermute | solution.py:35
  12.5 0.8 collective-permute-start.7
  13.3 1.3 %collective-permute-start.3 = (bf16[48,768]{1,0:T(8,128)(2,1)}, bf16[48,768]{1,0:T(8,128)(2,1)S(1)}, u32[]{:S(2)}, u32[]{:S(2)}) collective-permute-start(bf16[48,768]{1,0:T(8,128)(2,1)} %param.14), channel_id=1, source_target_pairs={{0,1},{1,0},{2,3},{3,2},{4,5},{5,4},{6,7},{7,6},{8,9},{9,8},{10,11... | collective-permute-start | bytes 221192 | tf_op jit(solution)/shard_map/ppermute | solution.py:50
  14.6 1.5 %collective-permute-start.10 = (bf16[96,2304]{1,0:T(8,128)(2,1)S(1)}, bf16[96,2304]{1,0:T(8,128)(2,1)S(1)}, u32[]{:S(2)}, u32[]{:S(2)}) collective-permute-start(bf16[96,2304]{1,0:T(8,128)(2,1)S(1)} %get-tuple-element.48.refs_3_), channel_id=1, source_target_pairs={{0,4},{4,0},{8,12},{12,8},{1,5},{5,1},{9,13},{13,9},{2,6},{6,2},{1... | collective-permute-start | bytes 1327112 | tf_op jit(solution)/shard_map/ppermute | solution.py:50
  16.1 0.8 collective-permute-start.6
  16.9 4.7 %collective-permute-done.2.beside = bf16[23,8,768]{2,1,0:T(8,128)(2,1)S(1)} collective-permute-done((bf16[23,8,768]{2,1,0:T(8,128)(2,1)S(1)}, bf16[23,8,768]{2,1,0:T(8,128)(2,1)S(1)}, u32[]{:S(2)}, u32[]{:S(2)}) %collective-permute-start.2) | collective-permute-done | bytes 282656 | tf_op jit(solution)/shard_map/ppermute | solution.py:35
  21.6 3.4 %collective-permute-done.3 = bf16[48,768]{1,0:T(8,128)(2,1)S(1)} collective-permute-done((bf16[48,768]{1,0:T(8,128)(2,1)}, bf16[48,768]{1,0:T(8,128)(2,1)S(1)}, u32[]{:S(2)}, u32[]{:S(2)}) %collective-permute-start.3) | collective-permute-done | bytes 73760 | tf_op jit(solution)/shard_map/ppermute | solution.py:50
  25.0 0.9 pad_maximum_fusion
  26.0 8.6 %encode.1 = (bf16[512,768]{1,0:T(8,128)(2,1)S(1)}, bf16[512,768]{1,0:T(8,128)(2,1)S(1)}) custom-call(s32[3]{0:T(128)S(1)} %pad_add_fusion.place.refs_0_, f32[16,32,768]{2,1,0:T(8,128)S(1)} %get-tuple-element.49.tokens, bf16[7,32,768]{2,1,0:T(8,128)(2,1)S(1)} %collective-permute-done.1.above, bf16[23,8,768]{2,1,0:T(8,128)(2,1)S(1)} %collective-permute-done.2.beside, ...), custom_call_target="tpu_custom_call" | custom-call | flops 115000000 | tf_op jit(solution)/shard_map/encode/pallas_call | solution.py:187
  34.6 1.3 %collective-permute-start.8 = (bf16[96,1152]{1,0:T(8,128)(2,1)S(1)}, bf16[96,1152]{1,0:T(8,128)(2,1)S(1)}, u32[]{:S(2)}, u32[]{:S(2)}) collective-permute-start(bf16[96,1152]{1,0:T(8,128)(2,1)S(1)} %collective-permute-done.6.refs_5_), channel_id=1, source_target_pairs={{0,16},{16,0},{1,17},{17,1},{2,18},{18,2},{3,19},{19,3},{4,20},{20... | collective-permute-start | bytes 663560 | tf_op jit(solution)/shard_map/ppermute | solution.py:50
  35.9 0.7 collective-permute-start.9
  36.6 0.7 collective-permute-start.15
  37.6 1.1 %collective-permute-start.11 = (bf16[96,2304]{1,0:T(8,128)(2,1)S(1)}, bf16[96,2304]{1,0:T(8,128)(2,1)S(1)}, u32[]{:S(2)}, u32[]{:S(2)}) collective-permute-start(bf16[96,2304]{1,0:T(8,128)(2,1)S(1)} %collective-permute-done.7.refs_4_), channel_id=1, source_target_pairs={{0,4},{4,0},{8,12},{12,8},{1,5},{5,1},{9,13},{13,9},{2,6},{6,2},{1... | collective-permute-start | bytes 1327112 | tf_op jit(solution)/shard_map/ppermute | solution.py:50
  38.8 2.4 %collective-permute-done.8.refs_6_ = bf16[96,1152]{1,0:T(8,128)(2,1)S(1)} collective-permute-done((bf16[96,1152]{1,0:T(8,128)(2,1)S(1)}, bf16[96,1152]{1,0:T(8,128)(2,1)S(1)}, u32[]{:S(2)}, u32[]{:S(2)}) %collective-permute-start.8) | collective-permute-done | bytes 221216 | tf_op jit(solution)/shard_map/ppermute | solution.py:50
  41.2 1.4 %collective-permute-start.13 = (bf16[96,1152]{1,0:T(8,128)(2,1)S(1)}, bf16[96,1152]{1,0:T(8,128)(2,1)S(1)}, u32[]{:S(2)}, u32[]{:S(2)}) collective-permute-start(bf16[96,1152]{1,0:T(8,128)(2,1)S(1)} %collective-permute-done.8.refs_6_), channel_id=1, source_target_pairs={{0,4},{4,0},{8,12},{12,8},{1,5},{5,1},{9,13},{13,9},{2,6},{6,2},{1... | collective-permute-start | bytes 663560 | tf_op jit(solution)/shard_map/ppermute | solution.py:50
  42.6 2.4 %collective-permute-start.14 = (bf16[96,1152]{1,0:T(8,128)(2,1)S(1)}, bf16[96,1152]{1,0:T(8,128)(2,1)S(1)}, u32[]{:S(2)}, u32[]{:S(2)}) collective-permute-start(bf16[96,1152]{1,0:T(8,128)(2,1)S(1)} %collective-permute-done.9.refs_7_), channel_id=1, source_target_pairs={{0,4},{4,0},{8,12},{12,8},{1,5},{5,1},{9,13},{13,9},{2,6},{6,2},{1... | collective-permute-start | bytes 663560 | tf_op jit(solution)/shard_map/ppermute | solution.py:50
  45.0 1.8 %collective-permute-done.15.refs_13_ = bf16[96,1152]{1,0:T(8,128)(2,1)S(1)} collective-permute-done((bf16[96,1152]{1,0:T(8,128)(2,1)S(1)}, bf16[96,1152]{1,0:T(8,128)(2,1)S(1)}, u32[]{:S(2)}, u32[]{:S(2)}) %collective-permute-start.15) | collective-permute-done | bytes 221216 | tf_op jit(solution)/shard_map/ppermute | solution.py:539
  46.8 1.7 %collective-permute-start.16 = (bf16[96,1152]{1,0:T(8,128)(2,1)S(1)}, bf16[96,1152]{1,0:T(8,128)(2,1)S(1)}, u32[]{:S(2)}, u32[]{:S(2)}) collective-permute-start(bf16[96,1152]{1,0:T(8,128)(2,1)S(1)} %collective-permute-done.15.refs_13_), channel_id=1, source_target_pairs={{0,4},{4,0},{8,12},{12,8},{1,5},{5,1},{9,13},{13,9},{2,6},{6,2},{1... | collective-permute-start | bytes 663560 | tf_op jit(solution)/shard_map/ppermute | solution.py:50
  48.5 0.8 collective-permute-start.5
  49.6 8.6 %attend.1.refs_1_ = bf16[512,768]{1,0:T(8,128)(2,1)S(1)} custom-call(s32[3]{0:T(128)S(1)} %pad_add_fusion.place.refs_0_, bf16[512,768]{1,0:T(8,128)(2,1)S(1)} %get-tuple-element.53.refs_1_, f32[6,64,256]{2,1,0:T(8,128)S(1)} %get-tuple-element.54.refs_2_, bf16[96,2304]{1,0:T(8,128)(2,1)S(1)} %get-tuple-element.48.refs_3_, ...), custom_call_target="tpu_custom_call" | custom-call | flops 11500000256 | tf_op jit(solution)/shard_map/attend/pallas_call | solution.py:297
  58.6 1.2 %collective-permute-done.18.refs_6_ = bf16[192,768]{1,0:T(8,128)(2,1)S(1)} collective-permute-done((bf16[192,768]{1,0:T(8,128)(2,1)S(1)}, bf16[192,768]{1,0:T(8,128)(2,1)S(1)}, u32[]{:S(2)}, u32[]{:S(2)}) %collective-permute-start.18) | collective-permute-done | bytes 294944 | tf_op jit(solution)/shard_map/ppermute | solution.py:50
  59.8 3.1 %project.1 = (bf16[16,32,768]{2,1,0:T(8,128)(2,1)S(1)}, bf16[4,32,768]{2,1,0:T(8,128)(2,1)S(1)}, bf16[48,768]{1,0:T(8,128)(2,1)S(1)}, bf16[16,768]{1,0:T(8,128)(2,1)S(1)}) custom-call(s32[3]{0:T(128)S(1)} %pad_add_fusion.place.refs_0_, bf16[512,768]{1,0:T(8,128)(2,1)S(1)} %attend.1.refs_1_, bf16[512,768]{1,0:T(8,128)(2,1)S(1)} %get-tuple-element.58.refs_2_, ...), custom_call_target="tpu_custom_call" | custom-call | flops 3449999872 | tf_op jit(solution)/shard_map/project/pallas_call | solution.py:366
  63.4 1.4 %collective-permute-start.20 = (bf16[48,768]{1,0:T(8,128)(2,1)S(1)}, bf16[48,768]{1,0:T(8,128)(2,1)S(1)}, u32[]{:S(2)}, u32[]{:S(2)}) collective-permute-start(bf16[48,768]{1,0:T(8,128)(2,1)S(1)} %get-tuple-element.62), channel_id=1, source_target_pairs={{0,3},{1,0},{2,1},{3,2},{4,7},{5,4},{6,5},{7,6},{8,11},{9,8},{10,9... | collective-permute-start | bytes 221192 | tf_op jit(solution)/shard_map/ppermute | solution.py:35
  64.8 3.1 %collective-permute-start.21 = (bf16[16,768]{1,0:T(8,128)(2,1)S(1)}, bf16[16,768]{1,0:T(8,128)(2,1)S(1)}, u32[]{:S(2)}, u32[]{:S(2)}) collective-permute-start(bf16[16,768]{1,0:T(8,128)(2,1)S(1)} %get-tuple-element.63), channel_id=1, source_target_pairs={{0,15},{1,12},{2,13},{3,14},{4,3},{5,0},{6,1},{7,2},{8,7},{9,4},{1... | collective-permute-start | bytes 73736 | tf_op jit(solution)/shard_map/ppermute | solution.py:45
  68.0 1.1 %collective-permute-done.21.corner = bf16[16,768]{1,0:T(8,128)(2,1)S(1)} collective-permute-done((bf16[16,768]{1,0:T(8,128)(2,1)S(1)}, bf16[16,768]{1,0:T(8,128)(2,1)S(1)}, u32[]{:S(2)}, u32[]{:S(2)}) %collective-permute-start.21) | collective-permute-done | bytes 24608 | tf_op jit(solution)/shard_map/ppermute | solution.py:45
  69.1 1.6 %dispatch.1 = (bf16[512,768]{1,0:T(8,128)(2,1)S(1)}, bf16[64,768]{1,0:T(8,128)(2,1)S(1)}, bf16[64,768]{1,0:T(8,128)(2,1)S(1)}, bf16[64,768]{1,0:T(8,128)(2,1)S(1...) custom-call(s32[3]{0:T(128)S(1)} %pad_add_fusion.place.refs_0_, ...), custom_call_target="tpu_custom_call" | custom-call | tf_op jit(solution)/shard_map/dispatch/pallas_call | solution.py:429
  71.1 0.6 collective-permute-start.26
  71.7 1.3 %collective-permute-start.27 = (bf16[64,768]{1,0:T(8,128)(2,1)S(1)}, bf16[64,768]{1,0:T(8,128)(2,1)S(1)}, u32[]{:S(2)}, u32[]{:S(2)}) collective-permute-start(bf16[64,768]{1,0:T(8,128)(2,1)S(1)} %get-tuple-element.73), channel_id=1, source_target_pairs={{0,12},{4,8},{8,4},{12,0},{1,13},{5,9},{9,5},{13,1},{2,14},{6,10},... | collective-permute-start | bytes 294920 | tf_op jit(solution)/shard_map/ppermute | solution.py:50
  73.0 0.7 collective-permute-start.23
  73.7 1.5 %collective-permute-start.24 = (bf16[64,768]{1,0:T(8,128)(2,1)S(1)}, bf16[64,768]{1,0:T(8,128)(2,1)S(1)}, u32[]{:S(2)}, u32[]{:S(2)}) collective-permute-start(bf16[64,768]{1,0:T(8,128)(2,1)S(1)} %get-tuple-element.68), channel_id=1, source_target_pairs={{0,12},{4,8},{8,4},{12,0},{1,13},{5,9},{9,5},{13,1},{2,14},{6,10},... | collective-permute-start | bytes 294920 | tf_op jit(solution)/shard_map/ppermute | solution.py:50
  75.2 3.2 %collective-permute-done.27.refs_3_ = bf16[64,768]{1,0:T(8,128)(2,1)S(1)} collective-permute-done((bf16[64,768]{1,0:T(8,128)(2,1)S(1)}, bf16[64,768]{1,0:T(8,128)(2,1)S(1)}, u32[]{:S(2)}, u32[]{:S(2)}) %collective-permute-start.27) | collective-permute-done | bytes 98336 | tf_op jit(solution)/shard_map/ppermute | solution.py:50
  78.4 7.6 %experts.3 = (bf16[64,768]{1,0:T(8,128)(2,1)S(1)}, bf16[64,768]{1,0:T(8,128)(2,1)S(1)}, bf16[64,768]{1,0:T(8,128)(2,1)S(1)}, bf16[64,768]{1,0:T(8,128)(2,1)S(1)}) custom-call(bf16[64,768]{1,0:T(8,128)(2,1)S(1)} %get-tuple-element.70.refs_0_, bf16[64,768]{1,0:T(8,128)(2,1)S(1)} %collective-permute-done.25.refs_1_, ...), custom_call_target="tpu_custom_call" | custom-call | flops 8049999872 | tf_op jit(solution)/shard_map/experts/pallas_call | solution.py:471
  86.0 0.8 collective-permute-start.31
  86.8 1.4 %collective-permute-start.33 = (bf16[64,768]{1,0:T(8,128)(2,1)S(1)}, bf16[64,768]{1,0:T(8,128)(2,1)S(1)}, u32[]{:S(2)}, u32[]{:S(2)}) collective-permute-start(bf16[64,768]{1,0:T(8,128)(2,1)S(1)} %get-tuple-element.80), channel_id=1, source_target_pairs={{0,12},{4,8},{8,4},{12,0},{1,13},{5,9},{9,5},{13,1},{2,14},{6,10},... | collective-permute-start | bytes 294920 | tf_op jit(solution)/shard_map/ppermute | solution.py:50
  88.2 7.6 %experts.2 = (bf16[64,768]{1,0:T(8,128)(2,1)S(1)}, bf16[64,768]{1,0:T(8,128)(2,1)S(1)}, bf16[64,768]{1,0:T(8,128)(2,1)S(1)}, bf16[64,768]{1,0:T(8,128)(2,1)S(1)}) custom-call(bf16[64,768]{1,0:T(8,128)(2,1)S(1)} %get-tuple-element.65.refs_0_, bf16[64,768]{1,0:T(8,128)(2,1)S(1)} %collective-permute-done.22.refs_1_, ...), custom_call_target="tpu_custom_call" | custom-call | flops 8049999872 | tf_op jit(solution)/shard_map/experts/pallas_call | solution.py:471
  95.9 0.8 collective-permute-start.30
  96.6 1.4 %collective-permute-start.32 = (bf16[64,768]{1,0:T(8,128)(2,1)S(1)}, bf16[64,768]{1,0:T(8,128)(2,1)S(1)}, u32[]{:S(2)}, u32[]{:S(2)}) collective-permute-start(bf16[64,768]{1,0:T(8,128)(2,1)S(1)} %get-tuple-element.79), channel_id=1, source_target_pairs={{0,12},{4,8},{8,4},{12,0},{1,13},{5,9},{9,5},{13,1},{2,14},{6,10},... | collective-permute-start | bytes 294920 | tf_op jit(solution)/shard_map/ppermute | solution.py:50
  98.5 1.3 %collective-permute-done.30.refs_4_ = bf16[64,768]{1,0:T(8,128)(2,1)S(1)} collective-permute-done((bf16[64,768]{1,0:T(8,128)(2,1)S(1)}, bf16[64,768]{1,0:T(8,128)(2,1)S(1)}, u32[]{:S(2)}, u32[]{:S(2)}) %collective-permute-start.30) | collective-permute-done | bytes 98336 | tf_op jit(solution)/shard_map/ppermute | solution.py:50
  99.9 2.7 %collective-permute-done.32.refs_6_ = bf16[64,768]{1,0:T(8,128)(2,1)S(1)} collective-permute-done((bf16[64,768]{1,0:T(8,128)(2,1)S(1)}, bf16[64,768]{1,0:T(8,128)(2,1)S(1)}, u32[]{:S(2)}, u32[]{:S(2)}) %collective-permute-start.32) | collective-permute-done | bytes 98336 | tf_op jit(solution)/shard_map/ppermute | solution.py:50
  102.6 2.3 %combine.1 = bf16[512,768]{1,0:T(8,128)(2,1)} custom-call(s32[3]{0:T(128)S(1)} %pad_add_fusion.place.refs_0_, bf16[512,768]{1,0:T(8,128)(2,1)S(1)} %get-tuple-element.64.attended, s32[512,1]{1,0:T(8,128)S(1)} %select_n.42.position, s32[512,1]{1,0:T(8,128)S(1)} %select_n.43.constant_at, f32[16,768]{1,0:T(8,128)S(1)} %copy-done.1, ...), custom_call_target="tpu_custom_call" | custom-call | tf_op jit(solution)/shard_map/combine/pallas_call | solution.py:509
  (57 shorter events, 3.7 us)
Async XLA Ops:
  0.0 38.7 %copy-start.5 = (bf16[48,768]{1,0:T(8,128)(2,1)S(1)}, bf16[48,768]{1,0:T(8,128)(2,1)}, u32[]{:S(2)}) copy-start(bf16[48,768]{1,0:T(8,128)(2,1)} %param.14) | copy-start | bytes 221188
  1.0 9.0 %collective-permute-start.1 = (bf16[7,32,768]{2,1,0:T(8,128)(2,1)S(1)}, bf16[7,32,768]{2,1,0:T(8,128)(2,1)S(1)}, u32[]{:S(2)}, u32[]{:S(2)}) collective-permute-start(bf16[7,32,768]{2,1,0:T(8,128)(2,1)S(1)} %slice.3), channel_id=1, source_target_pairs={{0,4},{4,8},{8,12},{12,0},{1,5},{5,9},{9,13},{13,1},{2,6},{6,10},{... | collective-permute-start | bytes 1032200 | tf_op jit(solution)/shard_map/ppermute | solution.py:35
  3.7 6.4 %collective-permute-start = (bf16[48,2304]{1,0:T(8,128)(2,1)}, bf16[48,2304]{1,0:T(8,128)(2,1)S(1)}, u32[]{:S(2)}, u32[]{:S(2)}) collective-permute-start(bf16[48,2304]{1,0:T(8,128)(2,1)} %refs_0_.1), channel_id=1, source_target_pairs={{0,1},{1,0},{2,3},{3,2},{4,5},{5,4},{6,7},{7,6},{8,9},{9,8},{10,11... | collective-permute-start | bytes 663560 | tf_op jit(solution)/shard_map/ppermute | solution.py:50
  5.1 1.1 %copy-start = (bf16[16,32,768]{2,1,0:T(8,128)(2,1)S(1)}, bf16[16,32,768]{2,1,0:T(8,128)(2,1)}, u32[]{:S(2)}) copy-start(bf16[16,32,768]{2,1,0:T(8,128)(2,1)} %tokens.1) | copy-start | bytes 2359300
  6.2 1.1 %copy-start.2 = (f32[24,64,64]{2,1,0:T(8,128)S(1)}, f32[24,64,64]{2,1,0:T(8,128)}, u32[]{:S(2)}) copy-start(f32[24,64,64]{2,1,0:T(8,128)} %rel_bias.1) | copy-start | bytes 1179652
  7.3 0.9 copy-start.3
  8.3 0.9 copy-start.4
  10.7 10.9 %collective-permute-start.2 = (bf16[23,8,768]{2,1,0:T(8,128)(2,1)S(1)}, bf16[23,8,768]{2,1,0:T(8,128)(2,1)S(1)}, u32[]{:S(2)}, u32[]{:S(2)}) collective-permute-start(bf16[23,8,768]{2,1,0:T(8,128)(2,1)S(1)} %get-tuple-element.45), channel_id=1, source_target_pairs={{0,1},{1,2},{2,3},{3,0},{4,5},{5,6},{6,7},{7,4},{8,9},{9,10},{10,1... | collective-permute-start | bytes 847880 | tf_op jit(solution)/shard_map/ppermute | solution.py:35
  12.5 22.2 %collective-permute-start.7 = (bf16[96,2304]{1,0:T(8,128)(2,1)S(1)}, bf16[96,2304]{1,0:T(8,128)(2,1)S(1)}, u32[]{:S(2)}, u32[]{:S(2)}) collective-permute-start(bf16[96,2304]{1,0:T(8,128)(2,1)S(1)} %get-tuple-element.48.refs_3_), channel_id=1, source_target_pairs={{0,8},{4,12},{8,0},{12,4},{1,9},{5,13},{9,1},{13,5},{2,10},{6,14},... | collective-permute-start | bytes 1327112 | tf_op jit(solution)/shard_map/ppermute | solution.py:50
  13.3 11.7 %collective-permute-start.3 = (bf16[48,768]{1,0:T(8,128)(2,1)}, bf16[48,768]{1,0:T(8,128)(2,1)S(1)}, u32[]{:S(2)}, u32[]{:S(2)}) collective-permute-start(bf16[48,768]{1,0:T(8,128)(2,1)} %param.14), channel_id=1, source_target_pairs={{0,1},{1,0},{2,3},{3,2},{4,5},{5,4},{6,7},{7,6},{8,9},{9,8},{10,11... | collective-permute-start | bytes 221192 | tf_op jit(solution)/shard_map/ppermute | solution.py:50
  14.6 24.1 %collective-permute-start.10 = (bf16[96,2304]{1,0:T(8,128)(2,1)S(1)}, bf16[96,2304]{1,0:T(8,128)(2,1)S(1)}, u32[]{:S(2)}, u32[]{:S(2)}) collective-permute-start(bf16[96,2304]{1,0:T(8,128)(2,1)S(1)} %get-tuple-element.48.refs_3_), channel_id=1, source_target_pairs={{0,4},{4,0},{8,12},{12,8},{1,5},{5,1},{9,13},{13,9},{2,6},{6,2},{1... | collective-permute-start | bytes 1327112 | tf_op jit(solution)/shard_map/ppermute | solution.py:50
  16.1 18.5 %collective-permute-start.6 = (bf16[96,1152]{1,0:T(8,128)(2,1)S(1)}, bf16[96,1152]{1,0:T(8,128)(2,1)S(1)}, u32[]{:S(2)}, u32[]{:S(2)}) collective-permute-start(bf16[96,1152]{1,0:T(8,128)(2,1)S(1)} %get-tuple-element.47), channel_id=1, source_target_pairs={{0,2},{1,3},{2,0},{3,1},{4,6},{5,7},{6,4},{7,5},{8,10},{9,11},{10,... | collective-permute-start | bytes 663560 | tf_op jit(solution)/shard_map/ppermute | solution.py:50
  25.9 11.7 %collective-permute-start.4 = (bf16[96,768]{1,0:T(8,128)(2,1)S(1)}, bf16[96,768]{1,0:T(8,128)(2,1)S(1)}, u32[]{:S(2)}, u32[]{:S(2)}) collective-permute-start(bf16[96,768]{1,0:T(8,128)(2,1)S(1)} %pad_maximum_fusion), channel_id=1, source_target_pairs={{0,2},{1,3},{2,0},{3,1},{4,6},{5,7},{6,4},{7,5},{8,10},{9,11},{10,... | collective-permute-start | bytes 442376 | tf_op jit(solution)/shard_map/ppermute | solution.py:50
  34.6 6.6 %collective-permute-start.8 = (bf16[96,1152]{1,0:T(8,128)(2,1)S(1)}, bf16[96,1152]{1,0:T(8,128)(2,1)S(1)}, u32[]{:S(2)}, u32[]{:S(2)}) collective-permute-start(bf16[96,1152]{1,0:T(8,128)(2,1)S(1)} %collective-permute-done.6.refs_5_), channel_id=1, source_target_pairs={{0,16},{16,0},{1,17},{17,1},{2,18},{18,2},{3,19},{19,3},{4,20},{20... | collective-permute-start | bytes 663560 | tf_op jit(solution)/shard_map/ppermute | solution.py:50
  35.9 6.7 %collective-permute-start.9 = (bf16[96,1152]{1,0:T(8,128)(2,1)S(1)}, bf16[96,1152]{1,0:T(8,128)(2,1)S(1)}, u32[]{:S(2)}, u32[]{:S(2)}) collective-permute-start(bf16[96,1152]{1,0:T(8,128)(2,1)S(1)} %collective-permute-done.6.refs_5_), channel_id=1, source_target_pairs={{0,8},{4,12},{8,0},{12,4},{1,9},{5,13},{9,1},{13,5},{2,10},{6,14},... | collective-permute-start | bytes 663560 | tf_op jit(solution)/shard_map/ppermute | solution.py:50
  36.6 10.2 %collective-permute-start.15 = (bf16[96,1152]{1,0:T(8,128)(2,1)S(1)}, bf16[96,1152]{1,0:T(8,128)(2,1)S(1)}, u32[]{:S(2)}, u32[]{:S(2)}) collective-permute-start(bf16[96,1152]{1,0:T(8,128)(2,1)S(1)} %collective-permute-done.6.refs_5_), channel_id=1, source_target_pairs={{0,24},{4,28},{8,16},{12,20},{16,8},{20,12},{24,0},{28,4},{1,25},{... | collective-permute-start | bytes 663560 | tf_op jit(solution)/shard_map/ppermute | solution.py:539
  37.6 12.0 %collective-permute-start.11 = (bf16[96,2304]{1,0:T(8,128)(2,1)S(1)}, bf16[96,2304]{1,0:T(8,128)(2,1)S(1)}, u32[]{:S(2)}, u32[]{:S(2)}) collective-permute-start(bf16[96,2304]{1,0:T(8,128)(2,1)S(1)} %collective-permute-done.7.refs_4_), channel_id=1, source_target_pairs={{0,4},{4,0},{8,12},{12,8},{1,5},{5,1},{9,13},{13,9},{2,6},{6,2},{1... | collective-permute-start | bytes 1327112 | tf_op jit(solution)/shard_map/ppermute | solution.py:50
  38.7 9.8 %collective-permute-start.12 = (bf16[96,1152]{1,0:T(8,128)(2,1)S(1)}, bf16[96,1152]{1,0:T(8,128)(2,1)S(1)}, u32[]{:S(2)}, u32[]{:S(2)}) collective-permute-start(bf16[96,1152]{1,0:T(8,128)(2,1)S(1)} %collective-permute-done.6.refs_5_), channel_id=1, source_target_pairs={{0,4},{4,0},{8,12},{12,8},{1,5},{5,1},{9,13},{13,9},{2,6},{6,2},{1... | collective-permute-start | bytes 663560 | tf_op jit(solution)/shard_map/ppermute | solution.py:50
  41.2 8.1 %collective-permute-start.13 = (bf16[96,1152]{1,0:T(8,128)(2,1)S(1)}, bf16[96,1152]{1,0:T(8,128)(2,1)S(1)}, u32[]{:S(2)}, u32[]{:S(2)}) collective-permute-start(bf16[96,1152]{1,0:T(8,128)(2,1)S(1)} %collective-permute-done.8.refs_6_), channel_id=1, source_target_pairs={{0,4},{4,0},{8,12},{12,8},{1,5},{5,1},{9,13},{13,9},{2,6},{6,2},{1... | collective-permute-start | bytes 663560 | tf_op jit(solution)/shard_map/ppermute | solution.py:50
  42.6 6.9 %collective-permute-start.14 = (bf16[96,1152]{1,0:T(8,128)(2,1)S(1)}, bf16[96,1152]{1,0:T(8,128)(2,1)S(1)}, u32[]{:S(2)}, u32[]{:S(2)}) collective-permute-start(bf16[96,1152]{1,0:T(8,128)(2,1)S(1)} %collective-permute-done.9.refs_7_), channel_id=1, source_target_pairs={{0,4},{4,0},{8,12},{12,8},{1,5},{5,1},{9,13},{13,9},{2,6},{6,2},{1... | collective-permute-start | bytes 663560 | tf_op jit(solution)/shard_map/ppermute | solution.py:50
  46.8 2.8 %collective-permute-start.16 = (bf16[96,1152]{1,0:T(8,128)(2,1)S(1)}, bf16[96,1152]{1,0:T(8,128)(2,1)S(1)}, u32[]{:S(2)}, u32[]{:S(2)}) collective-permute-start(bf16[96,1152]{1,0:T(8,128)(2,1)S(1)} %collective-permute-done.15.refs_13_), channel_id=1, source_target_pairs={{0,4},{4,0},{8,12},{12,8},{1,5},{5,1},{9,13},{13,9},{2,6},{6,2},{1... | collective-permute-start | bytes 663560 | tf_op jit(solution)/shard_map/ppermute | solution.py:50
  48.5 9.7 %collective-permute-start.5 = (bf16[192,768]{1,0:T(8,128)(2,1)S(1)}, bf16[192,768]{1,0:T(8,128)(2,1)S(1)}, u32[]{:S(2)}, u32[]{:S(2)}) collective-permute-start(bf16[192,768]{1,0:T(8,128)(2,1)S(1)} %constant_dynamic-update-slice_fusion.refs_3_), channel_id=1, source_target_pairs={{0,8},{4,12},{8,0},{12,4},{1,9},{5,13},{9,1},{13,5},{2,10},{6,14},... | collective-permute-start | bytes 884744 | tf_op jit(solution)/shard_map/ppermute | solution.py:50
  49.2 9.4 %collective-permute-start.17 = (bf16[192,768]{1,0:T(8,128)(2,1)S(1)}, bf16[192,768]{1,0:T(8,128)(2,1)S(1)}, u32[]{:S(2)}, u32[]{:S(2)}) collective-permute-start(bf16[192,768]{1,0:T(8,128)(2,1)S(1)} %constant_dynamic-update-slice_fusion.refs_3_), channel_id=1, source_target_pairs={{0,4},{4,0},{8,12},{12,8},{1,5},{5,1},{9,13},{13,9},{2,6},{6,2},{1... | collective-permute-start | bytes 884744 | tf_op jit(solution)/shard_map/ppermute | solution.py:50
  49.6 18.3 %copy-start.6 = (s32[16,32]{1,0:T(8,128)S(1)}, s32[16,32]{1,0:T(8,128)}, u32[]{:S(2)}) copy-start(s32[16,32]{1,0:T(8,128)} %param.21) | copy-start | bytes 6148
  49.6 18.3 %copy-start.7 = (s32[16,32]{1,0:T(8,128)S(1)}, s32[16,32]{1,0:T(8,128)}, u32[]{:S(2)}) copy-start(s32[16,32]{1,0:T(8,128)} %param.19) | copy-start | bytes 6148
  49.6 18.3 %copy-start.8 = (s32[16,32]{1,0:T(8,128)S(1)}, s32[16,32]{1,0:T(8,128)}, u32[]{:S(2)}) copy-start(s32[16,32]{1,0:T(8,128)} %param.20) | copy-start | bytes 6148
  58.2 1.6 %collective-permute-start.18 = (bf16[192,768]{1,0:T(8,128)(2,1)S(1)}, bf16[192,768]{1,0:T(8,128)(2,1)S(1)}, u32[]{:S(2)}, u32[]{:S(2)}) collective-permute-start(bf16[192,768]{1,0:T(8,128)(2,1)S(1)} %collective-permute-done.5.refs_4_), channel_id=1, source_target_pairs={{0,4},{4,0},{8,12},{12,8},{1,5},{5,1},{9,13},{13,9},{2,6},{6,2},{1... | collective-permute-start | bytes 884744 | tf_op jit(solution)/shard_map/ppermute | solution.py:50
  63.0 6.2 %collective-permute-start.19 = (bf16[4,32,768]{2,1,0:T(8,128)(2,1)S(1)}, bf16[4,32,768]{2,1,0:T(8,128)(2,1)S(1)}, u32[]{:S(2)}, u32[]{:S(2)}) collective-permute-start(bf16[4,32,768]{2,1,0:T(8,128)(2,1)S(1)} %get-tuple-element.61), channel_id=1, source_target_pairs={{0,12},{4,0},{8,4},{12,8},{1,13},{5,1},{9,5},{13,9},{2,14},{6,2},{... | collective-permute-start | bytes 589832 | tf_op jit(solution)/shard_map/ppermute | solution.py:35
  63.4 5.8 %collective-permute-start.20 = (bf16[48,768]{1,0:T(8,128)(2,1)S(1)}, bf16[48,768]{1,0:T(8,128)(2,1)S(1)}, u32[]{:S(2)}, u32[]{:S(2)}) collective-permute-start(bf16[48,768]{1,0:T(8,128)(2,1)S(1)} %get-tuple-element.62), channel_id=1, source_target_pairs={{0,3},{1,0},{2,1},{3,2},{4,7},{5,4},{6,5},{7,6},{8,11},{9,8},{10,9... | collective-permute-start | bytes 221192 | tf_op jit(solution)/shard_map/ppermute | solution.py:35
  64.8 4.3 %collective-permute-start.21 = (bf16[16,768]{1,0:T(8,128)(2,1)S(1)}, bf16[16,768]{1,0:T(8,128)(2,1)S(1)}, u32[]{:S(2)}, u32[]{:S(2)}) collective-permute-start(bf16[16,768]{1,0:T(8,128)(2,1)S(1)} %get-tuple-element.63), channel_id=1, source_target_pairs={{0,15},{1,12},{2,13},{3,14},{4,3},{5,0},{6,1},{7,2},{8,7},{9,4},{1... | collective-permute-start | bytes 73736 | tf_op jit(solution)/shard_map/ppermute | solution.py:45
  70.8 2.9 %collective-permute-start.25 = (bf16[64,768]{1,0:T(8,128)(2,1)S(1)}, bf16[64,768]{1,0:T(8,128)(2,1)S(1)}, u32[]{:S(2)}, u32[]{:S(2)}) collective-permute-start(bf16[64,768]{1,0:T(8,128)(2,1)S(1)} %get-tuple-element.71), channel_id=1, source_target_pairs={{0,4},{4,0},{8,12},{12,8},{1,5},{5,1},{9,13},{13,9},{2,6},{6,2},{1... | collective-permute-start | bytes 294920 | tf_op jit(solution)/shard_map/ppermute | solution.py:50
  71.1 4.1 %collective-permute-start.26 = (bf16[64,768]{1,0:T(8,128)(2,1)S(1)}, bf16[64,768]{1,0:T(8,128)(2,1)S(1)}, u32[]{:S(2)}, u32[]{:S(2)}) collective-permute-start(bf16[64,768]{1,0:T(8,128)(2,1)S(1)} %get-tuple-element.72), channel_id=1, source_target_pairs={{0,8},{4,12},{8,0},{12,4},{1,9},{5,13},{9,1},{13,5},{2,10},{6,14},... | collective-permute-start | bytes 294920 | tf_op jit(solution)/shard_map/ppermute | solution.py:50
  71.7 6.7 %collective-permute-start.27 = (bf16[64,768]{1,0:T(8,128)(2,1)S(1)}, bf16[64,768]{1,0:T(8,128)(2,1)S(1)}, u32[]{:S(2)}, u32[]{:S(2)}) collective-permute-start(bf16[64,768]{1,0:T(8,128)(2,1)S(1)} %get-tuple-element.73), channel_id=1, source_target_pairs={{0,12},{4,8},{8,4},{12,0},{1,13},{5,9},{9,5},{13,1},{2,14},{6,10},... | collective-permute-start | bytes 294920 | tf_op jit(solution)/shard_map/ppermute | solution.py:50
  73.0 13.8 %collective-permute-start.22 = (bf16[64,768]{1,0:T(8,128)(2,1)S(1)}, bf16[64,768]{1,0:T(8,128)(2,1)S(1)}, u32[]{:S(2)}, u32[]{:S(2)}) collective-permute-start(bf16[64,768]{1,0:T(8,128)(2,1)S(1)} %get-tuple-element.66), channel_id=1, source_target_pairs={{0,4},{4,0},{8,12},{12,8},{1,5},{5,1},{9,13},{13,9},{2,6},{6,2},{1... | collective-permute-start | bytes 294920 | tf_op jit(solution)/shard_map/ppermute | solution.py:50
  73.0 15.2 %collective-permute-start.23 = (bf16[64,768]{1,0:T(8,128)(2,1)S(1)}, bf16[64,768]{1,0:T(8,128)(2,1)S(1)}, u32[]{:S(2)}, u32[]{:S(2)}) collective-permute-start(bf16[64,768]{1,0:T(8,128)(2,1)S(1)} %get-tuple-element.67), channel_id=1, source_target_pairs={{0,8},{4,12},{8,0},{12,4},{1,9},{5,13},{9,1},{13,5},{2,10},{6,14},... | collective-permute-start | bytes 294920 | tf_op jit(solution)/shard_map/ppermute | solution.py:50
  73.7 14.5 %collective-permute-start.24 = (bf16[64,768]{1,0:T(8,128)(2,1)S(1)}, bf16[64,768]{1,0:T(8,128)(2,1)S(1)}, u32[]{:S(2)}, u32[]{:S(2)}) collective-permute-start(bf16[64,768]{1,0:T(8,128)(2,1)S(1)} %get-tuple-element.68), channel_id=1, source_target_pairs={{0,12},{4,8},{8,4},{12,0},{1,13},{5,9},{9,5},{13,1},{2,14},{6,10},... | collective-permute-start | bytes 294920 | tf_op jit(solution)/shard_map/ppermute | solution.py:50
  86.0 10.6 %collective-permute-start.29 = (bf16[64,768]{1,0:T(8,128)(2,1)S(1)}, bf16[64,768]{1,0:T(8,128)(2,1)S(1)}, u32[]{:S(2)}, u32[]{:S(2)}) collective-permute-start(bf16[64,768]{1,0:T(8,128)(2,1)S(1)} %get-tuple-element.76), channel_id=1, source_target_pairs={{0,4},{4,0},{8,12},{12,8},{1,5},{5,1},{9,13},{13,9},{2,6},{6,2},{1... | collective-permute-start | bytes 294920 | tf_op jit(solution)/shard_map/ppermute | solution.py:50
  86.0 12.5 %collective-permute-start.31 = (bf16[64,768]{1,0:T(8,128)(2,1)S(1)}, bf16[64,768]{1,0:T(8,128)(2,1)S(1)}, u32[]{:S(2)}, u32[]{:S(2)}) collective-permute-start(bf16[64,768]{1,0:T(8,128)(2,1)S(1)} %get-tuple-element.78), channel_id=1, source_target_pairs={{0,8},{4,12},{8,0},{12,4},{1,9},{5,13},{9,1},{13,5},{2,10},{6,14},... | collective-permute-start | bytes 294920 | tf_op jit(solution)/shard_map/ppermute | solution.py:50
  86.8 11.7 %collective-permute-start.33 = (bf16[64,768]{1,0:T(8,128)(2,1)S(1)}, bf16[64,768]{1,0:T(8,128)(2,1)S(1)}, u32[]{:S(2)}, u32[]{:S(2)}) collective-permute-start(bf16[64,768]{1,0:T(8,128)(2,1)S(1)} %get-tuple-element.80), channel_id=1, source_target_pairs={{0,12},{4,8},{8,4},{12,0},{1,13},{5,9},{9,5},{13,1},{2,14},{6,10},... | collective-permute-start | bytes 294920 | tf_op jit(solution)/shard_map/ppermute | solution.py:50
  88.2 14.4 %copy-start.1 = (f32[16,768]{1,0:T(8,128)S(1)}, f32[16,768]{1,0:T(8,128)}, u32[]{:S(2)}) copy-start(f32[16,768]{1,0:T(8,128)} %table.1) | copy-start | bytes 147460
  95.8 2.8 %collective-permute-start.28 = (bf16[64,768]{1,0:T(8,128)(2,1)S(1)}, bf16[64,768]{1,0:T(8,128)(2,1)S(1)}, u32[]{:S(2)}, u32[]{:S(2)}) collective-permute-start(bf16[64,768]{1,0:T(8,128)(2,1)S(1)} %get-tuple-element.75), channel_id=1, source_target_pairs={{0,4},{4,0},{8,12},{12,8},{1,5},{5,1},{9,13},{13,9},{2,6},{6,2},{1... | collective-permute-start | bytes 294920 | tf_op jit(solution)/shard_map/ppermute | solution.py:50
  95.9 4.0 %collective-permute-start.30 = (bf16[64,768]{1,0:T(8,128)(2,1)S(1)}, bf16[64,768]{1,0:T(8,128)(2,1)S(1)}, u32[]{:S(2)}, u32[]{:S(2)}) collective-permute-start(bf16[64,768]{1,0:T(8,128)(2,1)S(1)} %get-tuple-element.77), channel_id=1, source_target_pairs={{0,8},{4,12},{8,0},{12,4},{1,9},{5,13},{9,1},{13,5},{2,10},{6,14},... | collective-permute-start | bytes 294920 | tf_op jit(solution)/shard_map/ppermute | solution.py:50
  96.6 5.9 %collective-permute-start.32 = (bf16[64,768]{1,0:T(8,128)(2,1)S(1)}, bf16[64,768]{1,0:T(8,128)(2,1)S(1)}, u32[]{:S(2)}, u32[]{:S(2)}) collective-permute-start(bf16[64,768]{1,0:T(8,128)(2,1)S(1)} %get-tuple-element.79), channel_id=1, source_target_pairs={{0,12},{4,8},{8,4},{12,0},{1,13},{5,9},{9,5},{13,1},{2,14},{6,10},... | collective-permute-start | bytes 294920 | tf_op jit(solution)/shard_map/ppermute | solution.py:50
